TPU v7x, 256 devices: a whole 4x4x8 slice. The times are simulated.
256 devices in a mesh: tm: 4 (over x_lo, core), space: 64 (over x_hi, y, z).
Axes of the slice: x: 4 (x_hi: 2, x_lo: 2; x = x_hi * 2 + x_lo), y: 4, z: 8, core: 2. Of those that a mesh axis runs over, the one named last changes fastest.
Arguments:
- tokens: bfloat16 [2, 4, 6144, 1152], P(None, 'tm', 'space'), may hold values from -6 to 6
- modulation: float32 [6, 1152], replicated, may hold values from -3 to 3
- spatial_qkv: bfloat16 [1152, 3456], P('space'), may hold values from -0.1875 to 0.1875
- spatial_out: bfloat16 [1152, 1152], P('space'), may hold values from -0.1875 to 0.1875
- temporal_qkv: bfloat16 [1152, 3456], P('space'), may hold values from -0.1875 to 0.1875
- temporal_out: bfloat16 [1152, 1152], P('space'), may hold values from -0.1875 to 0.1875
- norm_gains: float32 [4, 72], replicated, may hold values from 1 to 2.5
Outputs:
- block_out: bfloat16 [2, 4, 6144, 1152], P(None, 'tm', 'space')
All inputs are finite; a program needn't handle non-finite values.
Results may differ from a plain program's by a relative error of at most 0.01.
Values may be sent and summed in bfloat16 or wider, within the bound.
No kernel may reach another device: no remote copies, remote signals or barrier semaphores. Data moves between devices by JAX's collectives and lax.ppermute only.
A program may use at most 128 MiB of HBM per device.

v0:
```python
import math

import jax
import jax.numpy as jnp
from jax import lax
from jax.sharding import PartitionSpec as P

HEADS = 16


def layer_norm(values):
    mean_val = jnp.mean(values, -1, keepdims=True)
    centred = values - mean_val
    variance = jnp.mean(centred * centred, -1, keepdims=True)
    return centred * lax.rsqrt(variance + 1e-06)


def rms_heads(values, gain):
    return values * lax.rsqrt(jnp.mean(values * values, -1, keepdims=True) + 1e-06) * gain


def per_device(
    tokens, modulation, spatial_qkv, spatial_out, temporal_qkv, temporal_out, norm_gains
):
    clip_count = tokens.shape[0]
    width = tokens.shape[3]
    tok_rows = tokens.shape[2]
    all_rows = clip_count * tok_rows
    head_dim = width // HEADS
    factor = 1.0 / math.sqrt(head_dim)
    full_qkv_a, full_out_a, full_qkv_b, full_out_b = (
        lax.all_gather(spatial_qkv, "space", axis=0, tiled=True),
        lax.all_gather(spatial_out, "space", axis=0, tiled=True),
        lax.all_gather(temporal_qkv, "space", axis=0, tiled=True),
        lax.all_gather(temporal_out, "space", axis=0, tiled=True),
    )
    start = tokens[:, 0].reshape(all_rows, width).astype(jnp.float32)
    normed = (layer_norm(start) * (1.0 + modulation[1]) + modulation[0]).astype(jnp.bfloat16)
    projected = jnp.dot(normed, full_qkv_a, preferred_element_type=jnp.float32).reshape(
        all_rows, 3, HEADS, head_dim
    )
    query_a = rms_heads(projected[:, 0], norm_gains[0]).astype(jnp.bfloat16)
    key_a = rms_heads(projected[:, 1], norm_gains[1]).astype(jnp.bfloat16)
    value_a = projected[:, 2].astype(jnp.bfloat16)
    space_count = lax.axis_size("space")
    heads_slot = max(1, HEADS // space_count)
    query_split = max(1, space_count // HEADS)
    groups = HEADS // heads_slot
    sub_rows = tok_rows // query_split
    query_send = query_a.reshape(clip_count, query_split, sub_rows, groups, heads_slot, head_dim)
    query_send = query_send.transpose(3, 1, 0, 2, 4, 5).reshape(
        space_count, clip_count * sub_rows * heads_slot * head_dim
    )
    pairs = jnp.stack(
        [
            key_a.reshape(clip_count, tok_rows, groups, heads_slot, head_dim),
            value_a.reshape(clip_count, tok_rows, groups, heads_slot, head_dim),
        ],
        axis=4,
    )
    pairs = pairs.transpose(2, 0, 1, 3, 4, 5).reshape(
        groups, 1, clip_count * tok_rows * heads_slot * 2 * head_dim
    )
    pair_send = jnp.broadcast_to(pairs, (groups, query_split, pairs.shape[2])).reshape(
        space_count, pairs.shape[2]
    )
    query_recv, pair_recv = (
        lax.all_to_all(query_send, "space", split_axis=0, concat_axis=1, tiled=True),
        lax.all_to_all(pair_send, "space", split_axis=0, concat_axis=1, tiled=True),
    )
    query_count = space_count * sub_rows
    queries = query_recv.reshape(space_count, clip_count, sub_rows, heads_slot, head_dim)
    queries = queries.transpose(1, 0, 2, 3, 4).reshape(
        clip_count, query_count, heads_slot, head_dim
    )
    key_values = pair_recv.reshape(space_count, clip_count, tok_rows, heads_slot, 2, head_dim)
    key_values = key_values.transpose(1, 0, 2, 3, 4, 5).reshape(
        clip_count, space_count * tok_rows, heads_slot, 2, head_dim
    )
    block_rows = math.gcd(query_count, 512)

    def clip_attention(triple):
        clip_queries, clip_keys, clip_values = triple

        def one_block(query_block):
            scores = (
                jnp.einsum(
                    "qhd,khd->hqk", query_block, clip_keys, preferred_element_type=jnp.float32
                )
                * factor
            )
            expo = jnp.exp(scores)
            totals = jnp.sum(expo, -1)
            result = jnp.einsum(
                "hqk,khd->qhd",
                expo.astype(jnp.bfloat16),
                clip_values,
                preferred_element_type=jnp.float32,
            )
            return (result / totals.T[:, :, None]).astype(jnp.bfloat16)

        blocks = lax.map(
            one_block,
            clip_queries.reshape(query_count // block_rows, block_rows, heads_slot, head_dim),
        )
        return blocks.reshape(query_count, heads_slot, head_dim)

    attended = lax.map(clip_attention, (queries, key_values[:, :, :, 0], key_values[:, :, :, 1]))
    attended = attended.reshape(clip_count, space_count, sub_rows, heads_slot, head_dim)
    attended = attended.transpose(1, 0, 2, 3, 4).reshape(
        space_count, clip_count * sub_rows * heads_slot * head_dim
    )
    returned = lax.all_to_all(attended, "space", split_axis=0, concat_axis=0, tiled=True)
    returned = returned.reshape(groups, query_split, clip_count, sub_rows, heads_slot, head_dim)
    returned = returned.transpose(2, 1, 3, 0, 4, 5).reshape(all_rows, width)
    branch_a = jnp.dot(returned, full_out_a, preferred_element_type=jnp.float32)
    resid = start + modulation[2] * branch_a
    normed_b = (layer_norm(resid) * (1.0 + modulation[4]) + modulation[3]).astype(jnp.bfloat16)
    proj_b = jnp.dot(normed_b, full_qkv_b, preferred_element_type=jnp.float32).reshape(
        all_rows, 3, HEADS, head_dim
    )
    query_b = rms_heads(proj_b[:, 0], norm_gains[2]).astype(jnp.bfloat16)
    key_b = rms_heads(proj_b[:, 1], norm_gains[3]).astype(jnp.bfloat16)
    value_b = proj_b[:, 2].astype(jnp.bfloat16)
    own_pairs = jnp.concatenate(
        [key_b.reshape(all_rows, width), value_b.reshape(all_rows, width)], axis=1
    )[None]
    gathered = lax.all_gather(own_pairs, "tm", axis=0, tiled=True)
    frame_count = gathered.shape[0]
    keys_all = gathered[:, :, :width].reshape(frame_count, all_rows, HEADS, head_dim)
    values_all = gathered[:, :, width:].reshape(frame_count, all_rows, HEADS, head_dim)
    scores = (
        jnp.einsum("lhd,glhd->lhg", query_b.astype(jnp.float32), keys_all.astype(jnp.float32))
        * factor
    )
    expo = jnp.exp(scores)
    totals = jnp.sum(expo, -1)
    rounded = lax.optimization_barrier(expo.astype(jnp.bfloat16)).astype(jnp.float32)
    mixed = jnp.einsum("lhg,glhd->lhd", rounded, values_all.astype(jnp.float32))
    mixed = (mixed / totals[..., None]).astype(jnp.bfloat16).reshape(all_rows, width)
    branch_b = jnp.dot(mixed, full_out_b, preferred_element_type=jnp.float32)
    result = resid + modulation[5] * branch_b
    return result.astype(jnp.bfloat16).reshape(clip_count, 1, tok_rows, width)


def solution(mesh):
    in_specs = (
        P(None, "tm", "space", None),
        P(),
        P("space", None),
        P("space", None),
        P("space", None),
        P("space", None),
        P(),
    )
    out_specs = P(None, "tm", "space", None)
    return jax.shard_map(
        per_device, mesh=mesh, in_specs=in_specs, out_specs=out_specs, check_vma=False
    )
```

profile of v0, /device:TPU:1, one launch (start us, length us, event | category | flops | bytes accessed | tf_op | source)
XLA Modules:
  0.0 708.0 jit_solution(7978633542148314903)
XLA Ops:
  15.8 163.4 %all-gather.13.cloned.1.call-done = bf16[64,18,3456]{2,1,0:T(8,128)(2,1)} async-done(((bf16[1,18,3456]{2,1,0:T(8,128)(2,1)}), bf16[64,18,3456]{2,1,0:T(8,128)(2,1)}) %all-gather.13.cloned.1.call-update) | async-done | bytes 7962640 | tf_op jit(solution)/shard_map/all_gather | solution.py:32
  179.2 13.2 %reshape.281 = bf16[1152,3456]{1,0:T(8,128)(2,1)} reshape(bf16[64,18,3456]{2,1,0:T(8,128)(2,1)} %all-gather.13.cloned.1.call-done) | data formatting | bytes 15925248
  192.3 11.5 %copy.145 = bf16[3456,1152]{1,0:T(8,128)(2,1)} copy(bf16[3456,1152]{0,1:T(8,128)(2,1)} %bitcast.161) | data formatting | bytes 15925248 | tf_op jit(solution)/shard_map/dot_general | solution.py:39
  203.9 5.8 fusion.45
  216.8 3.2 reduce.28
  221.3 8.0 %all-to-all-start = ((bf16[64,2,1728]{2,1,0:T(2,128)(2,1)}), bf16[64,2,1728]{2,1,0:T(2,128)(2,1)}, u32[]{:S(2)}, u32[]{:S(2)}) async-start(bf16[64,2,1728]{2,1,0:T(2,128)(2,1)} %reshape.302), calls=%async_computation | async-start | bytes 917504 | tf_op jit(solution)/shard_map/all_to_all | solution.py:68
  232.4 2.6 copy.154
  234.9 3.7 broadcast_in_dim.17
  240.7 7.7 %all_to_all.33 = bf16[64,1,27648]{2,1,0:T(2,128)(2,1)} reshape(bf16[16,4,27648]{2,1,0:T(4,128)(2,1)S(1)} %broadcast_in_dim.18) | data formatting | bytes 7077888 | tf_op jit(solution)/shard_map/all_to_all | solution.py:69
  248.4 63.8 %reduce.29 = bf16[64,27648]{1,0:T(8,128)(2,1)S(1)} reduce(bf16[64,1,27648]{2,1,0:T(2,128)(2,1)} %all_to_all.33, bf16[]{:T(256)} %broadcast.215), dimensions={1}, to_apply=%all_to_all.33.reduce_sub_computation | reduce | bytes 7077890 | tf_op jit(solution)/shard_map/all_to_all | solution.py:69
  312.2 3.9 reshape.304
  316.1 12.3 %all-to-all-start.1 = ((bf16[64,2,13824]{2,1,0:T(2,128)(2,1)}), bf16[64,2,13824]{2,1,0:T(2,128)(2,1)S(1)}, u32[]{:S(2)}, u32[]{:S(2)}) async-start(bf16[64,2,13824]{2,1,0:T(2,128)(2,1)} %reshape.304), calls=%async_computation.1 | async-start | bytes 7077888 | tf_op jit(solution)/shard_map/all_to_all | solution.py:69
  329.0 4.0 reshape.303
  333.0 4.4 reduce.14
  337.4 3.2 reshape.266
  344.8 79.5 %all-to-all-done.1 = bf16[64,2,13824]{2,1,0:T(2,128)(2,1)S(1)} async-done(((bf16[64,2,13824]{2,1,0:T(2,128)(2,1)}), bf16[64,2,13824]{2,1,0:T(2,128)(2,1)S(1)}, u32[]{:S(2)}, u32[]{:S(2)}) %all-to-all-start.1) | async-done | bytes 3538976 | tf_op jit(solution)/shard_map/all_to_all | solution.py:69
  424.3 12.5 %reshape.305 = bf16[64,1,27648]{2,1,0:T(2,128)(2,1)} reshape(bf16[64,2,13824]{2,1,0:T(2,128)(2,1)S(1)} %all-to-all-done.1) | data formatting | bytes 7077888
  436.8 63.4 %reduce.15 = bf16[64,27648]{1,0:T(8,128)(2,1)S(1)} reduce(bf16[64,1,27648]{2,1,0:T(2,128)(2,1)} %reshape.305, bf16[]{:T(256)} %constant.63), dimensions={1}, to_apply=%all_to_all.29.reduce_sub_computation | reduce | bytes 7077890 | tf_op jit(solution)/shard_map/all_to_all | solution.py:69
  500.2 15.2 %reshape.268 = bf16[64,2,96,1,2,72]{5,4,2,1,0,3:T(2,128)(2,1)} reshape(bf16[64,27648]{1,0:T(8,128)(2,1)S(1)} %reduce.15) | data formatting | bytes 7077888 | tf_op jit(solution)/shard_map/reshape | solution.py:76
  515.4 12.8 %copy.156 = bf16[2,64,96,1,2,72]{2,1,5,4,0,3:T(8,128)(2,1)} copy(bf16[2,64,96,1,2,72]{5,4,2,0,1,3:T(2,128)(2,1)} %bitcast.162) | data formatting | bytes 7077888 | tf_op jit(solution)/shard_map/transpose | solution.py:77
  528.3 8.4 %reshape.269 = bf16[2,6144,1,2,72]{1,4,3,0,2:T(8,128)(2,1)S(1)} reshape(bf16[2,64,96,1,2,72]{2,1,5,4,0,3:T(8,128)(2,1)} %copy.156) | data formatting | bytes 7077888 | tf_op jit(solution)/shard_map/reshape | solution.py:77
  538.8 32.8 %while.21 = (s32[]{:T(128)}, bf16[2,1536,1,72]{1,3,2,0:T(8,128)(2,1)}, bf16[2,1536,1,72]{1,3,2,0:T(8,128)(2,1)}, bf16[2,6144,1,72]{1,3,2,0:T(8,128)(2,1)}, bf16[...) while((s32[]{:T(128)}, bf16[2,1536,1,72]{1,3,2,0:T(8,128)(2,1)}, ...), condition=%wide.region_8.9_spmd, body=%wide.region_4.8_spmd.sunk | while | flops 918625792 | bytes 38588728 | solution.py:108
  540.7 13.2 %while.22 = (s32[]{:T(128)}, bf16[3,512,1,72]{1,3,2,0:T(8,128)(2,1)S(1)}, bf16[3,512,1,72]{1,3,2,0:T(8,128)(2,1)S(1)}, bf16[6144,1,72]{0,2,1:T(8,128)(2,1)S(1)}, bf16[6144,1,72]{0,2,1:T(8,128)(2,1)S(1)}, /*index=5*/s32[]{:T(128)}) while((s32[]{:T(128)}, bf16[3,512,1,72]{1,3,2,0:T(8,128)(2,1)S(1)}, bf16[3,512,1,72]{1,3,2,0:T(8,128)(2,1)S(1)}, ...), condition=%wide.region_7.7_spmd, body=%wide.region_5.6_spmd.sunk | while | flops 918625792 | bytes 27086924 | solution.py:102
  540.7 2.2 fusion.59
  545.1 2.2 fusion.59
  549.5 2.2 fusion.59
  557.0 13.2 %while.22 = (s32[]{:T(128)}, bf16[3,512,1,72]{1,3,2,0:T(8,128)(2,1)S(1)}, bf16[3,512,1,72]{1,3,2,0:T(8,128)(2,1)S(1)}, bf16[6144,1,72]{0,2,1:T(8,128)(2,1)S(1)}, bf16[6144,1,72]{0,2,1:T(8,128)(2,1)S(1)}, /*index=5*/s32[]{:T(128)}) while((s32[]{:T(128)}, bf16[3,512,1,72]{1,3,2,0:T(8,128)(2,1)S(1)}, bf16[3,512,1,72]{1,3,2,0:T(8,128)(2,1)S(1)}, ...), condition=%wide.region_7.7_spmd, body=%wide.region_5.6_spmd.sunk | while | flops 918625792 | bytes 27086924 | solution.py:102
  557.1 2.2 fusion.59
  559.3 2.2 fusion.60
  561.5 2.2 fusion.59
  565.9 2.2 fusion.59
  574.5 3.2 reduce.30
  578.9 12.4 %all-to-all-start.2 = ((bf16[64,2,1728]{2,1,0:T(2,128)(2,1)}), bf16[64,2,1728]{2,1,0:T(2,128)(2,1)}, u32[]{:S(2)}, u32[]{:S(2)}) async-start(bf16[64,2,1728]{2,1,0:T(2,128)(2,1)} %reshape.306), calls=%async_computation.2 | async-start | bytes 917504 | tf_op jit(solution)/shard_map/all_to_all | solution.py:113
  591.5 4.1 reshape.283
  595.7 13.3 %reshape.285 = bf16[1152,3456]{1,0:T(8,128)(2,1)} reshape(bf16[64,18,3456]{2,1,0:T(8,128)(2,1)} %all-gather.17.cloned.1.call-done) | data formatting | bytes 15925248
  609.0 3.1 reshape.307
  612.1 3.4 reduce.16
  615.5 2.5 reshape.271
  619.4 2.7 reshape.272
  624.5 6.7 fusion.36
  634.7 4.1 reshape.287
  640.3 2.5 fusion.35
  642.7 38.8 %all-gather.11.cloned.1.call-done = bf16[768,2304]{1,0:T(8,128)(2,1)} async-done(((bf16[192,2304]{1,0:T(8,128)(2,1)}), bf16[768,2304]{1,0:T(8,128)(2,1)}) %all-gather.11.cloned.1.call-update) | async-done | bytes 3538960 | tf_op jit(solution)/shard_map/all_gather | solution.py:128
  681.5 4.1 fusion.43
  685.6 4.0 copy.183
  689.6 2.7 multiply_reduce_fusion.1
  692.9 4.0 copy.184
  696.9 2.4 multiply_reduce_fusion
  (118 shorter events, 61.7 us)
Async XLA Ops:
  6.5 172.6 %all-gather.13.cloned.1.call-start = ((), (), s32[]{:S(2)}) async-start(), calls=%async_computation.4 | async-start | bytes 10782720 | tf_op jit(solution)/shard_map/all_gather | solution.py:32
  7.3 584.3 %all-gather.15.cloned.1.call-start = ((), (), s32[]{:S(2)}) async-start(), calls=%async_computation.5 | async-start | bytes 3594240 | tf_op jit(solution)/shard_map/all_gather | solution.py:33
  8.0 587.7 %all-gather.17.cloned.1.call-start = ((), (), s32[]{:S(2)}) async-start(), calls=%async_computation.6 | async-start | bytes 10782720 | tf_op jit(solution)/shard_map/all_gather | solution.py:34
  209.7 2.2 copy-start.2
  221.3 94.8 %all-to-all-start = ((bf16[64,2,1728]{2,1,0:T(2,128)(2,1)}), bf16[64,2,1728]{2,1,0:T(2,128)(2,1)}, u32[]{:S(2)}, u32[]{:S(2)}) async-start(bf16[64,2,1728]{2,1,0:T(2,128)(2,1)} %reshape.302), calls=%async_computation | async-start | bytes 917504 | tf_op jit(solution)/shard_map/all_to_all | solution.py:68
  230.7 1.2 copy-start.11
  316.1 108.2 %all-to-all-start.1 = ((bf16[64,2,13824]{2,1,0:T(2,128)(2,1)}), bf16[64,2,13824]{2,1,0:T(2,128)(2,1)S(1)}, u32[]{:S(2)}, u32[]{:S(2)}) async-start(bf16[64,2,13824]{2,1,0:T(2,128)(2,1)} %reshape.304), calls=%async_computation.1 | async-start | bytes 7077888 | tf_op jit(solution)/shard_map/all_to_all | solution.py:69
  328.5 306.2 %all-gather.19.cloned.1.call-start = ((), (), s32[]{:S(2)}) async-start(), calls=%async_computation.7 | async-start | bytes 3594240 | tf_op jit(solution)/shard_map/all_gather | solution.py:35
  538.8 1.6 copy-start
  540.6 13.7 %copy-start.3 = (bf16[2,1536,1,72]{1,3,2,0:T(8,128)(2,1)S(1)}, bf16[2,1536,1,72]{1,3,2,0:T(8,128)(2,1)}, u32[]{:S(2)}) copy-start(bf16[2,1536,1,72]{1,3,2,0:T(8,128)(2,1)} %get-tuple-element.285) | copy-start | bytes 1327108 | tf_op jit(solution)/shard_map/while
  554.4 0.8 copy-start.4
  555.2 1.6 copy-start
  557.0 13.7 %copy-start.3 = (bf16[2,1536,1,72]{1,3,2,0:T(8,128)(2,1)S(1)}, bf16[2,1536,1,72]{1,3,2,0:T(8,128)(2,1)}, u32[]{:S(2)}) copy-start(bf16[2,1536,1,72]{1,3,2,0:T(8,128)(2,1)} %get-tuple-element.285) | copy-start | bytes 1327108 | tf_op jit(solution)/shard_map/while
  570.8 0.8 copy-start.4
  573.0 18.4 %copy-start.9 = (f32[72]{0:T(128)S(1)}, f32[72]{0:T(128)}, u32[]{:S(2)}) copy-start(f32[72]{0:T(128)} %get-tuple-element.170) | copy-start | bytes 868
  578.9 30.1 %all-to-all-start.2 = ((bf16[64,2,1728]{2,1,0:T(2,128)(2,1)}), bf16[64,2,1728]{2,1,0:T(2,128)(2,1)}, u32[]{:S(2)}, u32[]{:S(2)}) async-start(bf16[64,2,1728]{2,1,0:T(2,128)(2,1)} %reshape.306), calls=%async_computation.2 | async-start | bytes 917504 | tf_op jit(solution)/shard_map/all_to_all | solution.py:113
  591.4 90.1 %all-gather.11.cloned.1.call-start = ((), (), s32[]{:S(2)}) async-start(), calls=%async_computation.3 | async-start | bytes 4423680 | tf_op jit(solution)/shard_map/all_gather | solution.py:128
  612.1 10.0 %copy-start.5 = (f32[1152]{0:T(1024)S(1)}, f32[1152]{0:T(1024)}, u32[]{:S(2)}) copy-start(f32[1152]{0:T(1024)} %get-tuple-element.130) | copy-start | bytes 13828
  622.1 2.4 copy-start.7
  622.1 2.4 copy-start.8
  631.2 1.8 copy-start.1
  634.6 5.6 copy-start.10
  696.9 2.6 copy-start.6
Sparse Core Ops, SparseCore 0:
  10.8 168.2 all-gather.12
  182.8 120.2 all-gather.14
  306.5 201.3 all-gather.16
  511.4 121.2 all-gather.18
  634.8 46.6 all-gather.10
where the time goes:
time: 718 us; the launch traced here: 708 us
  waiting for transfers between devices  284 us (40%)
  local copies, waits for them, and re-layouts  174 us (24%)
  other arithmetic  160 us (22%)
  matrix products  42.6 us (6%)
  starting transfers between devices  33.3 us (5%)
  between operations  14 us (2%)
    all_gather x1, waiting for transfers between devices, per_device(): lax.all_gather(spatial_qkv, 'space', axis=0, tiled=True)  163 us
    all_to_all x2, other arithmetic, per_device(): lax.all_to_all(pair_send, 'space', split_axis=0, concat_axis=1, tiled=True)  127 us
    all_to_all x1, waiting for transfers between devices, per_device(): lax.all_to_all(pair_send, 'space', split_axis=0, concat_axis=1, tiled=True)  79.5 us
    unnamed x30, local copies, waits for them, and re-layouts  70.7 us
    all_gather x1, waiting for transfers between devices, per_device(): gathered = lax.all_gather(own_pairs, 'tm', axis=0, tiled=True)  38.8 us
    reshape x1, local copies, waits for them, and re-layouts, per_device(): pair_recv.reshape(space_count, clip_count, tok_rows, heads_slot, 2, head_...  15.2 us
  transfers between devices with their start and end apart: 8, of which 3 were waited for; matrix products, arithmetic and copies ran while one was open for 48% of the time, Pallas kernels for 0%

commit v1 on v0

v1 whole, which is shorter than its diff:
```python
import math

import jax
import jax.numpy as jnp
from jax import lax
from jax.experimental import pallas as pl
from jax.experimental.pallas import tpu as pltpu
from jax.sharding import Mesh
from jax.sharding import PartitionSpec as P

D = 1152
HEADS = 16
HD = 72
HP = 80
PATCH = 96
ROWS = 2 * PATCH
NZ, NY = 8, 4
PLANE = NZ * PATCH
BF = jnp.bfloat16
F32 = jnp.float32
FACTOR = 1.0 / math.sqrt(HD)
TN = (((0,), (0,)), ((), ()))
TT = (((0,), (1,)), ((), ()))
PARAMS = pltpu.CompilerParams(vmem_limit_bytes=48 * 1024 * 1024)


def normalise(values):
    mean_val = jnp.mean(values, -1, keepdims=True)
    centred = values - mean_val
    variance = jnp.mean(centred * centred, -1, keepdims=True)
    return centred * lax.rsqrt(variance + 1e-06)


def rms(values, gain):
    mean_sq = jnp.mean(values * values, 0, keepdims=True)
    return values * lax.rsqrt(mean_sq + 1e-06) * gain


def spatial_proj(tok_ref, mod_ref, w_ref, gain_ref, out_ref):
    cols = 4 * PATCH
    zeros = jnp.zeros((HP - HD, cols), F32)
    first = lax.broadcasted_iota(jnp.int32, (HP - HD, cols), 0) == 0
    ones = jnp.where(first, 1.0, 0.0)
    for clip in range(2):
        tok = tok_ref[:, clip * PATCH : (clip + 1) * PATCH, :].reshape(cols, D).astype(F32)
        normed = normalise(tok) * (1.0 + mod_ref[1:2, :]) + mod_ref[0:1, :]
        proj = lax.dot_general(w_ref[...], normed.astype(BF), TT, preferred_element_type=F32)
        for head in range(2):
            query, key, value = (
                proj[part * 2 * HD + head * HD : part * 2 * HD + (head + 1) * HD] for part in range(3)
            )
            query = rms(query, gain_ref[:, 0:1]) * (FACTOR * math.log2(math.e))
            key = rms(key, gain_ref[:, 1:2])
            place = clip * 2 + head
            parts = [key, zeros, value, ones, query, zeros]
            out_ref[place] = jnp.concatenate(parts, 0).astype(BF)


def attend_step(q_ref, kv_ref, keys, acc):
    query = jnp.concatenate([q_ref[0], jnp.zeros((128 - HP, PLANE), BF)], 0)
    total = None
    for part in range(PLANE // 256):
        here = slice(part * 256, (part + 1) * 256)
        score = jnp.dot(keys[here, :], query, preferred_element_type=F32)
        expo = jnp.exp2(score).astype(BF)
        add = jnp.dot(kv_ref[0, HP : 2 * HP, here], expo, preferred_element_type=F32)
        total = add if total is None else total + add
    return acc + total


def turn_keys(kv_ref, keys):
    wide = jnp.concatenate([kv_ref[0, :HP].astype(F32), jnp.zeros((128 - HP, PLANE), F32)], 0)
    keys[...] = wide.T.astype(BF)


def attend_own(q_ref, kv_ref, out_ref, keys, sums):
    step, block = pl.program_id(0), pl.program_id(1)

    @pl.when(block == 0)
    def _():
        turn_keys(kv_ref, keys)

    @pl.when(step == 0)
    def _():
        sums[block] = jnp.zeros((HP, PLANE), F32)

    sums[block] = attend_step(q_ref, kv_ref, keys, sums[block])

    @pl.when(step == NY - 1)
    def _():
        out_ref[0] = sums[block]


def attend_other(q_ref, kv_ref, part_ref, out_ref, keys, sums):
    step, block = pl.program_id(0), pl.program_id(1)

    @pl.when(block == 0)
    def _():
        turn_keys(kv_ref, keys)

    @pl.when(step == 0)
    def _():
        sums[block] = part_ref[0]

    sums[block] = attend_step(q_ref, kv_ref, keys, sums[block])

    @pl.when(step == NY - 1)
    def _():
        done = sums[block]
        done = done[:HD] / done[HD : HD + 1]
        for z in range(NZ):
            out_ref[0, z] = done[:, z * PATCH : (z + 1) * PATCH].astype(BF)


Q_SPEC = pl.BlockSpec((1, HP, PLANE), lambda k, q: (q, 2, 0))
KV_SPEC = pl.BlockSpec((1, 2 * HP, PLANE), lambda k, q: (k, 0, 0))
SCRATCH = [pltpu.VMEM((PLANE, 128), BF), pltpu.VMEM((NY, HP, PLANE), F32)]
COST = pl.CostEstimate(
    flops=4 * 128 * (NY * PLANE) ** 2, bytes_accessed=8_000_000, transcendentals=(NY * PLANE) ** 2
)


def last_only(k, q):
    return jnp.where(k == NY - 1, q, 0)


def first_only(k, q):
    return jnp.where(k == 0, q, NY - 1)


def attention_own(own):
    return pl.pallas_call(
        attend_own,
        grid=(NY, NY),
        in_specs=[Q_SPEC, KV_SPEC],
        out_specs=pl.BlockSpec((1, HP, PLANE), lambda k, q: (last_only(k, q), 0, 0)),
        out_shape=jax.ShapeDtypeStruct((NY, HP, PLANE), F32),
        scratch_shapes=SCRATCH,
        compiler_params=PARAMS,
        cost_estimate=COST,
        name="attend_own",
    )(own, own)


def attention_other(own, other, part):
    part_spec = pl.BlockSpec((1, HP, PLANE), lambda k, q: (first_only(k, q), 0, 0))
    return pl.pallas_call(
        attend_other,
        grid=(NY, NY),
        in_specs=[Q_SPEC, KV_SPEC, part_spec],
        out_specs=pl.BlockSpec((1, NZ, HD, PATCH), lambda k, q: (last_only(k, q), 0, 0, 0)),
        out_shape=jax.ShapeDtypeStruct((NY, NZ, HD, PATCH), BF),
        scratch_shapes=SCRATCH,
        compiler_params=PARAMS,
        cost_estimate=COST,
        name="attend_other",
    )(own, other, part)


def spatial_end(place_ref, att_ref, tok_ref, mod_ref, own, got, resid_ref, norm_ref):
    weight = jnp.where(place_ref[0] == 1, got[...], own[...])
    rows = []
    for clip in range(2):
        feats = [
            att_ref[clip * 2 + head, pair].astype(F32) for pair in range(NZ) for head in range(2)
        ]
        rows.append(jnp.concatenate(feats, 0).T.astype(BF))
    attended = jnp.concatenate(rows, 0)
    branch = jnp.dot(attended, weight, preferred_element_type=F32)
    resid = tok_ref[...].astype(F32) + mod_ref[2:3, :] * branch
    resid_ref[...] = resid
    norm_ref[...] = (normalise(resid) * (1.0 + mod_ref[4:5, :]) + mod_ref[3:4, :]).astype(BF)


def temporal(place_ref, n0, n1, n2, n3, weight, gain_ref, o0, o1, o2, o3):
    queries, keys, values = [], [], []
    for norm_ref in (n0, n1, n2, n3):
        proj = lax.dot_general(weight[...], norm_ref[...], TT, preferred_element_type=F32)
        heads = [proj[n * HD : (n + 1) * HD] for n in range(12)]
        queries.append([rms(v, gain_ref[:, 2:3]).astype(BF).astype(F32) for v in heads[:4]])
        keys.append([rms(v, gain_ref[:, 3:4]).astype(BF).astype(F32) for v in heads[4:8]])
        values.append([v.astype(BF).astype(F32) for v in heads[8:]])
    for f, out_ref in enumerate((o0, o1, o2, o3)):
        mixed = []
        for head in range(4):
            total, attended = 0.0, 0.0
            for g in range(4):
                score = jnp.sum(queries[f][head] * keys[g][head], 0, keepdims=True) * FACTOR
                expo = jnp.exp(score)
                total = total + expo
                attended = attended + expo.astype(BF).astype(F32) * values[g][head]
            mixed.append(attended / total)
        out_ref[...] = jnp.concatenate(mixed, 0).astype(BF)


def temporal_end(place_ref, m0, m1, m2, m3, resid_ref, mod_ref, own, got, out_ref):
    core = place_ref[0] == 1
    branch = None
    for step, att_ref in enumerate((m0, m1, m2, m3)):
        here = pl.ds(pl.multiple_of((place_ref[1] ^ step) * (4 * HD), 4 * HD), 4 * HD)
        rows = jnp.where(core, own[here, :], got[here, :])
        add = jnp.dot(att_ref[...].astype(F32).T.astype(BF), rows, preferred_element_type=F32)
        branch = add if branch is None else branch + add
    out_ref[...] = (resid_ref[...] + mod_ref[5:6, :] * branch).astype(BF)


def whole(shapes, kernel, name, *args):
    smem = pl.BlockSpec(memory_space=pltpu.SMEM)
    vmem = pl.BlockSpec(memory_space=pltpu.VMEM)
    return pl.pallas_call(
        kernel,
        in_specs=[smem] + [vmem] * (len(args) - 1),
        out_specs=[vmem] * len(shapes),
        out_shape=shapes,
        compiler_params=PARAMS,
        name=name,
    )(*args)


def per_device(tokens, modulation, spatial_qkv, spatial_out, temporal_qkv, temporal_out, norm_gains):
    core = lax.axis_index("c")
    frame = lax.axis_index("xl") * 2 + core
    place = jnp.stack([core, frame]).astype(jnp.int32)
    gains = norm_gains.T
    tok = tokens.reshape(ROWS, D)

    shard = spatial_qkv.reshape(18, 3, NZ, 2 * HD).transpose(2, 0, 1, 3).reshape(NZ, 18, 6 * HD)
    shard = jnp.pad(shard, ((0, 0), (0, 0), (0, 512 - 6 * HD)))
    part_b = lax.dynamic_slice_in_dim(temporal_qkv.reshape(18, 3, D), frame * 4 * HD, 4 * HD, 2)
    part_b = part_b.reshape(18, 12 * HD)
    bundle = jnp.concatenate([jnp.where(core == 0, spatial_out, temporal_out), part_b], 1)
    shard = jnp.concatenate([shard, jnp.broadcast_to(bundle, (NZ, 18, D + 12 * HD))], 2)
    shard = lax.all_to_all(shard, "z", 0, 0, tiled=True).reshape(NZ * 18, 512 + D + 12 * HD)
    weight_a = jnp.broadcast_to(shard[None, :, : 6 * HD], (8, NZ * 18, 6 * HD))
    weight_a = lax.all_to_all(weight_a, ("xh", "y"), 0, 0, tiled=True).reshape(D, 6 * HD)

    column = lax.all_gather(tok, "z", axis=0)
    projected = pl.pallas_call(
        spatial_proj,
        grid=(2,),
        in_specs=[
            pl.BlockSpec((4, ROWS, D), lambda i: (i, 0, 0)),
            pl.BlockSpec((6, D), lambda i: (0, 0)),
            pl.BlockSpec((D, 6 * HD), lambda i: (0, 0)),
            pl.BlockSpec((HD, 4), lambda i: (0, 0)),
        ],
        out_specs=pl.BlockSpec((4, 3 * HP, 4 * PATCH), lambda i: (0, 0, i)),
        out_shape=jax.ShapeDtypeStruct((4, 3 * HP, PLANE), BF),
        compiler_params=PARAMS,
        name="spatial_proj",
    )(column, modulation, weight_a, gains)

    swap = [(0, 1), (1, 0)]
    bundle, projected = lax.optimization_barrier((shard[:, 512:], projected))
    outs_own = lax.all_gather(bundle[:, :D], ("xh", "y"), axis=0, tiled=True)
    weight_b = lax.all_gather(bundle[:, D:], ("xh", "y"), axis=0, tiled=True)

    projected = lax.all_to_all(projected, "y", 0, 0, tiled=True)
    other = lax.ppermute(projected[:, : 2 * HP], "xh", swap)
    part = attention_own(projected)
    attended = attention_other(projected, other, part)
    attended, outs_own = lax.optimization_barrier((attended, outs_own))
    outs_got = lax.ppermute(outs_own, "c", swap)
    attended = attended.reshape(NY * NZ, HD, PATCH)
    attended = lax.all_to_all(attended, ("y", "z"), 0, 0, tiled=True)
    attended = attended.reshape(4, NZ, HD, PATCH)

    resid, normed_b = whole(
        [jax.ShapeDtypeStruct((ROWS, D), F32), jax.ShapeDtypeStruct((ROWS, D), BF)],
        spatial_end,
        "spatial_end",
        place, attended, tok, modulation, outs_own, outs_got,
    )
    norm_c = lax.ppermute(normed_b, "c", swap)
    norm_x = lax.ppermute(normed_b, "xl", swap)
    norm_cx = lax.ppermute(norm_x, "c", swap)
    mixed = whole(
        [jax.ShapeDtypeStruct((4 * HD, ROWS), BF)] * 4,
        temporal,
        "temporal",
        place, normed_b, norm_c, norm_x, norm_cx, weight_b, gains,
    )
    mixed = [
        mixed[0],
        lax.ppermute(mixed[1], "c", swap),
        lax.ppermute(mixed[2], "xl", swap),
        lax.ppermute(mixed[3], ("xl", "c"), [(0, 3), (3, 0), (1, 2), (2, 1)]),
    ]
    (result,) = whole(
        [jax.ShapeDtypeStruct((ROWS, D), BF)],
        temporal_end,
        "temporal_end",
        place, *mixed, resid, modulation, outs_own, outs_got,
    )
    return result.reshape(2, 1, PATCH, D)


def solution(mesh):
    fine = Mesh(mesh.devices.reshape(2, 2, 2, NY, NZ), ("xl", "c", "xh", "y", "z"))
    time, space = ("xl", "c"), ("xh", "y", "z")
    block = P(None, time, space, None)
    rows = P(space, None)
    return jax.shard_map(
        per_device,
        mesh=fine,
        in_specs=(block, P(), rows, rows, rows, rows, P()),
        out_specs=block,
        check_vma=False,
    )
```

time: 718 us -> 254 us (0.35); the launches traced: 708 us -> 253 us
  waiting for transfers between devices: 284 us -> 75.5 us
  local copies, waits for them, and re-layouts: 174 us -> 11.1 us
  other arithmetic: 160 us -> 0.19 us
  blocking collectives: 0 us -> 70.1 us
  Pallas kernels: 0 us -> 46.8 us
  matrix products: 42.6 us -> 0 us
    all_gather x5 -> x3, waiting for transfers between devices: 202 us -> 21.9 us  [the longest x1 17.7 us: per_device(): weight_b = lax.all_gather(bundle[:, D:], ('xh', 'y'), axis=0, tiled=True)]
    all_to_all x6 -> x0, other arithmetic: 141 us -> none  [the longest x2 127 us: per_device(): lax.all_to_all(pair_send, 'space', split_axis=0, concat_axis=1, tiled=True)]
    all_to_all x0 -> x2, blocking collectives: none -> 70.1 us  [the longest x1 42.5 us: per_device(): lax.all_to_all(shard, 'z', 0, 0, tiled=True)]
    unnamed x30 -> x28, local copies, waits for them, and re-layouts: 70.7 us -> 4.29 us
    all_to_all x3 -> x2, waiting for transfers between devices: 79.5 us -> 27.5 us  [the longest x1 15.9 us: per_device(): attended = lax.all_to_all(attended, ('y', 'z'), 0, 0, tiled=True)]
    pallas_call x0 -> x6, Pallas kernels: none -> 46.8 us  [the longest x1 15.1 us: attention_other(): pl.pallas_call(attend_other, grid=(NY, NY), in_specs=[Q_SPEC, KV_SPEC, pa...]
    dot_general x16 -> x0, matrix products: 42.6 us -> none  [the longest x6 13.4 us: one_block(): jnp.einsum('qhd,khd->hqk', query_block, clip_keys, preferred_element_type...]
    reshape x7 -> x6, local copies, waits for them, and re-layouts: 32.2 us -> 2.99 us  [the longest x3 1.53 us: per_device(): spatial_qkv.reshape(18, 3, NZ, 2 * HD).transpose(2, 0, 1, 3)]
  transfers between devices with their start and end apart: 8 -> 13, of which waited for: 3 -> 8; matrix products, arithmetic and copies ran while one was open for 48% -> 3% of each run, Pallas kernels for 0% -> 13%
where the time goes in v1:
time: 254 us; the launch traced here: 253 us
  waiting for transfers between devices  75.5 us (30%)
  blocking collectives  70.1 us (28%)
  Pallas kernels  46.8 us (18%)
  starting transfers between devices  35.9 us (14%)
  between operations  13.3 us (5%)
  local copies, waits for them, and re-layouts  11.1 us (4%)
    all_to_all x1, blocking collectives, per_device(): lax.all_to_all(shard, 'z', 0, 0, tiled=True)  42.5 us
    all_to_all x1, blocking collectives, per_device(): projected = lax.all_to_all(projected, 'y', 0, 0, tiled=True)  27.6 us
    all_gather x1, waiting for transfers between devices, per_device(): weight_b = lax.all_gather(bundle[:, D:], ('xh', 'y'), axis=0, tiled=True)  17.7 us
    all_to_all x1, waiting for transfers between devices, per_device(): attended = lax.all_to_all(attended, ('y', 'z'), 0, 0, tiled=True)  15.9 us
    pallas_call x1, Pallas kernels, attention_other(): pl.pallas_call(attend_other, grid=(NY, NY), in_specs=[Q_SPEC, KV_SPEC, pa...  15.1 us
    ppermute x1, waiting for transfers between devices, per_device(): other = lax.ppermute(projected[:, :2 * HP], 'xh', swap)  13.9 us
    pallas_call x1, Pallas kernels, attention_own(): pl.pallas_call(attend_own, grid=(NY, NY), in_specs=[Q_SPEC, KV_SPEC], out...  13.8 us
    pallas_call x3, Pallas kernels, whole(): pl.pallas_call(kernel, in_specs=[smem] + [vmem] * (len(args) - 1), out_sp...  12.3 us
  transfers between devices with their start and end apart: 13, of which 8 were waited for; matrix products, arithmetic and copies ran while one was open for 3% of the time, Pallas kernels for 13%

profile of v1, /device:TPU:1, one launch (start us, length us, event | category | flops | bytes accessed | tf_op | source)
XLA Modules:
  0.0 252.8 jit_solution(6814961424539174214)
XLA Ops:
  6.5 0.7 all-gather.4.cloned.1.call-update
  7.3 1.0 reshape.33
  8.2 0.1 constant_dynamic-slice_fusion
  8.4 0.1 reshape.34
  8.5 1.2 reshape.31
  9.7 0.1 copy.21
  9.8 0.2 reshape.32
  10.1 0.1 broadcast_in_dim.4
  10.2 0.1 fusion.1
  10.3 42.5 %all_to_all.20 = bf16[8,18,2528]{2,1,0:T(8,128)(2,1)S(1)} all-to-all(bf16[8,18,2528]{2,1,0:T(8,128)(2,1)S(1)} %fusion.1), channel_id=1, replica_groups=mesh['xl'=2,'c'=2,'xh'=2,'y'=4,'z'=8] {'z'}, dimensions={0} | all-to-all | bytes 1456128 | tf_op jit(solution)/shard_map/all_to_all | solution.py:233
  52.8 0.4 reshape.35
  53.3 1.1 broadcast_in_dim.10
  54.4 6.8 %all-to-all-start.1 = ((bf16[8,144,432]{2,1,0:T(8,128)(2,1)}), bf16[8,144,432]{2,1,0:T(8,128)(2,1)S(1)}, u32[]{:S(2)}, u32[]{:S(2)}) async-start(bf16[8,144,432]{2,1,0:T(8,128)(2,1)} %broadcast_in_dim.10), calls=%async_computation.1 | async-start | bytes 2359296 | tf_op jit(solution)/shard_map/all_to_all | solution.py:235
  61.2 0.0 all-gather.6.cloned.1.call-start
  61.2 0.1 copy.17
  61.3 0.9 slice.20
  62.2 11.6 %all-to-all-done.1 = bf16[8,144,432]{2,1,0:T(8,128)(2,1)S(1)} async-done(((bf16[8,144,432]{2,1,0:T(8,128)(2,1)}), bf16[8,144,432]{2,1,0:T(8,128)(2,1)S(1)}, u32[]{:S(2)}, u32[]{:S(2)}) %all-to-all-start.1) | async-done | bytes 995360 | tf_op jit(solution)/shard_map/all_to_all | solution.py:235
  73.9 4.2 %all-gather.4.cloned.1.call-done.tok_ref = bf16[8,192,1152]{2,1,0:T(8,128)(2,1)} async-done(((bf16[1,192,1152]{2,1,0:T(8,128)(2,1)}), bf16[8,192,1152]{2,1,0:T(8,128)(2,1)}) %all-gather.4.cloned.1.call-update) | async-done | bytes 3538960 | tf_op jit(solution)/shard_map/all_gather | solution.py:237
  78.1 5.6 %spatial_proj.1 = bf16[4,240,768]{2,1,0:T(8,128)(2,1)S(1)} custom-call(bf16[8,192,1152]{2,1,0:T(8,128)(2,1)} %all-gather.4.cloned.1.call-done.tok_ref, f32[6,1152]{1,0:T(8,128)S(1)} %copy-done.6, bf16[1152,432]{1,0:T(8,128)(2,1)S(1)} %bitcast.16, f32[72,4]{1,0:T(8,128)S(1)} %bitcast.20), custom_call_target="tpu_custom_call" | custom-call | tf_op jit(solution)/shard_map/spatial_proj/pallas_call | solution.py:238
  83.7 0.8 slice.18
  84.5 0.0 all-gather.6.cloned.1.call-update
  84.5 0.0 all-gather.8.cloned.1.call-start
  84.5 27.6 %all_to_all.21.q_ref.kv_ref = bf16[4,240,768]{2,1,0:T(8,128)(2,1)S(1)} all-to-all(bf16[4,240,768]{2,1,0:T(8,128)(2,1)S(1)} %spatial_proj.1), channel_id=1, replica_groups=mesh['xl'=2,'c'=2,'xh'=2,'y'=4,'z'=8] {'y'}, dimensions={0} | all-to-all | bytes 2949120 | tf_op jit(solution)/shard_map/all_to_all | solution.py:258
  112.1 0.1 slice.22
  112.2 2.5 collective-permute-start
  114.7 13.8 %attend_own.1.part_ref = f32[4,80,768]{2,1,0:T(8,128)S(1)} custom-call(bf16[4,240,768]{2,1,0:T(8,128)(2,1)S(1)} %all_to_all.21.q_ref.kv_ref, bf16[4,240,768]{2,1,0:T(8,128)(2,1)S(1)} %all_to_all.21.q_ref.kv_ref), custom_call_target="tpu_custom_call" | custom-call | flops 4831838208 | bytes 8000000 | tf_op jit(solution)/shard_map/attend_own/pallas_call | solution.py:132
  128.5 13.9 %collective-permute-done.kv_ref = bf16[4,160,768]{2,1,0:T(8,128)(2,1)S(1)} collective-permute-done((bf16[4,160,768]{2,1,0:T(8,128)(2,1)S(1)}, bf16[4,160,768]{2,1,0:T(8,128)(2,1)S(1)}, u32[]{:S(2)}, u32[]{:S(2)}) %collective-permute-start) | collective-permute-done | bytes 983072 | tf_op jit(solution)/shard_map/ppermute | solution.py:259
  142.4 15.1 %attend_other.1 = bf16[4,8,72,96]{3,2,1,0:T(8,128)(2,1)} custom-call(bf16[4,240,768]{2,1,0:T(8,128)(2,1)S(1)} %all_to_all.21.q_ref.kv_ref, bf16[4,160,768]{2,1,0:T(8,128)(2,1)S(1)} %collective-permute-done.kv_ref, f32[4,80,768]{2,1,0:T(8,128)S(1)} %attend_own.1.part_ref), custom_call_target="tpu_custom_call" | custom-call | flops 4831838208 | bytes 8000000 | tf_op jit(solution)/shard_map/attend_other/pallas_call | solution.py:147
  157.6 8.5 %collective-permute-start.1 = (bf16[1152,1152]{1,0:T(8,128)(2,1)}, bf16[1152,1152]{1,0:T(8,128)(2,1)}, u32[]{:S(2)}, u32[]{:S(2)}) collective-permute-start(bf16[1152,1152]{1,0:T(8,128)(2,1)} %all-gather.6.cloned.1.call-done.own), channel_id=1, source_target_pairs={{0,64},{64,0},{1,65},{65,1},{2,66},{66,2},{3,67},{67,3},{4,68},{68... | collective-permute-start | bytes 7962632 | tf_op jit(solution)/shard_map/ppermute | solution.py:263
  166.1 0.7 slice.19
  166.8 4.7 %all-to-all-start.3 = ((bf16[32,72,96]{2,1,0:T(8,128)(2,1)}), bf16[32,72,96]{2,1,0:T(8,128)(2,1)S(1)}, u32[]{:S(2)}, u32[]{:S(2)}) async-start(bf16[32,72,96]{2,1,0:T(8,128)(2,1)} %bitcast.6), calls=%async_computation.3 | async-start | bytes 1179648 | tf_op jit(solution)/shard_map/all_to_all | solution.py:265
  171.5 0.1 pad_add_fusion.place_ref
  171.6 15.9 %all-to-all-done.3 = bf16[32,72,96]{2,1,0:T(8,128)(2,1)S(1)} async-done(((bf16[32,72,96]{2,1,0:T(8,128)(2,1)}), bf16[32,72,96]{2,1,0:T(8,128)(2,1)S(1)}, u32[]{:S(2)}, u32[]{:S(2)}) %all-to-all-start.3) | async-done | bytes 442400 | tf_op jit(solution)/shard_map/all_to_all | solution.py:265
  187.5 1.8 copy-done
  189.2 3.7 %spatial_end.1 = (f32[192,1152]{1,0:T(8,128)S(1)}, bf16[192,1152]{1,0:T(8,128)(2,1)}) custom-call(s32[2]{0:T(128)S(1)} %pad_add_fusion.place_ref, bf16[4,8,72,96]{3,2,1,0:T(8,128)(2,1)S(1)} %bitcast.17, bf16[192,1152]{1,0:T(8,128)(2,1)S(1)} %bitcast.19, f32[6,1152]{1,0:T(8,128)S(1)} %copy-done.7, bf16[1152,1152]{1,0:T(8,128)(2,1)S(1)} %copy-done, ...), custom_call_target="tpu_custom_call" | custom-call | tf_op jit(solution)/shard_map/spatial_end/pallas_call | solution.py:210
  192.9 1.2 collective-permute-start.3
  194.1 3.4 %collective-permute-start.2 = (bf16[192,1152]{1,0:T(8,128)(2,1)}, bf16[192,1152]{1,0:T(8,128)(2,1)}, u32[]{:S(2)}, u32[]{:S(2)}) collective-permute-start(bf16[192,1152]{1,0:T(8,128)(2,1)} %get-tuple-element.19.n0), channel_id=1, source_target_pairs={{0,64},{64,0},{1,65},{65,1},{2,66},{66,2},{3,67},{67,3},{4,68},{68... | collective-permute-start | bytes 1327112 | tf_op jit(solution)/shard_map/ppermute | solution.py:274
  197.5 4.3 %collective-permute-done.3.n2 = bf16[192,1152]{1,0:T(8,128)(2,1)} collective-permute-done((bf16[192,1152]{1,0:T(8,128)(2,1)}, bf16[192,1152]{1,0:T(8,128)(2,1)}, u32[]{:S(2)}, u32[]{:S(2)}) %collective-permute-start.3) | collective-permute-done | bytes 442400 | tf_op jit(solution)/shard_map/ppermute | solution.py:275
  201.8 6.2 %collective-permute-start.4 = (bf16[192,1152]{1,0:T(8,128)(2,1)}, bf16[192,1152]{1,0:T(8,128)(2,1)}, u32[]{:S(2)}, u32[]{:S(2)}) collective-permute-start(bf16[192,1152]{1,0:T(8,128)(2,1)} %collective-permute-done.3.n2), channel_id=1, source_target_pairs={{0,64},{64,0},{1,65},{65,1},{2,66},{66,2},{3,67},{67,3},{4,68},{68... | collective-permute-start | bytes 1327112 | tf_op jit(solution)/shard_map/ppermute | solution.py:276
  208.0 17.7 %all-gather.8.cloned.1.call-done.weight = bf16[1152,864]{1,0:T(8,128)(2,1)} async-done(((bf16[144,864]{1,0:T(8,128)(2,1)}), bf16[1152,864]{1,0:T(8,128)(2,1)}) %all-gather.8.cloned.1.call-update) | async-done | bytes 1990672 | tf_op jit(solution)/shard_map/all_gather | solution.py:256
  225.7 1.6 copy-done.2
  227.3 0.8 copy-done.5
  228.1 4.8 %temporal.1 = (bf16[288,192]{1,0:T(8,128)(2,1)S(1)}, bf16[288,192]{1,0:T(8,128)(2,1)S(1)}, bf16[288,192]{1,0:T(8,128)(2,1)S(1)}, bf16[288,192]{1,0:T(8,128)(2,1)S(1)}) custom-call(s32[2]{0:T(128)S(1)} %pad_add_fusion.place_ref, bf16[192,1152]{1,0:T(8,128)(2,1)} %get-tuple-element.19.n0, bf16[192,1152]{1,0:T(8,128)(2,1)} %collective-permute-done.2.n1, ...), custom_call_target="tpu_custom_call" | custom-call | tf_op jit(solution)/shard_map/temporal/pallas_call | solution.py:210
  232.9 0.9 collective-permute-start.5
  233.8 1.7 collective-permute-start.7
  235.5 3.7 %collective-permute-done.6.m2 = bf16[288,192]{1,0:T(8,128)(2,1)S(1)} collective-permute-done((bf16[288,192]{1,0:T(8,128)(2,1)S(1)}, bf16[288,192]{1,0:T(8,128)(2,1)S(1)}, u32[]{:S(2)}, u32[]{:S(2)}) %collective-permute-start.6) | collective-permute-done | bytes 110624 | tf_op jit(solution)/shard_map/ppermute | solution.py:286
  239.2 3.3 %collective-permute-done.7.m3 = bf16[288,192]{1,0:T(8,128)(2,1)S(1)} collective-permute-done((bf16[288,192]{1,0:T(8,128)(2,1)S(1)}, bf16[288,192]{1,0:T(8,128)(2,1)S(1)}, u32[]{:S(2)}, u32[]{:S(2)}) %collective-permute-start.7) | collective-permute-done | bytes 110624 | tf_op jit(solution)/shard_map/ppermute | solution.py:287
  242.5 3.8 %temporal_end.1 = bf16[192,1152]{1,0:T(8,128)(2,1)} custom-call(s32[2]{0:T(128)S(1)} %pad_add_fusion.place_ref, bf16[288,192]{1,0:T(8,128)(2,1)S(1)} %get-tuple-element.20.m0, bf16[288,192]{1,0:T(8,128)(2,1)S(1)} %collective-permute-done.5.m1, bf16[288,192]{1,0:T(8,128)(2,1)S(1)} %collective-permute-done.6.m2, ...), custom_call_target="tpu_custom_call" | custom-call | tf_op jit(solution)/shard_map/temporal_end/pallas_call | solution.py:210
  (35 shorter events, 0.2 us)
Async XLA Ops:
  6.5 3.5 %copy-start.11 = (bf16[18,1152]{1,0:T(8,128)(2,1)S(1)}, bf16[18,1152]{1,0:T(8,128)(2,1)}, u32[]{:S(2)}) copy-start(bf16[18,1152]{1,0:T(8,128)(2,1)} %param.12) | copy-start | bytes 124420
  6.5 3.6 %copy-start.10 = (bf16[18,1152]{1,0:T(8,128)(2,1)S(1)}, bf16[18,1152]{1,0:T(8,128)(2,1)}, u32[]{:S(2)}) copy-start(bf16[18,1152]{1,0:T(8,128)(2,1)} %param.10) | copy-start | bytes 124420
  6.5 71.5 %all-gather.4.cloned.1.call-start = ((), (), s32[]{:S(2)}) async-start(), calls=%async_computation.4 | async-start | bytes 3981312 | tf_op jit(solution)/shard_map/all_gather | solution.py:237
  53.2 8.0 %copy-start.12 = (f32[4,72]{1,0:T(4,128)S(1)}, f32[4,72]{1,0:T(4,128)}, u32[]{:S(2)}) copy-start(f32[4,72]{1,0:T(4,128)} %param.13) | copy-start | bytes 3460
  54.4 23.7 %copy-start.6 = (f32[6,1152]{1,0:T(8,128)S(1)}, f32[6,1152]{1,0:T(8,128)}, u32[]{:S(2)}) copy-start(f32[6,1152]{1,0:T(8,128)} %mod_ref.5) | copy-start | bytes 82948
  54.4 19.5 %all-to-all-start.1 = ((bf16[8,144,432]{2,1,0:T(8,128)(2,1)}), bf16[8,144,432]{2,1,0:T(8,128)(2,1)S(1)}, u32[]{:S(2)}, u32[]{:S(2)}) async-start(bf16[8,144,432]{2,1,0:T(8,128)(2,1)} %broadcast_in_dim.10), calls=%async_computation.1 | async-start | bytes 2359296 | tf_op jit(solution)/shard_map/all_to_all | solution.py:235
  61.2 96.4 %all-gather.6.cloned.1.call-start = ((), (), s32[]{:S(2)}) async-start(), calls=%async_computation.5 | async-start | bytes 2985984 | tf_op jit(solution)/shard_map/all_gather | solution.py:255
  61.3 22.4 %copy-start.4 = (f32[4,72]{0,1:T(8,128)}, f32[4,72]{0,1:T(8,128)S(1)}, u32[]{:S(2)}) copy-start(f32[4,72]{0,1:T(8,128)S(1)} %copy.17) | copy-start | bytes 3460
  78.1 5.6 %copy-start.9 = (bf16[144,2016]{1,0:T(8,128)(2,1)S(1)}, bf16[144,2016]{1,0:T(8,128)(2,1)}, u32[]{:S(2)}) copy-start(bf16[144,2016]{1,0:T(8,128)(2,1)} %slice.20) | copy-start | bytes 1741828
  84.5 141.2 %all-gather.8.cloned.1.call-start = ((), (), s32[]{:S(2)}) async-start(), calls=%async_computation.6 | async-start | bytes 2322432 | tf_op jit(solution)/shard_map/all_gather | solution.py:256
  112.2 30.2 %collective-permute-start = (bf16[4,160,768]{2,1,0:T(8,128)(2,1)S(1)}, bf16[4,160,768]{2,1,0:T(8,128)(2,1)S(1)}, u32[]{:S(2)}, u32[]{:S(2)}) collective-permute-start(bf16[4,160,768]{2,1,0:T(8,128)(2,1)S(1)} %slice.22), channel_id=1, source_target_pairs={{0,32},{32,0},{1,33},{33,1},{2,34},{34,2},{3,35},{35,3},{4,36},{36... | collective-permute-start | bytes 2949128 | tf_op jit(solution)/shard_map/ppermute | solution.py:259
  157.6 29.9 %copy-start.3 = (bf16[2,1,96,1152]{3,2,1,0:T(8,128)(2,1)S(1)}, bf16[2,1,96,1152]{3,2,1,0:T(8,128)(2,1)}, u32[]{:S(2)}) copy-start(bf16[2,1,96,1152]{3,2,1,0:T(8,128)(2,1)} %param.7) | copy-start | bytes 1327108
  157.6 29.9 %copy-start.7 = (f32[6,1152]{1,0:T(8,128)S(1)}, f32[6,1152]{1,0:T(8,128)}, u32[]{:S(2)}) copy-start(f32[6,1152]{1,0:T(8,128)} %mod_ref.5) | copy-start | bytes 82948
  157.6 29.9 %collective-permute-start.1 = (bf16[1152,1152]{1,0:T(8,128)(2,1)}, bf16[1152,1152]{1,0:T(8,128)(2,1)}, u32[]{:S(2)}, u32[]{:S(2)}) collective-permute-start(bf16[1152,1152]{1,0:T(8,128)(2,1)} %all-gather.6.cloned.1.call-done.own), channel_id=1, source_target_pairs={{0,64},{64,0},{1,65},{65,1},{2,66},{66,2},{3,67},{67,3},{4,68},{68... | collective-permute-start | bytes 7962632 | tf_op jit(solution)/shard_map/ppermute | solution.py:263
  166.8 20.6 %all-to-all-start.3 = ((bf16[32,72,96]{2,1,0:T(8,128)(2,1)}), bf16[32,72,96]{2,1,0:T(8,128)(2,1)S(1)}, u32[]{:S(2)}, u32[]{:S(2)}) async-start(bf16[32,72,96]{2,1,0:T(8,128)(2,1)} %bitcast.6), calls=%async_computation.3 | async-start | bytes 1179648 | tf_op jit(solution)/shard_map/all_to_all | solution.py:265
  187.5 1.8 copy-start
  192.9 49.6 %copy-start.1 = (bf16[1152,1152]{1,0:T(8,128)(2,1)S(1)}, bf16[1152,1152]{1,0:T(8,128)(2,1)}, u32[]{:S(2)}) copy-start(bf16[1152,1152]{1,0:T(8,128)(2,1)} %all-gather.6.cloned.1.call-done.own) | copy-start | bytes 7962628
  192.9 8.9 %collective-permute-start.3 = (bf16[192,1152]{1,0:T(8,128)(2,1)}, bf16[192,1152]{1,0:T(8,128)(2,1)}, u32[]{:S(2)}, u32[]{:S(2)}) collective-permute-start(bf16[192,1152]{1,0:T(8,128)(2,1)} %get-tuple-element.19.n0), channel_id=1, source_target_pairs={{0,128},{128,0},{1,129},{129,1},{2,130},{130,2},{3,131},{131,3},{4... | collective-permute-start | bytes 1327112 | tf_op jit(solution)/shard_map/ppermute | solution.py:275
  194.1 31.6 %collective-permute-start.2 = (bf16[192,1152]{1,0:T(8,128)(2,1)}, bf16[192,1152]{1,0:T(8,128)(2,1)}, u32[]{:S(2)}, u32[]{:S(2)}) collective-permute-start(bf16[192,1152]{1,0:T(8,128)(2,1)} %get-tuple-element.19.n0), channel_id=1, source_target_pairs={{0,64},{64,0},{1,65},{65,1},{2,66},{66,2},{3,67},{67,3},{4,68},{68... | collective-permute-start | bytes 1327112 | tf_op jit(solution)/shard_map/ppermute | solution.py:274
  201.8 23.9 %collective-permute-start.4 = (bf16[192,1152]{1,0:T(8,128)(2,1)}, bf16[192,1152]{1,0:T(8,128)(2,1)}, u32[]{:S(2)}, u32[]{:S(2)}) collective-permute-start(bf16[192,1152]{1,0:T(8,128)(2,1)} %collective-permute-done.3.n2), channel_id=1, source_target_pairs={{0,64},{64,0},{1,65},{65,1},{2,66},{66,2},{3,67},{67,3},{4,68},{68... | collective-permute-start | bytes 1327112 | tf_op jit(solution)/shard_map/ppermute | solution.py:276
  225.7 1.6 copy-start.2
  227.3 0.8 copy-start.5
  228.0 14.5 %copy-start.8 = (f32[6,1152]{1,0:T(8,128)S(1)}, f32[6,1152]{1,0:T(8,128)}, u32[]{:S(2)}) copy-start(f32[6,1152]{1,0:T(8,128)} %mod_ref.5) | copy-start | bytes 82948
  232.9 2.6 %collective-permute-start.5 = (bf16[288,192]{1,0:T(8,128)(2,1)S(1)}, bf16[288,192]{1,0:T(8,128)(2,1)S(1)}, u32[]{:S(2)}, u32[]{:S(2)}) collective-permute-start(bf16[288,192]{1,0:T(8,128)(2,1)S(1)} %get-tuple-element.21), channel_id=1, source_target_pairs={{0,64},{64,0},{1,65},{65,1},{2,66},{66,2},{3,67},{67,3},{4,68},{68... | collective-permute-start | bytes 331784 | tf_op jit(solution)/shard_map/ppermute | solution.py:285
  233.8 5.4 %collective-permute-start.6 = (bf16[288,192]{1,0:T(8,128)(2,1)S(1)}, bf16[288,192]{1,0:T(8,128)(2,1)S(1)}, u32[]{:S(2)}, u32[]{:S(2)}) collective-permute-start(bf16[288,192]{1,0:T(8,128)(2,1)S(1)} %get-tuple-element.22), channel_id=1, source_target_pairs={{0,128},{128,0},{1,129},{129,1},{2,130},{130,2},{3,131},{131,3},{4... | collective-permute-start | bytes 331784 | tf_op jit(solution)/shard_map/ppermute | solution.py:286
  233.8 8.7 %collective-permute-start.7 = (bf16[288,192]{1,0:T(8,128)(2,1)S(1)}, bf16[288,192]{1,0:T(8,128)(2,1)S(1)}, u32[]{:S(2)}, u32[]{:S(2)}) collective-permute-start(bf16[288,192]{1,0:T(8,128)(2,1)S(1)} %get-tuple-element.23), channel_id=1, source_target_pairs={{0,192},{192,0},{64,128},{128,64},{1,193},{193,1},{65,129},{129,65... | collective-permute-start | bytes 331784 | tf_op jit(solution)/shard_map/ppermute | solution.py:287
Sparse Core Ops, SparseCore 0:
  9.1 68.8 all-gather.3
  84.6 72.8 all-gather.5
  167.0 58.6 all-gather.7

commit v2 on v1

v2 whole, which is shorter than its diff:
```python
import functools
import math

import jax
import jax.numpy as jnp
from jax import lax
from jax.experimental import pallas as pl
from jax.experimental.pallas import tpu as pltpu
from jax.sharding import Mesh
from jax.sharding import PartitionSpec as P

D = 1152
HEADS = 16
HD = 72
HP = 80
PATCH = 96
ROWS = 2 * PATCH
NZ, NY = 8, 4
PLANE = NZ * PATCH
BF = jnp.bfloat16
F32 = jnp.float32
FACTOR = 1.0 / math.sqrt(HD)
TN = (((0,), (0,)), ((), ()))
NT = (((1,), (1,)), ((), ()))
TT = (((0,), (1,)), ((), ()))
PARAMS = pltpu.CompilerParams(vmem_limit_bytes=48 * 1024 * 1024)


def normalise(values):
    mean_val = jnp.mean(values, -1, keepdims=True)
    centred = values - mean_val
    variance = jnp.mean(centred * centred, -1, keepdims=True)
    return centred * lax.rsqrt(variance + 1e-06)


def rms(values, gain):
    mean_sq = jnp.mean(values * values, 0, keepdims=True)
    return values * lax.rsqrt(mean_sq + 1e-06) * gain


def spatial_proj(tok_ref, mod_ref, w_ref, gain_ref, out_ref, turned):
    cols = 4 * PATCH
    zeros = jnp.zeros((HP - HD, cols), F32)
    first = lax.broadcasted_iota(jnp.int32, (HP - HD, cols), 0) == 0
    ones = jnp.where(first, 1.0, 0.0)

    @pl.when(pl.program_id(0) == 0)
    def _():
        turned[...] = w_ref[...].astype(F32).T.astype(BF)

    clips = []
    for clip in range(2):
        tok = tok_ref[:, clip * PATCH : (clip + 1) * PATCH, :].reshape(cols, D).astype(F32)
        normed = normalise(tok) * (1.0 + mod_ref[1:2, :]) + mod_ref[0:1, :]
        clips.append(normed.astype(BF))
    normed = jnp.concatenate(clips, 0)
    both = lax.dot_general(turned[: 6 * HD], normed, NT, preferred_element_type=F32)
    for clip in range(2):
        proj = both[:, clip * cols : (clip + 1) * cols]
        for head in range(2):
            query, key, value = (
                proj[part * 2 * HD + head * HD : part * 2 * HD + (head + 1) * HD] for part in range(3)
            )
            query = rms(query, gain_ref[:, 0:1]) * (FACTOR * math.log2(math.e))
            key = rms(key, gain_ref[:, 1:2])
            place = clip * 2 + head
            parts = [key, zeros, value, ones, query, zeros]
            out_ref[place] = jnp.concatenate(parts, 0).astype(BF)


def attend_step(q_ref, kv_ref, keys, acc):
    query = jnp.concatenate([q_ref[0], jnp.zeros((128 - HP, PLANE), BF)], 0)
    total = None
    for part in range(PLANE // 256):
        here = slice(part * 256, (part + 1) * 256)
        score = jnp.dot(keys[here, :], query, preferred_element_type=F32)
        expo = jnp.exp2(score).astype(BF)
        add = jnp.dot(kv_ref[0, HP : 2 * HP, here], expo, preferred_element_type=F32)
        total = add if total is None else total + add
    return acc + total


def turn_keys(kv_ref, keys):
    wide = jnp.concatenate([kv_ref[0, :HP].astype(F32), jnp.zeros((128 - HP, PLANE), F32)], 0)
    keys[...] = wide.T.astype(BF)


def attend(steps, resume, finish, *refs):
    q_ref, kv_ref = refs[:2]
    out_ref, keys, sums = refs[-3:]
    step, block = pl.program_id(0), pl.program_id(1)

    @pl.when(block == 0)
    def _():
        turn_keys(kv_ref, keys)

    @pl.when(step == 0)
    def _():
        sums[block] = refs[2][0] if resume else jnp.zeros((HP, PLANE), F32)

    sums[block] = attend_step(q_ref, kv_ref, keys, sums[block])

    @pl.when(step == steps - 1)
    def _():
        done = sums[block]
        if not finish:
            out_ref[0] = done
            return
        done = done[:HD] / done[HD : HD + 1]
        for z in range(NZ):
            out_ref[0, z] = done[:, z * PATCH : (z + 1) * PATCH].astype(BF)


def attention(query, key_value, part, finish):
    steps = key_value.shape[0]
    last = lambda k, q: jnp.where(k == steps - 1, q, 0)
    first = lambda k, q: jnp.where(k == 0, q, NY - 1)
    q_spec = pl.BlockSpec((1, HP, PLANE), lambda k, q: (q, 2, 0))
    kv_spec = pl.BlockSpec((1, 2 * HP, PLANE), lambda k, q: (k, 0, 0))
    in_specs, args = [q_spec, kv_spec], [query, key_value]
    if part is not None:
        in_specs.append(pl.BlockSpec((1, HP, PLANE), lambda k, q: (first(k, q), 0, 0)))
        args.append(part)
    if finish:
        out_spec = pl.BlockSpec((1, NZ, HD, PATCH), lambda k, q: (last(k, q), 0, 0, 0))
        out_shape = jax.ShapeDtypeStruct((NY, NZ, HD, PATCH), BF)
    else:
        out_spec = pl.BlockSpec((1, HP, PLANE), lambda k, q: (last(k, q), 0, 0))
        out_shape = jax.ShapeDtypeStruct((NY, HP, PLANE), F32)
    pairs = steps * NY * PLANE * PLANE
    return pl.pallas_call(
        functools.partial(attend, steps, part is not None, finish),
        grid=(steps, NY),
        in_specs=in_specs,
        out_specs=out_spec,
        out_shape=out_shape,
        scratch_shapes=[pltpu.VMEM((PLANE, 128), BF), pltpu.VMEM((NY, HP, PLANE), F32)],
        compiler_params=PARAMS,
        cost_estimate=pl.CostEstimate(
            flops=4 * 256 * pairs, bytes_accessed=4_000_000, transcendentals=pairs
        ),
        name="attend",
    )(*args)


def choose(flag, yes, no, rows):
    chunks = [jnp.where(flag, yes[n, rows, :], no[n, rows, :]) for n in range(5)]
    return jnp.concatenate(chunks, 1)[:, :D]


def spatial_end(place_ref, att_ref, tok_ref, mod_ref, own, got, resid_ref, norm_ref):
    weight = choose(place_ref[0] == 1, got, own, slice(0, D))
    rows = []
    for clip in range(2):
        feats = [
            att_ref[clip * 2 + head, pair].astype(F32) for pair in range(NZ) for head in range(2)
        ]
        rows.append(jnp.concatenate(feats, 0).T.astype(BF))
    attended = jnp.concatenate(rows, 0)
    branch = jnp.dot(attended, weight, preferred_element_type=F32)
    resid = tok_ref[...].astype(F32) + mod_ref[2:3, :] * branch
    resid_ref[...] = resid
    norm_ref[...] = (normalise(resid) * (1.0 + mod_ref[4:5, :]) + mod_ref[3:4, :]).astype(BF)


def temporal(place_ref, n0, n1, n2, n3, weight, gain_ref, o0, o1, o2, o3):
    weight = jnp.concatenate([weight[0, :, 128:], weight[1], weight[2], weight[3]], 1)
    gap = jnp.zeros((256 - ROWS, D), BF)
    rows = jnp.concatenate([n0[...], gap, n1[...], gap, n2[...], gap, n3[...], gap], 0)
    proj = lax.dot_general(weight, rows, TT, preferred_element_type=F32)
    queries, keys, values = [], [], []
    for frame in range(4):
        here = slice(frame * 256, (frame + 1) * 256)
        heads = [proj[n * HD : (n + 1) * HD, here] for n in range(12)]
        queries.append([rms(v, gain_ref[:, 2:3]).astype(BF).astype(F32) for v in heads[:4]])
        keys.append([rms(v, gain_ref[:, 3:4]).astype(BF).astype(F32) for v in heads[4:8]])
        values.append([v.astype(BF).astype(F32) for v in heads[8:]])
    for f, out_ref in enumerate((o0, o1, o2, o3)):
        mixed = []
        for head in range(4):
            total, attended = 0.0, 0.0
            for g in range(4):
                score = jnp.sum(queries[f][head] * keys[g][head], 0, keepdims=True) * FACTOR
                expo = jnp.exp(score)
                total = total + expo
                attended = attended + expo.astype(BF).astype(F32) * values[g][head]
            mixed.append((attended / total)[:, :ROWS])
        out_ref[...] = jnp.concatenate(mixed, 0).astype(BF)


def temporal_end(place_ref, m0, m1, m2, m3, resid_ref, mod_ref, own, got, out_ref):
    core = place_ref[0] == 1
    branch = None
    for step, att_ref in enumerate((m0, m1, m2, m3)):
        here = pl.ds(pl.multiple_of((place_ref[1] ^ step) * (4 * HD), 4 * HD), 4 * HD)
        rows = choose(core, own, got, here)
        add = jnp.dot(att_ref[...].astype(F32).T.astype(BF), rows, preferred_element_type=F32)
        branch = add if branch is None else branch + add
    out_ref[...] = (resid_ref[...] + mod_ref[5:6, :] * branch).astype(BF)


def whole(shapes, kernel, name, *args):
    specs, arrays = [pl.BlockSpec(memory_space=pltpu.SMEM)], [args[0]]
    for arg in args[1:]:
        array, count, n = arg if isinstance(arg, tuple) else (arg, arg.shape[0], 0)
        place = (n,) + (0,) * (array.ndim - 1)
        specs.append(pl.BlockSpec((count,) + array.shape[1:], lambda i, place=place: place))
        arrays.append(array)
    return pl.pallas_call(
        kernel,
        grid=(1,),
        in_specs=specs,
        out_specs=[pl.BlockSpec(s.shape, lambda i: (0, 0)) for s in shapes],
        out_shape=shapes,
        compiler_params=PARAMS,
        name=name,
    )(*arrays)


def per_device(tokens, modulation, spatial_qkv, spatial_out, temporal_qkv, temporal_out, norm_gains):
    core = lax.axis_index("c")
    frame = lax.axis_index("xl") * 2 + core
    place = jnp.stack([core, frame]).astype(jnp.int32)
    gains = norm_gains.T
    tok = tokens.reshape(ROWS, D)

    part_a = spatial_qkv.reshape(18, 3, NZ, 2 * HD).transpose(2, 0, 1, 3).reshape(NZ, 18, 6 * HD)
    part_a = jnp.pad(part_a, ((0, 0), (0, 0), (0, 512 - 6 * HD)))
    part_b = lax.dynamic_slice_in_dim(temporal_qkv.reshape(18, 3, D), frame * 4 * HD, 4 * HD, 2)
    rest = [jnp.where(core == 0, spatial_out, temporal_out), part_b.reshape(18, 12 * HD)]
    rest = jnp.pad(jnp.concatenate(rest, 1), ((0, 0), (0, 256 * NZ - D - 12 * HD)))
    rest = rest.reshape(18, NZ, 256).transpose(1, 0, 2)
    shard = jnp.concatenate([part_a, rest], 2)
    shard = lax.all_to_all(shard, "z", 0, 0, tiled=True).reshape(1, NZ * 18, 768)
    shard = jnp.broadcast_to(shard, (8, NZ * 18, 768))
    shard = lax.all_to_all(shard, ("xh", "y"), 0, 0, tiled=True).reshape(D, 768)

    column = lax.all_gather(tok, "z", axis=0)

    rest, column = lax.optimization_barrier((shard[:, 512:], column))
    rest = lax.all_gather(rest, "z", axis=0)

    projected = pl.pallas_call(
        spatial_proj,
        grid=(2,),
        in_specs=[
            pl.BlockSpec((4, ROWS, D), lambda i: (i, 0, 0)),
            pl.BlockSpec((6, D), lambda i: (0, 0)),
            pl.BlockSpec((D, 512), lambda i: (0, 0)),
            pl.BlockSpec((HD, 4), lambda i: (0, 0)),
        ],
        out_specs=pl.BlockSpec((4, 3 * HP, 4 * PATCH), lambda i: (0, 0, i)),
        out_shape=jax.ShapeDtypeStruct((4, 3 * HP, PLANE), BF),
        scratch_shapes=[pltpu.VMEM((512, D), BF)],
        compiler_params=PARAMS,
        name="spatial_proj",
    )(column, modulation, shard, gains)

    swap = [(0, 1), (1, 0)]
    projected = lax.all_to_all(projected, "y", 0, 0, tiled=True)
    other_a = lax.ppermute(projected[:2, : 2 * HP], "xh", swap)
    other_b = lax.ppermute(projected[2:, : 2 * HP], "xh", swap)
    part = attention(projected, projected, None, False)
    part = attention(projected, other_a, part, False)
    attended = attention(projected, other_b, part, True)
    attended, rest = lax.optimization_barrier((attended, rest))
    rest_got = lax.ppermute(rest, "c", swap)
    attended = attended.reshape(NY * NZ, HD, PATCH)
    attended = lax.all_to_all(attended, ("y", "z"), 0, 0, tiled=True)
    attended = attended.reshape(4, NZ, HD, PATCH)

    resid, normed_b = whole(
        [jax.ShapeDtypeStruct((ROWS, D), F32), jax.ShapeDtypeStruct((ROWS, D), BF)],
        spatial_end,
        "spatial_end",
        place, attended, tok, modulation, (rest, 5, 0), (rest_got, 5, 0),
    )
    norm_c = lax.ppermute(normed_b, "c", swap)
    norm_x = lax.ppermute(normed_b, "xl", swap)
    norm_cx = lax.ppermute(norm_x, "c", swap)
    mixed = whole(
        [jax.ShapeDtypeStruct((4 * HD, ROWS), BF)] * 4,
        temporal,
        "temporal",
        place, normed_b, norm_c, norm_x, norm_cx, (rest, 4, 1), gains,
    )
    mixed = [
        mixed[0],
        lax.ppermute(mixed[1], "c", swap),
        lax.ppermute(mixed[2], "xl", swap),
        lax.ppermute(mixed[3], ("xl", "c"), [(0, 3), (3, 0), (1, 2), (2, 1)]),
    ]
    (result,) = whole(
        [jax.ShapeDtypeStruct((ROWS, D), BF)],
        temporal_end,
        "temporal_end",
        place, *mixed, resid, modulation, (rest, 5, 0), (rest_got, 5, 0),
    )
    return result.reshape(2, 1, PATCH, D)


def solution(mesh):
    fine = Mesh(mesh.devices.reshape(2, 2, 2, NY, NZ), ("xl", "c", "xh", "y", "z"))
    time, space = ("xl", "c"), ("xh", "y", "z")
    block = P(None, time, space, None)
    rows = P(space, None)
    return jax.shard_map(
        per_device,
        mesh=fine,
        in_specs=(block, P(), rows, rows, rows, rows, P()),
        out_specs=block,
        check_vma=False,
    )
```

time: 254 us -> 194 us (0.76)
  waiting for transfers between devices: 75.5 us -> 34.5 us
  starting transfers between devices: 35.9 us -> 21.5 us
  local copies, waits for them, and re-layouts: 11.1 us -> 4.05 us
    all_gather x2 -> x1, waiting for transfers between devices: 17.7 us -> 0.01 us  [per_device(): rest = lax.all_gather(rest, 'z', axis=0)]
    ppermute x2 -> x3, waiting for transfers between devices: 13.9 us -> 0.01 us  [the longest x1 0.01 us: per_device(): other_a = lax.ppermute(projected[:2, :2 * HP], 'xh', swap)]
    all_to_all x1 -> x0, waiting for transfers between devices: 11.6 us -> none  [per_device(): lax.all_to_all(weight_a, ('xh', 'y'), 0, 0, tiled=True).reshape(D, 6 * HD)]
    all_to_all x1 -> x0, starting transfers between devices: 6.82 us -> none  [per_device(): lax.all_to_all(weight_a, ('xh', 'y'), 0, 0, tiled=True).reshape(D, 6 * HD)]
    ppermute x2 -> x3, starting transfers between devices: 11 us -> 5.23 us  [the longest x1 2.82 us: per_device(): other_a = lax.ppermute(projected[:2, :2 * HP], 'xh', swap)]
    all_to_all x1, blocking collectives: 27.6 us -> 23 us  [per_device(): projected = lax.all_to_all(projected, 'y', 0, 0, tiled=True)]
    unnamed x28 -> x8, local copies, waits for them, and re-layouts: 4.29 us -> 0.13 us
    all_to_all x1 -> x2, blocking collectives: 42.5 us -> 46.2 us  [the longest x1 26.3 us: per_device(): shard = lax.all_to_all(shard, ('xh', 'y'), 0, 0, tiled=True).reshape(D, 768)]
  transfers between devices with their start and end apart: 13 -> 12, of which waited for: 8 -> 6; matrix products, arithmetic and copies ran while one was open for 3% -> 3% of each run, Pallas kernels for 13% -> 18%
where the time goes in v2:
time: 194 us; the launch traced here: 192 us
  blocking collectives  69.2 us (36%)
  Pallas kernels  48.6 us (25%)
  waiting for transfers between devices  34.5 us (18%)
  starting transfers between devices  21.5 us (11%)
  between operations  13.6 us (7%)
  local copies, waits for them, and re-layouts  4.05 us (2%)
    pallas_call x3, Pallas kernels, attention(): pl.pallas_call(functools.partial(attend, steps, part is not None, finish)...  29.2 us
    all_to_all x1, blocking collectives, per_device(): shard = lax.all_to_all(shard, ('xh', 'y'), 0, 0, tiled=True).reshape(D, 768)  26.3 us
    all_to_all x1, blocking collectives, per_device(): projected = lax.all_to_all(projected, 'y', 0, 0, tiled=True)  23 us
    all_to_all x1, blocking collectives, per_device(): lax.all_to_all(shard, 'z', 0, 0, tiled=True).reshape(1, NZ * 18, 768)  19.9 us
    all_to_all x1, waiting for transfers between devices, per_device(): attended = lax.all_to_all(attended, ('y', 'z'), 0, 0, tiled=True)  15.8 us
    pallas_call x3, Pallas kernels, whole(): pl.pallas_call(kernel, grid=(1,), in_specs=specs, out_specs=[pl.BlockSpec...  13.7 us
    pallas_call x1, Pallas kernels, per_device(): pl.pallas_call(spatial_proj, grid=(2,), in_specs=[pl.BlockSpec((4, ROWS,...  5.76 us
    all_gather x1, waiting for transfers between devices, per_device(): column = lax.all_gather(tok, 'z', axis=0)  5.67 us
  transfers between devices with their start and end apart: 12, of which 6 were waited for; matrix products, arithmetic and copies ran while one was open for 3% of the time, Pallas kernels for 18%

profile of v2, /device:TPU:1, one launch (start us, length us, event | category | flops | bytes accessed | tf_op | source)
XLA Modules:
  0.0 192.5 jit_solution(8296377673301288635)
XLA Ops:
  6.5 0.7 all-gather.4.cloned.1.call-update
  7.3 0.0 all-gather.6.cloned.1.call-start
  7.3 1.0 reshape.34
  8.3 0.1 constant_dynamic-slice_fusion
  8.4 0.1 reshape.35
  8.5 0.8 broadcast_select_fusion
  9.4 1.2 reshape.32
  10.6 0.1 copy.21
  10.8 0.2 reshape.33
  11.0 19.9 %all_to_all.20 = bf16[8,18,768]{2,1,0:T(8,128)(2,1)S(1)} all-to-all(bf16[8,18,768]{2,1,0:T(8,128)(2,1)S(1)} %copy.16), channel_id=1, replica_groups=mesh['xl'=2,'c'=2,'xh'=2,'y'=4,'z'=8] {'z'}, dimensions={0} | all-to-all | bytes 442368 | tf_op jit(solution)/shard_map/all_to_all | solution.py:234
  30.9 0.1 broadcast_in_dim.7
  31.0 0.1 broadcast_in_dim.8
  31.1 26.3 %all_to_all.21 = bf16[8,144,768]{2,1,0:T(8,128)(2,1)S(1)} all-to-all(bf16[8,144,768]{2,1,0:T(8,128)(2,1)S(1)} %broadcast_in_dim.8), channel_id=1, replica_groups=mesh['xl'=2,'c'=2,'xh'=2,'y'=4,'z'=8] {'xh','y'}, dimensions={0} | all-to-all | bytes 3538944 | tf_op jit(solution)/shard_map/all_to_all | solution.py:236
  57.5 0.9 slice.12
  58.4 5.7 %all-gather.4.cloned.1.call-done.tok_ref = bf16[8,192,1152]{2,1,0:T(8,128)(2,1)} async-done(((bf16[1,192,1152]{2,1,0:T(8,128)(2,1)}), bf16[8,192,1152]{2,1,0:T(8,128)(2,1)}) %all-gather.4.cloned.1.call-update) | async-done | bytes 3538960 | tf_op jit(solution)/shard_map/all_gather | solution.py:238
  64.1 0.0 all-gather.6.cloned.1.call-update
  64.1 0.1 copy.17
  64.2 5.8 %spatial_proj.1 = bf16[4,240,768]{2,1,0:T(8,128)(2,1)S(1)} custom-call(bf16[8,192,1152]{2,1,0:T(8,128)(2,1)} %all-gather.4.cloned.1.call-done.tok_ref, f32[6,1152]{1,0:T(8,128)S(1)} %copy-done.1, bf16[1152,768]{1,0:T(8,128)(2,1)S(1)} %bitcast.23, f32[72,4]{1,0:T(8,128)S(1)} %bitcast.27), custom_call_target="tpu_custom_call" | custom-call | tf_op jit(solution)/shard_map/spatial_proj/pallas_call | solution.py:243
  70.0 23.0 %all_to_all.22.refs_0_.refs_1_ = bf16[4,240,768]{2,1,0:T(8,128)(2,1)S(1)} all-to-all(bf16[4,240,768]{2,1,0:T(8,128)(2,1)S(1)} %spatial_proj.1), channel_id=1, replica_groups=mesh['xl'=2,'c'=2,'xh'=2,'y'=4,'z'=8] {'y'}, dimensions={0} | all-to-all | bytes 2949120 | tf_op jit(solution)/shard_map/all_to_all | solution.py:260
  93.0 0.1 fusion.5
  93.0 2.8 %collective-permute-start.1 = (bf16[2,160,768]{2,1,0:T(8,128)(2,1)S(1)}, bf16[2,160,768]{2,1,0:T(8,128)(2,1)S(1)}, u32[]{:S(2)}, u32[]{:S(2)}) collective-permute-start(bf16[2,160,768]{2,1,0:T(8,128)(2,1)S(1)} %get-tuple-element.25), channel_id=1, source_target_pairs={{0,32},{32,0},{1,33},{33,1},{2,34},{34,2},{3,35},{35,3},{4,36},{36... | collective-permute-start | bytes 1474568 | tf_op jit(solution)/shard_map/ppermute | solution.py:261
  95.9 0.2 collective-permute-start
  96.1 13.9 %attend.3.refs_2_ = f32[4,80,768]{2,1,0:T(8,128)S(1)} custom-call(bf16[4,240,768]{2,1,0:T(8,128)(2,1)S(1)} %all_to_all.22.refs_0_.refs_1_, bf16[4,240,768]{2,1,0:T(8,128)(2,1)S(1)} %all_to_all.22.refs_0_.refs_1_), custom_call_target="tpu_custom_call" | custom-call | flops 9663676416 | bytes 4000000 | tf_op jit(solution)/shard_map/attend/pallas_call | solution.py:131
  110.0 0.0 collective-permute-done.1.refs_1_
  110.0 7.0 %attend.4.refs_2_ = f32[4,80,768]{2,1,0:T(8,128)S(1)} custom-call(bf16[4,240,768]{2,1,0:T(8,128)(2,1)S(1)} %all_to_all.22.refs_0_.refs_1_, bf16[2,160,768]{2,1,0:T(8,128)(2,1)S(1)} %collective-permute-done.1.refs_1_, f32[4,80,768]{2,1,0:T(8,128)S(1)} %attend.3.refs_2_), custom_call_target="tpu_custom_call" | custom-call | flops 4831838208 | bytes 4000000 | tf_op jit(solution)/shard_map/attend/pallas_call | solution.py:131
  117.1 0.0 copy-start
  117.1 0.0 collective-permute-done.refs_1_
  117.1 8.2 %attend.5 = bf16[4,8,72,96]{3,2,1,0:T(8,128)(2,1)} custom-call(bf16[4,240,768]{2,1,0:T(8,128)(2,1)S(1)} %all_to_all.22.refs_0_.refs_1_, bf16[2,160,768]{2,1,0:T(8,128)(2,1)S(1)} %collective-permute-done.refs_1_, f32[4,80,768]{2,1,0:T(8,128)S(1)} %attend.4.refs_2_), custom_call_target="tpu_custom_call" | custom-call | flops 4831838208 | bytes 4000000 | tf_op jit(solution)/shard_map/attend/pallas_call | solution.py:131
  125.3 2.2 %collective-permute-start.2 = (bf16[8,1152,256]{2,1,0:T(8,128)(2,1)}, bf16[8,1152,256]{2,1,0:T(8,128)(2,1)}, u32[]{:S(2)}, u32[]{:S(2)}) collective-permute-start(bf16[8,1152,256]{2,1,0:T(8,128)(2,1)} %bitcast.29), channel_id=1, source_target_pairs={{0,64},{64,0},{1,65},{65,1},{2,66},{66,2},{3,67},{67,3},{4,68},{68... | collective-permute-start | bytes 14155784 | tf_op jit(solution)/shard_map/ppermute | solution.py:267
  127.5 5.2 %all-to-all-start.3 = ((bf16[32,72,96]{2,1,0:T(8,128)(2,1)}), bf16[32,72,96]{2,1,0:T(8,128)(2,1)S(1)}, u32[]{:S(2)}, u32[]{:S(2)}) async-start(bf16[32,72,96]{2,1,0:T(8,128)(2,1)} %bitcast.8), calls=%async_computation.3 | async-start | bytes 1179648 | tf_op jit(solution)/shard_map/all_to_all | solution.py:269
  132.7 0.1 pad_add_fusion.place_ref
  132.8 15.8 %all-to-all-done.3 = bf16[32,72,96]{2,1,0:T(8,128)(2,1)S(1)} async-done(((bf16[32,72,96]{2,1,0:T(8,128)(2,1)}), bf16[32,72,96]{2,1,0:T(8,128)(2,1)S(1)}, u32[]{:S(2)}, u32[]{:S(2)}) %all-to-all-start.3) | async-done | bytes 442400 | tf_op jit(solution)/shard_map/all_to_all | solution.py:269
  148.7 0.0 collective-permute-done.2.got
  148.7 3.9 %spatial_end.1 = (f32[192,1152]{1,0:T(8,128)S(1)}, bf16[192,1152]{1,0:T(8,128)(2,1)S(1)}) custom-call(s32[2]{0:T(128)S(1)} %pad_add_fusion.place_ref, bf16[4,8,72,96]{3,2,1,0:T(8,128)(2,1)S(1)} %bitcast.24, bf16[192,1152]{1,0:T(8,128)(2,1)S(1)} %bitcast.26, f32[6,1152]{1,0:T(8,128)S(1)} %copy-done.1, bf16[8,1152,256]{2,1,0:T(8,128)(2,1)} %bitcast.30, ...), custom_call_target="tpu_custom_call" | custom-call | tf_op jit(solution)/shard_map/spatial_end/pallas_call | solution.py:209
  152.6 1.3 collective-permute-start.4
  153.9 3.4 %collective-permute-start.3 = (bf16[192,1152]{1,0:T(8,128)(2,1)S(1)}, bf16[192,1152]{1,0:T(8,128)(2,1)S(1)}, u32[]{:S(2)}, u32[]{:S(2)}) collective-permute-start(bf16[192,1152]{1,0:T(8,128)(2,1)S(1)} %get-tuple-element.19.n0), channel_id=1, source_target_pairs={{0,64},{64,0},{1,65},{65,1},{2,66},{66,2},{3,67},{67,3},{4,68},{68... | collective-permute-start | bytes 1327112 | tf_op jit(solution)/shard_map/ppermute | solution.py:278
  157.3 3.9 %collective-permute-done.4.n2 = bf16[192,1152]{1,0:T(8,128)(2,1)S(1)} collective-permute-done((bf16[192,1152]{1,0:T(8,128)(2,1)S(1)}, bf16[192,1152]{1,0:T(8,128)(2,1)S(1)}, u32[]{:S(2)}, u32[]{:S(2)}) %collective-permute-start.4) | collective-permute-done | bytes 442400 | tf_op jit(solution)/shard_map/ppermute | solution.py:279
  161.2 4.0 %collective-permute-start.5 = (bf16[192,1152]{1,0:T(8,128)(2,1)S(1)}, bf16[192,1152]{1,0:T(8,128)(2,1)S(1)}, u32[]{:S(2)}, u32[]{:S(2)}) collective-permute-start(bf16[192,1152]{1,0:T(8,128)(2,1)S(1)} %collective-permute-done.4.n2), channel_id=1, source_target_pairs={{0,64},{64,0},{1,65},{65,1},{2,66},{66,2},{3,67},{67,3},{4,68},{68... | collective-permute-start | bytes 1327112 | tf_op jit(solution)/shard_map/ppermute | solution.py:280
  165.3 0.0 collective-permute-done.3.n1
  165.3 1.4 collective-permute-done.5.n3
  166.7 5.0 %temporal.1 = (bf16[288,192]{1,0:T(8,128)(2,1)S(1)}, bf16[288,192]{1,0:T(8,128)(2,1)S(1)}, bf16[288,192]{1,0:T(8,128)(2,1)S(1)}, bf16[288,192]{1,0:T(8,128)(2,1)S(1)}) custom-call(s32[2]{0:T(128)S(1)} %pad_add_fusion.place_ref, bf16[192,1152]{1,0:T(8,128)(2,1)S(1)} %get-tuple-element.19.n0, bf16[192,1152]{1,0:T(8,128)(2,1)S(1)} %collective-permute-done.3.n1, ...), custom_call_target="tpu_custom_call" | custom-call | tf_op jit(solution)/shard_map/temporal/pallas_call | solution.py:209
  171.7 0.5 collective-permute-start.6
  172.2 1.2 collective-permute-start.7
  173.4 0.6 collective-permute-start.8
  173.9 0.0 collective-permute-done.6.m1
  174.0 3.5 %collective-permute-done.7.m2 = bf16[288,192]{1,0:T(8,128)(2,1)S(1)} collective-permute-done((bf16[288,192]{1,0:T(8,128)(2,1)S(1)}, bf16[288,192]{1,0:T(8,128)(2,1)S(1)}, u32[]{:S(2)}, u32[]{:S(2)}) %collective-permute-start.7) | collective-permute-done | bytes 110624 | tf_op jit(solution)/shard_map/ppermute | solution.py:290
  177.5 3.4 %collective-permute-done.8.m3 = bf16[288,192]{1,0:T(8,128)(2,1)S(1)} collective-permute-done((bf16[288,192]{1,0:T(8,128)(2,1)S(1)}, bf16[288,192]{1,0:T(8,128)(2,1)S(1)}, u32[]{:S(2)}, u32[]{:S(2)}) %collective-permute-start.8) | collective-permute-done | bytes 110624 | tf_op jit(solution)/shard_map/ppermute | solution.py:291
  180.9 4.7 %temporal_end.1 = bf16[192,1152]{1,0:T(8,128)(2,1)} custom-call(s32[2]{0:T(128)S(1)} %pad_add_fusion.place_ref, bf16[288,192]{1,0:T(8,128)(2,1)S(1)} %get-tuple-element.20.m0, bf16[288,192]{1,0:T(8,128)(2,1)S(1)} %collective-permute-done.6.m1, bf16[288,192]{1,0:T(8,128)(2,1)S(1)} %collective-permute-done.7.m2, ...), custom_call_target="tpu_custom_call" | custom-call | tf_op jit(solution)/shard_map/temporal_end/pallas_call | solution.py:209
  (12 shorter events, 0.1 us)
Async XLA Ops:
  6.5 57.5 %all-gather.4.cloned.1.call-start = ((), (), s32[]{:S(2)}) async-start(), calls=%async_computation.4 | async-start | bytes 3981312 | tf_op jit(solution)/shard_map/all_gather | solution.py:238
  7.3 118.1 %all-gather.6.cloned.1.call-start = ((), (), s32[]{:S(2)}) async-start(), calls=%async_computation.5 | async-start | bytes 5308416 | tf_op jit(solution)/shard_map/all_gather | solution.py:241
  57.5 6.6 %copy-start.2 = (f32[4,72]{1,0:T(4,128)S(1)}, f32[4,72]{1,0:T(4,128)}, u32[]{:S(2)}) copy-start(f32[4,72]{1,0:T(4,128)} %param.13) | copy-start | bytes 3460
  57.5 6.7 %copy-start.1 = (f32[6,1152]{1,0:T(8,128)S(1)}, f32[6,1152]{1,0:T(8,128)}, u32[]{:S(2)}) copy-start(f32[6,1152]{1,0:T(8,128)} %mod_ref.5) | copy-start | bytes 82948
  93.0 17.0 %collective-permute-start.1 = (bf16[2,160,768]{2,1,0:T(8,128)(2,1)S(1)}, bf16[2,160,768]{2,1,0:T(8,128)(2,1)S(1)}, u32[]{:S(2)}, u32[]{:S(2)}) collective-permute-start(bf16[2,160,768]{2,1,0:T(8,128)(2,1)S(1)} %get-tuple-element.25), channel_id=1, source_target_pairs={{0,32},{32,0},{1,33},{33,1},{2,34},{34,2},{3,35},{35,3},{4,36},{36... | collective-permute-start | bytes 1474568 | tf_op jit(solution)/shard_map/ppermute | solution.py:261
  95.9 21.2 %collective-permute-start = (bf16[2,160,768]{2,1,0:T(8,128)(2,1)S(1)}, bf16[2,160,768]{2,1,0:T(8,128)(2,1)S(1)}, u32[]{:S(2)}, u32[]{:S(2)}) collective-permute-start(bf16[2,160,768]{2,1,0:T(8,128)(2,1)S(1)} %get-tuple-element.26), channel_id=1, source_target_pairs={{0,32},{32,0},{1,33},{33,1},{2,34},{34,2},{3,35},{35,3},{4,36},{36... | collective-permute-start | bytes 1474568 | tf_op jit(solution)/shard_map/ppermute | solution.py:262
  117.1 31.6 %copy-start = (bf16[2,1,96,1152]{3,2,1,0:T(8,128)(2,1)S(1)}, bf16[2,1,96,1152]{3,2,1,0:T(8,128)(2,1)}, u32[]{:S(2)}) copy-start(bf16[2,1,96,1152]{3,2,1,0:T(8,128)(2,1)} %param.7) | copy-start | bytes 1327108
  125.3 23.3 %collective-permute-start.2 = (bf16[8,1152,256]{2,1,0:T(8,128)(2,1)}, bf16[8,1152,256]{2,1,0:T(8,128)(2,1)}, u32[]{:S(2)}, u32[]{:S(2)}) collective-permute-start(bf16[8,1152,256]{2,1,0:T(8,128)(2,1)} %bitcast.29), channel_id=1, source_target_pairs={{0,64},{64,0},{1,65},{65,1},{2,66},{66,2},{3,67},{67,3},{4,68},{68... | collective-permute-start | bytes 14155784 | tf_op jit(solution)/shard_map/ppermute | solution.py:267
  127.5 21.2 %all-to-all-start.3 = ((bf16[32,72,96]{2,1,0:T(8,128)(2,1)}), bf16[32,72,96]{2,1,0:T(8,128)(2,1)S(1)}, u32[]{:S(2)}, u32[]{:S(2)}) async-start(bf16[32,72,96]{2,1,0:T(8,128)(2,1)} %bitcast.8), calls=%async_computation.3 | async-start | bytes 1179648 | tf_op jit(solution)/shard_map/all_to_all | solution.py:269
  152.6 8.6 %collective-permute-start.4 = (bf16[192,1152]{1,0:T(8,128)(2,1)S(1)}, bf16[192,1152]{1,0:T(8,128)(2,1)S(1)}, u32[]{:S(2)}, u32[]{:S(2)}) collective-permute-start(bf16[192,1152]{1,0:T(8,128)(2,1)S(1)} %get-tuple-element.19.n0), channel_id=1, source_target_pairs={{0,128},{128,0},{1,129},{129,1},{2,130},{130,2},{3,131},{131,3},{4... | collective-permute-start | bytes 1327112 | tf_op jit(solution)/shard_map/ppermute | solution.py:279
  153.9 11.4 %collective-permute-start.3 = (bf16[192,1152]{1,0:T(8,128)(2,1)S(1)}, bf16[192,1152]{1,0:T(8,128)(2,1)S(1)}, u32[]{:S(2)}, u32[]{:S(2)}) collective-permute-start(bf16[192,1152]{1,0:T(8,128)(2,1)S(1)} %get-tuple-element.19.n0), channel_id=1, source_target_pairs={{0,64},{64,0},{1,65},{65,1},{2,66},{66,2},{3,67},{67,3},{4,68},{68... | collective-permute-start | bytes 1327112 | tf_op jit(solution)/shard_map/ppermute | solution.py:278
  161.2 5.5 %collective-permute-start.5 = (bf16[192,1152]{1,0:T(8,128)(2,1)S(1)}, bf16[192,1152]{1,0:T(8,128)(2,1)S(1)}, u32[]{:S(2)}, u32[]{:S(2)}) collective-permute-start(bf16[192,1152]{1,0:T(8,128)(2,1)S(1)} %collective-permute-done.4.n2), channel_id=1, source_target_pairs={{0,64},{64,0},{1,65},{65,1},{2,66},{66,2},{3,67},{67,3},{4,68},{68... | collective-permute-start | bytes 1327112 | tf_op jit(solution)/shard_map/ppermute | solution.py:280
  171.7 2.2 %collective-permute-start.6 = (bf16[288,192]{1,0:T(8,128)(2,1)S(1)}, bf16[288,192]{1,0:T(8,128)(2,1)S(1)}, u32[]{:S(2)}, u32[]{:S(2)}) collective-permute-start(bf16[288,192]{1,0:T(8,128)(2,1)S(1)} %get-tuple-element.21), channel_id=1, source_target_pairs={{0,64},{64,0},{1,65},{65,1},{2,66},{66,2},{3,67},{67,3},{4,68},{68... | collective-permute-start | bytes 331784 | tf_op jit(solution)/shard_map/ppermute | solution.py:289
  172.2 5.3 %collective-permute-start.7 = (bf16[288,192]{1,0:T(8,128)(2,1)S(1)}, bf16[288,192]{1,0:T(8,128)(2,1)S(1)}, u32[]{:S(2)}, u32[]{:S(2)}) collective-permute-start(bf16[288,192]{1,0:T(8,128)(2,1)S(1)} %get-tuple-element.22), channel_id=1, source_target_pairs={{0,128},{128,0},{1,129},{129,1},{2,130},{130,2},{3,131},{131,3},{4... | collective-permute-start | bytes 331784 | tf_op jit(solution)/shard_map/ppermute | solution.py:290
  173.4 7.5 %collective-permute-start.8 = (bf16[288,192]{1,0:T(8,128)(2,1)S(1)}, bf16[288,192]{1,0:T(8,128)(2,1)S(1)}, u32[]{:S(2)}, u32[]{:S(2)}) collective-permute-start(bf16[288,192]{1,0:T(8,128)(2,1)S(1)} %get-tuple-element.23), channel_id=1, source_target_pairs={{0,192},{192,0},{64,128},{128,64},{1,193},{193,1},{65,129},{129,65... | collective-permute-start | bytes 331784 | tf_op jit(solution)/shard_map/ppermute | solution.py:291
Sparse Core Ops, SparseCore 0:
  9.1 54.8 all-gather.3
  65.8 58.5 all-gather.5

commit v3 on v2

v3 whole, which is shorter than its diff:
```python
import functools
import math

import jax
import jax.numpy as jnp
from jax import lax
from jax.experimental import pallas as pl
from jax.experimental.pallas import tpu as pltpu
from jax.sharding import Mesh
from jax.sharding import PartitionSpec as P

D = 1152
HEADS = 16
HD = 72
HP = 80
PATCH = 96
ROWS = 2 * PATCH
NZ, NY = 8, 4
PLANE = NZ * PATCH
BF = jnp.bfloat16
F32 = jnp.float32
FACTOR = 1.0 / math.sqrt(HD)
TN = (((0,), (0,)), ((), ()))
NT = (((1,), (1,)), ((), ()))
PARAMS = pltpu.CompilerParams(vmem_limit_bytes=48 * 1024 * 1024)


def normalise(values):
    mean_val = jnp.mean(values, -1, keepdims=True)
    centred = values - mean_val
    variance = jnp.mean(centred * centred, -1, keepdims=True)
    return centred * lax.rsqrt(variance + 1e-06)


def rms(values, gain):
    mean_sq = jnp.mean(values * values, 0, keepdims=True)
    return values * lax.rsqrt(mean_sq + 1e-06) * gain


def spatial_proj(tok_ref, mod_ref, w_ref, gain_ref, out_ref, turned):
    cols = 4 * PATCH
    zeros = jnp.zeros((HP - HD, cols), F32)
    first = lax.broadcasted_iota(jnp.int32, (HP - HD, cols), 0) == 0
    ones = jnp.where(first, 1.0, 0.0)

    @pl.when(pl.program_id(0) == 0)
    def _():
        turned[...] = w_ref[...].astype(F32).T.astype(BF)

    clips = []
    for clip in range(2):
        tok = tok_ref[:, clip * PATCH : (clip + 1) * PATCH, :].reshape(cols, D).astype(F32)
        normed = normalise(tok) * (1.0 + mod_ref[1:2, :]) + mod_ref[0:1, :]
        clips.append(normed.astype(BF))
    normed = jnp.concatenate(clips, 0)
    both = lax.dot_general(turned[: 6 * HD], normed, NT, preferred_element_type=F32)
    for clip in range(2):
        proj = both[:, clip * cols : (clip + 1) * cols]
        for head in range(2):
            query, key, value = (
                proj[part * 2 * HD + head * HD : part * 2 * HD + (head + 1) * HD] for part in range(3)
            )
            query = rms(query, gain_ref[:, 0:1]) * (FACTOR * math.log2(math.e))
            key = rms(key, gain_ref[:, 1:2])
            place = clip * 2 + head
            parts = [key, zeros, value, ones, query, zeros]
            out_ref[place] = jnp.concatenate(parts, 0).astype(BF)


def attend(steps, resume, finish, *refs):
    q_ref, kv_ref = refs[:2]
    out_ref, keys = refs[-2:]

    @pl.when(pl.program_id(0) == 0)
    def _():
        gap = jnp.zeros((128 - HP, PLANE), F32)
        for n in range(steps):
            keys[n] = jnp.concatenate([kv_ref[n, :HP].astype(F32), gap], 0).T.astype(BF)

    query = jnp.concatenate([q_ref[0], jnp.zeros((128 - HP, PLANE), BF)], 0)
    parts = [(n, slice(p, p + 256)) for n in range(steps) for p in range(0, PLANE, 256)]

    def scores(n, here):
        return jnp.dot(keys[n, here, :], query, preferred_element_type=F32)

    done = refs[2][0] if resume else None
    ahead = scores(*parts[0])
    for place, (n, here) in enumerate(parts):
        score = ahead
        if place + 1 < len(parts):
            ahead = scores(*parts[place + 1])
        expo = jnp.exp2(score).astype(BF)
        add = jnp.dot(kv_ref[n, HP : 2 * HP, here], expo, preferred_element_type=F32)
        done = add if done is None else done + add
    if not finish:
        out_ref[0] = done
        return
    done = done[:HD] / done[HD : HD + 1]
    for z in range(NZ):
        out_ref[0, z] = done[:, z * PATCH : (z + 1) * PATCH].astype(BF)


def attention(query, key_value, part, finish):
    steps = key_value.shape[0]
    sums = pl.BlockSpec((1, HP, PLANE), lambda q: (q, 0, 0))
    in_specs = [
        pl.BlockSpec((1, HP, PLANE), lambda q: (q, 2, 0)),
        pl.BlockSpec((steps, 2 * HP, PLANE), lambda q: (0, 0, 0)),
    ]
    args = [query, key_value]
    if part is not None:
        in_specs.append(sums)
        args.append(part)
    if finish:
        out_spec = pl.BlockSpec((1, NZ, HD, PATCH), lambda q: (q, 0, 0, 0))
        out_shape = jax.ShapeDtypeStruct((NY, NZ, HD, PATCH), BF)
    else:
        out_spec = sums
        out_shape = jax.ShapeDtypeStruct((NY, HP, PLANE), F32)
    pairs = steps * NY * PLANE * PLANE
    return pl.pallas_call(
        functools.partial(attend, steps, part is not None, finish),
        grid=(NY,),
        in_specs=in_specs,
        out_specs=out_spec,
        out_shape=out_shape,
        scratch_shapes=[pltpu.VMEM((steps, PLANE, 128), BF)],
        compiler_params=PARAMS,
        cost_estimate=pl.CostEstimate(
            flops=4 * 256 * pairs, bytes_accessed=4_000_000, transcendentals=pairs
        ),
        name="attend",
    )(*args)


def prepare(place_ref, own, got, out_a, out_b, turned):
    second = place_ref[0] == 1
    for n in range(5):
        width = min(256, D - n * 256)
        here = slice(n * 256, n * 256 + width)
        out_a[:, here] = jnp.where(second, got[n, :, :width], own[n, :, :width])
        out_b[:, here] = jnp.where(second, own[n, :, :width], got[n, :, :width])
    turned[:128] = own[4, :, 128:].astype(F32).T.astype(BF)
    for n in range(3):
        turned[128 + n * 256 : 384 + n * 256] = own[5 + n].astype(F32).T.astype(BF)


def spatial_end(att_ref, tok_ref, mod_ref, weight, resid_ref, norm_ref):
    feats = [att_ref[head, pair].astype(F32) for pair in range(NZ) for head in range(2)]
    attended = jnp.concatenate(feats, 0).T.astype(BF)
    branch = jnp.dot(attended, weight[...], preferred_element_type=F32)
    resid = tok_ref[...].astype(F32) + mod_ref[2:3, :] * branch
    resid_ref[...] = resid
    norm_ref[...] = (normalise(resid) * (1.0 + mod_ref[4:5, :]) + mod_ref[3:4, :]).astype(BF)


def temporal(n0, n1, n2, n3, weight, gain_ref, *out_refs):
    gap = jnp.zeros((128 - PATCH, D), BF)
    rows = jnp.concatenate([n0[...], gap, n1[...], gap, n2[...], gap, n3[...], gap], 0)
    proj = lax.dot_general(weight[...], rows, NT, preferred_element_type=F32)
    queries, keys, values = [], [], []
    for frame in range(4):
        here = slice(frame * 128, (frame + 1) * 128)
        heads = [proj[n * HD : (n + 1) * HD, here] for n in range(12)]
        queries.append([rms(v, gain_ref[:, 2:3]).astype(BF).astype(F32) for v in heads[:4]])
        keys.append([rms(v, gain_ref[:, 3:4]).astype(BF).astype(F32) for v in heads[4:8]])
        values.append([v.astype(BF).astype(F32) for v in heads[8:]])
    for f, out_ref in enumerate(out_refs):
        mixed = []
        for head in range(4):
            total, attended = 0.0, 0.0
            for g in range(4):
                score = jnp.sum(queries[f][head] * keys[g][head], 0, keepdims=True) * FACTOR
                expo = jnp.exp(score)
                total = total + expo
                attended = attended + expo.astype(BF).astype(F32) * values[g][head]
            mixed.append(attended / total)
        tail = [mixed[3][:, n * 32 : (n + 1) * 32] for n in range(3)]
        body = jnp.concatenate([m[:, :PATCH] for m in mixed[:3]], 0)
        out_ref[...] = jnp.concatenate([body, jnp.concatenate(tail, 0)], 1).astype(BF)


def temporal_end(place_ref, m0, m1, m2, m3, resid_ref, mod_ref, weight, *out_refs):
    branch = None
    for step, att_ref in enumerate((m0, m1, m2, m3)):
        packed = att_ref[...].astype(F32)
        tail = [packed[n * HD : (n + 1) * HD, PATCH:] for n in range(3)]
        feats = jnp.concatenate([packed[:, :PATCH], jnp.concatenate(tail, 1)], 0)
        here = pl.ds(pl.multiple_of((place_ref[1] ^ step) * (4 * HD), 4 * HD), 4 * HD)
        add = jnp.dot(feats.T.astype(BF), weight[here, :], preferred_element_type=F32)
        branch = add if branch is None else branch + add
    out_refs[-1][...] = (resid_ref[...] + mod_ref[5:6, :] * branch).astype(BF)


SMEM = pl.BlockSpec(memory_space=pltpu.SMEM)


def full(array, lead=None, n=0):
    block = array.shape if lead is None else (lead,) + array.shape[1:]
    place = (n,) + (0,) * (array.ndim - 1)
    return pl.BlockSpec(block, lambda i: place)


def once(kernel, args, specs, shapes, out_specs=None, aliases=None):
    return pl.pallas_call(
        kernel,
        grid=(1,),
        in_specs=specs,
        out_specs=out_specs or [full(s) for s in shapes],
        out_shape=shapes,
        input_output_aliases=aliases or {},
        compiler_params=PARAMS,
        cost_estimate=pl.CostEstimate(
            flops=2_000_000_000, bytes_accessed=8_000_000, transcendentals=0
        ),
        name=kernel.__name__,
    )(*args)


def shape(dtype, *sizes):
    return jax.ShapeDtypeStruct(sizes, dtype)


def per_device(tokens, modulation, spatial_qkv, spatial_out, temporal_qkv, temporal_out, norm_gains):
    core = lax.axis_index("c")
    frame = lax.axis_index("xl") * 2 + core
    place = jnp.stack([core, frame]).astype(jnp.int32)
    gains = norm_gains.T
    tok = tokens.reshape(ROWS, D)

    part_a = spatial_qkv.reshape(18, 3, NZ, 2 * HD).transpose(2, 0, 1, 3).reshape(NZ, 18, 6 * HD)
    part_a = jnp.pad(part_a, ((0, 0), (0, 0), (0, 512 - 6 * HD)))
    part_b = lax.dynamic_slice_in_dim(temporal_qkv.reshape(18, 3, D), frame * 4 * HD, 4 * HD, 2)
    rest = [jnp.where(core == 0, spatial_out, temporal_out), part_b.reshape(18, 12 * HD)]
    rest = jnp.pad(jnp.concatenate(rest, 1), ((0, 0), (0, 256 * NZ - D - 12 * HD)))
    rest = rest.reshape(18, NZ, 256).transpose(1, 0, 2)
    shard = jnp.concatenate([part_a, rest], 2)
    shard = lax.all_to_all(shard, "z", 0, 0, tiled=True).reshape(1, NZ * 18, 768)
    shard = jnp.broadcast_to(shard, (8, NZ * 18, 768))
    shard = lax.all_to_all(shard, ("xh", "y"), 0, 0, tiled=True).reshape(D, 768)

    column = lax.all_gather(tok, "z", axis=0)

    rest, column = lax.optimization_barrier((shard[:, 512:], column))
    rest = lax.all_gather(rest, "z", axis=0)

    projected = pl.pallas_call(
        spatial_proj,
        grid=(2,),
        in_specs=[
            pl.BlockSpec((4, ROWS, D), lambda i: (i, 0, 0)),
            pl.BlockSpec((6, D), lambda i: (0, 0)),
            pl.BlockSpec((D, 512), lambda i: (0, 0)),
            pl.BlockSpec((HD, 4), lambda i: (0, 0)),
        ],
        out_specs=pl.BlockSpec((4, 3 * HP, 4 * PATCH), lambda i: (0, 0, i)),
        out_shape=jax.ShapeDtypeStruct((4, 3 * HP, PLANE), BF),
        scratch_shapes=[pltpu.VMEM((512, D), BF)],
        compiler_params=PARAMS,
        name="spatial_proj",
    )(column, modulation, shard, gains)

    swap = [(0, 1), (1, 0)]
    projected = lax.all_to_all(projected, "y", 0, 0, tiled=True)
    other_a = lax.ppermute(projected[:2, : 2 * HP], "xh", swap)
    other_b = lax.ppermute(projected[2:, : 2 * HP], "xh", swap)
    part = attention(projected, projected, None, False)
    part = attention(projected, other_a, part, False)
    attended = attention(projected, other_b, part, True)
    attended, rest = lax.optimization_barrier((attended, rest))
    rest_got = lax.ppermute(rest, "c", swap)
    attended = attended.reshape(NY * NZ, HD, PATCH)
    attended = lax.all_to_all(attended, ("y", "z"), 0, 0, tiled=True)
    attended = attended.reshape(4, NZ, HD, PATCH)
    out_a, out_b, turned = once(
        prepare,
        [place, rest, rest_got],
        [SMEM, full(rest), full(rest, 5)],
        [shape(BF, D, D), shape(BF, D, D), shape(BF, 896, D)],
    )

    steps = []
    for clip in range(2):
        args = [attended, tok, modulation, out_a]
        specs = [full(attended, 2, clip), full(tok, PATCH, clip), full(modulation), full(out_a)]
        steps.append(once(spatial_end, args, specs, [shape(F32, PATCH, D), shape(BF, PATCH, D)]))
    diagonal = [(0, 3), (3, 0), (1, 2), (2, 1)]
    sent = []
    moved = [lax.ppermute(norm, "xl", swap) for _, norm in steps]
    moved[0], _ = lax.optimization_barrier((moved[0], steps[1][1]))
    for (_, norm), norm_x in zip(steps, moved):
        if sent:
            norm_x, sent[0][0] = lax.optimization_barrier((norm_x, sent[0][0]))
        args = [norm, lax.ppermute(norm, "c", swap), norm_x, lax.ppermute(norm_x, "c", swap)]
        args += [turned, gains]
        mixed = once(temporal, args, [full(a) for a in args], [shape(BF, 3 * HD, 128)] * 4)
        sent.append(
            [
                mixed[0],
                lax.ppermute(mixed[1], "c", swap),
                lax.ppermute(mixed[2], "xl", swap),
                lax.ppermute(mixed[3], ("xl", "c"), diagonal),
            ]
        )
    result = None
    for clip in range(2):
        args = sent[clip] + [steps[clip][0], modulation, out_b]
        specs = [SMEM] + [full(a) for a in args]
        aliases = None
        if result is not None:
            args, specs = args + [result], specs + [pl.BlockSpec(memory_space=pl.ANY)]
            aliases = {len(args): 0}
        whole = shape(BF, ROWS, D)
        out_specs = [full(whole, PATCH, clip)]
        (result,) = once(temporal_end, [place] + args, specs, [whole], out_specs, aliases)
    return result.reshape(2, 1, PATCH, D)


def solution(mesh):
    fine = Mesh(mesh.devices.reshape(2, 2, 2, NY, NZ), ("xl", "c", "xh", "y", "z"))
    time, space = ("xl", "c"), ("xh", "y", "z")
    block = P(None, time, space, None)
    rows = P(space, None)
    return jax.shard_map(
        per_device,
        mesh=fine,
        in_specs=(block, P(), rows, rows, rows, rows, P()),
        out_specs=block,
        check_vma=False,
    )
```

time: 194 us -> 187 us (0.964)
  Pallas kernels: 48.6 us -> 40.9 us
  waiting for transfers between devices: 34.5 us -> 27.2 us
  local copies, waits for them, and re-layouts: 4.05 us -> 8.7 us
  starting transfers between devices: 21.5 us -> 25.7 us
    pallas_call x3, Pallas kernels: 29.2 us -> 18.9 us  [attention(): pl.pallas_call(functools.partial(attend, steps, part is not None, finish)...]
    all_to_all x1, waiting for transfers between devices: 15.8 us -> 6.13 us  [per_device(): attended = lax.all_to_all(attended, ('y', 'z'), 0, 0, tiled=True)]
    ppermute x1, waiting for transfers between devices: 0.01 us -> 5.9 us  [per_device(): other_b = lax.ppermute(projected[2:, :2 * HP], 'xh', swap)]
    unnamed x8 -> x18, local copies, waits for them, and re-layouts: 0.13 us -> 4.73 us
    ppermute x4 -> x8, waiting for transfers between devices: 8.77 us -> 4.87 us  [the longest x2 3.42 us: per_device(): moved = [lax.ppermute(norm, 'xl', swap) for _, norm in steps]]
    ppermute x1 -> x2, waiting for transfers between devices: 3.52 us -> 0.01 us  [per_device(): lax.ppermute(mixed[2], 'xl', swap)]
    ppermute x4 -> x8, starting transfers between devices: 9.32 us -> 12.3 us  [the longest x2 4.35 us: per_device(): lax.ppermute(norm_x, 'c', swap)]
    pallas_call x3 -> x7, Pallas kernels: 13.7 us -> 16.3 us  [once(): pl.pallas_call(kernel, grid=(1,), in_specs=specs, out_specs=out_specs or...]
  transfers between devices with their start and end apart: 12 -> 18, of which waited for: 6 -> 8; matrix products, arithmetic and copies ran while one was open for 3% -> 3% of each run, Pallas kernels for 18% -> 20%
where the time goes in v3:
time: 187 us
  blocking collectives  69.5 us (37%)
  Pallas kernels  40.9 us (22%)
  waiting for transfers between devices  27.2 us (15%)
  starting transfers between devices  25.7 us (14%)
  between operations  13.6 us (7%)
  local copies, waits for them, and re-layouts  8.7 us (5%)
    all_to_all x1, blocking collectives, per_device(): shard = lax.all_to_all(shard, ('xh', 'y'), 0, 0, tiled=True).reshape(D, 768)  26.6 us
    all_to_all x1, blocking collectives, per_device(): projected = lax.all_to_all(projected, 'y', 0, 0, tiled=True)  23 us
    all_to_all x1, blocking collectives, per_device(): lax.all_to_all(shard, 'z', 0, 0, tiled=True).reshape(1, NZ * 18, 768)  19.9 us
    pallas_call x3, Pallas kernels, attention(): pl.pallas_call(functools.partial(attend, steps, part is not None, finish)...  18.9 us
    pallas_call x7, Pallas kernels, once(): pl.pallas_call(kernel, grid=(1,), in_specs=specs, out_specs=out_specs or...  16.3 us
    all_to_all x1, starting transfers between devices, per_device(): attended = lax.all_to_all(attended, ('y', 'z'), 0, 0, tiled=True)  7.06 us
    all_to_all x1, waiting for transfers between devices, per_device(): attended = lax.all_to_all(attended, ('y', 'z'), 0, 0, tiled=True)  6.13 us
    ppermute x1, waiting for transfers between devices, per_device(): other_b = lax.ppermute(projected[2:, :2 * HP], 'xh', swap)  5.9 us
  transfers between devices with their start and end apart: 18, of which 8 were waited for; matrix products, arithmetic and copies ran while one was open for 3% of the time, Pallas kernels for 20%

profile of v3, /device:TPU:1, one launch (start us, length us, event | category | flops | bytes accessed | tf_op | source)
XLA Modules:
  0.0 186.7 jit_solution(8722490287306194931)
XLA Ops:
  6.5 0.7 all-gather.4.cloned.1.call-update
  7.3 1.0 reshape.34
  8.4 0.1 reshape.35
  8.5 0.8 broadcast_select_fusion
  9.4 1.2 reshape.32
  10.6 0.1 copy.22
  10.8 0.2 reshape.33
  11.0 19.9 %all_to_all.20 = bf16[8,18,768]{2,1,0:T(8,128)(2,1)S(1)} all-to-all(bf16[8,18,768]{2,1,0:T(8,128)(2,1)S(1)} %copy.17), channel_id=1, replica_groups=mesh['xl'=2,'c'=2,'xh'=2,'y'=4,'z'=8] {'z'}, dimensions={0} | all-to-all | bytes 442368 | tf_op jit(solution)/shard_map/all_to_all | solution.py:238
  31.0 0.1 broadcast_in_dim.8
  31.2 26.6 %all_to_all.21 = bf16[8,144,768]{2,1,0:T(8,128)(2,1)S(1)} all-to-all(bf16[8,144,768]{2,1,0:T(8,128)(2,1)S(1)} %broadcast_in_dim.8), channel_id=1, replica_groups=mesh['xl'=2,'c'=2,'xh'=2,'y'=4,'z'=8] {'xh','y'}, dimensions={0} | all-to-all | bytes 3538944 | tf_op jit(solution)/shard_map/all_to_all | solution.py:240
  57.8 0.9 slice.12
  58.7 5.3 %all-gather.4.cloned.1.call-done.tok_ref = bf16[8,192,1152]{2,1,0:T(8,128)(2,1)} async-done(((bf16[1,192,1152]{2,1,0:T(8,128)(2,1)}), bf16[8,192,1152]{2,1,0:T(8,128)(2,1)}) %all-gather.4.cloned.1.call-update) | async-done | bytes 3538960 | tf_op jit(solution)/shard_map/all_gather | solution.py:242
  64.2 5.8 %spatial_proj.1 = bf16[4,240,768]{2,1,0:T(8,128)(2,1)S(1)} custom-call(bf16[8,192,1152]{2,1,0:T(8,128)(2,1)} %all-gather.4.cloned.1.call-done.tok_ref, f32[6,1152]{1,0:T(8,128)S(1)} %copy-done.1, bf16[1152,768]{1,0:T(8,128)(2,1)S(1)} %bitcast.23, f32[72,4]{1,0:T(8,128)S(1)} %bitcast.29), custom_call_target="tpu_custom_call" | custom-call | tf_op jit(solution)/shard_map/spatial_proj/pallas_call | solution.py:247
  70.0 23.0 %all_to_all.22.refs_0_.refs_1_ = bf16[4,240,768]{2,1,0:T(8,128)(2,1)S(1)} all-to-all(bf16[4,240,768]{2,1,0:T(8,128)(2,1)S(1)} %spatial_proj.1), channel_id=1, replica_groups=mesh['xl'=2,'c'=2,'xh'=2,'y'=4,'z'=8] {'y'}, dimensions={0} | all-to-all | bytes 2949120 | tf_op jit(solution)/shard_map/all_to_all | solution.py:264
  93.0 2.8 %collective-permute-start.1 = (bf16[2,160,768]{2,1,0:T(8,128)(2,1)S(1)}, bf16[2,160,768]{2,1,0:T(8,128)(2,1)S(1)}, u32[]{:S(2)}, u32[]{:S(2)}) collective-permute-start(bf16[2,160,768]{2,1,0:T(8,128)(2,1)S(1)} %get-tuple-element.49), channel_id=1, source_target_pairs={{0,32},{32,0},{1,33},{33,1},{2,34},{34,2},{3,35},{35,3},{4,36},{36... | collective-permute-start | bytes 1474568 | tf_op jit(solution)/shard_map/ppermute | solution.py:265
  95.9 0.2 collective-permute-start
  96.1 8.6 %attend.3.refs_2_ = f32[4,80,768]{2,1,0:T(8,128)S(1)} custom-call(bf16[4,240,768]{2,1,0:T(8,128)(2,1)S(1)} %all_to_all.22.refs_0_.refs_1_, bf16[4,240,768]{2,1,0:T(8,128)(2,1)S(1)} %all_to_all.22.refs_0_.refs_1_), custom_call_target="tpu_custom_call" | custom-call | flops 9663676416 | bytes 4000000 | tf_op jit(solution)/shard_map/attend/pallas_call | solution.py:121
  104.7 1.1 collective-permute-done.1.refs_1_
  105.7 4.6 %attend.4.refs_2_ = f32[4,80,768]{2,1,0:T(8,128)S(1)} custom-call(bf16[4,240,768]{2,1,0:T(8,128)(2,1)S(1)} %all_to_all.22.refs_0_.refs_1_, bf16[2,160,768]{2,1,0:T(8,128)(2,1)S(1)} %collective-permute-done.1.refs_1_, f32[4,80,768]{2,1,0:T(8,128)S(1)} %attend.3.refs_2_), custom_call_target="tpu_custom_call" | custom-call | flops 4831838208 | bytes 4000000 | tf_op jit(solution)/shard_map/attend/pallas_call | solution.py:121
  110.4 5.9 %collective-permute-done.refs_1_ = bf16[2,160,768]{2,1,0:T(8,128)(2,1)S(1)} collective-permute-done((bf16[2,160,768]{2,1,0:T(8,128)(2,1)S(1)}, bf16[2,160,768]{2,1,0:T(8,128)(2,1)S(1)}, u32[]{:S(2)}, u32[]{:S(2)}) %collective-permute-start) | collective-permute-done | bytes 491552 | tf_op jit(solution)/shard_map/ppermute | solution.py:266
  116.3 5.7 %attend.5 = bf16[4,8,72,96]{3,2,1,0:T(8,128)(2,1)} custom-call(bf16[4,240,768]{2,1,0:T(8,128)(2,1)S(1)} %all_to_all.22.refs_0_.refs_1_, bf16[2,160,768]{2,1,0:T(8,128)(2,1)S(1)} %collective-permute-done.refs_1_, f32[4,80,768]{2,1,0:T(8,128)S(1)} %attend.4.refs_2_), custom_call_target="tpu_custom_call" | custom-call | flops 4831838208 | bytes 4000000 | tf_op jit(solution)/shard_map/attend/pallas_call | solution.py:121
  121.9 2.5 %all-gather.6.cloned.1.call-done = bf16[9216,256]{1,0:T(8,128)(2,1)} async-done(((bf16[1152,256]{1,0:T(8,128)(2,1)}), bf16[9216,256]{1,0:T(8,128)(2,1)}) %all-gather.6.cloned.1.call-update) | async-done | bytes 4718608 | tf_op jit(solution)/shard_map/all_gather | solution.py:245
  124.4 0.7 collective-permute-start.2
  125.1 7.1 %all-to-all-start.3 = ((bf16[32,72,96]{2,1,0:T(8,128)(2,1)}), bf16[32,72,96]{2,1,0:T(8,128)(2,1)S(1)}, u32[]{:S(2)}, u32[]{:S(2)}) async-start(bf16[32,72,96]{2,1,0:T(8,128)(2,1)} %bitcast.8), calls=%async_computation.3 | async-start | bytes 1179648 | tf_op jit(solution)/shard_map/all_to_all | solution.py:273
  132.3 0.7 collective-permute-done.2.got
  133.0 6.0 %prepare.1 = (bf16[1152,1152]{1,0:T(8,128)(2,1)S(1)}, bf16[1152,1152]{1,0:T(8,128)(2,1)}, bf16[896,1152]{1,0:T(8,128)(2,1)S(1)}) custom-call(s32[2]{0:T(128)S(1)} %pad_add_fusion.place_ref, bf16[8,1152,256]{2,1,0:T(8,128)(2,1)} %bitcast.33, bf16[8,1152,256]{2,1,0:T(8,128)(2,1)} %collective-permute-done.2.got), custom_call_target="tpu_custom_call" | custom-call | flops 2000000000 | bytes 8000000 | tf_op jit(solution)/shard_map/prepare/pallas_call | solution.py:205
  138.9 1.5 copy-done.3
  140.4 1.3 copy-done.5
  141.8 6.1 %all-to-all-done.3 = bf16[32,72,96]{2,1,0:T(8,128)(2,1)S(1)} async-done(((bf16[32,72,96]{2,1,0:T(8,128)(2,1)}), bf16[32,72,96]{2,1,0:T(8,128)(2,1)S(1)}, u32[]{:S(2)}, u32[]{:S(2)}) %all-to-all-start.3) | async-done | bytes 442400 | tf_op jit(solution)/shard_map/all_to_all | solution.py:273
  147.9 1.7 copy-done.4
  149.7 0.9 spatial_end.3
  150.6 1.3 collective-permute-start.6
  151.8 3.4 %collective-permute-start.5 = (bf16[96,1152]{1,0:T(8,128)(2,1)S(1)}, bf16[96,1152]{1,0:T(8,128)(2,1)S(1)}, u32[]{:S(2)}, u32[]{:S(2)}) collective-permute-start(bf16[96,1152]{1,0:T(8,128)(2,1)S(1)} %get-tuple-element.33.n0), channel_id=1, source_target_pairs={{0,64},{64,0},{1,65},{65,1},{2,66},{66,2},{3,67},{67,3},{4,68},{68... | collective-permute-start | bytes 663560 | tf_op jit(solution)/shard_map/ppermute | solution.py:294
  155.2 0.9 spatial_end.2
  156.1 3.6 %collective-permute-start.7 = (bf16[96,1152]{1,0:T(8,128)(2,1)S(1)}, bf16[96,1152]{1,0:T(8,128)(2,1)S(1)}, u32[]{:S(2)}, u32[]{:S(2)}) collective-permute-start(bf16[96,1152]{1,0:T(8,128)(2,1)S(1)} %collective-permute-done.6.n2), channel_id=1, source_target_pairs={{0,64},{64,0},{1,65},{65,1},{2,66},{66,2},{3,67},{67,3},{4,68},{68... | collective-permute-start | bytes 663560 | tf_op jit(solution)/shard_map/ppermute | solution.py:294
  159.7 1.2 collective-permute-start.4
  160.9 0.3 collective-permute-start.3
  161.2 2.1 %temporal.2 = (bf16[216,128]{1,0:T(8,128)(2,1)S(1)}, bf16[216,128]{1,0:T(8,128)(2,1)S(1)}, bf16[216,128]{1,0:T(8,128)(2,1)S(1)}, bf16[216,128]{1,0:T(8,128)(2,1)S(1)}) custom-call(bf16[96,1152]{1,0:T(8,128)(2,1)S(1)} %get-tuple-element.33.n0, bf16[96,1152]{1,0:T(8,128)(2,1)S(1)} %collective-permute-done.5.n1, ...), custom_call_target="tpu_custom_call" | custom-call | flops 2000000000 | bytes 8000000 | tf_op jit(solution)/shard_map/temporal/pallas_call | solution.py:205
  163.3 3.4 %collective-permute-done.4.n2 = bf16[96,1152]{1,0:T(8,128)(2,1)S(1)} collective-permute-done((bf16[96,1152]{1,0:T(8,128)(2,1)S(1)}, bf16[96,1152]{1,0:T(8,128)(2,1)S(1)}, u32[]{:S(2)}, u32[]{:S(2)}) %collective-permute-start.4) | collective-permute-done | bytes 221216 | tf_op jit(solution)/shard_map/ppermute | solution.py:289
  166.8 0.8 collective-permute-start.8
  167.6 1.2 collective-permute-start.13
  168.7 0.9 collective-permute-start.14
  169.7 2.1 %temporal.3 = (bf16[216,128]{1,0:T(8,128)(2,1)S(1)}, bf16[216,128]{1,0:T(8,128)(2,1)S(1)}, bf16[216,128]{1,0:T(8,128)(2,1)S(1)}, bf16[216,128]{1,0:T(8,128)(2,1)S(1)}) custom-call(bf16[96,1152]{1,0:T(8,128)(2,1)S(1)} %get-tuple-element.32.n0, bf16[96,1152]{1,0:T(8,128)(2,1)S(1)} %collective-permute-done.3.n1, ...), custom_call_target="tpu_custom_call" | custom-call | flops 2000000000 | bytes 8000000 | tf_op jit(solution)/shard_map/temporal/pallas_call | solution.py:205
  171.9 1.3 collective-permute-start.10
  173.2 0.8 collective-permute-start.11
  174.1 2.1 %temporal_end.2.out_refs_0_ = bf16[192,1152]{1,0:T(8,128)(2,1)} custom-call(s32[2]{0:T(128)S(1)} %pad_add_fusion.place_ref, bf16[216,128]{1,0:T(8,128)(2,1)S(1)} %get-tuple-element.44.m0, bf16[216,128]{1,0:T(8,128)(2,1)S(1)} %collective-permute-done.12.m1, bf16[216,128]{1,0:T(8,128)(2,1)S(1)} %collective-permute-done.13.m2, ...), custom_call_target="tpu_custom_call" | custom-call | flops 2000000000 | bytes 8000000 | tf_op jit(solution)/shard_map/temporal_end/pallas_call | solution.py:205
  176.2 1.4 collective-permute-done.11.m3
  177.7 2.1 %temporal_end.3 = bf16[192,1152]{1,0:T(8,128)(2,1)} custom-call(s32[2]{0:T(128)S(1)} %pad_add_fusion.place_ref, bf16[216,128]{1,0:T(8,128)(2,1)S(1)} %get-tuple-element.38.m0, bf16[216,128]{1,0:T(8,128)(2,1)S(1)} %collective-permute-done.9.m1, bf16[216,128]{1,0:T(8,128)(2,1)S(1)} %collective-permute-done.10.m2, ...), custom_call_target="tpu_custom_call", output_to_operand_aliasing={{}: (8, {})} | custom-call | flops 2000000000 | bytes 8000000 | tf_op jit(solution)/shard_map/temporal_end/pallas_call | solution.py:205
  (38 shorter events, 0.7 us)
Async XLA Ops:
  6.5 57.5 %all-gather.4.cloned.1.call-start = ((), (), s32[]{:S(2)}) async-start(), calls=%async_computation.4 | async-start | bytes 3981312 | tf_op jit(solution)/shard_map/all_gather | solution.py:242
  7.3 117.2 %all-gather.6.cloned.1.call-start = ((), (), s32[]{:S(2)}) async-start(), calls=%async_computation.5 | async-start | bytes 5308416 | tf_op jit(solution)/shard_map/all_gather | solution.py:245
  31.1 32.9 %copy-start.7 = (f32[4,72]{1,0:T(4,128)S(1)}, f32[4,72]{1,0:T(4,128)}, u32[]{:S(2)}) copy-start(f32[4,72]{1,0:T(4,128)} %param.13) | copy-start | bytes 3460
  31.2 33.0 %copy-start.1 = (f32[6,1152]{1,0:T(8,128)S(1)}, f32[6,1152]{1,0:T(8,128)}, u32[]{:S(2)}) copy-start(f32[6,1152]{1,0:T(8,128)} %mod_ref.9) | copy-start | bytes 82948
  93.0 12.7 %collective-permute-start.1 = (bf16[2,160,768]{2,1,0:T(8,128)(2,1)S(1)}, bf16[2,160,768]{2,1,0:T(8,128)(2,1)S(1)}, u32[]{:S(2)}, u32[]{:S(2)}) collective-permute-start(bf16[2,160,768]{2,1,0:T(8,128)(2,1)S(1)} %get-tuple-element.49), channel_id=1, source_target_pairs={{0,32},{32,0},{1,33},{33,1},{2,34},{34,2},{3,35},{35,3},{4,36},{36... | collective-permute-start | bytes 1474568 | tf_op jit(solution)/shard_map/ppermute | solution.py:265
  95.9 20.4 %collective-permute-start = (bf16[2,160,768]{2,1,0:T(8,128)(2,1)S(1)}, bf16[2,160,768]{2,1,0:T(8,128)(2,1)S(1)}, u32[]{:S(2)}, u32[]{:S(2)}) collective-permute-start(bf16[2,160,768]{2,1,0:T(8,128)(2,1)S(1)} %get-tuple-element.50), channel_id=1, source_target_pairs={{0,32},{32,0},{1,33},{33,1},{2,34},{34,2},{3,35},{35,3},{4,36},{36... | collective-permute-start | bytes 1474568 | tf_op jit(solution)/shard_map/ppermute | solution.py:266
  124.4 8.6 %collective-permute-start.2 = (bf16[8,1152,256]{2,1,0:T(8,128)(2,1)}, bf16[8,1152,256]{2,1,0:T(8,128)(2,1)}, u32[]{:S(2)}, u32[]{:S(2)}) collective-permute-start(bf16[8,1152,256]{2,1,0:T(8,128)(2,1)} %bitcast.32), channel_id=1, source_target_pairs={{0,64},{64,0},{1,65},{65,1},{2,66},{66,2},{3,67},{67,3},{4,68},{68... | collective-permute-start | bytes 14155784 | tf_op jit(solution)/shard_map/ppermute | solution.py:271
  125.1 22.8 %all-to-all-start.3 = ((bf16[32,72,96]{2,1,0:T(8,128)(2,1)}), bf16[32,72,96]{2,1,0:T(8,128)(2,1)S(1)}, u32[]{:S(2)}, u32[]{:S(2)}) async-start(bf16[32,72,96]{2,1,0:T(8,128)(2,1)} %bitcast.8), calls=%async_computation.3 | async-start | bytes 1179648 | tf_op jit(solution)/shard_map/all_to_all | solution.py:273
  132.3 15.7 %copy-start = (bf16[2,1,96,1152]{3,2,1,0:T(8,128)(2,1)S(1)}, bf16[2,1,96,1152]{3,2,1,0:T(8,128)(2,1)}, u32[]{:S(2)}) copy-start(bf16[2,1,96,1152]{3,2,1,0:T(8,128)(2,1)} %param.7) | copy-start | bytes 1327108
  138.9 1.5 copy-start.3
  140.4 1.3 copy-start.5
  147.9 1.8 copy-start.4
  150.6 10.6 %copy-start.6 = (bf16[896,1152]{1,0:T(8,128)(2,1)S(1)}, bf16[896,1152]{1,0:T(8,128)(2,1)}, u32[]{:S(2)}) copy-start(bf16[896,1152]{1,0:T(8,128)(2,1)} %copy-done.5) | copy-start | bytes 6193156
  150.6 5.6 %collective-permute-start.6 = (bf16[96,1152]{1,0:T(8,128)(2,1)S(1)}, bf16[96,1152]{1,0:T(8,128)(2,1)S(1)}, u32[]{:S(2)}, u32[]{:S(2)}) collective-permute-start(bf16[96,1152]{1,0:T(8,128)(2,1)S(1)} %get-tuple-element.33.n0), channel_id=1, source_target_pairs={{0,128},{128,0},{1,129},{129,1},{2,130},{130,2},{3,131},{131,3},{4... | collective-permute-start | bytes 663560 | tf_op jit(solution)/shard_map/ppermute | solution.py:289
  151.8 9.3 %collective-permute-start.5 = (bf16[96,1152]{1,0:T(8,128)(2,1)S(1)}, bf16[96,1152]{1,0:T(8,128)(2,1)S(1)}, u32[]{:S(2)}, u32[]{:S(2)}) collective-permute-start(bf16[96,1152]{1,0:T(8,128)(2,1)S(1)} %get-tuple-element.33.n0), channel_id=1, source_target_pairs={{0,64},{64,0},{1,65},{65,1},{2,66},{66,2},{3,67},{67,3},{4,68},{68... | collective-permute-start | bytes 663560 | tf_op jit(solution)/shard_map/ppermute | solution.py:294
  156.1 5.0 %collective-permute-start.7 = (bf16[96,1152]{1,0:T(8,128)(2,1)S(1)}, bf16[96,1152]{1,0:T(8,128)(2,1)S(1)}, u32[]{:S(2)}, u32[]{:S(2)}) collective-permute-start(bf16[96,1152]{1,0:T(8,128)(2,1)S(1)} %collective-permute-done.6.n2), channel_id=1, source_target_pairs={{0,64},{64,0},{1,65},{65,1},{2,66},{66,2},{3,67},{67,3},{4,68},{68... | collective-permute-start | bytes 663560 | tf_op jit(solution)/shard_map/ppermute | solution.py:294
  159.7 7.1 %collective-permute-start.4 = (bf16[96,1152]{1,0:T(8,128)(2,1)S(1)}, bf16[96,1152]{1,0:T(8,128)(2,1)S(1)}, u32[]{:S(2)}, u32[]{:S(2)}) collective-permute-start(bf16[96,1152]{1,0:T(8,128)(2,1)S(1)} %get-tuple-element.32.n0), channel_id=1, source_target_pairs={{0,128},{128,0},{1,129},{129,1},{2,130},{130,2},{3,131},{131,3},{4... | collective-permute-start | bytes 663560 | tf_op jit(solution)/shard_map/ppermute | solution.py:289
  160.9 8.8 %collective-permute-start.3 = (bf16[96,1152]{1,0:T(8,128)(2,1)S(1)}, bf16[96,1152]{1,0:T(8,128)(2,1)S(1)}, u32[]{:S(2)}, u32[]{:S(2)}) collective-permute-start(bf16[96,1152]{1,0:T(8,128)(2,1)S(1)} %get-tuple-element.32.n0), channel_id=1, source_target_pairs={{0,64},{64,0},{1,65},{65,1},{2,66},{66,2},{3,67},{67,3},{4,68},{68... | collective-permute-start | bytes 663560 | tf_op jit(solution)/shard_map/ppermute | solution.py:294
  166.8 2.9 %collective-permute-start.8 = (bf16[96,1152]{1,0:T(8,128)(2,1)S(1)}, bf16[96,1152]{1,0:T(8,128)(2,1)S(1)}, u32[]{:S(2)}, u32[]{:S(2)}) collective-permute-start(bf16[96,1152]{1,0:T(8,128)(2,1)S(1)} %collective-permute-done.4.n2), channel_id=1, source_target_pairs={{0,64},{64,0},{1,65},{65,1},{2,66},{66,2},{3,67},{67,3},{4,68},{68... | collective-permute-start | bytes 663560 | tf_op jit(solution)/shard_map/ppermute | solution.py:294
  167.5 5.7 %collective-permute-start.12 = (bf16[216,128]{1,0:T(8,128)(2,1)S(1)}, bf16[216,128]{1,0:T(8,128)(2,1)S(1)}, u32[]{:S(2)}, u32[]{:S(2)}) collective-permute-start(bf16[216,128]{1,0:T(8,128)(2,1)S(1)} %get-tuple-element.45), channel_id=1, source_target_pairs={{0,64},{64,0},{1,65},{65,1},{2,66},{66,2},{3,67},{67,3},{4,68},{68... | collective-permute-start | bytes 165896 | tf_op jit(solution)/shard_map/ppermute | solution.py:300
  167.6 6.5 %collective-permute-start.13 = (bf16[216,128]{1,0:T(8,128)(2,1)S(1)}, bf16[216,128]{1,0:T(8,128)(2,1)S(1)}, u32[]{:S(2)}, u32[]{:S(2)}) collective-permute-start(bf16[216,128]{1,0:T(8,128)(2,1)S(1)} %get-tuple-element.46), channel_id=1, source_target_pairs={{0,128},{128,0},{1,129},{129,1},{2,130},{130,2},{3,131},{131,3},{4... | collective-permute-start | bytes 165896 | tf_op jit(solution)/shard_map/ppermute | solution.py:301
  168.7 5.3 %copy-start.2 = (bf16[1152,1152]{1,0:T(8,128)(2,1)S(1)}, bf16[1152,1152]{1,0:T(8,128)(2,1)}, u32[]{:S(2)}) copy-start(bf16[1152,1152]{1,0:T(8,128)(2,1)} %get-tuple-element.43.weight) | copy-start | bytes 7962628
  168.7 5.3 %collective-permute-start.14 = (bf16[216,128]{1,0:T(8,128)(2,1)S(1)}, bf16[216,128]{1,0:T(8,128)(2,1)S(1)}, u32[]{:S(2)}, u32[]{:S(2)}) collective-permute-start(bf16[216,128]{1,0:T(8,128)(2,1)S(1)} %get-tuple-element.47), channel_id=1, source_target_pairs={{0,192},{192,0},{64,128},{128,64},{1,193},{193,1},{65,129},{129,65... | collective-permute-start | bytes 165896 | tf_op jit(solution)/shard_map/ppermute | solution.py:302
  171.8 4.4 %collective-permute-start.9 = (bf16[216,128]{1,0:T(8,128)(2,1)S(1)}, bf16[216,128]{1,0:T(8,128)(2,1)S(1)}, u32[]{:S(2)}, u32[]{:S(2)}) collective-permute-start(bf16[216,128]{1,0:T(8,128)(2,1)S(1)} %get-tuple-element.39), channel_id=1, source_target_pairs={{0,64},{64,0},{1,65},{65,1},{2,66},{66,2},{3,67},{67,3},{4,68},{68... | collective-permute-start | bytes 165896 | tf_op jit(solution)/shard_map/ppermute | solution.py:300
  171.9 4.3 %collective-permute-start.10 = (bf16[216,128]{1,0:T(8,128)(2,1)S(1)}, bf16[216,128]{1,0:T(8,128)(2,1)S(1)}, u32[]{:S(2)}, u32[]{:S(2)}) collective-permute-start(bf16[216,128]{1,0:T(8,128)(2,1)S(1)} %get-tuple-element.40), channel_id=1, source_target_pairs={{0,128},{128,0},{1,129},{129,1},{2,130},{130,2},{3,131},{131,3},{4... | collective-permute-start | bytes 165896 | tf_op jit(solution)/shard_map/ppermute | solution.py:301
  173.2 4.4 %collective-permute-start.11 = (bf16[216,128]{1,0:T(8,128)(2,1)S(1)}, bf16[216,128]{1,0:T(8,128)(2,1)S(1)}, u32[]{:S(2)}, u32[]{:S(2)}) collective-permute-start(bf16[216,128]{1,0:T(8,128)(2,1)S(1)} %get-tuple-element.41), channel_id=1, source_target_pairs={{0,192},{192,0},{64,128},{128,64},{1,193},{193,1},{65,129},{129,65... | collective-permute-start | bytes 165896 | tf_op jit(solution)/shard_map/ppermute | solution.py:302
Sparse Core Ops, SparseCore 0:
  9.1 54.8 all-gather.3
  65.8 58.5 all-gather.5

commit v4 on v3

--- a/solution.py
+++ b/solution.py
@@ -19,6 +19,7 @@
 PLANE = NZ * PATCH
 BF = jnp.bfloat16
 F32 = jnp.float32
+PIECES = (slice(0, 2), slice(2, 3), slice(3, 4))
 FACTOR = 1.0 / math.sqrt(HD)
 TN = (((0,), (0,)), ((), ()))
 NT = (((1,), (1,)), ((), ()))
@@ -40,8 +41,6 @@
 def spatial_proj(tok_ref, mod_ref, w_ref, gain_ref, out_ref, turned):
     cols = 4 * PATCH
     zeros = jnp.zeros((HP - HD, cols), F32)
-    first = lax.broadcasted_iota(jnp.int32, (HP - HD, cols), 0) == 0
-    ones = jnp.where(first, 1.0, 0.0)
 
     @pl.when(pl.program_id(0) == 0)
     def _():
@@ -63,21 +62,38 @@
             query = rms(query, gain_ref[:, 0:1]) * (FACTOR * math.log2(math.e))
             key = rms(key, gain_ref[:, 1:2])
             place = clip * 2 + head
-            parts = [key, zeros, value, ones, query, zeros]
+            parts = [key, value, query, zeros]
             out_ref[place] = jnp.concatenate(parts, 0).astype(BF)
+
+
+def pack(block, rows):
+    strips = [block[rows:, n * 32 : (n + 1) * 32] for n in range(3)]
+    spare = rows - 3 * strips[0].shape[0]
+    if spare:
+        strips.append(jnp.zeros((spare, 32), block.dtype))
+    return jnp.concatenate([block[:rows], jnp.concatenate(strips, 0)], 1)
+
+
+def unpack(packed, tall):
+    strips = [packed[n * tall : (n + 1) * tall, PATCH:] for n in range(3)]
+    return jnp.concatenate([packed[:, :PATCH], jnp.concatenate(strips, 1)], 0)
 
 
 def attend(steps, resume, finish, *refs):
     q_ref, kv_ref = refs[:2]
-    out_ref, keys = refs[-2:]
+    out_ref, keys, values = refs[-3:]
 
     @pl.when(pl.program_id(0) == 0)
     def _():
-        gap = jnp.zeros((128 - HP, PLANE), F32)
+        gap = jnp.zeros((128 - HD, PLANE), F32)
+        first = lax.broadcasted_iota(jnp.int32, (HP - HD, PLANE), 0) == 0
+        ones = jnp.where(first, 1.0, 0.0)
         for n in range(steps):
-            keys[n] = jnp.concatenate([kv_ref[n, :HP].astype(F32), gap], 0).T.astype(BF)
-
-    query = jnp.concatenate([q_ref[0], jnp.zeros((128 - HP, PLANE), BF)], 0)
+            both = kv_ref[n, : 2 * HD].astype(F32)
+            keys[n] = jnp.concatenate([both[:HD], gap], 0).T.astype(BF)
+            values[n] = jnp.concatenate([both[HD:], ones], 0).astype(BF)
+
+    query = jnp.concatenate([q_ref[0, 2 * HD :], jnp.zeros((128 - HP, PLANE), BF)], 0)
     parts = [(n, slice(p, p + 256)) for n in range(steps) for p in range(0, PLANE, 256)]
 
     def scores(n, here):
@@ -90,33 +106,33 @@
         if place + 1 < len(parts):
             ahead = scores(*parts[place + 1])
         expo = jnp.exp2(score).astype(BF)
-        add = jnp.dot(kv_ref[n, HP : 2 * HP, here], expo, preferred_element_type=F32)
+        add = jnp.dot(values[n, :, here], expo, preferred_element_type=F32)
         done = add if done is None else done + add
     if not finish:
         out_ref[0] = done
         return
     done = done[:HD] / done[HD : HD + 1]
     for z in range(NZ):
-        out_ref[0, z] = done[:, z * PATCH : (z + 1) * PATCH].astype(BF)
+        out_ref[0, z] = pack(done[:, z * PATCH : (z + 1) * PATCH], 56).astype(BF)
 
 
 def attention(query, key_value, part, finish):
     steps = key_value.shape[0]
     sums = pl.BlockSpec((1, HP, PLANE), lambda q: (q, 0, 0))
     in_specs = [
-        pl.BlockSpec((1, HP, PLANE), lambda q: (q, 2, 0)),
-        pl.BlockSpec((steps, 2 * HP, PLANE), lambda q: (0, 0, 0)),
+        pl.BlockSpec((1, 3 * HD + 8, PLANE), lambda q: (q, 0, 0)),
+        pl.BlockSpec((steps,) + key_value.shape[1:], lambda q: (0, 0, 0)),
     ]
     args = [query, key_value]
     if part is not None:
         in_specs.append(sums)
         args.append(part)
     if finish:
-        out_spec = pl.BlockSpec((1, NZ, HD, PATCH), lambda q: (q, 0, 0, 0))
-        out_shape = jax.ShapeDtypeStruct((NY, NZ, HD, PATCH), BF)
+        out_spec = pl.BlockSpec((1, NZ, 56, 128), lambda q: (q, 0, 0, 0))
+        out_shape = shape(BF, NY, NZ, 56, 128)
     else:
         out_spec = sums
-        out_shape = jax.ShapeDtypeStruct((NY, HP, PLANE), F32)
+        out_shape = shape(F32, NY, HP, PLANE)
     pairs = steps * NY * PLANE * PLANE
     return pl.pallas_call(
         functools.partial(attend, steps, part is not None, finish),
@@ -124,10 +140,10 @@
         in_specs=in_specs,
         out_specs=out_spec,
         out_shape=out_shape,
-        scratch_shapes=[pltpu.VMEM((steps, PLANE, 128), BF)],
+        scratch_shapes=[pltpu.VMEM((steps, PLANE, 128), BF), pltpu.VMEM((steps, HP, PLANE), BF)],
         compiler_params=PARAMS,
         cost_estimate=pl.CostEstimate(
-            flops=4 * 256 * pairs, bytes_accessed=4_000_000, transcendentals=pairs
+            flops=4 * pairs, bytes_accessed=1_000_000, transcendentals=0
         ),
         name="attend",
     )(*args)
@@ -146,7 +162,7 @@
 
 
 def spatial_end(att_ref, tok_ref, mod_ref, weight, resid_ref, norm_ref):
-    feats = [att_ref[head, pair].astype(F32) for pair in range(NZ) for head in range(2)]
+    feats = [unpack(att_ref[n % 2, n // 2].astype(F32), 16) for n in range(HEADS)]
     attended = jnp.concatenate(feats, 0).T.astype(BF)
     branch = jnp.dot(attended, weight[...], preferred_element_type=F32)
     resid = tok_ref[...].astype(F32) + mod_ref[2:3, :] * branch
@@ -175,17 +191,13 @@
                 total = total + expo
                 attended = attended + expo.astype(BF).astype(F32) * values[g][head]
             mixed.append(attended / total)
-        tail = [mixed[3][:, n * 32 : (n + 1) * 32] for n in range(3)]
-        body = jnp.concatenate([m[:, :PATCH] for m in mixed[:3]], 0)
-        out_ref[...] = jnp.concatenate([body, jnp.concatenate(tail, 0)], 1).astype(BF)
+        out_ref[...] = pack(jnp.concatenate(mixed, 0)[:, :PATCH], 3 * HD).astype(BF)
 
 
 def temporal_end(place_ref, m0, m1, m2, m3, resid_ref, mod_ref, weight, *out_refs):
     branch = None
     for step, att_ref in enumerate((m0, m1, m2, m3)):
-        packed = att_ref[...].astype(F32)
-        tail = [packed[n * HD : (n + 1) * HD, PATCH:] for n in range(3)]
-        feats = jnp.concatenate([packed[:, :PATCH], jnp.concatenate(tail, 1)], 0)
+        feats = unpack(att_ref[...].astype(F32), HD)
         here = pl.ds(pl.multiple_of((place_ref[1] ^ step) * (4 * HD), 4 * HD), 4 * HD)
         add = jnp.dot(feats.T.astype(BF), weight[here, :], preferred_element_type=F32)
         branch = add if branch is None else branch + add
@@ -253,8 +265,8 @@
             pl.BlockSpec((D, 512), lambda i: (0, 0)),
             pl.BlockSpec((HD, 4), lambda i: (0, 0)),
         ],
-        out_specs=pl.BlockSpec((4, 3 * HP, 4 * PATCH), lambda i: (0, 0, i)),
-        out_shape=jax.ShapeDtypeStruct((4, 3 * HP, PLANE), BF),
+        out_specs=pl.BlockSpec((4, 3 * HD + 8, 4 * PATCH), lambda i: (0, 0, i)),
+        out_shape=shape(BF, 4, 3 * HD + 8, PLANE),
         scratch_shapes=[pltpu.VMEM((512, D), BF)],
         compiler_params=PARAMS,
         name="spatial_proj",
@@ -262,16 +274,16 @@
 
     swap = [(0, 1), (1, 0)]
     projected = lax.all_to_all(projected, "y", 0, 0, tiled=True)
-    other_a = lax.ppermute(projected[:2, : 2 * HP], "xh", swap)
-    other_b = lax.ppermute(projected[2:, : 2 * HP], "xh", swap)
+    others = [lax.ppermute(projected[n, : 2 * HD], "xh", swap) for n in PIECES]
     part = attention(projected, projected, None, False)
-    part = attention(projected, other_a, part, False)
-    attended = attention(projected, other_b, part, True)
+    part = attention(projected, others[0], part, False)
+    part = attention(projected, others[1], part, False)
+    attended = attention(projected, others[2], part, True)
     attended, rest = lax.optimization_barrier((attended, rest))
     rest_got = lax.ppermute(rest, "c", swap)
-    attended = attended.reshape(NY * NZ, HD, PATCH)
+    attended = attended.reshape(NY * NZ, 56, 128)
     attended = lax.all_to_all(attended, ("y", "z"), 0, 0, tiled=True)
-    attended = attended.reshape(4, NZ, HD, PATCH)
+    attended = attended.reshape(4, NZ, 56, 128)
     out_a, out_b, turned = once(
         prepare,
         [place, rest, rest_got],

time: 187 us -> 185 us (0.989)
  waiting for transfers between devices: 27.2 us -> 22.2 us
  starting transfers between devices: 25.7 us -> 27.8 us
    ppermute x2 -> x3, waiting for transfers between devices: 6.95 us -> 0.01 us  [per_device(): others = [lax.ppermute(projected[n, :2 * HD], 'xh', swap) for n in PIECES]]
    all_gather x1, waiting for transfers between devices: 2.49 us -> 6.31 us  [per_device(): rest = lax.all_gather(rest, 'z', axis=0)]
    ppermute x2 -> x3, starting transfers between devices: 3.06 us -> 5.89 us  [per_device(): others = [lax.ppermute(projected[n, :2 * HD], 'xh', swap) for n in PIECES]]
    all_to_all x1, waiting for transfers between devices: 6.13 us -> 4.14 us  [per_device(): attended = lax.all_to_all(attended, ('y', 'z'), 0, 0, tiled=True)]
    pallas_call x3 -> x4, Pallas kernels: 18.9 us -> 20.2 us  [attention(): pl.pallas_call(functools.partial(attend, steps, part is not None, finish)...]
  transfers between devices with their start and end apart: 18 -> 19, of which waited for: 8 -> 6; matrix products, arithmetic and copies ran while one was open for 3% -> 3% of each run, Pallas kernels for 20% -> 21%
where the time goes in v4:
time: 185 us; the launch traced here: 184 us
  blocking collectives  68.4 us (37%)
  Pallas kernels  42.4 us (23%)
  starting transfers between devices  27.8 us (15%)
  waiting for transfers between devices  22.2 us (12%)
  between operations  13.7 us (7%)
  local copies, waits for them, and re-layouts  8.66 us (5%)
    all_to_all x1, blocking collectives, per_device(): shard = lax.all_to_all(shard, ('xh', 'y'), 0, 0, tiled=True).reshape(D, 768)  26.6 us
    all_to_all x1, blocking collectives, per_device(): projected = lax.all_to_all(projected, 'y', 0, 0, tiled=True)  21.9 us
    pallas_call x4, Pallas kernels, attention(): pl.pallas_call(functools.partial(attend, steps, part is not None, finish)...  20.2 us
    all_to_all x1, blocking collectives, per_device(): lax.all_to_all(shard, 'z', 0, 0, tiled=True).reshape(1, NZ * 18, 768)  19.9 us
    pallas_call x7, Pallas kernels, once(): pl.pallas_call(kernel, grid=(1,), in_specs=specs, out_specs=out_specs or...  16.4 us
    all_to_all x1, starting transfers between devices, per_device(): attended = lax.all_to_all(attended, ('y', 'z'), 0, 0, tiled=True)  7.06 us
    all_gather x1, waiting for transfers between devices, per_device(): rest = lax.all_gather(rest, 'z', axis=0)  6.31 us
    ppermute x3, starting transfers between devices, per_device(): others = [lax.ppermute(projected[n, :2 * HD], 'xh', swap) for n in PIECES]  5.89 us
  transfers between devices with their start and end apart: 19, of which 6 were waited for; matrix products, arithmetic and copies ran while one was open for 3% of the time, Pallas kernels for 21%

profile of v4, /device:TPU:1, one launch (start us, length us, event | category | flops | bytes accessed | tf_op | source)
XLA Modules:
  0.0 184.1 jit_solution(15033200333776420099)
XLA Ops:
  6.5 0.7 all-gather.4.cloned.1.call-update
  7.3 1.0 reshape.34
  8.4 0.1 reshape.35
  8.5 0.8 broadcast_select_fusion
  9.4 1.2 reshape.32
  10.6 0.1 copy.22
  10.8 0.2 reshape.33
  11.0 19.9 %all_to_all.20 = bf16[8,18,768]{2,1,0:T(8,128)(2,1)S(1)} all-to-all(bf16[8,18,768]{2,1,0:T(8,128)(2,1)S(1)} %copy.17), channel_id=1, replica_groups=mesh['xl'=2,'c'=2,'xh'=2,'y'=4,'z'=8] {'z'}, dimensions={0} | all-to-all | bytes 442368 | tf_op jit(solution)/shard_map/all_to_all | solution.py:250
  31.0 0.1 broadcast_in_dim.8
  31.2 26.6 %all_to_all.21 = bf16[8,144,768]{2,1,0:T(8,128)(2,1)S(1)} all-to-all(bf16[8,144,768]{2,1,0:T(8,128)(2,1)S(1)} %broadcast_in_dim.8), channel_id=1, replica_groups=mesh['xl'=2,'c'=2,'xh'=2,'y'=4,'z'=8] {'xh','y'}, dimensions={0} | all-to-all | bytes 3538944 | tf_op jit(solution)/shard_map/all_to_all | solution.py:252
  57.8 0.9 slice.16
  58.7 5.4 %all-gather.4.cloned.1.call-done.tok_ref = bf16[8,192,1152]{2,1,0:T(8,128)(2,1)} async-done(((bf16[1,192,1152]{2,1,0:T(8,128)(2,1)}), bf16[8,192,1152]{2,1,0:T(8,128)(2,1)}) %all-gather.4.cloned.1.call-update) | async-done | bytes 3538960 | tf_op jit(solution)/shard_map/all_gather | solution.py:254
  64.2 5.7 %spatial_proj.1 = bf16[4,224,768]{2,1,0:T(8,128)(2,1)S(1)} custom-call(bf16[8,192,1152]{2,1,0:T(8,128)(2,1)} %all-gather.4.cloned.1.call-done.tok_ref, f32[6,1152]{1,0:T(8,128)S(1)} %copy-done.1, bf16[1152,768]{1,0:T(8,128)(2,1)S(1)} %bitcast.23, f32[72,4]{1,0:T(8,128)S(1)} %bitcast.29), custom_call_target="tpu_custom_call" | custom-call | tf_op jit(solution)/shard_map/spatial_proj/pallas_call | solution.py:259
  70.0 21.9 %all_to_all.22.refs_0_.refs_1_ = bf16[4,224,768]{2,1,0:T(8,128)(2,1)S(1)} all-to-all(bf16[4,224,768]{2,1,0:T(8,128)(2,1)S(1)} %spatial_proj.1), channel_id=1, replica_groups=mesh['xl'=2,'c'=2,'xh'=2,'y'=4,'z'=8] {'y'}, dimensions={0} | all-to-all | bytes 2752512 | tf_op jit(solution)/shard_map/all_to_all | solution.py:276
  91.9 2.8 %collective-permute-start.2 = (bf16[2,144,768]{2,1,0:T(8,128)(2,1)S(1)}, bf16[2,144,768]{2,1,0:T(8,128)(2,1)S(1)}, u32[]{:S(2)}, u32[]{:S(2)}) collective-permute-start(bf16[2,144,768]{2,1,0:T(8,128)(2,1)S(1)} %slice.19), channel_id=1, source_target_pairs={{0,32},{32,0},{1,33},{33,1},{2,34},{34,2},{3,35},{35,3},{4,36},{36... | collective-permute-start | bytes 1327112 | tf_op jit(solution)/shard_map/ppermute | solution.py:277
  94.8 0.3 collective-permute-start.1
  95.1 2.7 %collective-permute-start = (bf16[1,144,768]{2,1,0:T(8,128)(2,1)S(1)}, bf16[1,144,768]{2,1,0:T(8,128)(2,1)S(1)}, u32[]{:S(2)}, u32[]{:S(2)}) collective-permute-start(bf16[1,144,768]{2,1,0:T(8,128)(2,1)S(1)} %get-tuple-element.50), channel_id=1, source_target_pairs={{0,32},{32,0},{1,33},{33,1},{2,34},{34,2},{3,35},{35,3},{4,36},{36... | collective-permute-start | bytes 663560 | tf_op jit(solution)/shard_map/ppermute | solution.py:277
  97.9 8.5 %attend.4.refs_2_ = f32[4,80,768]{2,1,0:T(8,128)S(1)} custom-call(bf16[4,224,768]{2,1,0:T(8,128)(2,1)S(1)} %all_to_all.22.refs_0_.refs_1_, bf16[4,224,768]{2,1,0:T(8,128)(2,1)S(1)} %all_to_all.22.refs_0_.refs_1_), custom_call_target="tpu_custom_call" | custom-call | flops 37748736 | bytes 1000000 | tf_op jit(solution)/shard_map/attend/pallas_call | solution.py:137
  106.4 4.7 %attend.5.refs_2_ = f32[4,80,768]{2,1,0:T(8,128)S(1)} custom-call(bf16[4,224,768]{2,1,0:T(8,128)(2,1)S(1)} %all_to_all.22.refs_0_.refs_1_, bf16[2,144,768]{2,1,0:T(8,128)(2,1)S(1)} %collective-permute-done.2.refs_1_, f32[4,80,768]{2,1,0:T(8,128)S(1)} %attend.4.refs_2_), custom_call_target="tpu_custom_call" | custom-call | flops 18874368 | bytes 1000000 | tf_op jit(solution)/shard_map/attend/pallas_call | solution.py:137
  111.1 2.9 %attend.6.refs_2_ = f32[4,80,768]{2,1,0:T(8,128)S(1)} custom-call(bf16[4,224,768]{2,1,0:T(8,128)(2,1)S(1)} %all_to_all.22.refs_0_.refs_1_, bf16[1,144,768]{2,1,0:T(8,128)(2,1)S(1)} %collective-permute-done.1.refs_1_, f32[4,80,768]{2,1,0:T(8,128)S(1)} %attend.5.refs_2_), custom_call_target="tpu_custom_call" | custom-call | flops 9437184 | bytes 1000000 | tf_op jit(solution)/shard_map/attend/pallas_call | solution.py:137
  113.9 4.2 %attend.7 = bf16[4,8,56,128]{3,2,1,0:T(8,128)(2,1)} custom-call(bf16[4,224,768]{2,1,0:T(8,128)(2,1)S(1)} %all_to_all.22.refs_0_.refs_1_, bf16[1,144,768]{2,1,0:T(8,128)(2,1)S(1)} %collective-permute-done.refs_1_, f32[4,80,768]{2,1,0:T(8,128)S(1)} %attend.6.refs_2_), custom_call_target="tpu_custom_call" | custom-call | flops 9437184 | bytes 1000000 | tf_op jit(solution)/shard_map/attend/pallas_call | solution.py:137
  118.1 6.3 %all-gather.6.cloned.1.call-done = bf16[9216,256]{1,0:T(8,128)(2,1)} async-done(((bf16[1152,256]{1,0:T(8,128)(2,1)}), bf16[9216,256]{1,0:T(8,128)(2,1)}) %all-gather.6.cloned.1.call-update) | async-done | bytes 4718608 | tf_op jit(solution)/shard_map/all_gather | solution.py:257
  124.4 0.7 collective-permute-start.3
  125.1 7.1 %all-to-all-start.3 = ((bf16[32,56,128]{2,1,0:T(8,128)(2,1)}), bf16[32,56,128]{2,1,0:T(8,128)(2,1)S(1)}, u32[]{:S(2)}, u32[]{:S(2)}) async-start(bf16[32,56,128]{2,1,0:T(8,128)(2,1)} %bitcast.8), calls=%async_computation.3 | async-start | bytes 917504 | tf_op jit(solution)/shard_map/all_to_all | solution.py:285
  132.3 0.7 collective-permute-done.3.got
  133.0 5.9 %prepare.1 = (bf16[1152,1152]{1,0:T(8,128)(2,1)S(1)}, bf16[1152,1152]{1,0:T(8,128)(2,1)}, bf16[896,1152]{1,0:T(8,128)(2,1)S(1)}) custom-call(s32[2]{0:T(128)S(1)} %pad_add_fusion.place_ref, bf16[8,1152,256]{2,1,0:T(8,128)(2,1)} %bitcast.33, bf16[8,1152,256]{2,1,0:T(8,128)(2,1)} %collective-permute-done.3.got), custom_call_target="tpu_custom_call" | custom-call | flops 2000000000 | bytes 8000000 | tf_op jit(solution)/shard_map/prepare/pallas_call | solution.py:217
  138.9 1.5 copy-done.3
  140.4 1.3 copy-done.5
  141.8 4.1 %all-to-all-done.3 = bf16[32,56,128]{2,1,0:T(8,128)(2,1)S(1)} async-done(((bf16[32,56,128]{2,1,0:T(8,128)(2,1)}), bf16[32,56,128]{2,1,0:T(8,128)(2,1)S(1)}, u32[]{:S(2)}, u32[]{:S(2)}) %all-to-all-start.3) | async-done | bytes 458784 | tf_op jit(solution)/shard_map/all_to_all | solution.py:285
  145.9 1.7 copy-done.4
  147.7 1.0 spatial_end.3
  148.6 1.3 collective-permute-start.7
  149.9 2.8 %collective-permute-start.6 = (bf16[96,1152]{1,0:T(8,128)(2,1)S(1)}, bf16[96,1152]{1,0:T(8,128)(2,1)S(1)}, u32[]{:S(2)}, u32[]{:S(2)}) collective-permute-start(bf16[96,1152]{1,0:T(8,128)(2,1)S(1)} %get-tuple-element.33.n0), channel_id=1, source_target_pairs={{0,64},{64,0},{1,65},{65,1},{2,66},{66,2},{3,67},{67,3},{4,68},{68... | collective-permute-start | bytes 663560 | tf_op jit(solution)/shard_map/ppermute | solution.py:306
  152.7 1.0 spatial_end.2
  153.7 3.5 %collective-permute-start.8 = (bf16[96,1152]{1,0:T(8,128)(2,1)S(1)}, bf16[96,1152]{1,0:T(8,128)(2,1)S(1)}, u32[]{:S(2)}, u32[]{:S(2)}) collective-permute-start(bf16[96,1152]{1,0:T(8,128)(2,1)S(1)} %collective-permute-done.7.n2), channel_id=1, source_target_pairs={{0,64},{64,0},{1,65},{65,1},{2,66},{66,2},{3,67},{67,3},{4,68},{68... | collective-permute-start | bytes 663560 | tf_op jit(solution)/shard_map/ppermute | solution.py:306
  157.2 1.2 collective-permute-start.5
  158.4 0.3 collective-permute-start.4
  158.6 2.1 %temporal.2 = (bf16[216,128]{1,0:T(8,128)(2,1)S(1)}, bf16[216,128]{1,0:T(8,128)(2,1)S(1)}, bf16[216,128]{1,0:T(8,128)(2,1)S(1)}, bf16[216,128]{1,0:T(8,128)(2,1)S(1)}) custom-call(bf16[96,1152]{1,0:T(8,128)(2,1)S(1)} %get-tuple-element.33.n0, bf16[96,1152]{1,0:T(8,128)(2,1)S(1)} %collective-permute-done.6.n1, ...), custom_call_target="tpu_custom_call" | custom-call | flops 2000000000 | bytes 8000000 | tf_op jit(solution)/shard_map/temporal/pallas_call | solution.py:217
  160.8 3.4 %collective-permute-done.5.n2 = bf16[96,1152]{1,0:T(8,128)(2,1)S(1)} collective-permute-done((bf16[96,1152]{1,0:T(8,128)(2,1)S(1)}, bf16[96,1152]{1,0:T(8,128)(2,1)S(1)}, u32[]{:S(2)}, u32[]{:S(2)}) %collective-permute-start.5) | collective-permute-done | bytes 221216 | tf_op jit(solution)/shard_map/ppermute | solution.py:301
  164.2 0.8 collective-permute-start.9
  165.0 1.2 collective-permute-start.14
  166.2 0.9 collective-permute-start.15
  167.2 2.1 %temporal.3 = (bf16[216,128]{1,0:T(8,128)(2,1)S(1)}, bf16[216,128]{1,0:T(8,128)(2,1)S(1)}, bf16[216,128]{1,0:T(8,128)(2,1)S(1)}, bf16[216,128]{1,0:T(8,128)(2,1)S(1)}) custom-call(bf16[96,1152]{1,0:T(8,128)(2,1)S(1)} %get-tuple-element.32.n0, bf16[96,1152]{1,0:T(8,128)(2,1)S(1)} %collective-permute-done.4.n1, ...), custom_call_target="tpu_custom_call" | custom-call | flops 2000000000 | bytes 8000000 | tf_op jit(solution)/shard_map/temporal/pallas_call | solution.py:217
  169.4 1.3 collective-permute-start.11
  170.7 0.9 collective-permute-start.12
  171.6 2.1 %temporal_end.2.out_refs_0_ = bf16[192,1152]{1,0:T(8,128)(2,1)} custom-call(s32[2]{0:T(128)S(1)} %pad_add_fusion.place_ref, bf16[216,128]{1,0:T(8,128)(2,1)S(1)} %get-tuple-element.44.m0, bf16[216,128]{1,0:T(8,128)(2,1)S(1)} %collective-permute-done.13.m1, bf16[216,128]{1,0:T(8,128)(2,1)S(1)} %collective-permute-done.14.m2, ...), custom_call_target="tpu_custom_call" | custom-call | flops 2000000000 | bytes 8000000 | tf_op jit(solution)/shard_map/temporal_end/pallas_call | solution.py:217
  173.7 1.4 collective-permute-done.12.m3
  175.1 2.1 %temporal_end.3 = bf16[192,1152]{1,0:T(8,128)(2,1)} custom-call(s32[2]{0:T(128)S(1)} %pad_add_fusion.place_ref, bf16[216,128]{1,0:T(8,128)(2,1)S(1)} %get-tuple-element.38.m0, bf16[216,128]{1,0:T(8,128)(2,1)S(1)} %collective-permute-done.10.m1, bf16[216,128]{1,0:T(8,128)(2,1)S(1)} %collective-permute-done.11.m2, ...), custom_call_target="tpu_custom_call", output_to_operand_aliasing={{}: (8, {})} | custom-call | flops 2000000000 | bytes 8000000 | tf_op jit(solution)/shard_map/temporal_end/pallas_call | solution.py:217
  (42 shorter events, 0.7 us)
Async XLA Ops:
  6.5 57.5 %all-gather.4.cloned.1.call-start = ((), (), s32[]{:S(2)}) async-start(), calls=%async_computation.4 | async-start | bytes 3981312 | tf_op jit(solution)/shard_map/all_gather | solution.py:254
  7.3 117.2 %all-gather.6.cloned.1.call-start = ((), (), s32[]{:S(2)}) async-start(), calls=%async_computation.5 | async-start | bytes 5308416 | tf_op jit(solution)/shard_map/all_gather | solution.py:257
  31.1 32.9 %copy-start.7 = (f32[4,72]{1,0:T(4,128)S(1)}, f32[4,72]{1,0:T(4,128)}, u32[]{:S(2)}) copy-start(f32[4,72]{1,0:T(4,128)} %param.13) | copy-start | bytes 3460
  31.2 33.0 %copy-start.1 = (f32[6,1152]{1,0:T(8,128)S(1)}, f32[6,1152]{1,0:T(8,128)}, u32[]{:S(2)}) copy-start(f32[6,1152]{1,0:T(8,128)} %mod_ref.9) | copy-start | bytes 82948
  91.9 14.4 %collective-permute-start.2 = (bf16[2,144,768]{2,1,0:T(8,128)(2,1)S(1)}, bf16[2,144,768]{2,1,0:T(8,128)(2,1)S(1)}, u32[]{:S(2)}, u32[]{:S(2)}) collective-permute-start(bf16[2,144,768]{2,1,0:T(8,128)(2,1)S(1)} %slice.19), channel_id=1, source_target_pairs={{0,32},{32,0},{1,33},{33,1},{2,34},{34,2},{3,35},{35,3},{4,36},{36... | collective-permute-start | bytes 1327112 | tf_op jit(solution)/shard_map/ppermute | solution.py:277
  94.8 16.3 %collective-permute-start.1 = (bf16[1,144,768]{2,1,0:T(8,128)(2,1)S(1)}, bf16[1,144,768]{2,1,0:T(8,128)(2,1)S(1)}, u32[]{:S(2)}, u32[]{:S(2)}) collective-permute-start(bf16[1,144,768]{2,1,0:T(8,128)(2,1)S(1)} %get-tuple-element.49), channel_id=1, source_target_pairs={{0,32},{32,0},{1,33},{33,1},{2,34},{34,2},{3,35},{35,3},{4,36},{36... | collective-permute-start | bytes 663560 | tf_op jit(solution)/shard_map/ppermute | solution.py:277
  95.1 18.8 %collective-permute-start = (bf16[1,144,768]{2,1,0:T(8,128)(2,1)S(1)}, bf16[1,144,768]{2,1,0:T(8,128)(2,1)S(1)}, u32[]{:S(2)}, u32[]{:S(2)}) collective-permute-start(bf16[1,144,768]{2,1,0:T(8,128)(2,1)S(1)} %get-tuple-element.50), channel_id=1, source_target_pairs={{0,32},{32,0},{1,33},{33,1},{2,34},{34,2},{3,35},{35,3},{4,36},{36... | collective-permute-start | bytes 663560 | tf_op jit(solution)/shard_map/ppermute | solution.py:277
  124.4 8.6 %collective-permute-start.3 = (bf16[8,1152,256]{2,1,0:T(8,128)(2,1)}, bf16[8,1152,256]{2,1,0:T(8,128)(2,1)}, u32[]{:S(2)}, u32[]{:S(2)}) collective-permute-start(bf16[8,1152,256]{2,1,0:T(8,128)(2,1)} %bitcast.32), channel_id=1, source_target_pairs={{0,64},{64,0},{1,65},{65,1},{2,66},{66,2},{3,67},{67,3},{4,68},{68... | collective-permute-start | bytes 14155784 | tf_op jit(solution)/shard_map/ppermute | solution.py:283
  125.1 20.8 %all-to-all-start.3 = ((bf16[32,56,128]{2,1,0:T(8,128)(2,1)}), bf16[32,56,128]{2,1,0:T(8,128)(2,1)S(1)}, u32[]{:S(2)}, u32[]{:S(2)}) async-start(bf16[32,56,128]{2,1,0:T(8,128)(2,1)} %bitcast.8), calls=%async_computation.3 | async-start | bytes 917504 | tf_op jit(solution)/shard_map/all_to_all | solution.py:285
  132.3 13.7 %copy-start = (bf16[2,1,96,1152]{3,2,1,0:T(8,128)(2,1)S(1)}, bf16[2,1,96,1152]{3,2,1,0:T(8,128)(2,1)}, u32[]{:S(2)}) copy-start(bf16[2,1,96,1152]{3,2,1,0:T(8,128)(2,1)} %param.7) | copy-start | bytes 1327108
  138.9 1.5 copy-start.3
  140.4 1.3 copy-start.5
  145.9 1.8 copy-start.4
  148.6 10.0 %copy-start.6 = (bf16[896,1152]{1,0:T(8,128)(2,1)S(1)}, bf16[896,1152]{1,0:T(8,128)(2,1)}, u32[]{:S(2)}) copy-start(bf16[896,1152]{1,0:T(8,128)(2,1)} %copy-done.5) | copy-start | bytes 6193156
  148.6 5.0 %collective-permute-start.7 = (bf16[96,1152]{1,0:T(8,128)(2,1)S(1)}, bf16[96,1152]{1,0:T(8,128)(2,1)S(1)}, u32[]{:S(2)}, u32[]{:S(2)}) collective-permute-start(bf16[96,1152]{1,0:T(8,128)(2,1)S(1)} %get-tuple-element.33.n0), channel_id=1, source_target_pairs={{0,128},{128,0},{1,129},{129,1},{2,130},{130,2},{3,131},{131,3},{4... | collective-permute-start | bytes 663560 | tf_op jit(solution)/shard_map/ppermute | solution.py:301
  149.9 8.7 %collective-permute-start.6 = (bf16[96,1152]{1,0:T(8,128)(2,1)S(1)}, bf16[96,1152]{1,0:T(8,128)(2,1)S(1)}, u32[]{:S(2)}, u32[]{:S(2)}) collective-permute-start(bf16[96,1152]{1,0:T(8,128)(2,1)S(1)} %get-tuple-element.33.n0), channel_id=1, source_target_pairs={{0,64},{64,0},{1,65},{65,1},{2,66},{66,2},{3,67},{67,3},{4,68},{68... | collective-permute-start | bytes 663560 | tf_op jit(solution)/shard_map/ppermute | solution.py:306
  153.7 5.0 %collective-permute-start.8 = (bf16[96,1152]{1,0:T(8,128)(2,1)S(1)}, bf16[96,1152]{1,0:T(8,128)(2,1)S(1)}, u32[]{:S(2)}, u32[]{:S(2)}) collective-permute-start(bf16[96,1152]{1,0:T(8,128)(2,1)S(1)} %collective-permute-done.7.n2), channel_id=1, source_target_pairs={{0,64},{64,0},{1,65},{65,1},{2,66},{66,2},{3,67},{67,3},{4,68},{68... | collective-permute-start | bytes 663560 | tf_op jit(solution)/shard_map/ppermute | solution.py:306
  157.2 7.1 %collective-permute-start.5 = (bf16[96,1152]{1,0:T(8,128)(2,1)S(1)}, bf16[96,1152]{1,0:T(8,128)(2,1)S(1)}, u32[]{:S(2)}, u32[]{:S(2)}) collective-permute-start(bf16[96,1152]{1,0:T(8,128)(2,1)S(1)} %get-tuple-element.32.n0), channel_id=1, source_target_pairs={{0,128},{128,0},{1,129},{129,1},{2,130},{130,2},{3,131},{131,3},{4... | collective-permute-start | bytes 663560 | tf_op jit(solution)/shard_map/ppermute | solution.py:301
  158.4 8.8 %collective-permute-start.4 = (bf16[96,1152]{1,0:T(8,128)(2,1)S(1)}, bf16[96,1152]{1,0:T(8,128)(2,1)S(1)}, u32[]{:S(2)}, u32[]{:S(2)}) collective-permute-start(bf16[96,1152]{1,0:T(8,128)(2,1)S(1)} %get-tuple-element.32.n0), channel_id=1, source_target_pairs={{0,64},{64,0},{1,65},{65,1},{2,66},{66,2},{3,67},{67,3},{4,68},{68... | collective-permute-start | bytes 663560 | tf_op jit(solution)/shard_map/ppermute | solution.py:306
  164.2 2.9 %collective-permute-start.9 = (bf16[96,1152]{1,0:T(8,128)(2,1)S(1)}, bf16[96,1152]{1,0:T(8,128)(2,1)S(1)}, u32[]{:S(2)}, u32[]{:S(2)}) collective-permute-start(bf16[96,1152]{1,0:T(8,128)(2,1)S(1)} %collective-permute-done.5.n2), channel_id=1, source_target_pairs={{0,64},{64,0},{1,65},{65,1},{2,66},{66,2},{3,67},{67,3},{4,68},{68... | collective-permute-start | bytes 663560 | tf_op jit(solution)/shard_map/ppermute | solution.py:306
  165.0 5.7 %collective-permute-start.13 = (bf16[216,128]{1,0:T(8,128)(2,1)S(1)}, bf16[216,128]{1,0:T(8,128)(2,1)S(1)}, u32[]{:S(2)}, u32[]{:S(2)}) collective-permute-start(bf16[216,128]{1,0:T(8,128)(2,1)S(1)} %get-tuple-element.45), channel_id=1, source_target_pairs={{0,64},{64,0},{1,65},{65,1},{2,66},{66,2},{3,67},{67,3},{4,68},{68... | collective-permute-start | bytes 165896 | tf_op jit(solution)/shard_map/ppermute | solution.py:312
  165.0 6.5 %collective-permute-start.14 = (bf16[216,128]{1,0:T(8,128)(2,1)S(1)}, bf16[216,128]{1,0:T(8,128)(2,1)S(1)}, u32[]{:S(2)}, u32[]{:S(2)}) collective-permute-start(bf16[216,128]{1,0:T(8,128)(2,1)S(1)} %get-tuple-element.46), channel_id=1, source_target_pairs={{0,128},{128,0},{1,129},{129,1},{2,130},{130,2},{3,131},{131,3},{4... | collective-permute-start | bytes 165896 | tf_op jit(solution)/shard_map/ppermute | solution.py:313
  166.2 5.3 %copy-start.2 = (bf16[1152,1152]{1,0:T(8,128)(2,1)S(1)}, bf16[1152,1152]{1,0:T(8,128)(2,1)}, u32[]{:S(2)}) copy-start(bf16[1152,1152]{1,0:T(8,128)(2,1)} %get-tuple-element.43.weight) | copy-start | bytes 7962628
  166.2 5.3 %collective-permute-start.15 = (bf16[216,128]{1,0:T(8,128)(2,1)S(1)}, bf16[216,128]{1,0:T(8,128)(2,1)S(1)}, u32[]{:S(2)}, u32[]{:S(2)}) collective-permute-start(bf16[216,128]{1,0:T(8,128)(2,1)S(1)} %get-tuple-element.47), channel_id=1, source_target_pairs={{0,192},{192,0},{64,128},{128,64},{1,193},{193,1},{65,129},{129,65... | collective-permute-start | bytes 165896 | tf_op jit(solution)/shard_map/ppermute | solution.py:314
  169.3 4.4 %collective-permute-start.10 = (bf16[216,128]{1,0:T(8,128)(2,1)S(1)}, bf16[216,128]{1,0:T(8,128)(2,1)S(1)}, u32[]{:S(2)}, u32[]{:S(2)}) collective-permute-start(bf16[216,128]{1,0:T(8,128)(2,1)S(1)} %get-tuple-element.39), channel_id=1, source_target_pairs={{0,64},{64,0},{1,65},{65,1},{2,66},{66,2},{3,67},{67,3},{4,68},{68... | collective-permute-start | bytes 165896 | tf_op jit(solution)/shard_map/ppermute | solution.py:312
  169.4 4.3 %collective-permute-start.11 = (bf16[216,128]{1,0:T(8,128)(2,1)S(1)}, bf16[216,128]{1,0:T(8,128)(2,1)S(1)}, u32[]{:S(2)}, u32[]{:S(2)}) collective-permute-start(bf16[216,128]{1,0:T(8,128)(2,1)S(1)} %get-tuple-element.40), channel_id=1, source_target_pairs={{0,128},{128,0},{1,129},{129,1},{2,130},{130,2},{3,131},{131,3},{4... | collective-permute-start | bytes 165896 | tf_op jit(solution)/shard_map/ppermute | solution.py:313
  170.7 4.4 %collective-permute-start.12 = (bf16[216,128]{1,0:T(8,128)(2,1)S(1)}, bf16[216,128]{1,0:T(8,128)(2,1)S(1)}, u32[]{:S(2)}, u32[]{:S(2)}) collective-permute-start(bf16[216,128]{1,0:T(8,128)(2,1)S(1)} %get-tuple-element.41), channel_id=1, source_target_pairs={{0,192},{192,0},{64,128},{128,64},{1,193},{193,1},{65,129},{129,65... | collective-permute-start | bytes 165896 | tf_op jit(solution)/shard_map/ppermute | solution.py:314
Sparse Core Ops, SparseCore 0:
  9.1 54.8 all-gather.3
  65.8 58.5 all-gather.5

commit v5 on v4

--- a/solution.py
+++ b/solution.py
@@ -38,32 +38,27 @@
     return values * lax.rsqrt(mean_sq + 1e-06) * gain
 
 
-def spatial_proj(tok_ref, mod_ref, w_ref, gain_ref, out_ref, turned):
+def spatial_proj(tok_ref, mod_ref, w_ref, gain_ref, out_ref, outs_ref, part_ref, turned):
     cols = 4 * PATCH
     zeros = jnp.zeros((HP - HD, cols), F32)
 
-    @pl.when(pl.program_id(0) == 0)
+    @pl.when((pl.program_id(0) == 0) & (pl.program_id(1) == 0))
     def _():
-        turned[...] = w_ref[...].astype(F32).T.astype(BF)
-
-    clips = []
-    for clip in range(2):
-        tok = tok_ref[:, clip * PATCH : (clip + 1) * PATCH, :].reshape(cols, D).astype(F32)
-        normed = normalise(tok) * (1.0 + mod_ref[1:2, :]) + mod_ref[0:1, :]
-        clips.append(normed.astype(BF))
-    normed = jnp.concatenate(clips, 0)
-    both = lax.dot_general(turned[: 6 * HD], normed, NT, preferred_element_type=F32)
-    for clip in range(2):
-        proj = both[:, clip * cols : (clip + 1) * cols]
-        for head in range(2):
-            query, key, value = (
-                proj[part * 2 * HD + head * HD : part * 2 * HD + (head + 1) * HD] for part in range(3)
-            )
-            query = rms(query, gain_ref[:, 0:1]) * (FACTOR * math.log2(math.e))
-            key = rms(key, gain_ref[:, 1:2])
-            place = clip * 2 + head
-            parts = [key, value, query, zeros]
-            out_ref[place] = jnp.concatenate(parts, 0).astype(BF)
+        turned[...] = w_ref[:, :512].astype(F32).T.astype(BF)
+        rest = w_ref[:, 512:].astype(F32).T
+        outs_ref[...] = rest[: 2 * HD].astype(BF)
+        part_ref[...] = rest[2 * HD :].astype(BF)
+
+    tok = tok_ref[...].reshape(cols, D).astype(F32)
+    normed = normalise(tok) * (1.0 + mod_ref[1:2, :]) + mod_ref[0:1, :]
+    proj = lax.dot_general(turned[: 6 * HD], normed.astype(BF), NT, preferred_element_type=F32)
+    for head in range(2):
+        query, key, value = (
+            proj[part * 2 * HD + head * HD : part * 2 * HD + (head + 1) * HD] for part in range(3)
+        )
+        query = rms(query, gain_ref[:, 0:1]) * (FACTOR * math.log2(math.e))
+        key = rms(key, gain_ref[:, 1:2])
+        out_ref[head] = jnp.concatenate([key, value, query, zeros], 0).astype(BF)
 
 
 def pack(block, rows):
@@ -149,22 +144,10 @@
     )(*args)
 
 
-def prepare(place_ref, own, got, out_a, out_b, turned):
-    second = place_ref[0] == 1
-    for n in range(5):
-        width = min(256, D - n * 256)
-        here = slice(n * 256, n * 256 + width)
-        out_a[:, here] = jnp.where(second, got[n, :, :width], own[n, :, :width])
-        out_b[:, here] = jnp.where(second, own[n, :, :width], got[n, :, :width])
-    turned[:128] = own[4, :, 128:].astype(F32).T.astype(BF)
-    for n in range(3):
-        turned[128 + n * 256 : 384 + n * 256] = own[5 + n].astype(F32).T.astype(BF)
-
-
 def spatial_end(att_ref, tok_ref, mod_ref, weight, resid_ref, norm_ref):
     feats = [unpack(att_ref[n % 2, n // 2].astype(F32), 16) for n in range(HEADS)]
     attended = jnp.concatenate(feats, 0).T.astype(BF)
-    branch = jnp.dot(attended, weight[...], preferred_element_type=F32)
+    branch = lax.dot_general(attended, weight[...], NT, preferred_element_type=F32)
     resid = tok_ref[...].astype(F32) + mod_ref[2:3, :] * branch
     resid_ref[...] = resid
     norm_ref[...] = (normalise(resid) * (1.0 + mod_ref[4:5, :]) + mod_ref[3:4, :]).astype(BF)
@@ -194,14 +177,14 @@
         out_ref[...] = pack(jnp.concatenate(mixed, 0)[:, :PATCH], 3 * HD).astype(BF)
 
 
-def temporal_end(place_ref, m0, m1, m2, m3, resid_ref, mod_ref, weight, *out_refs):
-    branch = None
+def temporal_end(place_ref, m0, m1, m2, m3, resid_ref, mod_ref, weight, *refs):
+    out_ref, feats = refs[-2:]
     for step, att_ref in enumerate((m0, m1, m2, m3)):
-        feats = unpack(att_ref[...].astype(F32), HD)
-        here = pl.ds(pl.multiple_of((place_ref[1] ^ step) * (4 * HD), 4 * HD), 4 * HD)
-        add = jnp.dot(feats.T.astype(BF), weight[here, :], preferred_element_type=F32)
-        branch = add if branch is None else branch + add
-    out_refs[-1][...] = (resid_ref[...] + mod_ref[5:6, :] * branch).astype(BF)
+        here = pl.ds(pl.multiple_of((place_ref[0] ^ step) * (4 * HD), 4 * HD), 4 * HD)
+        feats[here, :] = unpack(att_ref[...].astype(F32), HD)
+    attended = feats[...].T.astype(BF)
+    branch = lax.dot_general(attended, weight[...], NT, preferred_element_type=F32)
+    out_ref[...] = (resid_ref[...] + mod_ref[5:6, :] * branch).astype(BF)
 
 
 SMEM = pl.BlockSpec(memory_space=pltpu.SMEM)
@@ -213,7 +196,7 @@
     return pl.BlockSpec(block, lambda i: place)
 
 
-def once(kernel, args, specs, shapes, out_specs=None, aliases=None):
+def once(kernel, args, specs, shapes, out_specs=None, aliases=None, scratch=()):
     return pl.pallas_call(
         kernel,
         grid=(1,),
@@ -221,9 +204,10 @@
         out_specs=out_specs or [full(s) for s in shapes],
         out_shape=shapes,
         input_output_aliases=aliases or {},
-        compiler_params=PARAMS,
+        scratch_shapes=scratch,
+        compiler_params=pltpu.CompilerParams(vmem_limit_bytes=20 * 1024 * 1024),
         cost_estimate=pl.CostEstimate(
-            flops=2_000_000_000, bytes_accessed=8_000_000, transcendentals=0
+            flops=20_000_000, bytes_accessed=100_000, transcendentals=0
         ),
         name=kernel.__name__,
     )(*args)
@@ -236,16 +220,16 @@
 def per_device(tokens, modulation, spatial_qkv, spatial_out, temporal_qkv, temporal_out, norm_gains):
     core = lax.axis_index("c")
     frame = lax.axis_index("xl") * 2 + core
-    place = jnp.stack([core, frame]).astype(jnp.int32)
+    place = frame.astype(jnp.int32).reshape(1)
     gains = norm_gains.T
     tok = tokens.reshape(ROWS, D)
 
     part_a = spatial_qkv.reshape(18, 3, NZ, 2 * HD).transpose(2, 0, 1, 3).reshape(NZ, 18, 6 * HD)
     part_a = jnp.pad(part_a, ((0, 0), (0, 0), (0, 512 - 6 * HD)))
     part_b = lax.dynamic_slice_in_dim(temporal_qkv.reshape(18, 3, D), frame * 4 * HD, 4 * HD, 2)
-    rest = [jnp.where(core == 0, spatial_out, temporal_out), part_b.reshape(18, 12 * HD)]
-    rest = jnp.pad(jnp.concatenate(rest, 1), ((0, 0), (0, 256 * NZ - D - 12 * HD)))
-    rest = rest.reshape(18, NZ, 256).transpose(1, 0, 2)
+    part_b = jnp.pad(part_b.reshape(18, 12 * HD), ((0, 0), (0, 32))).reshape(18, NZ, 112)
+    outs = jnp.where(core == 0, spatial_out, temporal_out).reshape(18, NZ, 2 * HD)
+    rest = jnp.concatenate([outs, part_b], 2).transpose(1, 0, 2)
     shard = jnp.concatenate([part_a, rest], 2)
     shard = lax.all_to_all(shard, "z", 0, 0, tiled=True).reshape(1, NZ * 18, 768)
     shard = jnp.broadcast_to(shard, (8, NZ * 18, 768))
@@ -253,43 +237,47 @@
 
     column = lax.all_gather(tok, "z", axis=0)
 
-    rest, column = lax.optimization_barrier((shard[:, 512:], column))
-    rest = lax.all_gather(rest, "z", axis=0)
-
-    projected = pl.pallas_call(
+    projected, outs, part_b = pl.pallas_call(
         spatial_proj,
-        grid=(2,),
+        grid=(2, 2),
         in_specs=[
-            pl.BlockSpec((4, ROWS, D), lambda i: (i, 0, 0)),
-            pl.BlockSpec((6, D), lambda i: (0, 0)),
-            pl.BlockSpec((D, 512), lambda i: (0, 0)),
-            pl.BlockSpec((HD, 4), lambda i: (0, 0)),
+            pl.BlockSpec((4, PATCH, D), lambda i, clip: (i, clip, 0)),
+            pl.BlockSpec((6, D), lambda i, clip: (0, 0)),
+            pl.BlockSpec((D, 768), lambda i, clip: (0, 0)),
+            pl.BlockSpec((HD, 4), lambda i, clip: (0, 0)),
         ],
-        out_specs=pl.BlockSpec((4, 3 * HD + 8, 4 * PATCH), lambda i: (0, 0, i)),
-        out_shape=shape(BF, 4, 3 * HD + 8, PLANE),
+        out_specs=[
+            pl.BlockSpec((2, 3 * HD + 8, 4 * PATCH), lambda i, clip: (clip, 0, i)),
+            pl.BlockSpec((2 * HD, D), lambda i, clip: (0, 0)),
+            pl.BlockSpec((112, D), lambda i, clip: (0, 0)),
+        ],
+        out_shape=[
+            shape(BF, 4, 3 * HD + 8, PLANE),
+            shape(BF, 2 * HD, D),
+            shape(BF, 112, D),
+        ],
         scratch_shapes=[pltpu.VMEM((512, D), BF)],
         compiler_params=PARAMS,
         name="spatial_proj",
     )(column, modulation, shard, gains)
 
     swap = [(0, 1), (1, 0)]
+    outs = lax.all_gather(outs, "z", axis=0, tiled=True)
+    turned = lax.all_gather(part_b, "z", axis=0, tiled=True)
+
     projected = lax.all_to_all(projected, "y", 0, 0, tiled=True)
     others = [lax.ppermute(projected[n, : 2 * HD], "xh", swap) for n in PIECES]
     part = attention(projected, projected, None, False)
     part = attention(projected, others[0], part, False)
     part = attention(projected, others[1], part, False)
+    part, others[2], outs = lax.optimization_barrier((part, others[2], outs))
     attended = attention(projected, others[2], part, True)
-    attended, rest = lax.optimization_barrier((attended, rest))
-    rest_got = lax.ppermute(rest, "c", swap)
+    outs_got = lax.ppermute(outs, "c", swap)
     attended = attended.reshape(NY * NZ, 56, 128)
     attended = lax.all_to_all(attended, ("y", "z"), 0, 0, tiled=True)
     attended = attended.reshape(4, NZ, 56, 128)
-    out_a, out_b, turned = once(
-        prepare,
-        [place, rest, rest_got],
-        [SMEM, full(rest), full(rest, 5)],
-        [shape(BF, D, D), shape(BF, D, D), shape(BF, 896, D)],
-    )
+    out_a = jnp.where(core == 0, outs, outs_got)
+    out_b = jnp.where(core == 0, outs_got, outs)
 
     steps = []
     for clip in range(2):
@@ -324,7 +312,9 @@
             aliases = {len(args): 0}
         whole = shape(BF, ROWS, D)
         out_specs = [full(whole, PATCH, clip)]
-        (result,) = once(temporal_end, [place] + args, specs, [whole], out_specs, aliases)
+        scratch = [pltpu.VMEM((D, PATCH), F32)]
+        args = [place] + args
+        (result,) = once(temporal_end, args, specs, [whole], out_specs, aliases, scratch)
     return result.reshape(2, 1, PATCH, D)
 
 

time: 185 us -> 190 us (1.027)
  blocking collectives: 68.4 us -> 42.2 us
  waiting for transfers between devices: 22.2 us -> 39.2 us
  starting transfers between devices: 27.8 us -> 34.5 us
  local copies, waits for them, and re-layouts: 8.66 us -> 13.6 us
  other arithmetic: 0.95 us -> 5.56 us
    all_to_all x1 -> x0, blocking collectives: 26.6 us -> none  [per_device(): shard = lax.all_to_all(shard, ('xh', 'y'), 0, 0, tiled=True).reshape(D, 768)]
    all_to_all x0 -> x1, waiting for transfers between devices: none -> 18.3 us  [per_device(): shard = lax.all_to_all(shard, ('xh', 'y'), 0, 0, tiled=True).reshape(D, 768)]
    all_to_all x1, waiting for transfers between devices: 4.14 us -> 13.7 us  [per_device(): attended = lax.all_to_all(attended, ('y', 'z'), 0, 0, tiled=True)]
    all_to_all x0 -> x1, starting transfers between devices: none -> 6.8 us  [per_device(): shard = lax.all_to_all(shard, ('xh', 'y'), 0, 0, tiled=True).reshape(D, 768)]
    all_gather x1 -> x2, waiting for transfers between devices: 6.31 us -> 0.02 us  [the longest x1 0.02 us: per_device(): outs = lax.all_gather(outs, 'z', axis=0, tiled=True)]
    select_n x1 -> x2, other arithmetic: 0.84 us -> 5.45 us  [the longest x1 4.62 us: per_device(): out_b = jnp.where(core == 0, outs_got, outs)]
    unnamed x18 -> x31, local copies, waits for them, and re-layouts: 4.72 us -> 9.08 us
    ppermute x2, waiting for transfers between devices: 3.43 us -> 0.17 us  [per_device(): moved = [lax.ppermute(norm, 'xl', swap) for _, norm in steps]]
  transfers between devices with their start and end apart: 19 -> 21, of which waited for: 6 -> 5; matrix products, arithmetic and copies ran while one was open for 3% -> 5% of each run, Pallas kernels for 21% -> 17%
where the time goes in v5:
time: 190 us; the launch traced here: 189 us
  blocking collectives  42.2 us (22%)
  Pallas kernels  40.8 us (21%)
  waiting for transfers between devices  39.2 us (21%)
  starting transfers between devices  34.5 us (18%)
  local copies, waits for them, and re-layouts  13.6 us (7%)
  between operations  13.4 us (7%)
  other arithmetic  5.56 us (3%)
    all_to_all x1, blocking collectives, per_device(): projected = lax.all_to_all(projected, 'y', 0, 0, tiled=True)  21.9 us
    all_to_all x1, blocking collectives, per_device(): lax.all_to_all(shard, 'z', 0, 0, tiled=True).reshape(1, NZ * 18, 768)  20.2 us
    pallas_call x4, Pallas kernels, attention(): pl.pallas_call(functools.partial(attend, steps, part is not None, finish)...  19.4 us
    all_to_all x1, waiting for transfers between devices, per_device(): shard = lax.all_to_all(shard, ('xh', 'y'), 0, 0, tiled=True).reshape(D, 768)  18.3 us
    pallas_call x6, Pallas kernels, once(): pl.pallas_call(kernel, grid=(1,), in_specs=specs, out_specs=out_specs or...  13.8 us
    all_to_all x1, waiting for transfers between devices, per_device(): attended = lax.all_to_all(attended, ('y', 'z'), 0, 0, tiled=True)  13.7 us
    unnamed x31, local copies, waits for them, and re-layouts  9.08 us
    pallas_call x1, Pallas kernels, per_device(): pl.pallas_call(spatial_proj, grid=(2, 2), in_specs=[pl.BlockSpec((4, PATC...  7.6 us
  transfers between devices with their start and end apart: 21, of which 5 were waited for; matrix products, arithmetic and copies ran while one was open for 5% of the time, Pallas kernels for 17%

profile of v5, /device:TPU:1, one launch (start us, length us, event | category | flops | bytes accessed | tf_op | source)
XLA Modules:
  0.0 189.2 jit_solution(11507794639618374725)
XLA Ops:
  6.5 0.7 all-gather.4.cloned.1.call-update
  7.3 1.2 reshape.39
  8.8 1.0 reshape.42
  10.2 0.8 broadcast_select_fusion.2
  11.3 20.2 %all_to_all.20 = bf16[8,18,768]{2,1,0:T(8,128)(2,1)S(1)} all-to-all(bf16[8,18,768]{2,1,0:T(8,128)(2,1)S(1)} %copy.17), channel_id=1, replica_groups=mesh['xl'=2,'c'=2,'xh'=2,'y'=4,'z'=8] {'z'}, dimensions={0} | all-to-all | bytes 442368 | tf_op jit(solution)/shard_map/all_to_all | solution.py:234
  31.7 1.4 broadcast_in_dim.8
  33.0 6.8 %all-to-all-start.1 = ((bf16[8,144,768]{2,1,0:T(8,128)(2,1)}), bf16[8,144,768]{2,1,0:T(8,128)(2,1)S(1)}, u32[]{:S(2)}, u32[]{:S(2)}) async-start(bf16[8,144,768]{2,1,0:T(8,128)(2,1)} %broadcast_in_dim.8), calls=%async_computation.1 | async-start | bytes 3538944 | tf_op jit(solution)/shard_map/all_to_all | solution.py:236
  40.0 18.3 %all-to-all-done.1 = bf16[8,144,768]{2,1,0:T(8,128)(2,1)S(1)} async-done(((bf16[8,144,768]{2,1,0:T(8,128)(2,1)}), bf16[8,144,768]{2,1,0:T(8,128)(2,1)S(1)}, u32[]{:S(2)}, u32[]{:S(2)}) %all-to-all-start.1) | async-done | bytes 1769504 | tf_op jit(solution)/shard_map/all_to_all | solution.py:236
  58.3 6.0 %all-gather.4.cloned.1.call-done.tok_ref = bf16[8,192,1152]{2,1,0:T(8,128)(2,1)} async-done(((bf16[1,192,1152]{2,1,0:T(8,128)(2,1)}), bf16[8,192,1152]{2,1,0:T(8,128)(2,1)}) %all-gather.4.cloned.1.call-update) | async-done | bytes 3538960 | tf_op jit(solution)/shard_map/all_gather | solution.py:238
  64.3 7.6 %spatial_proj.1 = (bf16[4,224,768]{2,1,0:T(8,128)(2,1)S(1)}, bf16[144,1152]{1,0:T(8,128)(2,1)}, bf16[112,1152]{1,0:T(8,128)(2,1)}) custom-call(bf16[8,192,1152]{2,1,0:T(8,128)(2,1)} %all-gather.4.cloned.1.call-done.tok_ref, f32[6,1152]{1,0:T(8,128)S(1)} %copy-done.5, bf16[1152,768]{1,0:T(8,128)(2,1)S(1)} %bitcast.17, f32[72,4]{1,0:T(8,128)S(1)} %bitcast.24), custom_call_target="tpu_custom_call" | custom-call | tf_op jit(solution)/shard_map/spatial_proj/pallas_call | solution.py:240
  72.0 21.9 %all_to_all.21.refs_0_.refs_1_ = bf16[4,224,768]{2,1,0:T(8,128)(2,1)S(1)} all-to-all(bf16[4,224,768]{2,1,0:T(8,128)(2,1)S(1)} %get-tuple-element.26), channel_id=1, replica_groups=mesh['xl'=2,'c'=2,'xh'=2,'y'=4,'z'=8] {'y'}, dimensions={0} | all-to-all | bytes 2752512 | tf_op jit(solution)/shard_map/all_to_all | solution.py:268
  94.0 2.8 %collective-permute-start.1 = (bf16[2,144,768]{2,1,0:T(8,128)(2,1)S(1)}, bf16[2,144,768]{2,1,0:T(8,128)(2,1)S(1)}, u32[]{:S(2)}, u32[]{:S(2)}) collective-permute-start(bf16[2,144,768]{2,1,0:T(8,128)(2,1)S(1)} %slice.13), channel_id=1, source_target_pairs={{0,32},{32,0},{1,33},{33,1},{2,34},{34,2},{3,35},{35,3},{4,36},{36... | collective-permute-start | bytes 1327112 | tf_op jit(solution)/shard_map/ppermute | solution.py:269
  96.8 0.3 collective-permute-start
  97.2 2.7 %collective-permute-start.2 = (bf16[1,144,768]{2,1,0:T(8,128)(2,1)S(1)}, bf16[1,144,768]{2,1,0:T(8,128)(2,1)S(1)}, u32[]{:S(2)}, u32[]{:S(2)}) collective-permute-start(bf16[1,144,768]{2,1,0:T(8,128)(2,1)S(1)} %get-tuple-element.49), channel_id=1, source_target_pairs={{0,32},{32,0},{1,33},{33,1},{2,34},{34,2},{3,35},{35,3},{4,36},{36... | collective-permute-start | bytes 663560 | tf_op jit(solution)/shard_map/ppermute | solution.py:269
  99.9 8.4 %attend.4.refs_2_ = f32[4,80,768]{2,1,0:T(8,128)S(1)} custom-call(bf16[4,224,768]{2,1,0:T(8,128)(2,1)S(1)} %all_to_all.21.refs_0_.refs_1_, bf16[4,224,768]{2,1,0:T(8,128)(2,1)S(1)} %all_to_all.21.refs_0_.refs_1_), custom_call_target="tpu_custom_call" | custom-call | flops 37748736 | bytes 1000000 | tf_op jit(solution)/shard_map/attend/pallas_call | solution.py:132
  108.3 4.6 %attend.5.refs_2_ = f32[4,80,768]{2,1,0:T(8,128)S(1)} custom-call(bf16[4,224,768]{2,1,0:T(8,128)(2,1)S(1)} %all_to_all.21.refs_0_.refs_1_, bf16[2,144,768]{2,1,0:T(8,128)(2,1)S(1)} %collective-permute-done.1.refs_1_, f32[4,80,768]{2,1,0:T(8,128)S(1)} %attend.4.refs_2_), custom_call_target="tpu_custom_call" | custom-call | flops 18874368 | bytes 1000000 | tf_op jit(solution)/shard_map/attend/pallas_call | solution.py:132
  113.0 2.8 %attend.6.refs_2_ = f32[4,80,768]{2,1,0:T(8,128)S(1)} custom-call(bf16[4,224,768]{2,1,0:T(8,128)(2,1)S(1)} %all_to_all.21.refs_0_.refs_1_, bf16[1,144,768]{2,1,0:T(8,128)(2,1)S(1)} %collective-permute-done.refs_1_, f32[4,80,768]{2,1,0:T(8,128)S(1)} %attend.5.refs_2_), custom_call_target="tpu_custom_call" | custom-call | flops 9437184 | bytes 1000000 | tf_op jit(solution)/shard_map/attend/pallas_call | solution.py:132
  115.9 2.5 %collective-permute-start.3 = (bf16[1152,1152]{1,0:T(8,128)(2,1)}, bf16[1152,1152]{1,0:T(8,128)(2,1)}, u32[]{:S(2)}, u32[]{:S(2)}) collective-permute-start(bf16[1152,1152]{1,0:T(8,128)(2,1)} %all-gather.6.cloned.1.call-done), channel_id=1, source_target_pairs={{0,64},{64,0},{1,65},{65,1},{2,66},{66,2},{3,67},{67,3},{4,68},{68... | collective-permute-start | bytes 7962632 | tf_op jit(solution)/shard_map/ppermute | solution.py:275
  118.4 3.5 %attend.7 = bf16[4,8,56,128]{3,2,1,0:T(8,128)(2,1)S(1)} custom-call(bf16[4,224,768]{2,1,0:T(8,128)(2,1)S(1)} %all_to_all.21.refs_0_.refs_1_, bf16[1,144,768]{2,1,0:T(8,128)(2,1)S(1)} %collective-permute-done.2.refs_1_, f32[4,80,768]{2,1,0:T(8,128)S(1)} %attend.6.refs_2_), custom_call_target="tpu_custom_call" | custom-call | flops 9437184 | bytes 1000000 | tf_op jit(solution)/shard_map/attend/pallas_call | solution.py:132
  121.9 0.8 copy-done.4
  122.7 5.4 %all-to-all-start.3 = ((bf16[32,56,128]{2,1,0:T(8,128)(2,1)}), bf16[32,56,128]{2,1,0:T(8,128)(2,1)S(1)}, u32[]{:S(2)}, u32[]{:S(2)}) async-start(bf16[32,56,128]{2,1,0:T(8,128)(2,1)} %bitcast.23), calls=%async_computation.3 | async-start | bytes 917504 | tf_op jit(solution)/shard_map/all_to_all | solution.py:277
  128.2 4.6 %broadcast_select_fusion = (bf16[1152,1152]{1,0:T(8,128)(2,1)S(1)}, bf16[1152,1152]{1,0:T(8,128)(2,1)}) fusion(bf16[1152,1152]{1,0:T(8,128)(2,1)} %collective-permute-done.3, bf16[1152,1152]{1,0:T(8,128)(2,1)} %all-gather.6.cloned.1.call-done, pred[]{:T(512)S(6)} %eq.2), kind=kLoop, calls=%fused_computation | loop fusion | flops 2654208 | bytes 10616833 | tf_op jit(solution)/shard_map/jit(_where)/select_n | solution.py:280
  132.8 13.7 %all-to-all-done.3 = bf16[32,56,128]{2,1,0:T(8,128)(2,1)S(1)} async-done(((bf16[32,56,128]{2,1,0:T(8,128)(2,1)}), bf16[32,56,128]{2,1,0:T(8,128)(2,1)S(1)}, u32[]{:S(2)}, u32[]{:S(2)}) %all-to-all-start.3) | async-done | bytes 458784 | tf_op jit(solution)/shard_map/all_to_all | solution.py:277
  146.4 1.8 copy-done
  148.2 0.8 copy-done.6
  149.0 1.9 %spatial_end.3 = (f32[96,1152]{1,0:T(8,128)S(1)}, bf16[96,1152]{1,0:T(8,128)(2,1)}) custom-call(bf16[4,8,56,128]{3,2,1,0:T(8,128)(2,1)S(1)} %bitcast.18, bf16[192,1152]{1,0:T(8,128)(2,1)S(1)} %bitcast.21, f32[6,1152]{1,0:T(8,128)S(1)} %copy-done.6, bf16[1152,1152]{1,0:T(8,128)(2,1)S(1)} %copy-done), custom_call_target="tpu_custom_call" | custom-call | flops 20000000 | bytes 100000 | tf_op jit(solution)/shard_map/spatial_end/pallas_call | solution.py:200
  150.9 0.8 copy-done.12
  151.7 0.7 collective-permute-start.7
  152.4 2.6 %collective-permute-start.6 = (bf16[96,1152]{1,0:T(8,128)(2,1)}, bf16[96,1152]{1,0:T(8,128)(2,1)}, u32[]{:S(2)}, u32[]{:S(2)}) collective-permute-start(bf16[96,1152]{1,0:T(8,128)(2,1)} %get-tuple-element.32.n0), channel_id=1, source_target_pairs={{0,64},{64,0},{1,65},{65,1},{2,66},{66,2},{3,67},{67,3},{4,68},{68... | collective-permute-start | bytes 663560 | tf_op jit(solution)/shard_map/ppermute | solution.py:294
  155.0 1.9 %spatial_end.2 = (f32[96,1152]{1,0:T(8,128)S(1)}, bf16[96,1152]{1,0:T(8,128)(2,1)}) custom-call(bf16[4,8,56,128]{3,2,1,0:T(8,128)(2,1)S(1)} %bitcast.19, bf16[192,1152]{1,0:T(8,128)(2,1)S(1)} %bitcast.22, f32[6,1152]{1,0:T(8,128)S(1)} %copy-done.6, bf16[1152,1152]{1,0:T(8,128)(2,1)S(1)} %copy-done), custom_call_target="tpu_custom_call" | custom-call | flops 20000000 | bytes 100000 | tf_op jit(solution)/shard_map/spatial_end/pallas_call | solution.py:200
  156.9 0.8 copy-done.10
  157.6 2.4 %collective-permute-start.8 = (bf16[96,1152]{1,0:T(8,128)(2,1)}, bf16[96,1152]{1,0:T(8,128)(2,1)S(1)}, u32[]{:S(2)}, u32[]{:S(2)}) collective-permute-start(bf16[96,1152]{1,0:T(8,128)(2,1)} %collective-permute-done.7.n2), channel_id=1, source_target_pairs={{0,64},{64,0},{1,65},{65,1},{2,66},{66,2},{3,67},{67,3},{4,68},{68... | collective-permute-start | bytes 663560 | tf_op jit(solution)/shard_map/ppermute | solution.py:294
  160.1 0.8 collective-permute-start.5
  160.9 0.3 collective-permute-start.4
  161.2 0.2 collective-permute-done.8.n3
  161.4 1.6 copy-done.1
  163.0 0.8 copy-done.9
  163.7 3.4 %temporal.2 = (bf16[216,128]{1,0:T(8,128)(2,1)S(1)}, bf16[216,128]{1,0:T(8,128)(2,1)S(1)}, bf16[216,128]{1,0:T(8,128)(2,1)S(1)}, bf16[216,128]{1,0:T(8,128)(2,1)S(1)}) custom-call(bf16[96,1152]{1,0:T(8,128)(2,1)} %get-tuple-element.32.n0, bf16[96,1152]{1,0:T(8,128)(2,1)} %collective-permute-done.6.n1, bf16[96,1152]{1,0:T(8,128)(2,1)} %collective-permute-done.7.n2, ...), custom_call_target="tpu_custom_call" | custom-call | flops 20000000 | bytes 100000 | tf_op jit(solution)/shard_map/temporal/pallas_call | solution.py:200
  167.3 2.5 %collective-permute-start.9 = (bf16[96,1152]{1,0:T(8,128)(2,1)S(1)}, bf16[96,1152]{1,0:T(8,128)(2,1)S(1)}, u32[]{:S(2)}, u32[]{:S(2)}) collective-permute-start(bf16[96,1152]{1,0:T(8,128)(2,1)S(1)} %collective-permute-done.5.n2), channel_id=1, source_target_pairs={{0,64},{64,0},{1,65},{65,1},{2,66},{66,2},{3,67},{67,3},{4,68},{68... | collective-permute-start | bytes 663560 | tf_op jit(solution)/shard_map/ppermute | solution.py:294
  170.0 1.0 collective-permute-start.14
  171.0 1.0 collective-permute-start.15
  172.0 3.1 %temporal.3 = (bf16[216,128]{1,0:T(8,128)(2,1)S(1)}, bf16[216,128]{1,0:T(8,128)(2,1)S(1)}, bf16[216,128]{1,0:T(8,128)(2,1)S(1)}, bf16[216,128]{1,0:T(8,128)(2,1)S(1)}) custom-call(bf16[96,1152]{1,0:T(8,128)(2,1)} %get-tuple-element.31.n0, bf16[96,1152]{1,0:T(8,128)(2,1)S(1)} %collective-permute-done.4.n1, bf16[96,1152]{1,0:T(8,128)(2,1)S(1)} %collective-permute-done.5.n2, ...), custom_call_target="tpu_custom_call" | custom-call | flops 20000000 | bytes 100000 | tf_op jit(solution)/shard_map/temporal/pallas_call | solution.py:200
  175.2 1.1 collective-permute-start.11
  176.3 1.0 collective-permute-start.12
  177.4 0.8 copy-done.7
  178.1 1.0 copy-done.13
  179.1 1.7 temporal_end.2.refs_0_
  180.9 1.7 temporal_end.3
  (59 shorter events, 1.7 us)
Async XLA Ops:
  6.5 57.8 %all-gather.4.cloned.1.call-start = ((), (), s32[]{:S(2)}) async-start(), calls=%async_computation.4 | async-start | bytes 3981312 | tf_op jit(solution)/shard_map/all_gather | solution.py:238
  31.6 8.2 %copy-start.14 = (f32[4,72]{1,0:T(4,128)S(1)}, f32[4,72]{1,0:T(4,128)}, u32[]{:S(2)}) copy-start(f32[4,72]{1,0:T(4,128)} %param.13) | copy-start | bytes 3460
  31.6 32.7 %copy-start.5 = (f32[6,1152]{1,0:T(8,128)S(1)}, f32[6,1152]{1,0:T(8,128)}, u32[]{:S(2)}) copy-start(f32[6,1152]{1,0:T(8,128)} %mod_ref.9) | copy-start | bytes 82948
  33.0 25.3 %all-to-all-start.1 = ((bf16[8,144,768]{2,1,0:T(8,128)(2,1)}), bf16[8,144,768]{2,1,0:T(8,128)(2,1)S(1)}, u32[]{:S(2)}, u32[]{:S(2)}) async-start(bf16[8,144,768]{2,1,0:T(8,128)(2,1)} %broadcast_in_dim.8), calls=%async_computation.1 | async-start | bytes 3538944 | tf_op jit(solution)/shard_map/all_to_all | solution.py:236
  39.8 76.0 %all-gather.6.cloned.1.call-start = ((), (), s32[]{:S(2)}) async-start(), calls=%async_computation.5 | async-start | bytes 2985984 | tf_op jit(solution)/shard_map/all_gather | solution.py:265
  40.0 31.9 %copy-start.8 = (f32[4,72]{0,1:T(8,128)}, f32[4,72]{0,1:T(8,128)S(1)}, u32[]{:S(2)}) copy-start(f32[4,72]{0,1:T(8,128)S(1)} %copy.18) | copy-start | bytes 3460
  72.0 89.3 %all-gather.8.cloned.1.call-start = ((), (), s32[]{:S(2)}) async-start(), calls=%async_computation.6 | async-start | bytes 2322432 | tf_op jit(solution)/shard_map/all_gather | solution.py:266
  94.0 14.4 %collective-permute-start.1 = (bf16[2,144,768]{2,1,0:T(8,128)(2,1)S(1)}, bf16[2,144,768]{2,1,0:T(8,128)(2,1)S(1)}, u32[]{:S(2)}, u32[]{:S(2)}) collective-permute-start(bf16[2,144,768]{2,1,0:T(8,128)(2,1)S(1)} %slice.13), channel_id=1, source_target_pairs={{0,32},{32,0},{1,33},{33,1},{2,34},{34,2},{3,35},{35,3},{4,36},{36... | collective-permute-start | bytes 1327112 | tf_op jit(solution)/shard_map/ppermute | solution.py:269
  96.8 16.1 %collective-permute-start = (bf16[1,144,768]{2,1,0:T(8,128)(2,1)S(1)}, bf16[1,144,768]{2,1,0:T(8,128)(2,1)S(1)}, u32[]{:S(2)}, u32[]{:S(2)}) collective-permute-start(bf16[1,144,768]{2,1,0:T(8,128)(2,1)S(1)} %get-tuple-element.50), channel_id=1, source_target_pairs={{0,32},{32,0},{1,33},{33,1},{2,34},{34,2},{3,35},{35,3},{4,36},{36... | collective-permute-start | bytes 663560 | tf_op jit(solution)/shard_map/ppermute | solution.py:269
  97.2 18.7 %collective-permute-start.2 = (bf16[1,144,768]{2,1,0:T(8,128)(2,1)S(1)}, bf16[1,144,768]{2,1,0:T(8,128)(2,1)S(1)}, u32[]{:S(2)}, u32[]{:S(2)}) collective-permute-start(bf16[1,144,768]{2,1,0:T(8,128)(2,1)S(1)} %get-tuple-element.49), channel_id=1, source_target_pairs={{0,32},{32,0},{1,33},{33,1},{2,34},{34,2},{3,35},{35,3},{4,36},{36... | collective-permute-start | bytes 663560 | tf_op jit(solution)/shard_map/ppermute | solution.py:269
  115.9 12.3 %collective-permute-start.3 = (bf16[1152,1152]{1,0:T(8,128)(2,1)}, bf16[1152,1152]{1,0:T(8,128)(2,1)}, u32[]{:S(2)}, u32[]{:S(2)}) collective-permute-start(bf16[1152,1152]{1,0:T(8,128)(2,1)} %all-gather.6.cloned.1.call-done), channel_id=1, source_target_pairs={{0,64},{64,0},{1,65},{65,1},{2,66},{66,2},{3,67},{67,3},{4,68},{68... | collective-permute-start | bytes 7962632 | tf_op jit(solution)/shard_map/ppermute | solution.py:275
  121.9 0.8 copy-start.4
  122.7 23.7 %all-to-all-start.3 = ((bf16[32,56,128]{2,1,0:T(8,128)(2,1)}), bf16[32,56,128]{2,1,0:T(8,128)(2,1)S(1)}, u32[]{:S(2)}, u32[]{:S(2)}) async-start(bf16[32,56,128]{2,1,0:T(8,128)(2,1)} %bitcast.23), calls=%async_computation.3 | async-start | bytes 917504 | tf_op jit(solution)/shard_map/all_to_all | solution.py:277
  128.1 18.3 %copy-start.3 = (bf16[2,1,96,1152]{3,2,1,0:T(8,128)(2,1)S(1)}, bf16[2,1,96,1152]{3,2,1,0:T(8,128)(2,1)}, u32[]{:S(2)}) copy-start(bf16[2,1,96,1152]{3,2,1,0:T(8,128)(2,1)} %param.7) | copy-start | bytes 1327108
  146.4 1.8 copy-start
  148.2 0.8 copy-start.6
  150.9 0.8 copy-start.12
  151.7 6.0 %collective-permute-start.7 = (bf16[96,1152]{1,0:T(8,128)(2,1)}, bf16[96,1152]{1,0:T(8,128)(2,1)}, u32[]{:S(2)}, u32[]{:S(2)}) collective-permute-start(bf16[96,1152]{1,0:T(8,128)(2,1)} %get-tuple-element.32.n0), channel_id=1, source_target_pairs={{0,128},{128,0},{1,129},{129,1},{2,130},{130,2},{3,131},{131,3},{4... | collective-permute-start | bytes 663560 | tf_op jit(solution)/shard_map/ppermute | solution.py:289
  152.4 8.8 %collective-permute-start.6 = (bf16[96,1152]{1,0:T(8,128)(2,1)}, bf16[96,1152]{1,0:T(8,128)(2,1)}, u32[]{:S(2)}, u32[]{:S(2)}) collective-permute-start(bf16[96,1152]{1,0:T(8,128)(2,1)} %get-tuple-element.32.n0), channel_id=1, source_target_pairs={{0,64},{64,0},{1,65},{65,1},{2,66},{66,2},{3,67},{67,3},{4,68},{68... | collective-permute-start | bytes 663560 | tf_op jit(solution)/shard_map/ppermute | solution.py:294
  156.9 0.8 copy-start.10
  157.6 3.7 %collective-permute-start.8 = (bf16[96,1152]{1,0:T(8,128)(2,1)}, bf16[96,1152]{1,0:T(8,128)(2,1)S(1)}, u32[]{:S(2)}, u32[]{:S(2)}) collective-permute-start(bf16[96,1152]{1,0:T(8,128)(2,1)} %collective-permute-done.7.n2), channel_id=1, source_target_pairs={{0,64},{64,0},{1,65},{65,1},{2,66},{66,2},{3,67},{67,3},{4,68},{68... | collective-permute-start | bytes 663560 | tf_op jit(solution)/shard_map/ppermute | solution.py:294
  160.1 7.3 %collective-permute-start.5 = (bf16[96,1152]{1,0:T(8,128)(2,1)}, bf16[96,1152]{1,0:T(8,128)(2,1)S(1)}, u32[]{:S(2)}, u32[]{:S(2)}) collective-permute-start(bf16[96,1152]{1,0:T(8,128)(2,1)} %get-tuple-element.31.n0), channel_id=1, source_target_pairs={{0,128},{128,0},{1,129},{129,1},{2,130},{130,2},{3,131},{131,3},{4... | collective-permute-start | bytes 663560 | tf_op jit(solution)/shard_map/ppermute | solution.py:289
  160.9 11.1 %collective-permute-start.4 = (bf16[96,1152]{1,0:T(8,128)(2,1)}, bf16[96,1152]{1,0:T(8,128)(2,1)S(1)}, u32[]{:S(2)}, u32[]{:S(2)}) collective-permute-start(bf16[96,1152]{1,0:T(8,128)(2,1)} %get-tuple-element.31.n0), channel_id=1, source_target_pairs={{0,64},{64,0},{1,65},{65,1},{2,66},{66,2},{3,67},{67,3},{4,68},{68... | collective-permute-start | bytes 663560 | tf_op jit(solution)/shard_map/ppermute | solution.py:294
  161.4 1.6 copy-start.1
  163.0 0.8 copy-start.9
  163.7 8.3 %copy-start.2 = (bf16[896,1152]{1,0:T(8,128)(2,1)S(1)}, bf16[896,1152]{1,0:T(8,128)(2,1)}, u32[]{:S(2)}) copy-start(bf16[896,1152]{1,0:T(8,128)(2,1)} %all-gather.8.cloned.1.call-done.weight) | copy-start | bytes 6193156
  167.3 4.7 %collective-permute-start.9 = (bf16[96,1152]{1,0:T(8,128)(2,1)S(1)}, bf16[96,1152]{1,0:T(8,128)(2,1)S(1)}, u32[]{:S(2)}, u32[]{:S(2)}) collective-permute-start(bf16[96,1152]{1,0:T(8,128)(2,1)S(1)} %collective-permute-done.5.n2), channel_id=1, source_target_pairs={{0,64},{64,0},{1,65},{65,1},{2,66},{66,2},{3,67},{67,3},{4,68},{68... | collective-permute-start | bytes 663560 | tf_op jit(solution)/shard_map/ppermute | solution.py:294
  169.9 6.4 %collective-permute-start.13 = (bf16[216,128]{1,0:T(8,128)(2,1)S(1)}, bf16[216,128]{1,0:T(8,128)(2,1)S(1)}, u32[]{:S(2)}, u32[]{:S(2)}) collective-permute-start(bf16[216,128]{1,0:T(8,128)(2,1)S(1)} %get-tuple-element.43), channel_id=1, source_target_pairs={{0,64},{64,0},{1,65},{65,1},{2,66},{66,2},{3,67},{67,3},{4,68},{68... | collective-permute-start | bytes 165896 | tf_op jit(solution)/shard_map/ppermute | solution.py:300
  170.0 7.4 %collective-permute-start.14 = (bf16[216,128]{1,0:T(8,128)(2,1)S(1)}, bf16[216,128]{1,0:T(8,128)(2,1)S(1)}, u32[]{:S(2)}, u32[]{:S(2)}) collective-permute-start(bf16[216,128]{1,0:T(8,128)(2,1)S(1)} %get-tuple-element.44), channel_id=1, source_target_pairs={{0,128},{128,0},{1,129},{129,1},{2,130},{130,2},{3,131},{131,3},{4... | collective-permute-start | bytes 165896 | tf_op jit(solution)/shard_map/ppermute | solution.py:301
  171.0 9.9 %copy-start.11 = (f32[96,1152]{1,0:T(8,128)S(1)}, f32[96,1152]{1,0:T(8,128)}, u32[]{:S(2)}) copy-start(f32[96,1152]{1,0:T(8,128)} %copy-done.10) | copy-start | bytes 1327108
  171.0 6.4 %collective-permute-start.15 = (bf16[216,128]{1,0:T(8,128)(2,1)S(1)}, bf16[216,128]{1,0:T(8,128)(2,1)S(1)}, u32[]{:S(2)}, u32[]{:S(2)}) collective-permute-start(bf16[216,128]{1,0:T(8,128)(2,1)S(1)} %get-tuple-element.45), channel_id=1, source_target_pairs={{0,192},{192,0},{64,128},{128,64},{1,193},{193,1},{65,129},{129,65... | collective-permute-start | bytes 165896 | tf_op jit(solution)/shard_map/ppermute | solution.py:302
  175.1 5.8 %collective-permute-start.10 = (bf16[216,128]{1,0:T(8,128)(2,1)S(1)}, bf16[216,128]{1,0:T(8,128)(2,1)S(1)}, u32[]{:S(2)}, u32[]{:S(2)}) collective-permute-start(bf16[216,128]{1,0:T(8,128)(2,1)S(1)} %get-tuple-element.38), channel_id=1, source_target_pairs={{0,64},{64,0},{1,65},{65,1},{2,66},{66,2},{3,67},{67,3},{4,68},{68... | collective-permute-start | bytes 165896 | tf_op jit(solution)/shard_map/ppermute | solution.py:300
  175.2 5.7 %collective-permute-start.11 = (bf16[216,128]{1,0:T(8,128)(2,1)S(1)}, bf16[216,128]{1,0:T(8,128)(2,1)S(1)}, u32[]{:S(2)}, u32[]{:S(2)}) collective-permute-start(bf16[216,128]{1,0:T(8,128)(2,1)S(1)} %get-tuple-element.39), channel_id=1, source_target_pairs={{0,128},{128,0},{1,129},{129,1},{2,130},{130,2},{3,131},{131,3},{4... | collective-permute-start | bytes 165896 | tf_op jit(solution)/shard_map/ppermute | solution.py:301
  176.3 4.6 %collective-permute-start.12 = (bf16[216,128]{1,0:T(8,128)(2,1)S(1)}, bf16[216,128]{1,0:T(8,128)(2,1)S(1)}, u32[]{:S(2)}, u32[]{:S(2)}) collective-permute-start(bf16[216,128]{1,0:T(8,128)(2,1)S(1)} %get-tuple-element.40), channel_id=1, source_target_pairs={{0,192},{192,0},{64,128},{128,64},{1,193},{193,1},{65,129},{129,65... | collective-permute-start | bytes 165896 | tf_op jit(solution)/shard_map/ppermute | solution.py:302
  177.4 0.8 copy-start.7
  178.1 1.0 copy-start.13
Sparse Core Ops, SparseCore 0:
  9.1 55.1 all-gather.3
  72.1 38.3 all-gather.5
  118.5 42.2 all-gather.7

commit v6 on v4

--- a/solution.py
+++ b/solution.py
@@ -19,10 +19,10 @@
 PLANE = NZ * PATCH
 BF = jnp.bfloat16
 F32 = jnp.float32
-PIECES = (slice(0, 2), slice(2, 3), slice(3, 4))
 FACTOR = 1.0 / math.sqrt(HD)
 TN = (((0,), (0,)), ((), ()))
 NT = (((1,), (1,)), ((), ()))
+SMEM = pl.BlockSpec(memory_space=pltpu.SMEM)
 PARAMS = pltpu.CompilerParams(vmem_limit_bytes=48 * 1024 * 1024)
 
 
@@ -38,7 +38,7 @@
     return values * lax.rsqrt(mean_sq + 1e-06) * gain
 
 
-def spatial_proj(tok_ref, mod_ref, w_ref, gain_ref, out_ref, turned):
+def spatial_proj(y_ref, tok_ref, mod_ref, w_ref, gain_ref, s0, s1, s2, s3, turned):
     cols = 4 * PATCH
     zeros = jnp.zeros((HP - HD, cols), F32)
 
@@ -63,7 +63,13 @@
             key = rms(key, gain_ref[:, 1:2])
             place = clip * 2 + head
             parts = [key, value, query, zeros]
-            out_ref[place] = jnp.concatenate(parts, 0).astype(BF)
+            block = jnp.concatenate(parts, 0).astype(BF)
+            slot = (place + NY - y_ref[0]) % NY
+            for n, out_ref in enumerate((s0, s1, s2, s3)):
+
+                @pl.when(slot == n)
+                def _(out_ref=out_ref, block=block):
+                    out_ref[0] = block
 
 
 def pack(block, rows):
@@ -79,32 +85,39 @@
     return jnp.concatenate([packed[:, :PATCH], jnp.concatenate(strips, 1)], 0)
 
 
-def attend(steps, resume, finish, *refs):
-    q_ref, kv_ref = refs[:2]
-    out_ref, keys, values = refs[-3:]
-
-    @pl.when(pl.program_id(0) == 0)
+def attend(count, resume, finish, y_ref, *refs):
+    q_refs, kv_refs = refs[:NY], refs[NY : NY + count]
+    out_ref, query, keys, values = refs[-4:]
+    place = pl.program_id(0)
+
+    @pl.when(place == 0)
     def _():
         gap = jnp.zeros((128 - HD, PLANE), F32)
         first = lax.broadcasted_iota(jnp.int32, (HP - HD, PLANE), 0) == 0
         ones = jnp.where(first, 1.0, 0.0)
-        for n in range(steps):
-            both = kv_ref[n, : 2 * HD].astype(F32)
+        for n, kv_ref in enumerate(kv_refs):
+            both = kv_ref[0, : 2 * HD].astype(F32)
             keys[n] = jnp.concatenate([both[:HD], gap], 0).T.astype(BF)
             values[n] = jnp.concatenate([both[HD:], ones], 0).astype(BF)
-
-    query = jnp.concatenate([q_ref[0, 2 * HD :], jnp.zeros((128 - HP, PLANE), BF)], 0)
-    parts = [(n, slice(p, p + 256)) for n in range(steps) for p in range(0, PLANE, 256)]
+        query[HP:] = jnp.zeros((128 - HP, PLANE), BF)
+
+    for n, q_ref in enumerate(q_refs):
+
+        @pl.when(place == n)
+        def _(q_ref=q_ref):
+            query[:HP] = q_ref[0, 2 * HD :]
+
+    parts = [(n, slice(p, p + 256)) for n in range(count) for p in range(0, PLANE, 256)]
 
     def scores(n, here):
-        return jnp.dot(keys[n, here, :], query, preferred_element_type=F32)
-
-    done = refs[2][0] if resume else None
+        return jnp.dot(keys[n, here, :], query[...], preferred_element_type=F32)
+
+    done = refs[NY + count][0] if resume else None
     ahead = scores(*parts[0])
-    for place, (n, here) in enumerate(parts):
+    for index, (n, here) in enumerate(parts):
         score = ahead
-        if place + 1 < len(parts):
-            ahead = scores(*parts[place + 1])
+        if index + 1 < len(parts):
+            ahead = scores(*parts[index + 1])
         expo = jnp.exp2(score).astype(BF)
         add = jnp.dot(values[n, :, here], expo, preferred_element_type=F32)
         done = add if done is None else done + add
@@ -112,35 +125,37 @@
         out_ref[0] = done
         return
     done = done[:HD] / done[HD : HD + 1]
+    home = (y_ref[0] + NY - place) % NY
     for z in range(NZ):
-        out_ref[0, z] = pack(done[:, z * PATCH : (z + 1) * PATCH], 56).astype(BF)
-
-
-def attention(query, key_value, part, finish):
-    steps = key_value.shape[0]
+        out_ref[home, z] = pack(done[:, z * PATCH : (z + 1) * PATCH], 56).astype(BF)
+
+
+def attention(y_place, queries, key_values, part, finish):
+    count = len(key_values)
     sums = pl.BlockSpec((1, HP, PLANE), lambda q: (q, 0, 0))
-    in_specs = [
-        pl.BlockSpec((1, 3 * HD + 8, PLANE), lambda q: (q, 0, 0)),
-        pl.BlockSpec((steps,) + key_value.shape[1:], lambda q: (0, 0, 0)),
-    ]
-    args = [query, key_value]
+    args = [y_place, *queries, *key_values]
+    in_specs = [SMEM] + [pl.BlockSpec(a.shape, lambda q: (0, 0, 0)) for a in args[1:]]
     if part is not None:
         in_specs.append(sums)
         args.append(part)
     if finish:
-        out_spec = pl.BlockSpec((1, NZ, 56, 128), lambda q: (q, 0, 0, 0))
+        out_spec = pl.BlockSpec((NY, NZ, 56, 128), lambda q: (0, 0, 0, 0))
         out_shape = shape(BF, NY, NZ, 56, 128)
     else:
         out_spec = sums
         out_shape = shape(F32, NY, HP, PLANE)
-    pairs = steps * NY * PLANE * PLANE
+    pairs = count * NY * PLANE * PLANE
     return pl.pallas_call(
-        functools.partial(attend, steps, part is not None, finish),
+        functools.partial(attend, count, part is not None, finish),
         grid=(NY,),
         in_specs=in_specs,
         out_specs=out_spec,
         out_shape=out_shape,
-        scratch_shapes=[pltpu.VMEM((steps, PLANE, 128), BF), pltpu.VMEM((steps, HP, PLANE), BF)],
+        scratch_shapes=[
+            pltpu.VMEM((128, PLANE), BF),
+            pltpu.VMEM((count, PLANE, 128), BF),
+            pltpu.VMEM((count, HP, PLANE), BF),
+        ],
         compiler_params=PARAMS,
         cost_estimate=pl.CostEstimate(
             flops=4 * pairs, bytes_accessed=1_000_000, transcendentals=0
@@ -149,22 +164,20 @@
     )(*args)
 
 
-def prepare(place_ref, own, got, out_a, out_b, turned):
-    second = place_ref[0] == 1
+def prepare(rest, own, turned):
     for n in range(5):
         width = min(256, D - n * 256)
-        here = slice(n * 256, n * 256 + width)
-        out_a[:, here] = jnp.where(second, got[n, :, :width], own[n, :, :width])
-        out_b[:, here] = jnp.where(second, own[n, :, :width], got[n, :, :width])
-    turned[:128] = own[4, :, 128:].astype(F32).T.astype(BF)
+        own[:, n * 256 : n * 256 + width] = rest[n, :, :width]
+    turned[:128] = rest[4, :, 128:].astype(F32).T.astype(BF)
     for n in range(3):
-        turned[128 + n * 256 : 384 + n * 256] = own[5 + n].astype(F32).T.astype(BF)
-
-
-def spatial_end(att_ref, tok_ref, mod_ref, weight, resid_ref, norm_ref):
+        turned[128 + n * 256 : 384 + n * 256] = rest[5 + n].astype(F32).T.astype(BF)
+
+
+def spatial_end(place_ref, att_ref, tok_ref, mod_ref, own, got, resid_ref, norm_ref):
     feats = [unpack(att_ref[n % 2, n // 2].astype(F32), 16) for n in range(HEADS)]
     attended = jnp.concatenate(feats, 0).T.astype(BF)
-    branch = jnp.dot(attended, weight[...], preferred_element_type=F32)
+    weight = jnp.where(place_ref[0] == 1, got[...], own[...])
+    branch = jnp.dot(attended, weight, preferred_element_type=F32)
     resid = tok_ref[...].astype(F32) + mod_ref[2:3, :] * branch
     resid_ref[...] = resid
     norm_ref[...] = (normalise(resid) * (1.0 + mod_ref[4:5, :]) + mod_ref[3:4, :]).astype(BF)
@@ -194,17 +207,15 @@
         out_ref[...] = pack(jnp.concatenate(mixed, 0)[:, :PATCH], 3 * HD).astype(BF)
 
 
-def temporal_end(place_ref, m0, m1, m2, m3, resid_ref, mod_ref, weight, *out_refs):
-    branch = None
+def temporal_end(place_ref, m0, m1, m2, m3, resid_ref, mod_ref, own, got, *out_refs):
+    second, branch = place_ref[0] == 1, None
     for step, att_ref in enumerate((m0, m1, m2, m3)):
         feats = unpack(att_ref[...].astype(F32), HD)
         here = pl.ds(pl.multiple_of((place_ref[1] ^ step) * (4 * HD), 4 * HD), 4 * HD)
-        add = jnp.dot(feats.T.astype(BF), weight[here, :], preferred_element_type=F32)
+        rows = jnp.where(second, own[here, :], got[here, :])
+        add = jnp.dot(feats.T.astype(BF), rows, preferred_element_type=F32)
         branch = add if branch is None else branch + add
     out_refs[-1][...] = (resid_ref[...] + mod_ref[5:6, :] * branch).astype(BF)
-
-
-SMEM = pl.BlockSpec(memory_space=pltpu.SMEM)
 
 
 def full(array, lead=None, n=0):
@@ -256,45 +267,44 @@
     rest, column = lax.optimization_barrier((shard[:, 512:], column))
     rest = lax.all_gather(rest, "z", axis=0)
 
-    projected = pl.pallas_call(
+    y_place = lax.axis_index("y").astype(jnp.int32).reshape(1)
+    slots = pl.pallas_call(
         spatial_proj,
         grid=(2,),
         in_specs=[
+            SMEM,
             pl.BlockSpec((4, ROWS, D), lambda i: (i, 0, 0)),
             pl.BlockSpec((6, D), lambda i: (0, 0)),
             pl.BlockSpec((D, 512), lambda i: (0, 0)),
             pl.BlockSpec((HD, 4), lambda i: (0, 0)),
         ],
-        out_specs=pl.BlockSpec((4, 3 * HD + 8, 4 * PATCH), lambda i: (0, 0, i)),
-        out_shape=shape(BF, 4, 3 * HD + 8, PLANE),
+        out_specs=[pl.BlockSpec((1, 3 * HD + 8, 4 * PATCH), lambda i: (0, 0, i))] * NY,
+        out_shape=[shape(BF, 1, 3 * HD + 8, PLANE)] * NY,
         scratch_shapes=[pltpu.VMEM((512, D), BF)],
         compiler_params=PARAMS,
         name="spatial_proj",
-    )(column, modulation, shard, gains)
+    )(y_place, column, modulation, shard, gains)
 
     swap = [(0, 1), (1, 0)]
-    projected = lax.all_to_all(projected, "y", 0, 0, tiled=True)
-    others = [lax.ppermute(projected[n, : 2 * HD], "xh", swap) for n in PIECES]
-    part = attention(projected, projected, None, False)
-    part = attention(projected, others[0], part, False)
-    part = attention(projected, others[1], part, False)
-    attended = attention(projected, others[2], part, True)
-    attended, rest = lax.optimization_barrier((attended, rest))
-    rest_got = lax.ppermute(rest, "c", swap)
+    blocks = list(slots)
+    for n in (1, 3, 2):
+        blocks[n] = lax.ppermute(slots[n], "y", [(i, (i + n) % NY) for i in range(NY)])
+    others = [lax.ppermute(block[:, : 2 * HD], "xh", swap) for block in blocks]
+    part = attention(y_place, blocks, blocks, None, False)
+    part = attention(y_place, blocks, [others[n] for n in (0, 1, 3)], part, False)
+    attended = attention(y_place, blocks, [others[2]], part, True)
     attended = attended.reshape(NY * NZ, 56, 128)
     attended = lax.all_to_all(attended, ("y", "z"), 0, 0, tiled=True)
     attended = attended.reshape(4, NZ, 56, 128)
-    out_a, out_b, turned = once(
-        prepare,
-        [place, rest, rest_got],
-        [SMEM, full(rest), full(rest, 5)],
-        [shape(BF, D, D), shape(BF, D, D), shape(BF, 896, D)],
-    )
+    own, turned = once(prepare, [rest], [full(rest)], [shape(BF, D, D), shape(BF, 896, D)])
+    swapped, _ = lax.optimization_barrier((own, attended))
+    got = lax.ppermute(swapped, "c", swap)
 
     steps = []
     for clip in range(2):
-        args = [attended, tok, modulation, out_a]
-        specs = [full(attended, 2, clip), full(tok, PATCH, clip), full(modulation), full(out_a)]
+        args = [place, attended, tok, modulation, own, got]
+        specs = [SMEM, full(attended, 2, clip), full(tok, PATCH, clip)]
+        specs += [full(a) for a in args[3:]]
         steps.append(once(spatial_end, args, specs, [shape(F32, PATCH, D), shape(BF, PATCH, D)]))
     diagonal = [(0, 3), (3, 0), (1, 2), (2, 1)]
     sent = []
@@ -316,7 +326,7 @@
         )
     result = None
     for clip in range(2):
-        args = sent[clip] + [steps[clip][0], modulation, out_b]
+        args = sent[clip] + [steps[clip][0], modulation, own, got]
         specs = [SMEM] + [full(a) for a in args]
         aliases = None
         if result is not None:

time: 185 us -> 183 us (0.989)
  blocking collectives: 68.4 us -> 46.5 us
  waiting for transfers between devices: 22.2 us -> 35.2 us
  starting transfers between devices: 27.8 us -> 33.8 us
    all_to_all x1 -> x0, blocking collectives: 21.9 us -> none  [per_device(): projected = lax.all_to_all(projected, 'y', 0, 0, tiled=True)]
    ppermute x4 -> x8, waiting for transfers between devices: 0.74 us -> 13.2 us  [the longest x3 8.47 us: per_device(): lax.ppermute(slots[n], 'y', [(i, (i + n) % NY) for i in range(NY)])]
    ppermute x4 -> x8, starting transfers between devices: 6.57 us -> 18.7 us  [the longest x4 9.11 us: per_device(): others = [lax.ppermute(block[:, :2 * HD], 'xh', swap) for block in blocks]]
    all_to_all x1, waiting for transfers between devices: 4.14 us -> 0.01 us  [per_device(): attended = lax.all_to_all(attended, ('y', 'z'), 0, 0, tiled=True)]
    all_gather x1, waiting for transfers between devices: 6.31 us -> 9.07 us  [per_device(): rest = lax.all_gather(rest, 'z', axis=0)]
    ppermute x2, starting transfers between devices: 4.28 us -> 1.99 us  [per_device(): lax.ppermute(norm_x, 'c', swap)]
    ppermute x2, starting transfers between devices: 3.07 us -> 0.94 us  [per_device(): lax.ppermute(norm, 'c', swap)]
    ppermute x2, waiting for transfers between devices: 3.43 us -> 5.44 us  [per_device(): moved = [lax.ppermute(norm, 'xl', swap) for _, norm in steps]]
  transfers between devices with their start and end apart: 19 -> 23, of which waited for: 6 -> 8; matrix products, arithmetic and copies ran while one was open for 3% -> 3% of each run, Pallas kernels for 21% -> 21%
where the time goes in v6:
time: 183 us; the launch traced here: 182 us
  blocking collectives  46.5 us (25%)
  Pallas kernels  43.4 us (24%)
  waiting for transfers between devices  35.2 us (19%)
  starting transfers between devices  33.8 us (18%)
  between operations  13.7 us (7%)
  local copies, waits for them, and re-layouts  8.8 us (5%)
    all_to_all x1, blocking collectives, per_device(): shard = lax.all_to_all(shard, ('xh', 'y'), 0, 0, tiled=True).reshape(D, 768)  26.6 us
    all_to_all x1, blocking collectives, per_device(): lax.all_to_all(shard, 'z', 0, 0, tiled=True).reshape(1, NZ * 18, 768)  19.9 us
    pallas_call x3, Pallas kernels, attention(): pl.pallas_call(functools.partial(attend, count, part is not None, finish)...  19.5 us
    pallas_call x7, Pallas kernels, once(): pl.pallas_call(kernel, grid=(1,), in_specs=specs, out_specs=out_specs or...  17.5 us
    ppermute x4, starting transfers between devices, per_device(): others = [lax.ppermute(block[:, :2 * HD], 'xh', swap) for block in blocks]  9.11 us
    all_gather x1, waiting for transfers between devices, per_device(): rest = lax.all_gather(rest, 'z', axis=0)  9.07 us
    ppermute x3, waiting for transfers between devices, per_device(): lax.ppermute(slots[n], 'y', [(i, (i + n) % NY) for i in range(NY)])  8.47 us
    pallas_call x1, Pallas kernels, per_device(): pl.pallas_call(spatial_proj, grid=(2,), in_specs=[SMEM, pl.BlockSpec((4,...  6.5 us
  transfers between devices with their start and end apart: 23, of which 8 were waited for; matrix products, arithmetic and copies ran while one was open for 3% of the time, Pallas kernels for 21%

profile of v6, /device:TPU:1, one launch (start us, length us, event | category | flops | bytes accessed | tf_op | source)
XLA Modules:
  0.0 182.4 jit_solution(10671623824587631138)
XLA Ops:
  6.5 0.7 all-gather.4.cloned.1.call-update
  7.3 1.0 reshape.38
  8.5 0.8 broadcast_select_fusion
  9.4 1.2 reshape.36
  10.8 0.2 reshape.37
  11.0 19.9 %all_to_all.15 = bf16[8,18,768]{2,1,0:T(8,128)(2,1)S(1)} all-to-all(bf16[8,18,768]{2,1,0:T(8,128)(2,1)S(1)} %copy.17), channel_id=1, replica_groups=mesh['xl'=2,'c'=2,'xh'=2,'y'=4,'z'=8] {'z'}, dimensions={0} | all-to-all | bytes 442368 | tf_op jit(solution)/shard_map/all_to_all | solution.py:261
  31.2 26.6 %all_to_all.16 = bf16[8,144,768]{2,1,0:T(8,128)(2,1)S(1)} all-to-all(bf16[8,144,768]{2,1,0:T(8,128)(2,1)S(1)} %broadcast_in_dim.8), channel_id=1, replica_groups=mesh['xl'=2,'c'=2,'xh'=2,'y'=4,'z'=8] {'xh','y'}, dimensions={0} | all-to-all | bytes 3538944 | tf_op jit(solution)/shard_map/all_to_all | solution.py:263
  57.8 0.9 slice.20
  58.7 5.4 %all-gather.4.cloned.1.call-done.tok_ref = bf16[8,192,1152]{2,1,0:T(8,128)(2,1)} async-done(((bf16[1,192,1152]{2,1,0:T(8,128)(2,1)}), bf16[8,192,1152]{2,1,0:T(8,128)(2,1)}) %all-gather.4.cloned.1.call-update) | async-done | bytes 3538960 | tf_op jit(solution)/shard_map/all_gather | solution.py:265
  64.2 6.5 %spatial_proj.1 = (bf16[1,224,768]{2,1,0:T(8,128)(2,1)S(1)}, bf16[1,224,768]{2,1,0:T(8,128)(2,1)S(1)}, bf16[1,224,768]{2,1,0:T(8,128)(2,1)S(1)}, bf16[1,224,768]{2,1,0:T(8,128)(2,1)S(1)}) custom-call(s32[1]{0:T(128)} %bitcast.2.y_ref, bf16[8,192,1152]{2,1,0:T(8,128)(2,1)} %all-gather.4.cloned.1.call-done.tok_ref, f32[6,1152]{1,0:T(8,128)S(1)} %copy-done.1, ...), custom_call_target="tpu_custom_call" | custom-call | tf_op jit(solution)/shard_map/spatial_proj/pallas_call | solution.py:271
  70.7 1.4 collective-permute-start
  72.1 1.5 collective-permute-start.2
  73.6 1.6 collective-permute-start.1
  75.2 2.8 %collective-permute-start.4 = (bf16[1,144,768]{2,1,0:T(8,128)(2,1)S(1)}, bf16[1,144,768]{2,1,0:T(8,128)(2,1)S(1)}, u32[]{:S(2)}, u32[]{:S(2)}) collective-permute-start(bf16[1,144,768]{2,1,0:T(8,128)(2,1)S(1)} %slice.17), channel_id=1, source_target_pairs={{0,32},{32,0},{1,33},{33,1},{2,34},{34,2},{3,35},{35,3},{4,36},{36... | collective-permute-start | bytes 663560 | tf_op jit(solution)/shard_map/ppermute | solution.py:292
  78.0 3.1 %collective-permute-done.refs_1_.refs_5_ = bf16[1,224,768]{2,1,0:T(8,128)(2,1)S(1)} collective-permute-done((bf16[1,224,768]{2,1,0:T(8,128)(2,1)S(1)}, bf16[1,224,768]{2,1,0:T(8,128)(2,1)S(1)}, u32[]{:S(2)}, u32[]{:S(2)}) %collective-permute-start) | collective-permute-done | bytes 344096 | tf_op jit(solution)/shard_map/ppermute | solution.py:291
  81.1 3.2 %collective-permute-start.5 = (bf16[1,144,768]{2,1,0:T(8,128)(2,1)S(1)}, bf16[1,144,768]{2,1,0:T(8,128)(2,1)S(1)}, u32[]{:S(2)}, u32[]{:S(2)}) collective-permute-start(bf16[1,144,768]{2,1,0:T(8,128)(2,1)S(1)} %slice.22), channel_id=1, source_target_pairs={{0,32},{32,0},{1,33},{33,1},{2,34},{34,2},{3,35},{35,3},{4,36},{36... | collective-permute-start | bytes 663560 | tf_op jit(solution)/shard_map/ppermute | solution.py:292
  84.4 5.4 %collective-permute-done.1.refs_2_.refs_6_ = bf16[1,224,768]{2,1,0:T(8,128)(2,1)S(1)} collective-permute-done((bf16[1,224,768]{2,1,0:T(8,128)(2,1)S(1)}, bf16[1,224,768]{2,1,0:T(8,128)(2,1)S(1)}, u32[]{:S(2)}, u32[]{:S(2)}) %collective-permute-start.1) | collective-permute-done | bytes 344096 | tf_op jit(solution)/shard_map/ppermute | solution.py:291
  89.8 3.0 %collective-permute-start.3 = (bf16[1,144,768]{2,1,0:T(8,128)(2,1)S(1)}, bf16[1,144,768]{2,1,0:T(8,128)(2,1)S(1)}, u32[]{:S(2)}, u32[]{:S(2)}) collective-permute-start(bf16[1,144,768]{2,1,0:T(8,128)(2,1)S(1)} %slice.21), channel_id=1, source_target_pairs={{0,32},{32,0},{1,33},{33,1},{2,34},{34,2},{3,35},{35,3},{4,36},{36... | collective-permute-start | bytes 663560 | tf_op jit(solution)/shard_map/ppermute | solution.py:292
  92.8 8.5 %attend.3.refs_7_ = f32[4,80,768]{2,1,0:T(8,128)S(1)} custom-call(s32[1]{0:T(128)} %bitcast.2.y_ref, bf16[1,224,768]{2,1,0:T(8,128)(2,1)S(1)} %get-tuple-element.30.refs_0_.refs_4_, bf16[1,224,768]{2,1,0:T(8,128)(2,1)S(1)} %collective-permute-done.refs_1_.refs_5_, bf16[1,224,768]{2,1,0:T(8,128)(2,1)S(1)} %collective-permute-done.1.refs_2_.refs_6_, ...), custom_call_target="tpu_custom_call" | custom-call | flops 37748736 | bytes 1000000 | tf_op jit(solution)/shard_map/attend/pallas_call | solution.py:148
  101.4 6.5 %attend.4.refs_5_ = f32[4,80,768]{2,1,0:T(8,128)S(1)} custom-call(s32[1]{0:T(128)} %bitcast.2.y_ref, bf16[1,224,768]{2,1,0:T(8,128)(2,1)S(1)} %get-tuple-element.30.refs_0_.refs_4_, bf16[1,224,768]{2,1,0:T(8,128)(2,1)S(1)} %collective-permute-done.refs_1_.refs_5_, bf16[1,224,768]{2,1,0:T(8,128)(2,1)S(1)} %collective-permute-done.1.refs_2_.refs_6_, ...), custom_call_target="tpu_custom_call" | custom-call | flops 28311552 | bytes 1000000 | tf_op jit(solution)/shard_map/attend/pallas_call | solution.py:148
  107.9 4.4 %attend.5 = bf16[4,8,56,128]{3,2,1,0:T(8,128)(2,1)} custom-call(s32[1]{0:T(128)} %bitcast.2.y_ref, bf16[1,224,768]{2,1,0:T(8,128)(2,1)S(1)} %get-tuple-element.30.refs_0_.refs_4_, bf16[1,224,768]{2,1,0:T(8,128)(2,1)S(1)} %collective-permute-done.refs_1_.refs_5_, bf16[1,224,768]{2,1,0:T(8,128)(2,1)S(1)} %collective-permute-done.1.refs_2_.refs_6_, ...), custom_call_target="tpu_custom_call" | custom-call | flops 9437184 | bytes 1000000 | tf_op jit(solution)/shard_map/attend/pallas_call | solution.py:148
  112.3 5.3 %all-to-all-start.2 = ((bf16[32,56,128]{2,1,0:T(8,128)(2,1)}), bf16[32,56,128]{2,1,0:T(8,128)(2,1)S(1)}, u32[]{:S(2)}, u32[]{:S(2)}) async-start(bf16[32,56,128]{2,1,0:T(8,128)(2,1)} %bitcast.8), calls=%async_computation.2 | async-start | bytes 917504 | tf_op jit(solution)/shard_map/all_to_all | solution.py:297
  117.7 9.1 %all-gather.6.cloned.1.call-done = bf16[9216,256]{1,0:T(8,128)(2,1)} async-done(((bf16[1152,256]{1,0:T(8,128)(2,1)}), bf16[9216,256]{1,0:T(8,128)(2,1)}) %all-gather.6.cloned.1.call-update) | async-done | bytes 4718608 | tf_op jit(solution)/shard_map/all_gather | solution.py:268
  126.7 3.2 %prepare.1 = (bf16[1152,1152]{1,0:T(8,128)(2,1)S(1)}, bf16[896,1152]{1,0:T(8,128)(2,1)S(1)}) custom-call(bf16[8,1152,256]{2,1,0:T(8,128)(2,1)} %bitcast.36), custom_call_target="tpu_custom_call" | custom-call | flops 2000000000 | bytes 8000000 | tf_op jit(solution)/shard_map/prepare/pallas_call | solution.py:228
  129.9 1.5 copy-done.2
  131.4 5.2 %collective-permute-start.7 = (bf16[1152,1152]{1,0:T(8,128)(2,1)}, bf16[1152,1152]{1,0:T(8,128)(2,1)S(1)}, u32[]{:S(2)}, u32[]{:S(2)}) collective-permute-start(bf16[1152,1152]{1,0:T(8,128)(2,1)} %copy-done.2), channel_id=1, source_target_pairs={{0,64},{64,0},{1,65},{65,1},{2,66},{66,2},{3,67},{67,3},{4,68},{68... | collective-permute-start | bytes 7962632 | tf_op jit(solution)/shard_map/ppermute | solution.py:301
  136.7 4.7 %collective-permute-done.7.got = bf16[1152,1152]{1,0:T(8,128)(2,1)S(1)} collective-permute-done((bf16[1152,1152]{1,0:T(8,128)(2,1)}, bf16[1152,1152]{1,0:T(8,128)(2,1)S(1)}, u32[]{:S(2)}, u32[]{:S(2)}) %collective-permute-start.7) | collective-permute-done | bytes 2654240 | tf_op jit(solution)/shard_map/ppermute | solution.py:301
  141.4 1.5 copy-done.5
  142.9 1.7 copy-done.3
  144.7 2.9 %spatial_end.3 = (f32[96,1152]{1,0:T(8,128)S(1)}, bf16[96,1152]{1,0:T(8,128)(2,1)S(1)}) custom-call(s32[2]{0:T(128)S(1)} %pad_add_fusion.place_ref, bf16[4,8,56,128]{3,2,1,0:T(8,128)(2,1)S(1)} %bitcast.25, bf16[192,1152]{1,0:T(8,128)(2,1)S(1)} %bitcast.28, f32[6,1152]{1,0:T(8,128)S(1)} %copy-done.1, bf16[1152,1152]{1,0:T(8,128)(2,1)S(1)} %copy-done.3, ...), custom_call_target="tpu_custom_call" | custom-call | flops 2000000000 | bytes 8000000 | tf_op jit(solution)/shard_map/spatial_end/pallas_call | solution.py:228
  147.5 1.2 collective-permute-start.11
  148.8 0.7 collective-permute-start.10
  149.4 2.9 %spatial_end.2 = (f32[96,1152]{1,0:T(8,128)S(1)}, bf16[96,1152]{1,0:T(8,128)(2,1)S(1)}) custom-call(s32[2]{0:T(128)S(1)} %pad_add_fusion.place_ref, bf16[4,8,56,128]{3,2,1,0:T(8,128)(2,1)S(1)} %bitcast.26, bf16[192,1152]{1,0:T(8,128)(2,1)S(1)} %bitcast.29, f32[6,1152]{1,0:T(8,128)S(1)} %copy-done.1, bf16[1152,1152]{1,0:T(8,128)(2,1)S(1)} %copy-done.3, ...), custom_call_target="tpu_custom_call" | custom-call | flops 2000000000 | bytes 8000000 | tf_op jit(solution)/shard_map/spatial_end/pallas_call | solution.py:228
  152.3 2.0 %collective-permute-done.11.n2 = bf16[96,1152]{1,0:T(8,128)(2,1)S(1)} collective-permute-done((bf16[96,1152]{1,0:T(8,128)(2,1)S(1)}, bf16[96,1152]{1,0:T(8,128)(2,1)S(1)}, u32[]{:S(2)}, u32[]{:S(2)}) %collective-permute-start.11) | collective-permute-done | bytes 221216 | tf_op jit(solution)/shard_map/ppermute | solution.py:311
  154.2 1.2 collective-permute-start.12
  155.4 1.2 collective-permute-start.9
  156.6 0.3 collective-permute-start.8
  156.9 2.1 %temporal.2 = (bf16[216,128]{1,0:T(8,128)(2,1)S(1)}, bf16[216,128]{1,0:T(8,128)(2,1)S(1)}, bf16[216,128]{1,0:T(8,128)(2,1)S(1)}, bf16[216,128]{1,0:T(8,128)(2,1)S(1)}) custom-call(bf16[96,1152]{1,0:T(8,128)(2,1)S(1)} %get-tuple-element.38.n0, bf16[96,1152]{1,0:T(8,128)(2,1)S(1)} %collective-permute-done.10.n1, ...), custom_call_target="tpu_custom_call" | custom-call | flops 2000000000 | bytes 8000000 | tf_op jit(solution)/shard_map/temporal/pallas_call | solution.py:228
  159.0 3.5 %collective-permute-done.9.n2 = bf16[96,1152]{1,0:T(8,128)(2,1)S(1)} collective-permute-done((bf16[96,1152]{1,0:T(8,128)(2,1)S(1)}, bf16[96,1152]{1,0:T(8,128)(2,1)S(1)}, u32[]{:S(2)}, u32[]{:S(2)}) %collective-permute-start.9) | collective-permute-done | bytes 221216 | tf_op jit(solution)/shard_map/ppermute | solution.py:311
  162.5 0.8 collective-permute-start.13
  163.3 1.2 collective-permute-start.18
  164.5 1.0 collective-permute-start.19
  165.4 2.1 %temporal.3 = (bf16[216,128]{1,0:T(8,128)(2,1)S(1)}, bf16[216,128]{1,0:T(8,128)(2,1)S(1)}, bf16[216,128]{1,0:T(8,128)(2,1)S(1)}, bf16[216,128]{1,0:T(8,128)(2,1)S(1)}) custom-call(bf16[96,1152]{1,0:T(8,128)(2,1)S(1)} %get-tuple-element.37.n0, bf16[96,1152]{1,0:T(8,128)(2,1)S(1)} %collective-permute-done.8.n1, ...), custom_call_target="tpu_custom_call" | custom-call | flops 2000000000 | bytes 8000000 | tf_op jit(solution)/shard_map/temporal/pallas_call | solution.py:228
  167.7 1.2 collective-permute-start.15
  168.9 0.9 collective-permute-start.16
  169.9 2.1 %temporal_end.2.out_refs_0_ = bf16[192,1152]{1,0:T(8,128)(2,1)} custom-call(s32[2]{0:T(128)S(1)} %pad_add_fusion.place_ref, bf16[216,128]{1,0:T(8,128)(2,1)S(1)} %get-tuple-element.48.m0, bf16[216,128]{1,0:T(8,128)(2,1)S(1)} %collective-permute-done.17.m1, bf16[216,128]{1,0:T(8,128)(2,1)S(1)} %collective-permute-done.18.m2, ...), custom_call_target="tpu_custom_call" | custom-call | flops 2000000000 | bytes 8000000 | tf_op jit(solution)/shard_map/temporal_end/pallas_call | solution.py:228
  172.0 1.4 collective-permute-done.16.m3
  173.4 2.1 %temporal_end.3 = bf16[192,1152]{1,0:T(8,128)(2,1)} custom-call(s32[2]{0:T(128)S(1)} %pad_add_fusion.place_ref, bf16[216,128]{1,0:T(8,128)(2,1)S(1)} %get-tuple-element.43.m0, bf16[216,128]{1,0:T(8,128)(2,1)S(1)} %collective-permute-done.14.m1, bf16[216,128]{1,0:T(8,128)(2,1)S(1)} %collective-permute-done.15.m2, ...), custom_call_target="tpu_custom_call", output_to_operand_aliasing={{}: (9, {})} | custom-call | flops 2000000000 | bytes 8000000 | tf_op jit(solution)/shard_map/temporal_end/pallas_call | solution.py:228
  (50 shorter events, 1.2 us)
Async XLA Ops:
  6.5 57.5 %all-gather.4.cloned.1.call-start = ((), (), s32[]{:S(2)}) async-start(), calls=%async_computation.3 | async-start | bytes 3981312 | tf_op jit(solution)/shard_map/all_gather | solution.py:265
  7.3 119.5 %all-gather.6.cloned.1.call-start = ((), (), s32[]{:S(2)}) async-start(), calls=%async_computation.4 | async-start | bytes 5308416 | tf_op jit(solution)/shard_map/all_gather | solution.py:268
  31.1 32.9 %copy-start.7 = (f32[4,72]{1,0:T(4,128)S(1)}, f32[4,72]{1,0:T(4,128)}, u32[]{:S(2)}) copy-start(f32[4,72]{1,0:T(4,128)} %param.13) | copy-start | bytes 3460
  31.2 33.0 %copy-start.1 = (f32[6,1152]{1,0:T(8,128)S(1)}, f32[6,1152]{1,0:T(8,128)}, u32[]{:S(2)}) copy-start(f32[6,1152]{1,0:T(8,128)} %mod_ref.9) | copy-start | bytes 82948
  70.7 10.4 %collective-permute-start = (bf16[1,224,768]{2,1,0:T(8,128)(2,1)S(1)}, bf16[1,224,768]{2,1,0:T(8,128)(2,1)S(1)}, u32[]{:S(2)}, u32[]{:S(2)}) collective-permute-start(bf16[1,224,768]{2,1,0:T(8,128)(2,1)S(1)} %get-tuple-element.31), channel_id=1, source_target_pairs={{0,8},{8,16},{16,24},{24,0},{1,9},{9,17},{17,25},{25,1},{2,10},{10... | collective-permute-start | bytes 1032200 | tf_op jit(solution)/shard_map/ppermute | solution.py:291
  72.1 12.2 %collective-permute-start.2 = (bf16[1,224,768]{2,1,0:T(8,128)(2,1)S(1)}, bf16[1,224,768]{2,1,0:T(8,128)(2,1)S(1)}, u32[]{:S(2)}, u32[]{:S(2)}) collective-permute-start(bf16[1,224,768]{2,1,0:T(8,128)(2,1)S(1)} %get-tuple-element.33), channel_id=1, source_target_pairs={{0,24},{8,0},{16,8},{24,16},{1,25},{9,1},{17,9},{25,17},{2,26},{10... | collective-permute-start | bytes 1032200 | tf_op jit(solution)/shard_map/ppermute | solution.py:291
  73.6 16.2 %collective-permute-start.1 = (bf16[1,224,768]{2,1,0:T(8,128)(2,1)S(1)}, bf16[1,224,768]{2,1,0:T(8,128)(2,1)S(1)}, u32[]{:S(2)}, u32[]{:S(2)}) collective-permute-start(bf16[1,224,768]{2,1,0:T(8,128)(2,1)S(1)} %get-tuple-element.32), channel_id=1, source_target_pairs={{0,16},{8,24},{16,0},{24,8},{1,17},{9,25},{17,1},{25,9},{2,18},{10... | collective-permute-start | bytes 1032200 | tf_op jit(solution)/shard_map/ppermute | solution.py:291
  75.2 26.2 %collective-permute-start.4 = (bf16[1,144,768]{2,1,0:T(8,128)(2,1)S(1)}, bf16[1,144,768]{2,1,0:T(8,128)(2,1)S(1)}, u32[]{:S(2)}, u32[]{:S(2)}) collective-permute-start(bf16[1,144,768]{2,1,0:T(8,128)(2,1)S(1)} %slice.17), channel_id=1, source_target_pairs={{0,32},{32,0},{1,33},{33,1},{2,34},{34,2},{3,35},{35,3},{4,36},{36... | collective-permute-start | bytes 663560 | tf_op jit(solution)/shard_map/ppermute | solution.py:292
  81.1 20.3 %collective-permute-start.5 = (bf16[1,144,768]{2,1,0:T(8,128)(2,1)S(1)}, bf16[1,144,768]{2,1,0:T(8,128)(2,1)S(1)}, u32[]{:S(2)}, u32[]{:S(2)}) collective-permute-start(bf16[1,144,768]{2,1,0:T(8,128)(2,1)S(1)} %slice.22), channel_id=1, source_target_pairs={{0,32},{32,0},{1,33},{33,1},{2,34},{34,2},{3,35},{35,3},{4,36},{36... | collective-permute-start | bytes 663560 | tf_op jit(solution)/shard_map/ppermute | solution.py:292
  84.3 17.1 %collective-permute-start.6 = (bf16[1,144,768]{2,1,0:T(8,128)(2,1)S(1)}, bf16[1,144,768]{2,1,0:T(8,128)(2,1)S(1)}, u32[]{:S(2)}, u32[]{:S(2)}) collective-permute-start(bf16[1,144,768]{2,1,0:T(8,128)(2,1)S(1)} %slice.23), channel_id=1, source_target_pairs={{0,32},{32,0},{1,33},{33,1},{2,34},{34,2},{3,35},{35,3},{4,36},{36... | collective-permute-start | bytes 663560 | tf_op jit(solution)/shard_map/ppermute | solution.py:292
  89.8 18.1 %collective-permute-start.3 = (bf16[1,144,768]{2,1,0:T(8,128)(2,1)S(1)}, bf16[1,144,768]{2,1,0:T(8,128)(2,1)S(1)}, u32[]{:S(2)}, u32[]{:S(2)}) collective-permute-start(bf16[1,144,768]{2,1,0:T(8,128)(2,1)S(1)} %slice.21), channel_id=1, source_target_pairs={{0,32},{32,0},{1,33},{33,1},{2,34},{34,2},{3,35},{35,3},{4,36},{36... | collective-permute-start | bytes 663560 | tf_op jit(solution)/shard_map/ppermute | solution.py:292
  112.3 19.1 %all-to-all-start.2 = ((bf16[32,56,128]{2,1,0:T(8,128)(2,1)}), bf16[32,56,128]{2,1,0:T(8,128)(2,1)S(1)}, u32[]{:S(2)}, u32[]{:S(2)}) async-start(bf16[32,56,128]{2,1,0:T(8,128)(2,1)} %bitcast.8), calls=%async_computation.2 | async-start | bytes 917504 | tf_op jit(solution)/shard_map/all_to_all | solution.py:297
  126.7 16.2 %copy-start = (bf16[2,1,96,1152]{3,2,1,0:T(8,128)(2,1)S(1)}, bf16[2,1,96,1152]{3,2,1,0:T(8,128)(2,1)}, u32[]{:S(2)}) copy-start(bf16[2,1,96,1152]{3,2,1,0:T(8,128)(2,1)} %param.7) | copy-start | bytes 1327108
  129.9 1.5 copy-start.2
  131.4 10.0 %collective-permute-start.7 = (bf16[1152,1152]{1,0:T(8,128)(2,1)}, bf16[1152,1152]{1,0:T(8,128)(2,1)S(1)}, u32[]{:S(2)}, u32[]{:S(2)}) collective-permute-start(bf16[1152,1152]{1,0:T(8,128)(2,1)} %copy-done.2), channel_id=1, source_target_pairs={{0,64},{64,0},{1,65},{65,1},{2,66},{66,2},{3,67},{67,3},{4,68},{68... | collective-permute-start | bytes 7962632 | tf_op jit(solution)/shard_map/ppermute | solution.py:301
  141.4 1.5 copy-start.5
  142.9 1.8 copy-start.3
  147.5 6.7 %collective-permute-start.11 = (bf16[96,1152]{1,0:T(8,128)(2,1)S(1)}, bf16[96,1152]{1,0:T(8,128)(2,1)S(1)}, u32[]{:S(2)}, u32[]{:S(2)}) collective-permute-start(bf16[96,1152]{1,0:T(8,128)(2,1)S(1)} %get-tuple-element.38.n0), channel_id=1, source_target_pairs={{0,128},{128,0},{1,129},{129,1},{2,130},{130,2},{3,131},{131,3},{4... | collective-permute-start | bytes 663560 | tf_op jit(solution)/shard_map/ppermute | solution.py:311
  148.8 8.1 %collective-permute-start.10 = (bf16[96,1152]{1,0:T(8,128)(2,1)S(1)}, bf16[96,1152]{1,0:T(8,128)(2,1)S(1)}, u32[]{:S(2)}, u32[]{:S(2)}) collective-permute-start(bf16[96,1152]{1,0:T(8,128)(2,1)S(1)} %get-tuple-element.38.n0), channel_id=1, source_target_pairs={{0,64},{64,0},{1,65},{65,1},{2,66},{66,2},{3,67},{67,3},{4,68},{68... | collective-permute-start | bytes 663560 | tf_op jit(solution)/shard_map/ppermute | solution.py:316
  154.2 2.6 %collective-permute-start.12 = (bf16[96,1152]{1,0:T(8,128)(2,1)S(1)}, bf16[96,1152]{1,0:T(8,128)(2,1)S(1)}, u32[]{:S(2)}, u32[]{:S(2)}) collective-permute-start(bf16[96,1152]{1,0:T(8,128)(2,1)S(1)} %collective-permute-done.11.n2), channel_id=1, source_target_pairs={{0,64},{64,0},{1,65},{65,1},{2,66},{66,2},{3,67},{67,3},{4,68},{68... | collective-permute-start | bytes 663560 | tf_op jit(solution)/shard_map/ppermute | solution.py:316
  155.4 7.1 %collective-permute-start.9 = (bf16[96,1152]{1,0:T(8,128)(2,1)S(1)}, bf16[96,1152]{1,0:T(8,128)(2,1)S(1)}, u32[]{:S(2)}, u32[]{:S(2)}) collective-permute-start(bf16[96,1152]{1,0:T(8,128)(2,1)S(1)} %get-tuple-element.37.n0), channel_id=1, source_target_pairs={{0,128},{128,0},{1,129},{129,1},{2,130},{130,2},{3,131},{131,3},{4... | collective-permute-start | bytes 663560 | tf_op jit(solution)/shard_map/ppermute | solution.py:311
  156.6 8.8 %collective-permute-start.8 = (bf16[96,1152]{1,0:T(8,128)(2,1)S(1)}, bf16[96,1152]{1,0:T(8,128)(2,1)S(1)}, u32[]{:S(2)}, u32[]{:S(2)}) collective-permute-start(bf16[96,1152]{1,0:T(8,128)(2,1)S(1)} %get-tuple-element.37.n0), channel_id=1, source_target_pairs={{0,64},{64,0},{1,65},{65,1},{2,66},{66,2},{3,67},{67,3},{4,68},{68... | collective-permute-start | bytes 663560 | tf_op jit(solution)/shard_map/ppermute | solution.py:316
  162.5 2.9 %collective-permute-start.13 = (bf16[96,1152]{1,0:T(8,128)(2,1)S(1)}, bf16[96,1152]{1,0:T(8,128)(2,1)S(1)}, u32[]{:S(2)}, u32[]{:S(2)}) collective-permute-start(bf16[96,1152]{1,0:T(8,128)(2,1)S(1)} %collective-permute-done.9.n2), channel_id=1, source_target_pairs={{0,64},{64,0},{1,65},{65,1},{2,66},{66,2},{3,67},{67,3},{4,68},{68... | collective-permute-start | bytes 663560 | tf_op jit(solution)/shard_map/ppermute | solution.py:316
  163.3 5.6 %collective-permute-start.17 = (bf16[216,128]{1,0:T(8,128)(2,1)S(1)}, bf16[216,128]{1,0:T(8,128)(2,1)S(1)}, u32[]{:S(2)}, u32[]{:S(2)}) collective-permute-start(bf16[216,128]{1,0:T(8,128)(2,1)S(1)} %get-tuple-element.49), channel_id=1, source_target_pairs={{0,64},{64,0},{1,65},{65,1},{2,66},{66,2},{3,67},{67,3},{4,68},{68... | collective-permute-start | bytes 165896 | tf_op jit(solution)/shard_map/ppermute | solution.py:322
  163.3 6.5 %collective-permute-start.18 = (bf16[216,128]{1,0:T(8,128)(2,1)S(1)}, bf16[216,128]{1,0:T(8,128)(2,1)S(1)}, u32[]{:S(2)}, u32[]{:S(2)}) collective-permute-start(bf16[216,128]{1,0:T(8,128)(2,1)S(1)} %get-tuple-element.50), channel_id=1, source_target_pairs={{0,128},{128,0},{1,129},{129,1},{2,130},{130,2},{3,131},{131,3},{4... | collective-permute-start | bytes 165896 | tf_op jit(solution)/shard_map/ppermute | solution.py:323
  164.4 5.4 %copy-start.4 = (bf16[1152,1152]{1,0:T(8,128)(2,1)S(1)}, bf16[1152,1152]{1,0:T(8,128)(2,1)}, u32[]{:S(2)}) copy-start(bf16[1152,1152]{1,0:T(8,128)(2,1)} %copy-done.2) | copy-start | bytes 7962628
  164.5 5.4 %copy-start.6 = (bf16[1152,1152]{1,0:T(8,128)(2,1)S(1)}, bf16[1152,1152]{1,0:T(8,128)(2,1)}, u32[]{:S(2)}) copy-start(bf16[1152,1152]{1,0:T(8,128)(2,1)} %copy-done.5) | copy-start | bytes 7962628
  164.5 5.4 %collective-permute-start.19 = (bf16[216,128]{1,0:T(8,128)(2,1)S(1)}, bf16[216,128]{1,0:T(8,128)(2,1)S(1)}, u32[]{:S(2)}, u32[]{:S(2)}) collective-permute-start(bf16[216,128]{1,0:T(8,128)(2,1)S(1)} %get-tuple-element.51), channel_id=1, source_target_pairs={{0,192},{192,0},{64,128},{128,64},{1,193},{193,1},{65,129},{129,65... | collective-permute-start | bytes 165896 | tf_op jit(solution)/shard_map/ppermute | solution.py:324
  167.6 4.4 %collective-permute-start.14 = (bf16[216,128]{1,0:T(8,128)(2,1)S(1)}, bf16[216,128]{1,0:T(8,128)(2,1)S(1)}, u32[]{:S(2)}, u32[]{:S(2)}) collective-permute-start(bf16[216,128]{1,0:T(8,128)(2,1)S(1)} %get-tuple-element.44), channel_id=1, source_target_pairs={{0,64},{64,0},{1,65},{65,1},{2,66},{66,2},{3,67},{67,3},{4,68},{68... | collective-permute-start | bytes 165896 | tf_op jit(solution)/shard_map/ppermute | solution.py:322
  167.7 4.3 %collective-permute-start.15 = (bf16[216,128]{1,0:T(8,128)(2,1)S(1)}, bf16[216,128]{1,0:T(8,128)(2,1)S(1)}, u32[]{:S(2)}, u32[]{:S(2)}) collective-permute-start(bf16[216,128]{1,0:T(8,128)(2,1)S(1)} %get-tuple-element.45), channel_id=1, source_target_pairs={{0,128},{128,0},{1,129},{129,1},{2,130},{130,2},{3,131},{131,3},{4... | collective-permute-start | bytes 165896 | tf_op jit(solution)/shard_map/ppermute | solution.py:323
  168.9 4.5 %collective-permute-start.16 = (bf16[216,128]{1,0:T(8,128)(2,1)S(1)}, bf16[216,128]{1,0:T(8,128)(2,1)S(1)}, u32[]{:S(2)}, u32[]{:S(2)}) collective-permute-start(bf16[216,128]{1,0:T(8,128)(2,1)S(1)} %get-tuple-element.46), channel_id=1, source_target_pairs={{0,192},{192,0},{64,128},{128,64},{1,193},{193,1},{65,129},{129,65... | collective-permute-start | bytes 165896 | tf_op jit(solution)/shard_map/ppermute | solution.py:324
Sparse Core Ops, SparseCore 0:
  9.1 54.8 all-gather.3
  65.8 60.8 all-gather.5

commit v7 on v6

--- a/solution.py
+++ b/solution.py
@@ -164,20 +164,28 @@
     )(*args)
 
 
-def prepare(rest, own, turned):
-    for n in range(5):
-        width = min(256, D - n * 256)
-        own[:, n * 256 : n * 256 + width] = rest[n, :, :width]
-    turned[:128] = rest[4, :, 128:].astype(F32).T.astype(BF)
-    for n in range(3):
-        turned[128 + n * 256 : 384 + n * 256] = rest[5 + n].astype(F32).T.astype(BF)
+def prepare(rest, out_a, turned, out_b):
+    half, last = D // 2, D // 2 + 12 * HD
+    for n in range(NZ):
+        chunk = rest[n].astype(F32).T.astype(BF)
+        low, high = n * 256, (n + 1) * 256
+        for ref, begin, end in ((out_a, 0, half), (turned, half, last), (out_b, last, last + half)):
+            first, stop = max(low, begin), min(high, end)
+            if first < stop:
+                ref[first - begin : stop - begin] = chunk[first - low : stop - low]
+
+
+def both_halves(second, own, got):
+    return jnp.where(second, jnp.concatenate([got, own], 1), jnp.concatenate([own, got], 1))
 
 
 def spatial_end(place_ref, att_ref, tok_ref, mod_ref, own, got, resid_ref, norm_ref):
     feats = [unpack(att_ref[n % 2, n // 2].astype(F32), 16) for n in range(HEADS)]
     attended = jnp.concatenate(feats, 0).T.astype(BF)
-    weight = jnp.where(place_ref[0] == 1, got[...], own[...])
-    branch = jnp.dot(attended, weight, preferred_element_type=F32)
+    halves = [
+        lax.dot_general(attended, w[...], NT, preferred_element_type=F32) for w in (own, got)
+    ]
+    branch = both_halves(place_ref[0] == 1, *halves)
     resid = tok_ref[...].astype(F32) + mod_ref[2:3, :] * branch
     resid_ref[...] = resid
     norm_ref[...] = (normalise(resid) * (1.0 + mod_ref[4:5, :]) + mod_ref[3:4, :]).astype(BF)
@@ -207,15 +215,17 @@
         out_ref[...] = pack(jnp.concatenate(mixed, 0)[:, :PATCH], 3 * HD).astype(BF)
 
 
-def temporal_end(place_ref, m0, m1, m2, m3, resid_ref, mod_ref, own, got, *out_refs):
-    second, branch = place_ref[0] == 1, None
+def temporal_end(place_ref, m0, m1, m2, m3, resid_ref, mod_ref, own, got, *refs):
+    out_ref, feats = refs[-2:]
     for step, att_ref in enumerate((m0, m1, m2, m3)):
-        feats = unpack(att_ref[...].astype(F32), HD)
         here = pl.ds(pl.multiple_of((place_ref[1] ^ step) * (4 * HD), 4 * HD), 4 * HD)
-        rows = jnp.where(second, own[here, :], got[here, :])
-        add = jnp.dot(feats.T.astype(BF), rows, preferred_element_type=F32)
-        branch = add if branch is None else branch + add
-    out_refs[-1][...] = (resid_ref[...] + mod_ref[5:6, :] * branch).astype(BF)
+        feats[here, :] = unpack(att_ref[...].astype(F32), HD)
+    attended = feats[...].T.astype(BF)
+    halves = [
+        lax.dot_general(attended, w[...], NT, preferred_element_type=F32) for w in (own, got)
+    ]
+    branch = both_halves(place_ref[0] == 1, *halves)
+    out_ref[...] = (resid_ref[...] + mod_ref[5:6, :] * branch).astype(BF)
 
 
 def full(array, lead=None, n=0):
@@ -224,7 +234,7 @@
     return pl.BlockSpec(block, lambda i: place)
 
 
-def once(kernel, args, specs, shapes, out_specs=None, aliases=None):
+def once(kernel, args, specs, shapes, out_specs=None, aliases=None, scratch=()):
     return pl.pallas_call(
         kernel,
         grid=(1,),
@@ -232,7 +242,8 @@
         out_specs=out_specs or [full(s) for s in shapes],
         out_shape=shapes,
         input_output_aliases=aliases or {},
-        compiler_params=PARAMS,
+        scratch_shapes=scratch,
+        compiler_params=pltpu.CompilerParams(vmem_limit_bytes=24 * 1024 * 1024),
         cost_estimate=pl.CostEstimate(
             flops=2_000_000_000, bytes_accessed=8_000_000, transcendentals=0
         ),
@@ -251,10 +262,15 @@
     gains = norm_gains.T
     tok = tokens.reshape(ROWS, D)
 
+    half = D // 2
     part_a = spatial_qkv.reshape(18, 3, NZ, 2 * HD).transpose(2, 0, 1, 3).reshape(NZ, 18, 6 * HD)
     part_a = jnp.pad(part_a, ((0, 0), (0, 0), (0, 512 - 6 * HD)))
     part_b = lax.dynamic_slice_in_dim(temporal_qkv.reshape(18, 3, D), frame * 4 * HD, 4 * HD, 2)
-    rest = [jnp.where(core == 0, spatial_out, temporal_out), part_b.reshape(18, 12 * HD)]
+    rest = [
+        jnp.where(core == 0, spatial_out[:, :half], spatial_out[:, half:]),
+        part_b.reshape(18, 12 * HD),
+        jnp.where(core == 0, temporal_out[:, :half], temporal_out[:, half:]),
+    ]
     rest = jnp.pad(jnp.concatenate(rest, 1), ((0, 0), (0, 256 * NZ - D - 12 * HD)))
     rest = rest.reshape(18, NZ, 256).transpose(1, 0, 2)
     shard = jnp.concatenate([part_a, rest], 2)
@@ -296,16 +312,19 @@
     attended = attended.reshape(NY * NZ, 56, 128)
     attended = lax.all_to_all(attended, ("y", "z"), 0, 0, tiled=True)
     attended = attended.reshape(4, NZ, 56, 128)
-    own, turned = once(prepare, [rest], [full(rest)], [shape(BF, D, D), shape(BF, 896, D)])
-    swapped, _ = lax.optimization_barrier((own, attended))
-    got = lax.ppermute(swapped, "c", swap)
+    shapes = [shape(BF, half, D), shape(BF, 12 * HD, D), shape(BF, half, D)]
+    out_a, turned, out_b = once(prepare, [rest], [full(rest)], shapes)
+    swapped, _ = lax.optimization_barrier((out_a, attended))
+    got_a = lax.ppermute(swapped, "c", swap)
 
     steps = []
     for clip in range(2):
-        args = [place, attended, tok, modulation, own, got]
+        args = [place, attended, tok, modulation, out_a, got_a]
         specs = [SMEM, full(attended, 2, clip), full(tok, PATCH, clip)]
         specs += [full(a) for a in args[3:]]
         steps.append(once(spatial_end, args, specs, [shape(F32, PATCH, D), shape(BF, PATCH, D)]))
+    swapped, _ = lax.optimization_barrier((out_b, steps[1][1]))
+    got_b = lax.ppermute(swapped, "c", swap)
     diagonal = [(0, 3), (3, 0), (1, 2), (2, 1)]
     sent = []
     moved = [lax.ppermute(norm, "xl", swap) for _, norm in steps]
@@ -326,7 +345,7 @@
         )
     result = None
     for clip in range(2):
-        args = sent[clip] + [steps[clip][0], modulation, own, got]
+        args = sent[clip] + [steps[clip][0], modulation, out_b, got_b]
         specs = [SMEM] + [full(a) for a in args]
         aliases = None
         if result is not None:
@@ -334,7 +353,9 @@
             aliases = {len(args): 0}
         whole = shape(BF, ROWS, D)
         out_specs = [full(whole, PATCH, clip)]
-        (result,) = once(temporal_end, [place] + args, specs, [whole], out_specs, aliases)
+        scratch = [pltpu.VMEM((D, PATCH), F32)]
+        args = [place] + args
+        (result,) = once(temporal_end, args, specs, [whole], out_specs, aliases, scratch)
     return result.reshape(2, 1, PATCH, D)
 
 

time: 183 us -> 179 us (0.978)
  Pallas kernels: 43.4 us -> 40.1 us
  starting transfers between devices: 33.8 us -> 31.9 us
    pallas_call x7, Pallas kernels: 17.5 us -> 14.1 us  [once(): pl.pallas_call(kernel, grid=(1,), in_specs=specs, out_specs=out_specs or...]
    ppermute x2, waiting for transfers between devices: 5.44 us -> 8.82 us  [per_device(): moved = [lax.ppermute(norm, 'xl', swap) for _, norm in steps]]
    ppermute x1 -> x2, waiting for transfers between devices: 4.72 us -> 2.82 us  [the longest x1 2.82 us: per_device(): got_a = lax.ppermute(swapped, 'c', swap)]
    unnamed x18 -> x26, local copies, waits for them, and re-layouts: 4.88 us -> 6.18 us
    ppermute x1 -> x2, starting transfers between devices: 5.18 us -> 4.31 us  [the longest x1 3.85 us: per_device(): got_a = lax.ppermute(swapped, 'c', swap)]
  transfers between devices with their start and end apart: 23 -> 24, of which waited for: 8 -> 8; matrix products, arithmetic and copies ran while one was open for 3% -> 2% of each run, Pallas kernels for 21% -> 20%
where the time goes in v7:
time: 179 us
  blocking collectives  46.7 us (26%)
  Pallas kernels  40.1 us (22%)
  waiting for transfers between devices  36.7 us (21%)
  starting transfers between devices  31.9 us (18%)
  between operations  13.7 us (8%)
  local copies, waits for them, and re-layouts  9.32 us (5%)
    all_to_all x1, blocking collectives, per_device(): shard = lax.all_to_all(shard, ('xh', 'y'), 0, 0, tiled=True).reshape(D, 768)  27 us
    all_to_all x1, blocking collectives, per_device(): lax.all_to_all(shard, 'z', 0, 0, tiled=True).reshape(1, NZ * 18, 768)  19.7 us
    pallas_call x3, Pallas kernels, attention(): pl.pallas_call(functools.partial(attend, count, part is not None, finish)...  19.5 us
    pallas_call x7, Pallas kernels, once(): pl.pallas_call(kernel, grid=(1,), in_specs=specs, out_specs=out_specs or...  14.1 us
    all_gather x1, waiting for transfers between devices, per_device(): rest = lax.all_gather(rest, 'z', axis=0)  9.04 us
    ppermute x4, starting transfers between devices, per_device(): others = [lax.ppermute(block[:, :2 * HD], 'xh', swap) for block in blocks]  8.82 us
    ppermute x2, waiting for transfers between devices, per_device(): moved = [lax.ppermute(norm, 'xl', swap) for _, norm in steps]  8.82 us
    ppermute x3, waiting for transfers between devices, per_device(): lax.ppermute(slots[n], 'y', [(i, (i + n) % NY) for i in range(NY)])  8.36 us
  transfers between devices with their start and end apart: 24, of which 8 were waited for; matrix products, arithmetic and copies ran while one was open for 2% of the time, Pallas kernels for 20%

profile of v7, /device:TPU:1, one launch (start us, length us, event | category | flops | bytes accessed | tf_op | source)
XLA Modules:
  0.0 178.7 jit_solution(1670193752911677577)
XLA Ops:
  6.5 0.7 all-gather.4.cloned.1.call-update
  7.3 1.2 reshape.36
  9.6 19.7 %all_to_all.15 = bf16[8,18,768]{2,1,0:T(8,128)(2,1)S(1)} all-to-all(bf16[8,18,768]{2,1,0:T(8,128)(2,1)S(1)} %copy.16), channel_id=1, replica_groups=mesh['xl'=2,'c'=2,'xh'=2,'y'=4,'z'=8] {'z'}, dimensions={0} | all-to-all | bytes 442368 | tf_op jit(solution)/shard_map/all_to_all | solution.py:277
  29.4 27.0 %all_to_all.16 = bf16[8,144,768]{2,1,0:T(8,128)(2,1)S(1)} all-to-all(bf16[8,144,768]{2,1,0:T(8,128)(2,1)S(1)} %broadcast_in_dim.8), channel_id=1, replica_groups=mesh['xl'=2,'c'=2,'xh'=2,'y'=4,'z'=8] {'xh','y'}, dimensions={0} | all-to-all | bytes 3538944 | tf_op jit(solution)/shard_map/all_to_all | solution.py:279
  56.5 0.9 slice.36
  57.4 5.8 %all-gather.4.cloned.1.call-done.tok_ref = bf16[8,192,1152]{2,1,0:T(8,128)(2,1)} async-done(((bf16[1,192,1152]{2,1,0:T(8,128)(2,1)}), bf16[8,192,1152]{2,1,0:T(8,128)(2,1)}) %all-gather.4.cloned.1.call-update) | async-done | bytes 3538960 | tf_op jit(solution)/shard_map/all_gather | solution.py:281
  63.3 6.5 %spatial_proj.1 = (bf16[1,224,768]{2,1,0:T(8,128)(2,1)S(1)}, bf16[1,224,768]{2,1,0:T(8,128)(2,1)S(1)}, bf16[1,224,768]{2,1,0:T(8,128)(2,1)S(1)}, bf16[1,224,768]{2,1,0:T(8,128)(2,1)S(1)}) custom-call(s32[1]{0:T(128)} %bitcast.2.y_ref, bf16[8,192,1152]{2,1,0:T(8,128)(2,1)} %all-gather.4.cloned.1.call-done.tok_ref, f32[6,1152]{1,0:T(8,128)S(1)} %copy-done.1, ...), custom_call_target="tpu_custom_call" | custom-call | tf_op jit(solution)/shard_map/spatial_proj/pallas_call | solution.py:287
  69.8 1.3 collective-permute-start
  71.1 1.5 collective-permute-start.2
  72.6 1.5 collective-permute-start.1
  74.0 2.7 %collective-permute-start.4 = (bf16[1,144,768]{2,1,0:T(8,128)(2,1)S(1)}, bf16[1,144,768]{2,1,0:T(8,128)(2,1)S(1)}, u32[]{:S(2)}, u32[]{:S(2)}) collective-permute-start(bf16[1,144,768]{2,1,0:T(8,128)(2,1)S(1)} %slice.33), channel_id=1, source_target_pairs={{0,32},{32,0},{1,33},{33,1},{2,34},{34,2},{3,35},{35,3},{4,36},{36... | collective-permute-start | bytes 663560 | tf_op jit(solution)/shard_map/ppermute | solution.py:308
  76.8 3.6 %collective-permute-done.refs_1_.refs_5_ = bf16[1,224,768]{2,1,0:T(8,128)(2,1)S(1)} collective-permute-done((bf16[1,224,768]{2,1,0:T(8,128)(2,1)S(1)}, bf16[1,224,768]{2,1,0:T(8,128)(2,1)S(1)}, u32[]{:S(2)}, u32[]{:S(2)}) %collective-permute-start) | collective-permute-done | bytes 344096 | tf_op jit(solution)/shard_map/ppermute | solution.py:307
  80.4 2.8 %collective-permute-start.5 = (bf16[1,144,768]{2,1,0:T(8,128)(2,1)S(1)}, bf16[1,144,768]{2,1,0:T(8,128)(2,1)S(1)}, u32[]{:S(2)}, u32[]{:S(2)}) collective-permute-start(bf16[1,144,768]{2,1,0:T(8,128)(2,1)S(1)} %slice.38), channel_id=1, source_target_pairs={{0,32},{32,0},{1,33},{33,1},{2,34},{34,2},{3,35},{35,3},{4,36},{36... | collective-permute-start | bytes 663560 | tf_op jit(solution)/shard_map/ppermute | solution.py:308
  83.2 0.3 collective-permute-start.6
  83.6 4.8 %collective-permute-done.1.refs_2_.refs_6_ = bf16[1,224,768]{2,1,0:T(8,128)(2,1)S(1)} collective-permute-done((bf16[1,224,768]{2,1,0:T(8,128)(2,1)S(1)}, bf16[1,224,768]{2,1,0:T(8,128)(2,1)S(1)}, u32[]{:S(2)}, u32[]{:S(2)}) %collective-permute-start.1) | collective-permute-done | bytes 344096 | tf_op jit(solution)/shard_map/ppermute | solution.py:307
  88.4 2.9 %collective-permute-start.3 = (bf16[1,144,768]{2,1,0:T(8,128)(2,1)S(1)}, bf16[1,144,768]{2,1,0:T(8,128)(2,1)S(1)}, u32[]{:S(2)}, u32[]{:S(2)}) collective-permute-start(bf16[1,144,768]{2,1,0:T(8,128)(2,1)S(1)} %slice.37), channel_id=1, source_target_pairs={{0,32},{32,0},{1,33},{33,1},{2,34},{34,2},{3,35},{35,3},{4,36},{36... | collective-permute-start | bytes 663560 | tf_op jit(solution)/shard_map/ppermute | solution.py:308
  91.3 8.5 %attend.3.refs_7_ = f32[4,80,768]{2,1,0:T(8,128)S(1)} custom-call(s32[1]{0:T(128)} %bitcast.2.y_ref, bf16[1,224,768]{2,1,0:T(8,128)(2,1)S(1)} %get-tuple-element.32.refs_0_.refs_4_, bf16[1,224,768]{2,1,0:T(8,128)(2,1)S(1)} %collective-permute-done.refs_1_.refs_5_, bf16[1,224,768]{2,1,0:T(8,128)(2,1)S(1)} %collective-permute-done.1.refs_2_.refs_6_, ...), custom_call_target="tpu_custom_call" | custom-call | flops 37748736 | bytes 1000000 | tf_op jit(solution)/shard_map/attend/pallas_call | solution.py:148
  99.9 6.5 %attend.4.refs_5_ = f32[4,80,768]{2,1,0:T(8,128)S(1)} custom-call(s32[1]{0:T(128)} %bitcast.2.y_ref, bf16[1,224,768]{2,1,0:T(8,128)(2,1)S(1)} %get-tuple-element.32.refs_0_.refs_4_, bf16[1,224,768]{2,1,0:T(8,128)(2,1)S(1)} %collective-permute-done.refs_1_.refs_5_, bf16[1,224,768]{2,1,0:T(8,128)(2,1)S(1)} %collective-permute-done.1.refs_2_.refs_6_, ...), custom_call_target="tpu_custom_call" | custom-call | flops 28311552 | bytes 1000000 | tf_op jit(solution)/shard_map/attend/pallas_call | solution.py:148
  106.4 4.5 %attend.5 = bf16[4,8,56,128]{3,2,1,0:T(8,128)(2,1)} custom-call(s32[1]{0:T(128)} %bitcast.2.y_ref, bf16[1,224,768]{2,1,0:T(8,128)(2,1)S(1)} %get-tuple-element.32.refs_0_.refs_4_, bf16[1,224,768]{2,1,0:T(8,128)(2,1)S(1)} %collective-permute-done.refs_1_.refs_5_, bf16[1,224,768]{2,1,0:T(8,128)(2,1)S(1)} %collective-permute-done.1.refs_2_.refs_6_, ...), custom_call_target="tpu_custom_call" | custom-call | flops 9437184 | bytes 1000000 | tf_op jit(solution)/shard_map/attend/pallas_call | solution.py:148
  110.8 5.3 %all-to-all-start.2 = ((bf16[32,56,128]{2,1,0:T(8,128)(2,1)}), bf16[32,56,128]{2,1,0:T(8,128)(2,1)S(1)}, u32[]{:S(2)}, u32[]{:S(2)}) async-start(bf16[32,56,128]{2,1,0:T(8,128)(2,1)} %bitcast.8), calls=%async_computation.2 | async-start | bytes 917504 | tf_op jit(solution)/shard_map/all_to_all | solution.py:313
  116.2 9.0 %all-gather.6.cloned.1.call-done = bf16[9216,256]{1,0:T(8,128)(2,1)} async-done(((bf16[1152,256]{1,0:T(8,128)(2,1)}), bf16[9216,256]{1,0:T(8,128)(2,1)}) %all-gather.6.cloned.1.call-update) | async-done | bytes 4718608 | tf_op jit(solution)/shard_map/all_gather | solution.py:284
  125.2 2.3 %copy-done.2 = bf16[9216,256]{1,0:T(8,128)(2,1)S(1)} copy-done((bf16[9216,256]{1,0:T(8,128)(2,1)S(1)}, bf16[9216,256]{1,0:T(8,128)(2,1)}, u32[]{:S(2)}) %copy-start.2) | copy-done | bytes 4718616
  127.6 1.3 prepare.1
  128.9 1.1 copy-done.3
  129.9 1.3 copy-done.6
  131.3 3.8 %collective-permute-start.7 = (bf16[576,1152]{1,0:T(8,128)(2,1)}, bf16[576,1152]{1,0:T(8,128)(2,1)S(1)}, u32[]{:S(2)}, u32[]{:S(2)}) collective-permute-start(bf16[576,1152]{1,0:T(8,128)(2,1)} %copy-done.3), channel_id=1, source_target_pairs={{0,64},{64,0},{1,65},{65,1},{2,66},{66,2},{3,67},{67,3},{4,68},{68... | collective-permute-start | bytes 3981320 | tf_op jit(solution)/shard_map/ppermute | solution.py:318
  135.2 2.8 %collective-permute-done.7.got = bf16[576,1152]{1,0:T(8,128)(2,1)S(1)} collective-permute-done((bf16[576,1152]{1,0:T(8,128)(2,1)}, bf16[576,1152]{1,0:T(8,128)(2,1)S(1)}, u32[]{:S(2)}, u32[]{:S(2)}) %collective-permute-start.7) | collective-permute-done | bytes 1327136 | tf_op jit(solution)/shard_map/ppermute | solution.py:318
  138.0 1.3 copy-done.4
  139.3 1.9 %spatial_end.2 = (f32[96,1152]{1,0:T(8,128)S(1)}, bf16[96,1152]{1,0:T(8,128)(2,1)S(1)}) custom-call(s32[2]{0:T(128)S(1)} %pad_add_fusion.place_ref, bf16[4,8,56,128]{3,2,1,0:T(8,128)(2,1)S(1)} %bitcast.25, bf16[192,1152]{1,0:T(8,128)(2,1)S(1)} %bitcast.28, f32[6,1152]{1,0:T(8,128)S(1)} %copy-done.1, bf16[576,1152]{1,0:T(8,128)(2,1)S(1)} %copy-done.4, ...), custom_call_target="tpu_custom_call" | custom-call | flops 2000000000 | bytes 8000000 | tf_op jit(solution)/shard_map/spatial_end/pallas_call | solution.py:238
  141.2 0.5 collective-permute-start.17
  141.7 1.9 %spatial_end.3 = (f32[96,1152]{1,0:T(8,128)S(1)}, bf16[96,1152]{1,0:T(8,128)(2,1)S(1)}) custom-call(s32[2]{0:T(128)S(1)} %pad_add_fusion.place_ref, bf16[4,8,56,128]{3,2,1,0:T(8,128)(2,1)S(1)} %bitcast.26, bf16[192,1152]{1,0:T(8,128)(2,1)S(1)} %bitcast.29, f32[6,1152]{1,0:T(8,128)S(1)} %copy-done.1, bf16[576,1152]{1,0:T(8,128)(2,1)S(1)} %copy-done.5, ...), custom_call_target="tpu_custom_call" | custom-call | flops 2000000000 | bytes 8000000 | tf_op jit(solution)/shard_map/spatial_end/pallas_call | solution.py:238
  143.6 1.2 collective-permute-start.11
  144.8 0.4 collective-permute-start.10
  145.2 5.3 %collective-permute-done.11.n2 = bf16[96,1152]{1,0:T(8,128)(2,1)S(1)} collective-permute-done((bf16[96,1152]{1,0:T(8,128)(2,1)S(1)}, bf16[96,1152]{1,0:T(8,128)(2,1)S(1)}, u32[]{:S(2)}, u32[]{:S(2)}) %collective-permute-start.11) | collective-permute-done | bytes 221216 | tf_op jit(solution)/shard_map/ppermute | solution.py:330
  150.6 1.0 collective-permute-start.12
  151.5 1.1 collective-permute-start.9
  152.7 0.3 collective-permute-start.8
  153.0 2.1 %temporal.2 = (bf16[216,128]{1,0:T(8,128)(2,1)S(1)}, bf16[216,128]{1,0:T(8,128)(2,1)S(1)}, bf16[216,128]{1,0:T(8,128)(2,1)S(1)}, bf16[216,128]{1,0:T(8,128)(2,1)S(1)}) custom-call(bf16[96,1152]{1,0:T(8,128)(2,1)S(1)} %get-tuple-element.40.n0, bf16[96,1152]{1,0:T(8,128)(2,1)S(1)} %collective-permute-done.10.n1, ...), custom_call_target="tpu_custom_call" | custom-call | flops 2000000000 | bytes 8000000 | tf_op jit(solution)/shard_map/temporal/pallas_call | solution.py:238
  155.1 3.5 %collective-permute-done.9.n2 = bf16[96,1152]{1,0:T(8,128)(2,1)S(1)} collective-permute-done((bf16[96,1152]{1,0:T(8,128)(2,1)S(1)}, bf16[96,1152]{1,0:T(8,128)(2,1)S(1)}, u32[]{:S(2)}, u32[]{:S(2)}) %collective-permute-start.9) | collective-permute-done | bytes 221216 | tf_op jit(solution)/shard_map/ppermute | solution.py:330
  158.6 0.8 collective-permute-start.13
  159.4 1.1 collective-permute-start.19
  160.5 1.0 collective-permute-start.20
  161.5 2.1 %temporal.3 = (bf16[216,128]{1,0:T(8,128)(2,1)S(1)}, bf16[216,128]{1,0:T(8,128)(2,1)S(1)}, bf16[216,128]{1,0:T(8,128)(2,1)S(1)}, bf16[216,128]{1,0:T(8,128)(2,1)S(1)}) custom-call(bf16[96,1152]{1,0:T(8,128)(2,1)S(1)} %get-tuple-element.39.n0, bf16[96,1152]{1,0:T(8,128)(2,1)S(1)} %collective-permute-done.8.n1, ...), custom_call_target="tpu_custom_call" | custom-call | flops 2000000000 | bytes 8000000 | tf_op jit(solution)/shard_map/temporal/pallas_call | solution.py:238
  163.7 1.2 collective-permute-start.15
  165.0 0.9 collective-permute-start.16
  165.8 2.4 %temporal_end.2.refs_0_ = bf16[192,1152]{1,0:T(8,128)(2,1)} custom-call(s32[2]{0:T(128)S(1)} %pad_add_fusion.place_ref, bf16[216,128]{1,0:T(8,128)(2,1)S(1)} %get-tuple-element.52.m0, bf16[216,128]{1,0:T(8,128)(2,1)S(1)} %collective-permute-done.18.m1, bf16[216,128]{1,0:T(8,128)(2,1)S(1)} %collective-permute-done.19.m2, ...), custom_call_target="tpu_custom_call" | custom-call | flops 2000000000 | bytes 8000000 | tf_op jit(solution)/shard_map/temporal_end/pallas_call | solution.py:238
  168.3 1.1 collective-permute-done.16.m3
  169.4 2.4 %temporal_end.3 = bf16[192,1152]{1,0:T(8,128)(2,1)} custom-call(s32[2]{0:T(128)S(1)} %pad_add_fusion.place_ref, bf16[216,128]{1,0:T(8,128)(2,1)S(1)} %get-tuple-element.45.m0, bf16[216,128]{1,0:T(8,128)(2,1)S(1)} %collective-permute-done.14.m1, bf16[216,128]{1,0:T(8,128)(2,1)S(1)} %collective-permute-done.15.m2, ...), custom_call_target="tpu_custom_call", output_to_operand_aliasing={{}: (9, {})} | custom-call | flops 2000000000 | bytes 8000000 | tf_op jit(solution)/shard_map/temporal_end/pallas_call | solution.py:238
  (61 shorter events, 1.5 us)
Async XLA Ops:
  6.5 2.3 %copy-start.8 = (bf16[18,3456]{1,0:T(8,128)(2,1)S(1)}, bf16[18,3456]{1,0:T(8,128)(2,1)}, u32[]{:S(2)}) copy-start(bf16[18,3456]{1,0:T(8,128)(2,1)} %param.11) | copy-start | bytes 373252
  6.5 2.6 %copy-start.9 = (bf16[18,1152]{1,0:T(8,128)(2,1)S(1)}, bf16[18,1152]{1,0:T(8,128)(2,1)}, u32[]{:S(2)}) copy-start(bf16[18,1152]{1,0:T(8,128)(2,1)} %param.12) | copy-start | bytes 124420
  6.5 2.6 %copy-start.10 = (bf16[18,1152]{1,0:T(8,128)(2,1)S(1)}, bf16[18,1152]{1,0:T(8,128)(2,1)}, u32[]{:S(2)}) copy-start(bf16[18,1152]{1,0:T(8,128)(2,1)} %param.10) | copy-start | bytes 124420
  6.5 56.6 %all-gather.4.cloned.1.call-start = ((), (), s32[]{:S(2)}) async-start(), calls=%async_computation.3 | async-start | bytes 3981312 | tf_op jit(solution)/shard_map/all_gather | solution.py:281
  7.3 118.0 %all-gather.6.cloned.1.call-start = ((), (), s32[]{:S(2)}) async-start(), calls=%async_computation.4 | async-start | bytes 5308416 | tf_op jit(solution)/shard_map/all_gather | solution.py:284
  56.4 6.8 %copy-start.11 = (f32[4,72]{1,0:T(4,128)S(1)}, f32[4,72]{1,0:T(4,128)}, u32[]{:S(2)}) copy-start(f32[4,72]{1,0:T(4,128)} %param.13) | copy-start | bytes 3460
  56.4 6.9 %copy-start.1 = (f32[6,1152]{1,0:T(8,128)S(1)}, f32[6,1152]{1,0:T(8,128)}, u32[]{:S(2)}) copy-start(f32[6,1152]{1,0:T(8,128)} %mod_ref.9) | copy-start | bytes 82948
  69.8 10.6 %collective-permute-start = (bf16[1,224,768]{2,1,0:T(8,128)(2,1)S(1)}, bf16[1,224,768]{2,1,0:T(8,128)(2,1)S(1)}, u32[]{:S(2)}, u32[]{:S(2)}) collective-permute-start(bf16[1,224,768]{2,1,0:T(8,128)(2,1)S(1)} %get-tuple-element.33), channel_id=1, source_target_pairs={{0,8},{8,16},{16,24},{24,0},{1,9},{9,17},{17,25},{25,1},{2,10},{10... | collective-permute-start | bytes 1032200 | tf_op jit(solution)/shard_map/ppermute | solution.py:307
  71.1 12.1 %collective-permute-start.2 = (bf16[1,224,768]{2,1,0:T(8,128)(2,1)S(1)}, bf16[1,224,768]{2,1,0:T(8,128)(2,1)S(1)}, u32[]{:S(2)}, u32[]{:S(2)}) collective-permute-start(bf16[1,224,768]{2,1,0:T(8,128)(2,1)S(1)} %get-tuple-element.35), channel_id=1, source_target_pairs={{0,24},{8,0},{16,8},{24,16},{1,25},{9,1},{17,9},{25,17},{2,26},{10... | collective-permute-start | bytes 1032200 | tf_op jit(solution)/shard_map/ppermute | solution.py:307
  72.6 15.8 %collective-permute-start.1 = (bf16[1,224,768]{2,1,0:T(8,128)(2,1)S(1)}, bf16[1,224,768]{2,1,0:T(8,128)(2,1)S(1)}, u32[]{:S(2)}, u32[]{:S(2)}) collective-permute-start(bf16[1,224,768]{2,1,0:T(8,128)(2,1)S(1)} %get-tuple-element.34), channel_id=1, source_target_pairs={{0,16},{8,24},{16,0},{24,8},{1,17},{9,25},{17,1},{25,9},{2,18},{10... | collective-permute-start | bytes 1032200 | tf_op jit(solution)/shard_map/ppermute | solution.py:307
  74.0 25.8 %collective-permute-start.4 = (bf16[1,144,768]{2,1,0:T(8,128)(2,1)S(1)}, bf16[1,144,768]{2,1,0:T(8,128)(2,1)S(1)}, u32[]{:S(2)}, u32[]{:S(2)}) collective-permute-start(bf16[1,144,768]{2,1,0:T(8,128)(2,1)S(1)} %slice.33), channel_id=1, source_target_pairs={{0,32},{32,0},{1,33},{33,1},{2,34},{34,2},{3,35},{35,3},{4,36},{36... | collective-permute-start | bytes 663560 | tf_op jit(solution)/shard_map/ppermute | solution.py:308
  80.4 19.4 %collective-permute-start.5 = (bf16[1,144,768]{2,1,0:T(8,128)(2,1)S(1)}, bf16[1,144,768]{2,1,0:T(8,128)(2,1)S(1)}, u32[]{:S(2)}, u32[]{:S(2)}) collective-permute-start(bf16[1,144,768]{2,1,0:T(8,128)(2,1)S(1)} %slice.38), channel_id=1, source_target_pairs={{0,32},{32,0},{1,33},{33,1},{2,34},{34,2},{3,35},{35,3},{4,36},{36... | collective-permute-start | bytes 663560 | tf_op jit(solution)/shard_map/ppermute | solution.py:308
  83.2 16.6 %collective-permute-start.6 = (bf16[1,144,768]{2,1,0:T(8,128)(2,1)S(1)}, bf16[1,144,768]{2,1,0:T(8,128)(2,1)S(1)}, u32[]{:S(2)}, u32[]{:S(2)}) collective-permute-start(bf16[1,144,768]{2,1,0:T(8,128)(2,1)S(1)} %slice.39), channel_id=1, source_target_pairs={{0,32},{32,0},{1,33},{33,1},{2,34},{34,2},{3,35},{35,3},{4,36},{36... | collective-permute-start | bytes 663560 | tf_op jit(solution)/shard_map/ppermute | solution.py:308
  88.4 18.0 %collective-permute-start.3 = (bf16[1,144,768]{2,1,0:T(8,128)(2,1)S(1)}, bf16[1,144,768]{2,1,0:T(8,128)(2,1)S(1)}, u32[]{:S(2)}, u32[]{:S(2)}) collective-permute-start(bf16[1,144,768]{2,1,0:T(8,128)(2,1)S(1)} %slice.37), channel_id=1, source_target_pairs={{0,32},{32,0},{1,33},{33,1},{2,34},{34,2},{3,35},{35,3},{4,36},{36... | collective-permute-start | bytes 663560 | tf_op jit(solution)/shard_map/ppermute | solution.py:308
  110.8 20.4 %all-to-all-start.2 = ((bf16[32,56,128]{2,1,0:T(8,128)(2,1)}), bf16[32,56,128]{2,1,0:T(8,128)(2,1)S(1)}, u32[]{:S(2)}, u32[]{:S(2)}) async-start(bf16[32,56,128]{2,1,0:T(8,128)(2,1)} %bitcast.8), calls=%async_computation.2 | async-start | bytes 917504 | tf_op jit(solution)/shard_map/all_to_all | solution.py:313
  125.2 2.3 %copy-start.2 = (bf16[9216,256]{1,0:T(8,128)(2,1)S(1)}, bf16[9216,256]{1,0:T(8,128)(2,1)}, u32[]{:S(2)}) copy-start(bf16[9216,256]{1,0:T(8,128)(2,1)} %all-gather.6.cloned.1.call-done) | copy-start | bytes 14155780
  127.6 10.4 %copy-start = (bf16[2,1,96,1152]{3,2,1,0:T(8,128)(2,1)S(1)}, bf16[2,1,96,1152]{3,2,1,0:T(8,128)(2,1)}, u32[]{:S(2)}) copy-start(bf16[2,1,96,1152]{3,2,1,0:T(8,128)(2,1)} %param.7) | copy-start | bytes 1327108
  128.9 1.1 copy-start.3
  129.9 1.3 copy-start.6
  131.3 6.7 %collective-permute-start.7 = (bf16[576,1152]{1,0:T(8,128)(2,1)}, bf16[576,1152]{1,0:T(8,128)(2,1)S(1)}, u32[]{:S(2)}, u32[]{:S(2)}) collective-permute-start(bf16[576,1152]{1,0:T(8,128)(2,1)} %copy-done.3), channel_id=1, source_target_pairs={{0,64},{64,0},{1,65},{65,1},{2,66},{66,2},{3,67},{67,3},{4,68},{68... | collective-permute-start | bytes 3981320 | tf_op jit(solution)/shard_map/ppermute | solution.py:318
  138.0 1.3 copy-start.4
  139.3 2.4 %copy-start.5 = (bf16[576,1152]{1,0:T(8,128)(2,1)S(1)}, bf16[576,1152]{1,0:T(8,128)(2,1)}, u32[]{:S(2)}) copy-start(bf16[576,1152]{1,0:T(8,128)(2,1)} %copy-done.3) | copy-start | bytes 3981316
  141.2 11.7 %copy-start.7 = (bf16[864,1152]{1,0:T(8,128)(2,1)S(1)}, bf16[864,1152]{1,0:T(8,128)(2,1)}, u32[]{:S(2)}) copy-start(bf16[864,1152]{1,0:T(8,128)(2,1)} %copy-done.6) | copy-start | bytes 5971972
  141.2 24.6 %collective-permute-start.17 = (bf16[576,1152]{1,0:T(8,128)(2,1)S(1)}, bf16[576,1152]{1,0:T(8,128)(2,1)S(1)}, u32[]{:S(2)}, u32[]{:S(2)}) collective-permute-start(bf16[576,1152]{1,0:T(8,128)(2,1)S(1)} %get-tuple-element.51.own), channel_id=1, source_target_pairs={{0,64},{64,0},{1,65},{65,1},{2,66},{66,2},{3,67},{67,3},{4,68},{68... | collective-permute-start | bytes 3981320 | tf_op jit(solution)/shard_map/ppermute | solution.py:327
  143.6 7.0 %collective-permute-start.11 = (bf16[96,1152]{1,0:T(8,128)(2,1)S(1)}, bf16[96,1152]{1,0:T(8,128)(2,1)S(1)}, u32[]{:S(2)}, u32[]{:S(2)}) collective-permute-start(bf16[96,1152]{1,0:T(8,128)(2,1)S(1)} %get-tuple-element.40.n0), channel_id=1, source_target_pairs={{0,128},{128,0},{1,129},{129,1},{2,130},{130,2},{3,131},{131,3},{4... | collective-permute-start | bytes 663560 | tf_op jit(solution)/shard_map/ppermute | solution.py:330
  144.8 8.1 %collective-permute-start.10 = (bf16[96,1152]{1,0:T(8,128)(2,1)S(1)}, bf16[96,1152]{1,0:T(8,128)(2,1)S(1)}, u32[]{:S(2)}, u32[]{:S(2)}) collective-permute-start(bf16[96,1152]{1,0:T(8,128)(2,1)S(1)} %get-tuple-element.40.n0), channel_id=1, source_target_pairs={{0,64},{64,0},{1,65},{65,1},{2,66},{66,2},{3,67},{67,3},{4,68},{68... | collective-permute-start | bytes 663560 | tf_op jit(solution)/shard_map/ppermute | solution.py:335
  150.6 2.4 %collective-permute-start.12 = (bf16[96,1152]{1,0:T(8,128)(2,1)S(1)}, bf16[96,1152]{1,0:T(8,128)(2,1)S(1)}, u32[]{:S(2)}, u32[]{:S(2)}) collective-permute-start(bf16[96,1152]{1,0:T(8,128)(2,1)S(1)} %collective-permute-done.11.n2), channel_id=1, source_target_pairs={{0,64},{64,0},{1,65},{65,1},{2,66},{66,2},{3,67},{67,3},{4,68},{68... | collective-permute-start | bytes 663560 | tf_op jit(solution)/shard_map/ppermute | solution.py:335
  151.5 7.1 %collective-permute-start.9 = (bf16[96,1152]{1,0:T(8,128)(2,1)S(1)}, bf16[96,1152]{1,0:T(8,128)(2,1)S(1)}, u32[]{:S(2)}, u32[]{:S(2)}) collective-permute-start(bf16[96,1152]{1,0:T(8,128)(2,1)S(1)} %get-tuple-element.39.n0), channel_id=1, source_target_pairs={{0,128},{128,0},{1,129},{129,1},{2,130},{130,2},{3,131},{131,3},{4... | collective-permute-start | bytes 663560 | tf_op jit(solution)/shard_map/ppermute | solution.py:330
  152.7 7.9 %collective-permute-start.8 = (bf16[96,1152]{1,0:T(8,128)(2,1)S(1)}, bf16[96,1152]{1,0:T(8,128)(2,1)S(1)}, u32[]{:S(2)}, u32[]{:S(2)}) collective-permute-start(bf16[96,1152]{1,0:T(8,128)(2,1)S(1)} %get-tuple-element.39.n0), channel_id=1, source_target_pairs={{0,64},{64,0},{1,65},{65,1},{2,66},{66,2},{3,67},{67,3},{4,68},{68... | collective-permute-start | bytes 663560 | tf_op jit(solution)/shard_map/ppermute | solution.py:335
  158.6 2.9 %collective-permute-start.13 = (bf16[96,1152]{1,0:T(8,128)(2,1)S(1)}, bf16[96,1152]{1,0:T(8,128)(2,1)S(1)}, u32[]{:S(2)}, u32[]{:S(2)}) collective-permute-start(bf16[96,1152]{1,0:T(8,128)(2,1)S(1)} %collective-permute-done.9.n2), channel_id=1, source_target_pairs={{0,64},{64,0},{1,65},{65,1},{2,66},{66,2},{3,67},{67,3},{4,68},{68... | collective-permute-start | bytes 663560 | tf_op jit(solution)/shard_map/ppermute | solution.py:335
  159.4 4.4 %collective-permute-start.18 = (bf16[216,128]{1,0:T(8,128)(2,1)S(1)}, bf16[216,128]{1,0:T(8,128)(2,1)S(1)}, u32[]{:S(2)}, u32[]{:S(2)}) collective-permute-start(bf16[216,128]{1,0:T(8,128)(2,1)S(1)} %get-tuple-element.53), channel_id=1, source_target_pairs={{0,64},{64,0},{1,65},{65,1},{2,66},{66,2},{3,67},{67,3},{4,68},{68... | collective-permute-start | bytes 165896 | tf_op jit(solution)/shard_map/ppermute | solution.py:341
  159.4 5.6 %collective-permute-start.19 = (bf16[216,128]{1,0:T(8,128)(2,1)S(1)}, bf16[216,128]{1,0:T(8,128)(2,1)S(1)}, u32[]{:S(2)}, u32[]{:S(2)}) collective-permute-start(bf16[216,128]{1,0:T(8,128)(2,1)S(1)} %get-tuple-element.54), channel_id=1, source_target_pairs={{0,128},{128,0},{1,129},{129,1},{2,130},{130,2},{3,131},{131,3},{4... | collective-permute-start | bytes 165896 | tf_op jit(solution)/shard_map/ppermute | solution.py:342
  160.5 5.3 %collective-permute-start.20 = (bf16[216,128]{1,0:T(8,128)(2,1)S(1)}, bf16[216,128]{1,0:T(8,128)(2,1)S(1)}, u32[]{:S(2)}, u32[]{:S(2)}) collective-permute-start(bf16[216,128]{1,0:T(8,128)(2,1)S(1)} %get-tuple-element.55), channel_id=1, source_target_pairs={{0,192},{192,0},{64,128},{128,64},{1,193},{193,1},{65,129},{129,65... | collective-permute-start | bytes 165896 | tf_op jit(solution)/shard_map/ppermute | solution.py:343
  163.6 4.7 %collective-permute-start.14 = (bf16[216,128]{1,0:T(8,128)(2,1)S(1)}, bf16[216,128]{1,0:T(8,128)(2,1)S(1)}, u32[]{:S(2)}, u32[]{:S(2)}) collective-permute-start(bf16[216,128]{1,0:T(8,128)(2,1)S(1)} %get-tuple-element.46), channel_id=1, source_target_pairs={{0,64},{64,0},{1,65},{65,1},{2,66},{66,2},{3,67},{67,3},{4,68},{68... | collective-permute-start | bytes 165896 | tf_op jit(solution)/shard_map/ppermute | solution.py:341
  163.7 4.6 %collective-permute-start.15 = (bf16[216,128]{1,0:T(8,128)(2,1)S(1)}, bf16[216,128]{1,0:T(8,128)(2,1)S(1)}, u32[]{:S(2)}, u32[]{:S(2)}) collective-permute-start(bf16[216,128]{1,0:T(8,128)(2,1)S(1)} %get-tuple-element.47), channel_id=1, source_target_pairs={{0,128},{128,0},{1,129},{129,1},{2,130},{130,2},{3,131},{131,3},{4... | collective-permute-start | bytes 165896 | tf_op jit(solution)/shard_map/ppermute | solution.py:342
  165.0 4.5 %collective-permute-start.16 = (bf16[216,128]{1,0:T(8,128)(2,1)S(1)}, bf16[216,128]{1,0:T(8,128)(2,1)S(1)}, u32[]{:S(2)}, u32[]{:S(2)}) collective-permute-start(bf16[216,128]{1,0:T(8,128)(2,1)S(1)} %get-tuple-element.48), channel_id=1, source_target_pairs={{0,192},{192,0},{64,128},{128,64},{1,193},{193,1},{65,129},{129,65... | collective-permute-start | bytes 165896 | tf_op jit(solution)/shard_map/ppermute | solution.py:343
Sparse Core Ops, SparseCore 0:
  9.2 53.9 all-gather.3
  65.0 60.2 all-gather.5

commit v8 on v7

--- a/solution.py
+++ b/solution.py
@@ -23,7 +23,7 @@
 TN = (((0,), (0,)), ((), ()))
 NT = (((1,), (1,)), ((), ()))
 SMEM = pl.BlockSpec(memory_space=pltpu.SMEM)
-PARAMS = pltpu.CompilerParams(vmem_limit_bytes=48 * 1024 * 1024)
+PARAMS = pltpu.CompilerParams(vmem_limit_bytes=32 * 1024 * 1024)
 
 
 def normalise(values):
@@ -166,10 +166,13 @@
 
 def prepare(rest, out_a, turned, out_b):
     half, last = D // 2, D // 2 + 12 * HD
-    for n in range(NZ):
+    out_a[:, :256] = rest[0]
+    out_a[:, 256:512] = rest[1]
+    out_a[:, 512:] = rest[2, :, :128]
+    for n in range(2, NZ):
         chunk = rest[n].astype(F32).T.astype(BF)
         low, high = n * 256, (n + 1) * 256
-        for ref, begin, end in ((out_a, 0, half), (turned, half, last), (out_b, last, last + half)):
+        for ref, begin, end in ((turned, half, last), (out_b, last, last + half)):
             first, stop = max(low, begin), min(high, end)
             if first < stop:
                 ref[first - begin : stop - begin] = chunk[first - low : stop - low]
@@ -182,10 +185,8 @@
 def spatial_end(place_ref, att_ref, tok_ref, mod_ref, own, got, resid_ref, norm_ref):
     feats = [unpack(att_ref[n % 2, n // 2].astype(F32), 16) for n in range(HEADS)]
     attended = jnp.concatenate(feats, 0).T.astype(BF)
-    halves = [
-        lax.dot_general(attended, w[...], NT, preferred_element_type=F32) for w in (own, got)
-    ]
-    branch = both_halves(place_ref[0] == 1, *halves)
+    halves = [jnp.dot(attended, w[...], preferred_element_type=F32) for w in (own, got)]
+    branch = both_halves(place_ref[0] == 1, *(h[:, : D // 2] for h in halves))
     resid = tok_ref[...].astype(F32) + mod_ref[2:3, :] * branch
     resid_ref[...] = resid
     norm_ref[...] = (normalise(resid) * (1.0 + mod_ref[4:5, :]) + mod_ref[3:4, :]).astype(BF)
@@ -234,7 +235,7 @@
     return pl.BlockSpec(block, lambda i: place)
 
 
-def once(kernel, args, specs, shapes, out_specs=None, aliases=None, scratch=()):
+def once(kernel, args, specs, shapes, out_specs=None, aliases=None, scratch=(), grant=16):
     return pl.pallas_call(
         kernel,
         grid=(1,),
@@ -243,7 +244,7 @@
         out_shape=shapes,
         input_output_aliases=aliases or {},
         scratch_shapes=scratch,
-        compiler_params=pltpu.CompilerParams(vmem_limit_bytes=24 * 1024 * 1024),
+        compiler_params=pltpu.CompilerParams(vmem_limit_bytes=grant * 1024 * 1024),
         cost_estimate=pl.CostEstimate(
             flops=2_000_000_000, bytes_accessed=8_000_000, transcendentals=0
         ),
@@ -312,8 +313,8 @@
     attended = attended.reshape(NY * NZ, 56, 128)
     attended = lax.all_to_all(attended, ("y", "z"), 0, 0, tiled=True)
     attended = attended.reshape(4, NZ, 56, 128)
-    shapes = [shape(BF, half, D), shape(BF, 12 * HD, D), shape(BF, half, D)]
-    out_a, turned, out_b = once(prepare, [rest], [full(rest)], shapes)
+    shapes = [shape(BF, D, 640), shape(BF, 12 * HD, D), shape(BF, half, D)]
+    out_a, turned, out_b = once(prepare, [rest], [full(rest)], shapes, grant=24)
     swapped, _ = lax.optimization_barrier((out_a, attended))
     got_a = lax.ppermute(swapped, "c", swap)
 
@@ -323,8 +324,6 @@
         specs = [SMEM, full(attended, 2, clip), full(tok, PATCH, clip)]
         specs += [full(a) for a in args[3:]]
         steps.append(once(spatial_end, args, specs, [shape(F32, PATCH, D), shape(BF, PATCH, D)]))
-    swapped, _ = lax.optimization_barrier((out_b, steps[1][1]))
-    got_b = lax.ppermute(swapped, "c", swap)
     diagonal = [(0, 3), (3, 0), (1, 2), (2, 1)]
     sent = []
     moved = [lax.ppermute(norm, "xl", swap) for _, norm in steps]
@@ -335,6 +334,9 @@
         args = [norm, lax.ppermute(norm, "c", swap), norm_x, lax.ppermute(norm_x, "c", swap)]
         args += [turned, gains]
         mixed = once(temporal, args, [full(a) for a in args], [shape(BF, 3 * HD, 128)] * 4)
+        if not sent:
+            swapped, _ = lax.optimization_barrier((out_b, mixed[0]))
+            got_b = lax.ppermute(swapped, "c", swap)
         sent.append(
             [
                 mixed[0],

time: 179 us -> 179 us (level)
  Pallas kernels: 40.1 us -> 37.9 us
  starting transfers between devices: 31.9 us -> 33.8 us
  transfers between devices with their start and end apart: 24 -> 24, of which waited for: 8 -> 9; matrix products, arithmetic and copies ran while one was open for 2% -> 2% of each run, Pallas kernels for 20% -> 18%
where the time goes in v8:
time: 179 us; the launch traced here: 178 us
  blocking collectives  46.7 us (26%)
  Pallas kernels  37.9 us (21%)
  waiting for transfers between devices  36.1 us (20%)
  starting transfers between devices  33.8 us (19%)
  between operations  13.8 us (8%)
  local copies, waits for them, and re-layouts  9.99 us (6%)
    all_to_all x1, blocking collectives, per_device(): shard = lax.all_to_all(shard, ('xh', 'y'), 0, 0, tiled=True).reshape(D, 768)  27 us
    all_to_all x1, blocking collectives, per_device(): lax.all_to_all(shard, 'z', 0, 0, tiled=True).reshape(1, NZ * 18, 768)  19.7 us
    pallas_call x3, Pallas kernels, attention(): pl.pallas_call(functools.partial(attend, count, part is not None, finish)...  19.5 us
    pallas_call x7, Pallas kernels, once(): pl.pallas_call(kernel, grid=(1,), in_specs=specs, out_specs=out_specs or...  13.3 us
    ppermute x4, starting transfers between devices, per_device(): others = [lax.ppermute(block[:, :2 * HD], 'xh', swap) for block in blocks]  8.82 us
    ppermute x2, waiting for transfers between devices, per_device(): moved = [lax.ppermute(norm, 'xl', swap) for _, norm in steps]  8.5 us
    ppermute x3, waiting for transfers between devices, per_device(): lax.ppermute(slots[n], 'y', [(i, (i + n) % NY) for i in range(NY)])  8.35 us
    all_gather x1, waiting for transfers between devices, per_device(): rest = lax.all_gather(rest, 'z', axis=0)  7.82 us
  transfers between devices with their start and end apart: 24, of which 9 were waited for; matrix products, arithmetic and copies ran while one was open for 2% of the time, Pallas kernels for 18%

profile of v8, /device:TPU:1, one launch (start us, length us, event | category | flops | bytes accessed | tf_op | source)
XLA Modules:
  0.0 178.4 jit_solution(5043966426343776430)
XLA Ops:
  6.5 0.7 all-gather.4.cloned.1.call-update
  7.3 1.2 reshape.36
  9.6 19.7 %all_to_all.15 = bf16[8,18,768]{2,1,0:T(8,128)(2,1)S(1)} all-to-all(bf16[8,18,768]{2,1,0:T(8,128)(2,1)S(1)} %copy.16), channel_id=1, replica_groups=mesh['xl'=2,'c'=2,'xh'=2,'y'=4,'z'=8] {'z'}, dimensions={0} | all-to-all | bytes 442368 | tf_op jit(solution)/shard_map/all_to_all | solution.py:278
  29.4 27.0 %all_to_all.16 = bf16[8,144,768]{2,1,0:T(8,128)(2,1)S(1)} all-to-all(bf16[8,144,768]{2,1,0:T(8,128)(2,1)S(1)} %broadcast_in_dim.8), channel_id=1, replica_groups=mesh['xl'=2,'c'=2,'xh'=2,'y'=4,'z'=8] {'xh','y'}, dimensions={0} | all-to-all | bytes 3538944 | tf_op jit(solution)/shard_map/all_to_all | solution.py:280
  56.5 0.9 slice.36
  57.4 5.8 %all-gather.4.cloned.1.call-done.tok_ref = bf16[8,192,1152]{2,1,0:T(8,128)(2,1)} async-done(((bf16[1,192,1152]{2,1,0:T(8,128)(2,1)}), bf16[8,192,1152]{2,1,0:T(8,128)(2,1)}) %all-gather.4.cloned.1.call-update) | async-done | bytes 3538960 | tf_op jit(solution)/shard_map/all_gather | solution.py:282
  63.3 2.0 %copy-done = bf16[8,192,1152]{2,1,0:T(8,128)(2,1)S(1)} copy-done((bf16[8,192,1152]{2,1,0:T(8,128)(2,1)S(1)}, bf16[8,192,1152]{2,1,0:T(8,128)(2,1)}, u32[]{:S(2)}) %copy-start) | copy-done | bytes 3538968
  65.3 5.1 %spatial_proj.1 = (bf16[1,224,768]{2,1,0:T(8,128)(2,1)S(1)}, bf16[1,224,768]{2,1,0:T(8,128)(2,1)S(1)}, bf16[1,224,768]{2,1,0:T(8,128)(2,1)S(1)}, bf16[1,224,768]{2,1,0:T(8,128)(2,1)S(1)}) custom-call(s32[1]{0:T(128)} %bitcast.2.y_ref, bf16[8,192,1152]{2,1,0:T(8,128)(2,1)S(1)} %copy-done, f32[6,1152]{1,0:T(8,128)S(1)} %copy-done.2, ...), custom_call_target="tpu_custom_call" | custom-call | tf_op jit(solution)/shard_map/spatial_proj/pallas_call | solution.py:288
  70.4 1.3 collective-permute-start
  71.7 1.5 collective-permute-start.2
  73.2 1.5 collective-permute-start.1
  74.6 2.7 %collective-permute-start.4 = (bf16[1,144,768]{2,1,0:T(8,128)(2,1)S(1)}, bf16[1,144,768]{2,1,0:T(8,128)(2,1)S(1)}, u32[]{:S(2)}, u32[]{:S(2)}) collective-permute-start(bf16[1,144,768]{2,1,0:T(8,128)(2,1)S(1)} %slice.33), channel_id=1, source_target_pairs={{0,32},{32,0},{1,33},{33,1},{2,34},{34,2},{3,35},{35,3},{4,36},{36... | collective-permute-start | bytes 663560 | tf_op jit(solution)/shard_map/ppermute | solution.py:309
  77.4 3.6 %collective-permute-done.refs_1_.refs_5_ = bf16[1,224,768]{2,1,0:T(8,128)(2,1)S(1)} collective-permute-done((bf16[1,224,768]{2,1,0:T(8,128)(2,1)S(1)}, bf16[1,224,768]{2,1,0:T(8,128)(2,1)S(1)}, u32[]{:S(2)}, u32[]{:S(2)}) %collective-permute-start) | collective-permute-done | bytes 344096 | tf_op jit(solution)/shard_map/ppermute | solution.py:308
  81.0 2.8 %collective-permute-start.5 = (bf16[1,144,768]{2,1,0:T(8,128)(2,1)S(1)}, bf16[1,144,768]{2,1,0:T(8,128)(2,1)S(1)}, u32[]{:S(2)}, u32[]{:S(2)}) collective-permute-start(bf16[1,144,768]{2,1,0:T(8,128)(2,1)S(1)} %slice.38), channel_id=1, source_target_pairs={{0,32},{32,0},{1,33},{33,1},{2,34},{34,2},{3,35},{35,3},{4,36},{36... | collective-permute-start | bytes 663560 | tf_op jit(solution)/shard_map/ppermute | solution.py:309
  84.2 4.7 %collective-permute-done.1.refs_2_.refs_6_ = bf16[1,224,768]{2,1,0:T(8,128)(2,1)S(1)} collective-permute-done((bf16[1,224,768]{2,1,0:T(8,128)(2,1)S(1)}, bf16[1,224,768]{2,1,0:T(8,128)(2,1)S(1)}, u32[]{:S(2)}, u32[]{:S(2)}) %collective-permute-start.1) | collective-permute-done | bytes 344096 | tf_op jit(solution)/shard_map/ppermute | solution.py:308
  88.9 2.9 %collective-permute-start.3 = (bf16[1,144,768]{2,1,0:T(8,128)(2,1)S(1)}, bf16[1,144,768]{2,1,0:T(8,128)(2,1)S(1)}, u32[]{:S(2)}, u32[]{:S(2)}) collective-permute-start(bf16[1,144,768]{2,1,0:T(8,128)(2,1)S(1)} %slice.37), channel_id=1, source_target_pairs={{0,32},{32,0},{1,33},{33,1},{2,34},{34,2},{3,35},{35,3},{4,36},{36... | collective-permute-start | bytes 663560 | tf_op jit(solution)/shard_map/ppermute | solution.py:309
  91.9 8.5 %attend.3.refs_7_ = f32[4,80,768]{2,1,0:T(8,128)S(1)} custom-call(s32[1]{0:T(128)} %bitcast.2.y_ref, bf16[1,224,768]{2,1,0:T(8,128)(2,1)S(1)} %get-tuple-element.32.refs_0_.refs_4_, bf16[1,224,768]{2,1,0:T(8,128)(2,1)S(1)} %collective-permute-done.refs_1_.refs_5_, bf16[1,224,768]{2,1,0:T(8,128)(2,1)S(1)} %collective-permute-done.1.refs_2_.refs_6_, ...), custom_call_target="tpu_custom_call" | custom-call | flops 37748736 | bytes 1000000 | tf_op jit(solution)/shard_map/attend/pallas_call | solution.py:148
  100.4 6.5 %attend.4.refs_5_ = f32[4,80,768]{2,1,0:T(8,128)S(1)} custom-call(s32[1]{0:T(128)} %bitcast.2.y_ref, bf16[1,224,768]{2,1,0:T(8,128)(2,1)S(1)} %get-tuple-element.32.refs_0_.refs_4_, bf16[1,224,768]{2,1,0:T(8,128)(2,1)S(1)} %collective-permute-done.refs_1_.refs_5_, bf16[1,224,768]{2,1,0:T(8,128)(2,1)S(1)} %collective-permute-done.1.refs_2_.refs_6_, ...), custom_call_target="tpu_custom_call" | custom-call | flops 28311552 | bytes 1000000 | tf_op jit(solution)/shard_map/attend/pallas_call | solution.py:148
  107.0 4.5 %attend.5 = bf16[4,8,56,128]{3,2,1,0:T(8,128)(2,1)} custom-call(s32[1]{0:T(128)} %bitcast.2.y_ref, bf16[1,224,768]{2,1,0:T(8,128)(2,1)S(1)} %get-tuple-element.32.refs_0_.refs_4_, bf16[1,224,768]{2,1,0:T(8,128)(2,1)S(1)} %collective-permute-done.refs_1_.refs_5_, bf16[1,224,768]{2,1,0:T(8,128)(2,1)S(1)} %collective-permute-done.1.refs_2_.refs_6_, ...), custom_call_target="tpu_custom_call" | custom-call | flops 9437184 | bytes 1000000 | tf_op jit(solution)/shard_map/attend/pallas_call | solution.py:148
  111.4 5.4 %all-to-all-start.2 = ((bf16[32,56,128]{2,1,0:T(8,128)(2,1)}), bf16[32,56,128]{2,1,0:T(8,128)(2,1)S(1)}, u32[]{:S(2)}, u32[]{:S(2)}) async-start(bf16[32,56,128]{2,1,0:T(8,128)(2,1)} %bitcast.8), calls=%async_computation.2 | async-start | bytes 917504 | tf_op jit(solution)/shard_map/all_to_all | solution.py:314
  116.8 7.8 %all-gather.6.cloned.1.call-done = bf16[9216,256]{1,0:T(8,128)(2,1)} async-done(((bf16[1152,256]{1,0:T(8,128)(2,1)}), bf16[9216,256]{1,0:T(8,128)(2,1)}) %all-gather.6.cloned.1.call-update) | async-done | bytes 4718608 | tf_op jit(solution)/shard_map/all_gather | solution.py:285
  124.6 2.3 %copy-done.3 = bf16[9216,256]{1,0:T(8,128)(2,1)S(1)} copy-done((bf16[9216,256]{1,0:T(8,128)(2,1)S(1)}, bf16[9216,256]{1,0:T(8,128)(2,1)}, u32[]{:S(2)}) %copy-start.3) | copy-done | bytes 4718616
  127.0 1.1 prepare.1
  128.0 1.1 copy-done.4
  129.1 1.3 copy-done.6
  130.4 4.9 %collective-permute-start.7 = (bf16[1152,640]{1,0:T(8,128)(2,1)S(1)}, bf16[1152,640]{1,0:T(8,128)(2,1)S(1)}, u32[]{:S(2)}, u32[]{:S(2)}) collective-permute-start(bf16[1152,640]{1,0:T(8,128)(2,1)S(1)} %get-tuple-element.38.own), channel_id=1, source_target_pairs={{0,64},{64,0},{1,65},{65,1},{2,66},{66,2},{3,67},{67,3},{4,68},{68... | collective-permute-start | bytes 4423688 | tf_op jit(solution)/shard_map/ppermute | solution.py:319
  135.4 2.8 %collective-permute-done.7.got = bf16[1152,640]{1,0:T(8,128)(2,1)S(1)} collective-permute-done((bf16[1152,640]{1,0:T(8,128)(2,1)S(1)}, bf16[1152,640]{1,0:T(8,128)(2,1)S(1)}, u32[]{:S(2)}, u32[]{:S(2)}) %collective-permute-start.7) | collective-permute-done | bytes 1474592 | tf_op jit(solution)/shard_map/ppermute | solution.py:319
  138.2 1.6 spatial_end.3
  139.8 1.1 collective-permute-start.11
  140.9 0.7 collective-permute-start.10
  141.6 1.6 spatial_end.2
  143.2 3.4 %collective-permute-done.11.n2 = bf16[96,1152]{1,0:T(8,128)(2,1)S(1)} collective-permute-done((bf16[96,1152]{1,0:T(8,128)(2,1)S(1)}, bf16[96,1152]{1,0:T(8,128)(2,1)S(1)}, u32[]{:S(2)}, u32[]{:S(2)}) %collective-permute-start.11) | collective-permute-done | bytes 221216 | tf_op jit(solution)/shard_map/ppermute | solution.py:329
  146.6 1.2 collective-permute-start.12
  147.8 1.1 collective-permute-done.12.n3
  148.9 2.1 %temporal.2 = (bf16[216,128]{1,0:T(8,128)(2,1)S(1)}, bf16[216,128]{1,0:T(8,128)(2,1)S(1)}, bf16[216,128]{1,0:T(8,128)(2,1)S(1)}, bf16[216,128]{1,0:T(8,128)(2,1)S(1)}) custom-call(bf16[96,1152]{1,0:T(8,128)(2,1)S(1)} %get-tuple-element.40.n0, bf16[96,1152]{1,0:T(8,128)(2,1)S(1)} %collective-permute-done.10.n1, ...), custom_call_target="tpu_custom_call" | custom-call | flops 2000000000 | bytes 8000000 | tf_op jit(solution)/shard_map/temporal/pallas_call | solution.py:239
  151.0 0.5 collective-permute-start.17
  151.5 1.0 collective-permute-start.9
  152.4 0.6 collective-permute-start.8
  153.0 5.1 %collective-permute-done.9.n2 = bf16[96,1152]{1,0:T(8,128)(2,1)S(1)} collective-permute-done((bf16[96,1152]{1,0:T(8,128)(2,1)S(1)}, bf16[96,1152]{1,0:T(8,128)(2,1)S(1)}, u32[]{:S(2)}, u32[]{:S(2)}) %collective-permute-start.9) | collective-permute-done | bytes 221216 | tf_op jit(solution)/shard_map/ppermute | solution.py:329
  158.2 1.1 collective-permute-start.13
  159.3 1.0 collective-permute-start.19
  160.3 1.2 collective-permute-start.20
  161.4 2.1 %temporal.3 = (bf16[216,128]{1,0:T(8,128)(2,1)S(1)}, bf16[216,128]{1,0:T(8,128)(2,1)S(1)}, bf16[216,128]{1,0:T(8,128)(2,1)S(1)}, bf16[216,128]{1,0:T(8,128)(2,1)S(1)}) custom-call(bf16[96,1152]{1,0:T(8,128)(2,1)S(1)} %get-tuple-element.39.n0, bf16[96,1152]{1,0:T(8,128)(2,1)S(1)} %collective-permute-done.8.n1, ...), custom_call_target="tpu_custom_call" | custom-call | flops 2000000000 | bytes 8000000 | tf_op jit(solution)/shard_map/temporal/pallas_call | solution.py:239
  163.7 1.1 collective-permute-start.15
  164.7 1.1 collective-permute-start.16
  165.8 2.4 %temporal_end.2.refs_0_ = bf16[192,1152]{1,0:T(8,128)(2,1)} custom-call(s32[2]{0:T(128)S(1)} %pad_add_fusion.place_ref, bf16[216,128]{1,0:T(8,128)(2,1)S(1)} %get-tuple-element.52.m0, bf16[216,128]{1,0:T(8,128)(2,1)S(1)} %collective-permute-done.18.m1, bf16[216,128]{1,0:T(8,128)(2,1)S(1)} %collective-permute-done.19.m2, ...), custom_call_target="tpu_custom_call" | custom-call | flops 2000000000 | bytes 8000000 | tf_op jit(solution)/shard_map/temporal_end/pallas_call | solution.py:239
  168.2 1.0 collective-permute-done.16.m3
  169.2 2.4 %temporal_end.3 = bf16[192,1152]{1,0:T(8,128)(2,1)} custom-call(s32[2]{0:T(128)S(1)} %pad_add_fusion.place_ref, bf16[216,128]{1,0:T(8,128)(2,1)S(1)} %get-tuple-element.45.m0, bf16[216,128]{1,0:T(8,128)(2,1)S(1)} %collective-permute-done.14.m1, bf16[216,128]{1,0:T(8,128)(2,1)S(1)} %collective-permute-done.15.m2, ...), custom_call_target="tpu_custom_call", output_to_operand_aliasing={{}: (9, {})} | custom-call | flops 2000000000 | bytes 8000000 | tf_op jit(solution)/shard_map/temporal_end/pallas_call | solution.py:239
  (61 shorter events, 1.9 us)
Async XLA Ops:
  6.5 2.3 %copy-start.8 = (bf16[18,3456]{1,0:T(8,128)(2,1)S(1)}, bf16[18,3456]{1,0:T(8,128)(2,1)}, u32[]{:S(2)}) copy-start(bf16[18,3456]{1,0:T(8,128)(2,1)} %param.11) | copy-start | bytes 373252
  6.5 2.6 %copy-start.9 = (bf16[18,1152]{1,0:T(8,128)(2,1)S(1)}, bf16[18,1152]{1,0:T(8,128)(2,1)}, u32[]{:S(2)}) copy-start(bf16[18,1152]{1,0:T(8,128)(2,1)} %param.12) | copy-start | bytes 124420
  6.5 2.6 %copy-start.10 = (bf16[18,1152]{1,0:T(8,128)(2,1)S(1)}, bf16[18,1152]{1,0:T(8,128)(2,1)}, u32[]{:S(2)}) copy-start(bf16[18,1152]{1,0:T(8,128)(2,1)} %param.10) | copy-start | bytes 124420
  6.5 56.6 %all-gather.4.cloned.1.call-start = ((), (), s32[]{:S(2)}) async-start(), calls=%async_computation.3 | async-start | bytes 3981312 | tf_op jit(solution)/shard_map/all_gather | solution.py:282
  7.3 117.3 %all-gather.6.cloned.1.call-start = ((), (), s32[]{:S(2)}) async-start(), calls=%async_computation.4 | async-start | bytes 5308416 | tf_op jit(solution)/shard_map/all_gather | solution.py:285
  56.4 6.8 %copy-start.11 = (f32[4,72]{1,0:T(4,128)S(1)}, f32[4,72]{1,0:T(4,128)}, u32[]{:S(2)}) copy-start(f32[4,72]{1,0:T(4,128)} %param.13) | copy-start | bytes 3460
  56.4 6.9 %copy-start.2 = (f32[6,1152]{1,0:T(8,128)S(1)}, f32[6,1152]{1,0:T(8,128)}, u32[]{:S(2)}) copy-start(f32[6,1152]{1,0:T(8,128)} %mod_ref.9) | copy-start | bytes 82948
  63.3 2.0 %copy-start = (bf16[8,192,1152]{2,1,0:T(8,128)(2,1)S(1)}, bf16[8,192,1152]{2,1,0:T(8,128)(2,1)}, u32[]{:S(2)}) copy-start(bf16[8,192,1152]{2,1,0:T(8,128)(2,1)} %all-gather.4.cloned.1.call-done.tok_ref) | copy-start | bytes 10616836
  70.4 10.6 %collective-permute-start = (bf16[1,224,768]{2,1,0:T(8,128)(2,1)S(1)}, bf16[1,224,768]{2,1,0:T(8,128)(2,1)S(1)}, u32[]{:S(2)}, u32[]{:S(2)}) collective-permute-start(bf16[1,224,768]{2,1,0:T(8,128)(2,1)S(1)} %get-tuple-element.33), channel_id=1, source_target_pairs={{0,8},{8,16},{16,24},{24,0},{1,9},{9,17},{17,25},{25,1},{2,10},{10... | collective-permute-start | bytes 1032200 | tf_op jit(solution)/shard_map/ppermute | solution.py:308
  71.7 12.1 %collective-permute-start.2 = (bf16[1,224,768]{2,1,0:T(8,128)(2,1)S(1)}, bf16[1,224,768]{2,1,0:T(8,128)(2,1)S(1)}, u32[]{:S(2)}, u32[]{:S(2)}) collective-permute-start(bf16[1,224,768]{2,1,0:T(8,128)(2,1)S(1)} %get-tuple-element.35), channel_id=1, source_target_pairs={{0,24},{8,0},{16,8},{24,16},{1,25},{9,1},{17,9},{25,17},{2,26},{10... | collective-permute-start | bytes 1032200 | tf_op jit(solution)/shard_map/ppermute | solution.py:308
  73.2 15.8 %collective-permute-start.1 = (bf16[1,224,768]{2,1,0:T(8,128)(2,1)S(1)}, bf16[1,224,768]{2,1,0:T(8,128)(2,1)S(1)}, u32[]{:S(2)}, u32[]{:S(2)}) collective-permute-start(bf16[1,224,768]{2,1,0:T(8,128)(2,1)S(1)} %get-tuple-element.34), channel_id=1, source_target_pairs={{0,16},{8,24},{16,0},{24,8},{1,17},{9,25},{17,1},{25,9},{2,18},{10... | collective-permute-start | bytes 1032200 | tf_op jit(solution)/shard_map/ppermute | solution.py:308
  74.6 25.8 %collective-permute-start.4 = (bf16[1,144,768]{2,1,0:T(8,128)(2,1)S(1)}, bf16[1,144,768]{2,1,0:T(8,128)(2,1)S(1)}, u32[]{:S(2)}, u32[]{:S(2)}) collective-permute-start(bf16[1,144,768]{2,1,0:T(8,128)(2,1)S(1)} %slice.33), channel_id=1, source_target_pairs={{0,32},{32,0},{1,33},{33,1},{2,34},{34,2},{3,35},{35,3},{4,36},{36... | collective-permute-start | bytes 663560 | tf_op jit(solution)/shard_map/ppermute | solution.py:309
  81.0 19.4 %collective-permute-start.5 = (bf16[1,144,768]{2,1,0:T(8,128)(2,1)S(1)}, bf16[1,144,768]{2,1,0:T(8,128)(2,1)S(1)}, u32[]{:S(2)}, u32[]{:S(2)}) collective-permute-start(bf16[1,144,768]{2,1,0:T(8,128)(2,1)S(1)} %slice.38), channel_id=1, source_target_pairs={{0,32},{32,0},{1,33},{33,1},{2,34},{34,2},{3,35},{35,3},{4,36},{36... | collective-permute-start | bytes 663560 | tf_op jit(solution)/shard_map/ppermute | solution.py:309
  83.8 16.6 %collective-permute-start.6 = (bf16[1,144,768]{2,1,0:T(8,128)(2,1)S(1)}, bf16[1,144,768]{2,1,0:T(8,128)(2,1)S(1)}, u32[]{:S(2)}, u32[]{:S(2)}) collective-permute-start(bf16[1,144,768]{2,1,0:T(8,128)(2,1)S(1)} %slice.39), channel_id=1, source_target_pairs={{0,32},{32,0},{1,33},{33,1},{2,34},{34,2},{3,35},{35,3},{4,36},{36... | collective-permute-start | bytes 663560 | tf_op jit(solution)/shard_map/ppermute | solution.py:309
  88.9 18.0 %collective-permute-start.3 = (bf16[1,144,768]{2,1,0:T(8,128)(2,1)S(1)}, bf16[1,144,768]{2,1,0:T(8,128)(2,1)S(1)}, u32[]{:S(2)}, u32[]{:S(2)}) collective-permute-start(bf16[1,144,768]{2,1,0:T(8,128)(2,1)S(1)} %slice.37), channel_id=1, source_target_pairs={{0,32},{32,0},{1,33},{33,1},{2,34},{34,2},{3,35},{35,3},{4,36},{36... | collective-permute-start | bytes 663560 | tf_op jit(solution)/shard_map/ppermute | solution.py:309
  111.4 19.0 %all-to-all-start.2 = ((bf16[32,56,128]{2,1,0:T(8,128)(2,1)}), bf16[32,56,128]{2,1,0:T(8,128)(2,1)S(1)}, u32[]{:S(2)}, u32[]{:S(2)}) async-start(bf16[32,56,128]{2,1,0:T(8,128)(2,1)} %bitcast.8), calls=%async_computation.2 | async-start | bytes 917504 | tf_op jit(solution)/shard_map/all_to_all | solution.py:314
  124.6 2.3 %copy-start.3 = (bf16[9216,256]{1,0:T(8,128)(2,1)S(1)}, bf16[9216,256]{1,0:T(8,128)(2,1)}, u32[]{:S(2)}) copy-start(bf16[9216,256]{1,0:T(8,128)(2,1)} %all-gather.6.cloned.1.call-done) | copy-start | bytes 14155780
  126.9 11.2 %copy-start.1 = (bf16[2,1,96,1152]{3,2,1,0:T(8,128)(2,1)S(1)}, bf16[2,1,96,1152]{3,2,1,0:T(8,128)(2,1)}, u32[]{:S(2)}) copy-start(bf16[2,1,96,1152]{3,2,1,0:T(8,128)(2,1)} %param.7) | copy-start | bytes 1327108
  128.0 1.1 copy-start.4
  129.1 1.3 copy-start.6
  130.4 7.8 %collective-permute-start.7 = (bf16[1152,640]{1,0:T(8,128)(2,1)S(1)}, bf16[1152,640]{1,0:T(8,128)(2,1)S(1)}, u32[]{:S(2)}, u32[]{:S(2)}) collective-permute-start(bf16[1152,640]{1,0:T(8,128)(2,1)S(1)} %get-tuple-element.38.own), channel_id=1, source_target_pairs={{0,64},{64,0},{1,65},{65,1},{2,66},{66,2},{3,67},{67,3},{4,68},{68... | collective-permute-start | bytes 4423688 | tf_op jit(solution)/shard_map/ppermute | solution.py:319
  139.8 9.0 %copy-start.7 = (bf16[864,1152]{1,0:T(8,128)(2,1)S(1)}, bf16[864,1152]{1,0:T(8,128)(2,1)}, u32[]{:S(2)}) copy-start(bf16[864,1152]{1,0:T(8,128)(2,1)} %copy-done.6) | copy-start | bytes 5971972
  139.8 6.7 %collective-permute-start.11 = (bf16[96,1152]{1,0:T(8,128)(2,1)S(1)}, bf16[96,1152]{1,0:T(8,128)(2,1)S(1)}, u32[]{:S(2)}, u32[]{:S(2)}) collective-permute-start(bf16[96,1152]{1,0:T(8,128)(2,1)S(1)} %get-tuple-element.40.n0), channel_id=1, source_target_pairs={{0,128},{128,0},{1,129},{129,1},{2,130},{130,2},{3,131},{131,3},{4... | collective-permute-start | bytes 663560 | tf_op jit(solution)/shard_map/ppermute | solution.py:329
  140.9 6.9 %collective-permute-start.10 = (bf16[96,1152]{1,0:T(8,128)(2,1)S(1)}, bf16[96,1152]{1,0:T(8,128)(2,1)S(1)}, u32[]{:S(2)}, u32[]{:S(2)}) collective-permute-start(bf16[96,1152]{1,0:T(8,128)(2,1)S(1)} %get-tuple-element.40.n0), channel_id=1, source_target_pairs={{0,64},{64,0},{1,65},{65,1},{2,66},{66,2},{3,67},{67,3},{4,68},{68... | collective-permute-start | bytes 663560 | tf_op jit(solution)/shard_map/ppermute | solution.py:334
  146.6 2.3 %collective-permute-start.12 = (bf16[96,1152]{1,0:T(8,128)(2,1)S(1)}, bf16[96,1152]{1,0:T(8,128)(2,1)S(1)}, u32[]{:S(2)}, u32[]{:S(2)}) collective-permute-start(bf16[96,1152]{1,0:T(8,128)(2,1)S(1)} %collective-permute-done.11.n2), channel_id=1, source_target_pairs={{0,64},{64,0},{1,65},{65,1},{2,66},{66,2},{3,67},{67,3},{4,68},{68... | collective-permute-start | bytes 663560 | tf_op jit(solution)/shard_map/ppermute | solution.py:334
  148.9 2.1 %copy-start.5 = (bf16[576,1152]{1,0:T(8,128)(2,1)S(1)}, bf16[576,1152]{1,0:T(8,128)(2,1)}, u32[]{:S(2)}) copy-start(bf16[576,1152]{1,0:T(8,128)(2,1)} %copy-done.4) | copy-start | bytes 3981316
  151.0 14.8 %collective-permute-start.17 = (bf16[576,1152]{1,0:T(8,128)(2,1)S(1)}, bf16[576,1152]{1,0:T(8,128)(2,1)S(1)}, u32[]{:S(2)}, u32[]{:S(2)}) collective-permute-start(bf16[576,1152]{1,0:T(8,128)(2,1)S(1)} %copy-done.5), channel_id=1, source_target_pairs={{0,64},{64,0},{1,65},{65,1},{2,66},{66,2},{3,67},{67,3},{4,68},{68... | collective-permute-start | bytes 3981320 | tf_op jit(solution)/shard_map/ppermute | solution.py:339
  151.5 6.7 %collective-permute-start.9 = (bf16[96,1152]{1,0:T(8,128)(2,1)S(1)}, bf16[96,1152]{1,0:T(8,128)(2,1)S(1)}, u32[]{:S(2)}, u32[]{:S(2)}) collective-permute-start(bf16[96,1152]{1,0:T(8,128)(2,1)S(1)} %get-tuple-element.39.n0), channel_id=1, source_target_pairs={{0,128},{128,0},{1,129},{129,1},{2,130},{130,2},{3,131},{131,3},{4... | collective-permute-start | bytes 663560 | tf_op jit(solution)/shard_map/ppermute | solution.py:329
  152.4 7.9 %collective-permute-start.8 = (bf16[96,1152]{1,0:T(8,128)(2,1)S(1)}, bf16[96,1152]{1,0:T(8,128)(2,1)S(1)}, u32[]{:S(2)}, u32[]{:S(2)}) collective-permute-start(bf16[96,1152]{1,0:T(8,128)(2,1)S(1)} %get-tuple-element.39.n0), channel_id=1, source_target_pairs={{0,64},{64,0},{1,65},{65,1},{2,66},{66,2},{3,67},{67,3},{4,68},{68... | collective-permute-start | bytes 663560 | tf_op jit(solution)/shard_map/ppermute | solution.py:334
  158.2 3.3 %collective-permute-start.13 = (bf16[96,1152]{1,0:T(8,128)(2,1)S(1)}, bf16[96,1152]{1,0:T(8,128)(2,1)S(1)}, u32[]{:S(2)}, u32[]{:S(2)}) collective-permute-start(bf16[96,1152]{1,0:T(8,128)(2,1)S(1)} %collective-permute-done.9.n2), channel_id=1, source_target_pairs={{0,64},{64,0},{1,65},{65,1},{2,66},{66,2},{3,67},{67,3},{4,68},{68... | collective-permute-start | bytes 663560 | tf_op jit(solution)/shard_map/ppermute | solution.py:334
  159.3 4.4 %collective-permute-start.18 = (bf16[216,128]{1,0:T(8,128)(2,1)S(1)}, bf16[216,128]{1,0:T(8,128)(2,1)S(1)}, u32[]{:S(2)}, u32[]{:S(2)}) collective-permute-start(bf16[216,128]{1,0:T(8,128)(2,1)S(1)} %get-tuple-element.53), channel_id=1, source_target_pairs={{0,64},{64,0},{1,65},{65,1},{2,66},{66,2},{3,67},{67,3},{4,68},{68... | collective-permute-start | bytes 165896 | tf_op jit(solution)/shard_map/ppermute | solution.py:343
  159.3 5.4 %collective-permute-start.19 = (bf16[216,128]{1,0:T(8,128)(2,1)S(1)}, bf16[216,128]{1,0:T(8,128)(2,1)S(1)}, u32[]{:S(2)}, u32[]{:S(2)}) collective-permute-start(bf16[216,128]{1,0:T(8,128)(2,1)S(1)} %get-tuple-element.54), channel_id=1, source_target_pairs={{0,128},{128,0},{1,129},{129,1},{2,130},{130,2},{3,131},{131,3},{4... | collective-permute-start | bytes 165896 | tf_op jit(solution)/shard_map/ppermute | solution.py:344
  160.3 5.5 %collective-permute-start.20 = (bf16[216,128]{1,0:T(8,128)(2,1)S(1)}, bf16[216,128]{1,0:T(8,128)(2,1)S(1)}, u32[]{:S(2)}, u32[]{:S(2)}) collective-permute-start(bf16[216,128]{1,0:T(8,128)(2,1)S(1)} %get-tuple-element.55), channel_id=1, source_target_pairs={{0,192},{192,0},{64,128},{128,64},{1,193},{193,1},{65,129},{129,65... | collective-permute-start | bytes 165896 | tf_op jit(solution)/shard_map/ppermute | solution.py:345
  163.6 4.7 %collective-permute-start.14 = (bf16[216,128]{1,0:T(8,128)(2,1)S(1)}, bf16[216,128]{1,0:T(8,128)(2,1)S(1)}, u32[]{:S(2)}, u32[]{:S(2)}) collective-permute-start(bf16[216,128]{1,0:T(8,128)(2,1)S(1)} %get-tuple-element.46), channel_id=1, source_target_pairs={{0,64},{64,0},{1,65},{65,1},{2,66},{66,2},{3,67},{67,3},{4,68},{68... | collective-permute-start | bytes 165896 | tf_op jit(solution)/shard_map/ppermute | solution.py:343
  163.7 4.6 %collective-permute-start.15 = (bf16[216,128]{1,0:T(8,128)(2,1)S(1)}, bf16[216,128]{1,0:T(8,128)(2,1)S(1)}, u32[]{:S(2)}, u32[]{:S(2)}) collective-permute-start(bf16[216,128]{1,0:T(8,128)(2,1)S(1)} %get-tuple-element.47), channel_id=1, source_target_pairs={{0,128},{128,0},{1,129},{129,1},{2,130},{130,2},{3,131},{131,3},{4... | collective-permute-start | bytes 165896 | tf_op jit(solution)/shard_map/ppermute | solution.py:344
  164.7 4.5 %collective-permute-start.16 = (bf16[216,128]{1,0:T(8,128)(2,1)S(1)}, bf16[216,128]{1,0:T(8,128)(2,1)S(1)}, u32[]{:S(2)}, u32[]{:S(2)}) collective-permute-start(bf16[216,128]{1,0:T(8,128)(2,1)S(1)} %get-tuple-element.48), channel_id=1, source_target_pairs={{0,192},{192,0},{64,128},{128,64},{1,193},{193,1},{65,129},{129,65... | collective-permute-start | bytes 165896 | tf_op jit(solution)/shard_map/ppermute | solution.py:345
Sparse Core Ops, SparseCore 0:
  9.2 53.9 all-gather.3
  65.0 59.6 all-gather.5

commit v9 on v8

--- a/solution.py
+++ b/solution.py
@@ -124,7 +124,7 @@
     if not finish:
         out_ref[0] = done
         return
-    done = done[:HD] / done[HD : HD + 1]
+    done = done[:HD] * (1.0 / done[HD : HD + 1])
     home = (y_ref[0] + NY - place) % NY
     for z in range(NZ):
         out_ref[home, z] = pack(done[:, z * PATCH : (z + 1) * PATCH], 56).astype(BF)
@@ -298,7 +298,7 @@
         out_specs=[pl.BlockSpec((1, 3 * HD + 8, 4 * PATCH), lambda i: (0, 0, i))] * NY,
         out_shape=[shape(BF, 1, 3 * HD + 8, PLANE)] * NY,
         scratch_shapes=[pltpu.VMEM((512, D), BF)],
-        compiler_params=PARAMS,
+        compiler_params=pltpu.CompilerParams(vmem_limit_bytes=48 * 1024 * 1024),
         name="spatial_proj",
     )(y_place, column, modulation, shard, gains)
 
@@ -307,9 +307,8 @@
     for n in (1, 3, 2):
         blocks[n] = lax.ppermute(slots[n], "y", [(i, (i + n) % NY) for i in range(NY)])
     others = [lax.ppermute(block[:, : 2 * HD], "xh", swap) for block in blocks]
-    part = attention(y_place, blocks, blocks, None, False)
-    part = attention(y_place, blocks, [others[n] for n in (0, 1, 3)], part, False)
-    attended = attention(y_place, blocks, [others[2]], part, True)
+    part = attention(y_place, blocks, [blocks[n] for n in (0, 1, 3, 2)], None, False)
+    attended = attention(y_place, blocks, [others[n] for n in (0, 1, 3, 2)], part, True)
     attended = attended.reshape(NY * NZ, 56, 128)
     attended = lax.all_to_all(attended, ("y", "z"), 0, 0, tiled=True)
     attended = attended.reshape(4, NZ, 56, 128)
@@ -317,6 +316,8 @@
     out_a, turned, out_b = once(prepare, [rest], [full(rest)], shapes, grant=24)
     swapped, _ = lax.optimization_barrier((out_a, attended))
     got_a = lax.ppermute(swapped, "c", swap)
+    swapped, _ = lax.optimization_barrier((out_b, got_a))
+    got_b = lax.ppermute(swapped, "c", swap)
 
     steps = []
     for clip in range(2):
@@ -334,9 +335,6 @@
         args = [norm, lax.ppermute(norm, "c", swap), norm_x, lax.ppermute(norm_x, "c", swap)]
         args += [turned, gains]
         mixed = once(temporal, args, [full(a) for a in args], [shape(BF, 3 * HD, 128)] * 4)
-        if not sent:
-            swapped, _ = lax.optimization_barrier((out_b, mixed[0]))
-            got_b = lax.ppermute(swapped, "c", swap)
         sent.append(
             [
                 mixed[0],

time: 179 us -> 176 us (0.983)
  starting transfers between devices: 33.8 us -> 31 us
  waiting for transfers between devices: 36.1 us -> 38.4 us
  local copies, waits for them, and re-layouts: 9.99 us -> 8.01 us
    all_gather x1, waiting for transfers between devices: 7.82 us -> 12.3 us  [per_device(): rest = lax.all_gather(rest, 'z', axis=0)]
    ppermute x1, starting transfers between devices: 4.9 us -> 1.97 us  [per_device(): got_a = lax.ppermute(swapped, 'c', swap)]
    unnamed x26 -> x24, local copies, waits for them, and re-layouts: 6.86 us -> 4.87 us
    pallas_call x3 -> x2, Pallas kernels: 19.5 us -> 18.3 us  [attention(): pl.pallas_call(functools.partial(attend, count, part is not None, finish)...]
  transfers between devices with their start and end apart: 24 -> 24, of which waited for: 9 -> 8; matrix products, arithmetic and copies ran while one was open for 2% -> 2% of each run, Pallas kernels for 18% -> 20%
where the time goes in v9:
time: 176 us
  blocking collectives  46.7 us (27%)
  waiting for transfers between devices  38.4 us (22%)
  Pallas kernels  38.1 us (22%)
  starting transfers between devices  31 us (18%)
  between operations  13.7 us (8%)
  local copies, waits for them, and re-layouts  8.01 us (5%)
    all_to_all x1, blocking collectives, per_device(): shard = lax.all_to_all(shard, ('xh', 'y'), 0, 0, tiled=True).reshape(D, 768)  27 us
    all_to_all x1, blocking collectives, per_device(): lax.all_to_all(shard, 'z', 0, 0, tiled=True).reshape(1, NZ * 18, 768)  19.7 us
    pallas_call x2, Pallas kernels, attention(): pl.pallas_call(functools.partial(attend, count, part is not None, finish)...  18.3 us
    pallas_call x7, Pallas kernels, once(): pl.pallas_call(kernel, grid=(1,), in_specs=specs, out_specs=out_specs or...  13.3 us
    all_gather x1, waiting for transfers between devices, per_device(): rest = lax.all_gather(rest, 'z', axis=0)  12.3 us
    ppermute x4, starting transfers between devices, per_device(): others = [lax.ppermute(block[:, :2 * HD], 'xh', swap) for block in blocks]  8.82 us
    ppermute x3, waiting for transfers between devices, per_device(): lax.ppermute(slots[n], 'y', [(i, (i + n) % NY) for i in range(NY)])  8.36 us
    ppermute x2, waiting for transfers between devices, per_device(): moved = [lax.ppermute(norm, 'xl', swap) for _, norm in steps]  6.8 us
  transfers between devices with their start and end apart: 24, of which 8 were waited for; matrix products, arithmetic and copies ran while one was open for 2% of the time, Pallas kernels for 20%

profile of v9, /device:TPU:1, one launch (start us, length us, event | category | flops | bytes accessed | tf_op | source)
XLA Modules:
  0.0 176.1 jit_solution(9311702142512322146)
XLA Ops:
  6.5 0.7 all-gather.4.cloned.1.call-update
  7.3 1.2 reshape.36
  8.7 0.2 reshape.37
  9.6 19.7 %all_to_all.15 = bf16[8,18,768]{2,1,0:T(8,128)(2,1)S(1)} all-to-all(bf16[8,18,768]{2,1,0:T(8,128)(2,1)S(1)} %copy.16), channel_id=1, replica_groups=mesh['xl'=2,'c'=2,'xh'=2,'y'=4,'z'=8] {'z'}, dimensions={0} | all-to-all | bytes 442368 | tf_op jit(solution)/shard_map/all_to_all | solution.py:278
  29.4 27.0 %all_to_all.16 = bf16[8,144,768]{2,1,0:T(8,128)(2,1)S(1)} all-to-all(bf16[8,144,768]{2,1,0:T(8,128)(2,1)S(1)} %broadcast_in_dim.8), channel_id=1, replica_groups=mesh['xl'=2,'c'=2,'xh'=2,'y'=4,'z'=8] {'xh','y'}, dimensions={0} | all-to-all | bytes 3538944 | tf_op jit(solution)/shard_map/all_to_all | solution.py:280
  56.5 0.9 slice.36
  57.4 5.8 %all-gather.4.cloned.1.call-done.tok_ref = bf16[8,192,1152]{2,1,0:T(8,128)(2,1)} async-done(((bf16[1,192,1152]{2,1,0:T(8,128)(2,1)}), bf16[8,192,1152]{2,1,0:T(8,128)(2,1)}) %all-gather.4.cloned.1.call-update) | async-done | bytes 3538960 | tf_op jit(solution)/shard_map/all_gather | solution.py:282
  63.3 6.5 %spatial_proj.1 = (bf16[1,224,768]{2,1,0:T(8,128)(2,1)S(1)}, bf16[1,224,768]{2,1,0:T(8,128)(2,1)S(1)}, bf16[1,224,768]{2,1,0:T(8,128)(2,1)S(1)}, bf16[1,224,768]{2,1,0:T(8,128)(2,1)S(1)}) custom-call(s32[1]{0:T(128)} %bitcast.2.y_ref, bf16[8,192,1152]{2,1,0:T(8,128)(2,1)} %all-gather.4.cloned.1.call-done.tok_ref, f32[6,1152]{1,0:T(8,128)S(1)} %copy-done.1, ...), custom_call_target="tpu_custom_call" | custom-call | tf_op jit(solution)/shard_map/spatial_proj/pallas_call | solution.py:288
  69.8 1.3 collective-permute-start
  71.1 1.5 collective-permute-start.2
  72.6 1.5 collective-permute-start.1
  74.0 2.7 %collective-permute-start.3 = (bf16[1,144,768]{2,1,0:T(8,128)(2,1)S(1)}, bf16[1,144,768]{2,1,0:T(8,128)(2,1)S(1)}, u32[]{:S(2)}, u32[]{:S(2)}) collective-permute-start(bf16[1,144,768]{2,1,0:T(8,128)(2,1)S(1)} %slice.32), channel_id=1, source_target_pairs={{0,32},{32,0},{1,33},{33,1},{2,34},{34,2},{3,35},{35,3},{4,36},{36... | collective-permute-start | bytes 663560 | tf_op jit(solution)/shard_map/ppermute | solution.py:309
  76.8 3.6 %collective-permute-done.refs_1_.refs_5_ = bf16[1,224,768]{2,1,0:T(8,128)(2,1)S(1)} collective-permute-done((bf16[1,224,768]{2,1,0:T(8,128)(2,1)S(1)}, bf16[1,224,768]{2,1,0:T(8,128)(2,1)S(1)}, u32[]{:S(2)}, u32[]{:S(2)}) %collective-permute-start) | collective-permute-done | bytes 344096 | tf_op jit(solution)/shard_map/ppermute | solution.py:308
  80.4 2.8 %collective-permute-start.4 = (bf16[1,144,768]{2,1,0:T(8,128)(2,1)S(1)}, bf16[1,144,768]{2,1,0:T(8,128)(2,1)S(1)}, u32[]{:S(2)}, u32[]{:S(2)}) collective-permute-start(bf16[1,144,768]{2,1,0:T(8,128)(2,1)S(1)} %slice.37), channel_id=1, source_target_pairs={{0,32},{32,0},{1,33},{33,1},{2,34},{34,2},{3,35},{35,3},{4,36},{36... | collective-permute-start | bytes 663560 | tf_op jit(solution)/shard_map/ppermute | solution.py:309
  83.2 0.3 collective-permute-start.5
  83.6 4.8 %collective-permute-done.1.refs_2_.refs_7_ = bf16[1,224,768]{2,1,0:T(8,128)(2,1)S(1)} collective-permute-done((bf16[1,224,768]{2,1,0:T(8,128)(2,1)S(1)}, bf16[1,224,768]{2,1,0:T(8,128)(2,1)S(1)}, u32[]{:S(2)}, u32[]{:S(2)}) %collective-permute-start.1) | collective-permute-done | bytes 344096 | tf_op jit(solution)/shard_map/ppermute | solution.py:308
  88.4 2.9 %collective-permute-start.6 = (bf16[1,144,768]{2,1,0:T(8,128)(2,1)S(1)}, bf16[1,144,768]{2,1,0:T(8,128)(2,1)S(1)}, u32[]{:S(2)}, u32[]{:S(2)}) collective-permute-start(bf16[1,144,768]{2,1,0:T(8,128)(2,1)S(1)} %slice.39), channel_id=1, source_target_pairs={{0,32},{32,0},{1,33},{33,1},{2,34},{34,2},{3,35},{35,3},{4,36},{36... | collective-permute-start | bytes 663560 | tf_op jit(solution)/shard_map/ppermute | solution.py:309
  91.3 8.5 %attend.2.refs_8_ = f32[4,80,768]{2,1,0:T(8,128)S(1)} custom-call(s32[1]{0:T(128)} %bitcast.2.y_ref, bf16[1,224,768]{2,1,0:T(8,128)(2,1)S(1)} %get-tuple-element.32.refs_0_.refs_4_, bf16[1,224,768]{2,1,0:T(8,128)(2,1)S(1)} %collective-permute-done.refs_1_.refs_5_, bf16[1,224,768]{2,1,0:T(8,128)(2,1)S(1)} %collective-permute-done.1.refs_2_.refs_7_, ...), custom_call_target="tpu_custom_call" | custom-call | flops 37748736 | bytes 1000000 | tf_op jit(solution)/shard_map/attend/pallas_call | solution.py:148
  99.9 9.8 %attend.3 = bf16[4,8,56,128]{3,2,1,0:T(8,128)(2,1)} custom-call(s32[1]{0:T(128)} %bitcast.2.y_ref, bf16[1,224,768]{2,1,0:T(8,128)(2,1)S(1)} %get-tuple-element.32.refs_0_.refs_4_, bf16[1,224,768]{2,1,0:T(8,128)(2,1)S(1)} %collective-permute-done.refs_1_.refs_5_, bf16[1,224,768]{2,1,0:T(8,128)(2,1)S(1)} %collective-permute-done.1.refs_2_.refs_7_, ...), custom_call_target="tpu_custom_call" | custom-call | flops 37748736 | bytes 1000000 | tf_op jit(solution)/shard_map/attend/pallas_call | solution.py:148
  109.6 5.3 %all-to-all-start.2 = ((bf16[32,56,128]{2,1,0:T(8,128)(2,1)}), bf16[32,56,128]{2,1,0:T(8,128)(2,1)S(1)}, u32[]{:S(2)}, u32[]{:S(2)}) async-start(bf16[32,56,128]{2,1,0:T(8,128)(2,1)} %bitcast.8), calls=%async_computation.2 | async-start | bytes 917504 | tf_op jit(solution)/shard_map/all_to_all | solution.py:313
  115.0 12.3 %all-gather.6.cloned.1.call-done = bf16[9216,256]{1,0:T(8,128)(2,1)} async-done(((bf16[1152,256]{1,0:T(8,128)(2,1)}), bf16[9216,256]{1,0:T(8,128)(2,1)}) %all-gather.6.cloned.1.call-update) | async-done | bytes 4718608 | tf_op jit(solution)/shard_map/all_gather | solution.py:285
  127.3 2.3 %copy-done.2 = bf16[9216,256]{1,0:T(8,128)(2,1)S(1)} copy-done((bf16[9216,256]{1,0:T(8,128)(2,1)S(1)}, bf16[9216,256]{1,0:T(8,128)(2,1)}, u32[]{:S(2)}) %copy-start.2) | copy-done | bytes 4718616
  129.6 1.1 prepare.1
  130.7 1.1 copy-done.3
  131.8 1.3 copy-done.5
  133.1 2.0 %collective-permute-start.7 = (bf16[1152,640]{1,0:T(8,128)(2,1)S(1)}, bf16[1152,640]{1,0:T(8,128)(2,1)S(1)}, u32[]{:S(2)}, u32[]{:S(2)}) collective-permute-start(bf16[1152,640]{1,0:T(8,128)(2,1)S(1)} %get-tuple-element.38.own), channel_id=1, source_target_pairs={{0,64},{64,0},{1,65},{65,1},{2,66},{66,2},{3,67},{67,3},{4,68},{68... | collective-permute-start | bytes 4423688 | tf_op jit(solution)/shard_map/ppermute | solution.py:318
  135.1 2.9 %collective-permute-done.7.got = bf16[1152,640]{1,0:T(8,128)(2,1)S(1)} collective-permute-done((bf16[1152,640]{1,0:T(8,128)(2,1)S(1)}, bf16[1152,640]{1,0:T(8,128)(2,1)S(1)}, u32[]{:S(2)}, u32[]{:S(2)}) %collective-permute-start.7) | collective-permute-done | bytes 1474592 | tf_op jit(solution)/shard_map/ppermute | solution.py:318
  138.0 0.4 collective-permute-start.17
  138.4 1.6 spatial_end.3
  140.0 2.2 %collective-permute-start.11 = (bf16[96,1152]{1,0:T(8,128)(2,1)S(1)}, bf16[96,1152]{1,0:T(8,128)(2,1)S(1)}, u32[]{:S(2)}, u32[]{:S(2)}) collective-permute-start(bf16[96,1152]{1,0:T(8,128)(2,1)S(1)} %get-tuple-element.40.n0), channel_id=1, source_target_pairs={{0,128},{128,0},{1,129},{129,1},{2,130},{130,2},{3,131},{131,3},{4... | collective-permute-start | bytes 663560 | tf_op jit(solution)/shard_map/ppermute | solution.py:330
  142.2 0.4 collective-permute-start.10
  142.7 1.6 spatial_end.2
  144.3 3.6 %collective-permute-done.11.n2 = bf16[96,1152]{1,0:T(8,128)(2,1)S(1)} collective-permute-done((bf16[96,1152]{1,0:T(8,128)(2,1)S(1)}, bf16[96,1152]{1,0:T(8,128)(2,1)S(1)}, u32[]{:S(2)}, u32[]{:S(2)}) %collective-permute-start.11) | collective-permute-done | bytes 221216 | tf_op jit(solution)/shard_map/ppermute | solution.py:330
  147.9 0.7 collective-permute-start.12
  148.6 1.5 collective-permute-start.9
  150.1 0.3 collective-permute-start.8
  150.4 2.1 %temporal.2 = (bf16[216,128]{1,0:T(8,128)(2,1)S(1)}, bf16[216,128]{1,0:T(8,128)(2,1)S(1)}, bf16[216,128]{1,0:T(8,128)(2,1)S(1)}, bf16[216,128]{1,0:T(8,128)(2,1)S(1)}) custom-call(bf16[96,1152]{1,0:T(8,128)(2,1)S(1)} %get-tuple-element.40.n0, bf16[96,1152]{1,0:T(8,128)(2,1)S(1)} %collective-permute-done.10.n1, ...), custom_call_target="tpu_custom_call" | custom-call | flops 2000000000 | bytes 8000000 | tf_op jit(solution)/shard_map/temporal/pallas_call | solution.py:239
  152.5 3.2 %collective-permute-done.9.n2 = bf16[96,1152]{1,0:T(8,128)(2,1)S(1)} collective-permute-done((bf16[96,1152]{1,0:T(8,128)(2,1)S(1)}, bf16[96,1152]{1,0:T(8,128)(2,1)S(1)}, u32[]{:S(2)}, u32[]{:S(2)}) %collective-permute-start.9) | collective-permute-done | bytes 221216 | tf_op jit(solution)/shard_map/ppermute | solution.py:330
  155.7 0.8 collective-permute-start.13
  156.5 1.5 collective-permute-start.19
  157.9 0.7 collective-permute-start.20
  158.6 2.1 %temporal.3 = (bf16[216,128]{1,0:T(8,128)(2,1)S(1)}, bf16[216,128]{1,0:T(8,128)(2,1)S(1)}, bf16[216,128]{1,0:T(8,128)(2,1)S(1)}, bf16[216,128]{1,0:T(8,128)(2,1)S(1)}) custom-call(bf16[96,1152]{1,0:T(8,128)(2,1)S(1)} %get-tuple-element.39.n0, bf16[96,1152]{1,0:T(8,128)(2,1)S(1)} %collective-permute-done.8.n1, ...), custom_call_target="tpu_custom_call" | custom-call | flops 2000000000 | bytes 8000000 | tf_op jit(solution)/shard_map/temporal/pallas_call | solution.py:239
  160.7 0.2 collective-permute-start.14
  160.9 1.4 collective-permute-start.15
  162.4 0.6 collective-permute-start.16
  163.0 2.4 %temporal_end.2.refs_0_ = bf16[192,1152]{1,0:T(8,128)(2,1)} custom-call(s32[2]{0:T(128)S(1)} %pad_add_fusion.place_ref, bf16[216,128]{1,0:T(8,128)(2,1)S(1)} %get-tuple-element.52.m0, bf16[216,128]{1,0:T(8,128)(2,1)S(1)} %collective-permute-done.18.m1, bf16[216,128]{1,0:T(8,128)(2,1)S(1)} %collective-permute-done.19.m2, ...), custom_call_target="tpu_custom_call" | custom-call | flops 2000000000 | bytes 8000000 | tf_op jit(solution)/shard_map/temporal_end/pallas_call | solution.py:239
  165.4 1.4 collective-permute-done.16.m3
  166.8 2.4 %temporal_end.3 = bf16[192,1152]{1,0:T(8,128)(2,1)} custom-call(s32[2]{0:T(128)S(1)} %pad_add_fusion.place_ref, bf16[216,128]{1,0:T(8,128)(2,1)S(1)} %get-tuple-element.45.m0, bf16[216,128]{1,0:T(8,128)(2,1)S(1)} %collective-permute-done.14.m1, bf16[216,128]{1,0:T(8,128)(2,1)S(1)} %collective-permute-done.15.m2, ...), custom_call_target="tpu_custom_call", output_to_operand_aliasing={{}: (9, {})} | custom-call | flops 2000000000 | bytes 8000000 | tf_op jit(solution)/shard_map/temporal_end/pallas_call | solution.py:239
  (58 shorter events, 1.3 us)
Async XLA Ops:
  6.5 2.3 %copy-start.7 = (bf16[18,3456]{1,0:T(8,128)(2,1)S(1)}, bf16[18,3456]{1,0:T(8,128)(2,1)}, u32[]{:S(2)}) copy-start(bf16[18,3456]{1,0:T(8,128)(2,1)} %param.11) | copy-start | bytes 373252
  6.5 2.6 %copy-start.8 = (bf16[18,1152]{1,0:T(8,128)(2,1)S(1)}, bf16[18,1152]{1,0:T(8,128)(2,1)}, u32[]{:S(2)}) copy-start(bf16[18,1152]{1,0:T(8,128)(2,1)} %param.12) | copy-start | bytes 124420
  6.5 2.6 %copy-start.9 = (bf16[18,1152]{1,0:T(8,128)(2,1)S(1)}, bf16[18,1152]{1,0:T(8,128)(2,1)}, u32[]{:S(2)}) copy-start(bf16[18,1152]{1,0:T(8,128)(2,1)} %param.10) | copy-start | bytes 124420
  6.5 56.6 %all-gather.4.cloned.1.call-start = ((), (), s32[]{:S(2)}) async-start(), calls=%async_computation.3 | async-start | bytes 3981312 | tf_op jit(solution)/shard_map/all_gather | solution.py:282
  7.3 120.0 %all-gather.6.cloned.1.call-start = ((), (), s32[]{:S(2)}) async-start(), calls=%async_computation.4 | async-start | bytes 5308416 | tf_op jit(solution)/shard_map/all_gather | solution.py:285
  56.4 6.8 %copy-start.10 = (f32[4,72]{1,0:T(4,128)S(1)}, f32[4,72]{1,0:T(4,128)}, u32[]{:S(2)}) copy-start(f32[4,72]{1,0:T(4,128)} %param.13) | copy-start | bytes 3460
  56.4 6.9 %copy-start.1 = (f32[6,1152]{1,0:T(8,128)S(1)}, f32[6,1152]{1,0:T(8,128)}, u32[]{:S(2)}) copy-start(f32[6,1152]{1,0:T(8,128)} %mod_ref.9) | copy-start | bytes 82948
  69.8 10.6 %collective-permute-start = (bf16[1,224,768]{2,1,0:T(8,128)(2,1)S(1)}, bf16[1,224,768]{2,1,0:T(8,128)(2,1)S(1)}, u32[]{:S(2)}, u32[]{:S(2)}) collective-permute-start(bf16[1,224,768]{2,1,0:T(8,128)(2,1)S(1)} %get-tuple-element.33), channel_id=1, source_target_pairs={{0,8},{8,16},{16,24},{24,0},{1,9},{9,17},{17,25},{25,1},{2,10},{10... | collective-permute-start | bytes 1032200 | tf_op jit(solution)/shard_map/ppermute | solution.py:308
  71.1 12.1 %collective-permute-start.2 = (bf16[1,224,768]{2,1,0:T(8,128)(2,1)S(1)}, bf16[1,224,768]{2,1,0:T(8,128)(2,1)S(1)}, u32[]{:S(2)}, u32[]{:S(2)}) collective-permute-start(bf16[1,224,768]{2,1,0:T(8,128)(2,1)S(1)} %get-tuple-element.35), channel_id=1, source_target_pairs={{0,24},{8,0},{16,8},{24,16},{1,25},{9,1},{17,9},{25,17},{2,26},{10... | collective-permute-start | bytes 1032200 | tf_op jit(solution)/shard_map/ppermute | solution.py:308
  72.6 15.8 %collective-permute-start.1 = (bf16[1,224,768]{2,1,0:T(8,128)(2,1)S(1)}, bf16[1,224,768]{2,1,0:T(8,128)(2,1)S(1)}, u32[]{:S(2)}, u32[]{:S(2)}) collective-permute-start(bf16[1,224,768]{2,1,0:T(8,128)(2,1)S(1)} %get-tuple-element.34), channel_id=1, source_target_pairs={{0,16},{8,24},{16,0},{24,8},{1,17},{9,25},{17,1},{25,9},{2,18},{10... | collective-permute-start | bytes 1032200 | tf_op jit(solution)/shard_map/ppermute | solution.py:308
  74.0 25.8 %collective-permute-start.3 = (bf16[1,144,768]{2,1,0:T(8,128)(2,1)S(1)}, bf16[1,144,768]{2,1,0:T(8,128)(2,1)S(1)}, u32[]{:S(2)}, u32[]{:S(2)}) collective-permute-start(bf16[1,144,768]{2,1,0:T(8,128)(2,1)S(1)} %slice.32), channel_id=1, source_target_pairs={{0,32},{32,0},{1,33},{33,1},{2,34},{34,2},{3,35},{35,3},{4,36},{36... | collective-permute-start | bytes 663560 | tf_op jit(solution)/shard_map/ppermute | solution.py:309
  80.4 19.4 %collective-permute-start.4 = (bf16[1,144,768]{2,1,0:T(8,128)(2,1)S(1)}, bf16[1,144,768]{2,1,0:T(8,128)(2,1)S(1)}, u32[]{:S(2)}, u32[]{:S(2)}) collective-permute-start(bf16[1,144,768]{2,1,0:T(8,128)(2,1)S(1)} %slice.37), channel_id=1, source_target_pairs={{0,32},{32,0},{1,33},{33,1},{2,34},{34,2},{3,35},{35,3},{4,36},{36... | collective-permute-start | bytes 663560 | tf_op jit(solution)/shard_map/ppermute | solution.py:309
  83.2 16.6 %collective-permute-start.5 = (bf16[1,144,768]{2,1,0:T(8,128)(2,1)S(1)}, bf16[1,144,768]{2,1,0:T(8,128)(2,1)S(1)}, u32[]{:S(2)}, u32[]{:S(2)}) collective-permute-start(bf16[1,144,768]{2,1,0:T(8,128)(2,1)S(1)} %slice.38), channel_id=1, source_target_pairs={{0,32},{32,0},{1,33},{33,1},{2,34},{34,2},{3,35},{35,3},{4,36},{36... | collective-permute-start | bytes 663560 | tf_op jit(solution)/shard_map/ppermute | solution.py:309
  88.4 11.5 %collective-permute-start.6 = (bf16[1,144,768]{2,1,0:T(8,128)(2,1)S(1)}, bf16[1,144,768]{2,1,0:T(8,128)(2,1)S(1)}, u32[]{:S(2)}, u32[]{:S(2)}) collective-permute-start(bf16[1,144,768]{2,1,0:T(8,128)(2,1)S(1)} %slice.39), channel_id=1, source_target_pairs={{0,32},{32,0},{1,33},{33,1},{2,34},{34,2},{3,35},{35,3},{4,36},{36... | collective-permute-start | bytes 663560 | tf_op jit(solution)/shard_map/ppermute | solution.py:309
  109.6 23.4 %all-to-all-start.2 = ((bf16[32,56,128]{2,1,0:T(8,128)(2,1)}), bf16[32,56,128]{2,1,0:T(8,128)(2,1)S(1)}, u32[]{:S(2)}, u32[]{:S(2)}) async-start(bf16[32,56,128]{2,1,0:T(8,128)(2,1)} %bitcast.8), calls=%async_computation.2 | async-start | bytes 917504 | tf_op jit(solution)/shard_map/all_to_all | solution.py:313
  127.3 2.3 %copy-start.2 = (bf16[9216,256]{1,0:T(8,128)(2,1)S(1)}, bf16[9216,256]{1,0:T(8,128)(2,1)}, u32[]{:S(2)}) copy-start(bf16[9216,256]{1,0:T(8,128)(2,1)} %all-gather.6.cloned.1.call-done) | copy-start | bytes 14155780
  129.6 8.8 %copy-start = (bf16[2,1,96,1152]{3,2,1,0:T(8,128)(2,1)S(1)}, bf16[2,1,96,1152]{3,2,1,0:T(8,128)(2,1)}, u32[]{:S(2)}) copy-start(bf16[2,1,96,1152]{3,2,1,0:T(8,128)(2,1)} %param.7) | copy-start | bytes 1327108
  130.7 1.1 copy-start.3
  131.8 1.3 copy-start.5
  133.1 4.9 %collective-permute-start.7 = (bf16[1152,640]{1,0:T(8,128)(2,1)S(1)}, bf16[1152,640]{1,0:T(8,128)(2,1)S(1)}, u32[]{:S(2)}, u32[]{:S(2)}) collective-permute-start(bf16[1152,640]{1,0:T(8,128)(2,1)S(1)} %get-tuple-element.38.own), channel_id=1, source_target_pairs={{0,64},{64,0},{1,65},{65,1},{2,66},{66,2},{3,67},{67,3},{4,68},{68... | collective-permute-start | bytes 4423688 | tf_op jit(solution)/shard_map/ppermute | solution.py:318
  138.0 25.0 %collective-permute-start.17 = (bf16[576,1152]{1,0:T(8,128)(2,1)}, bf16[576,1152]{1,0:T(8,128)(2,1)S(1)}, u32[]{:S(2)}, u32[]{:S(2)}) collective-permute-start(bf16[576,1152]{1,0:T(8,128)(2,1)} %copy-done.3), channel_id=1, source_target_pairs={{0,64},{64,0},{1,65},{65,1},{2,66},{66,2},{3,67},{67,3},{4,68},{68... | collective-permute-start | bytes 3981320 | tf_op jit(solution)/shard_map/ppermute | solution.py:320
  140.0 10.3 %copy-start.6 = (bf16[864,1152]{1,0:T(8,128)(2,1)S(1)}, bf16[864,1152]{1,0:T(8,128)(2,1)}, u32[]{:S(2)}) copy-start(bf16[864,1152]{1,0:T(8,128)(2,1)} %copy-done.5) | copy-start | bytes 5971972
  140.0 7.9 %collective-permute-start.11 = (bf16[96,1152]{1,0:T(8,128)(2,1)S(1)}, bf16[96,1152]{1,0:T(8,128)(2,1)S(1)}, u32[]{:S(2)}, u32[]{:S(2)}) collective-permute-start(bf16[96,1152]{1,0:T(8,128)(2,1)S(1)} %get-tuple-element.40.n0), channel_id=1, source_target_pairs={{0,128},{128,0},{1,129},{129,1},{2,130},{130,2},{3,131},{131,3},{4... | collective-permute-start | bytes 663560 | tf_op jit(solution)/shard_map/ppermute | solution.py:330
  142.2 8.1 %collective-permute-start.10 = (bf16[96,1152]{1,0:T(8,128)(2,1)S(1)}, bf16[96,1152]{1,0:T(8,128)(2,1)S(1)}, u32[]{:S(2)}, u32[]{:S(2)}) collective-permute-start(bf16[96,1152]{1,0:T(8,128)(2,1)S(1)} %get-tuple-element.40.n0), channel_id=1, source_target_pairs={{0,64},{64,0},{1,65},{65,1},{2,66},{66,2},{3,67},{67,3},{4,68},{68... | collective-permute-start | bytes 663560 | tf_op jit(solution)/shard_map/ppermute | solution.py:335
  147.9 2.5 %collective-permute-start.12 = (bf16[96,1152]{1,0:T(8,128)(2,1)S(1)}, bf16[96,1152]{1,0:T(8,128)(2,1)S(1)}, u32[]{:S(2)}, u32[]{:S(2)}) collective-permute-start(bf16[96,1152]{1,0:T(8,128)(2,1)S(1)} %collective-permute-done.11.n2), channel_id=1, source_target_pairs={{0,64},{64,0},{1,65},{65,1},{2,66},{66,2},{3,67},{67,3},{4,68},{68... | collective-permute-start | bytes 663560 | tf_op jit(solution)/shard_map/ppermute | solution.py:335
  148.6 7.1 %collective-permute-start.9 = (bf16[96,1152]{1,0:T(8,128)(2,1)S(1)}, bf16[96,1152]{1,0:T(8,128)(2,1)S(1)}, u32[]{:S(2)}, u32[]{:S(2)}) collective-permute-start(bf16[96,1152]{1,0:T(8,128)(2,1)S(1)} %get-tuple-element.39.n0), channel_id=1, source_target_pairs={{0,128},{128,0},{1,129},{129,1},{2,130},{130,2},{3,131},{131,3},{4... | collective-permute-start | bytes 663560 | tf_op jit(solution)/shard_map/ppermute | solution.py:330
  150.1 7.9 %collective-permute-start.8 = (bf16[96,1152]{1,0:T(8,128)(2,1)S(1)}, bf16[96,1152]{1,0:T(8,128)(2,1)S(1)}, u32[]{:S(2)}, u32[]{:S(2)}) collective-permute-start(bf16[96,1152]{1,0:T(8,128)(2,1)S(1)} %get-tuple-element.39.n0), channel_id=1, source_target_pairs={{0,64},{64,0},{1,65},{65,1},{2,66},{66,2},{3,67},{67,3},{4,68},{68... | collective-permute-start | bytes 663560 | tf_op jit(solution)/shard_map/ppermute | solution.py:335
  155.7 2.9 %collective-permute-start.13 = (bf16[96,1152]{1,0:T(8,128)(2,1)S(1)}, bf16[96,1152]{1,0:T(8,128)(2,1)S(1)}, u32[]{:S(2)}, u32[]{:S(2)}) collective-permute-start(bf16[96,1152]{1,0:T(8,128)(2,1)S(1)} %collective-permute-done.9.n2), channel_id=1, source_target_pairs={{0,64},{64,0},{1,65},{65,1},{2,66},{66,2},{3,67},{67,3},{4,68},{68... | collective-permute-start | bytes 663560 | tf_op jit(solution)/shard_map/ppermute | solution.py:335
  156.5 4.5 %collective-permute-start.18 = (bf16[216,128]{1,0:T(8,128)(2,1)S(1)}, bf16[216,128]{1,0:T(8,128)(2,1)S(1)}, u32[]{:S(2)}, u32[]{:S(2)}) collective-permute-start(bf16[216,128]{1,0:T(8,128)(2,1)S(1)} %get-tuple-element.53), channel_id=1, source_target_pairs={{0,64},{64,0},{1,65},{65,1},{2,66},{66,2},{3,67},{67,3},{4,68},{68... | collective-permute-start | bytes 165896 | tf_op jit(solution)/shard_map/ppermute | solution.py:341
  156.5 5.9 %collective-permute-start.19 = (bf16[216,128]{1,0:T(8,128)(2,1)S(1)}, bf16[216,128]{1,0:T(8,128)(2,1)S(1)}, u32[]{:S(2)}, u32[]{:S(2)}) collective-permute-start(bf16[216,128]{1,0:T(8,128)(2,1)S(1)} %get-tuple-element.54), channel_id=1, source_target_pairs={{0,128},{128,0},{1,129},{129,1},{2,130},{130,2},{3,131},{131,3},{4... | collective-permute-start | bytes 165896 | tf_op jit(solution)/shard_map/ppermute | solution.py:342
  157.9 5.0 %copy-start.4 = (bf16[576,1152]{1,0:T(8,128)(2,1)S(1)}, bf16[576,1152]{1,0:T(8,128)(2,1)}, u32[]{:S(2)}) copy-start(bf16[576,1152]{1,0:T(8,128)(2,1)} %copy-done.3) | copy-start | bytes 3981316
  157.9 5.0 %collective-permute-start.20 = (bf16[216,128]{1,0:T(8,128)(2,1)S(1)}, bf16[216,128]{1,0:T(8,128)(2,1)S(1)}, u32[]{:S(2)}, u32[]{:S(2)}) collective-permute-start(bf16[216,128]{1,0:T(8,128)(2,1)S(1)} %get-tuple-element.55), channel_id=1, source_target_pairs={{0,192},{192,0},{64,128},{128,64},{1,193},{193,1},{65,129},{129,65... | collective-permute-start | bytes 165896 | tf_op jit(solution)/shard_map/ppermute | solution.py:343
  160.7 4.7 %collective-permute-start.14 = (bf16[216,128]{1,0:T(8,128)(2,1)S(1)}, bf16[216,128]{1,0:T(8,128)(2,1)S(1)}, u32[]{:S(2)}, u32[]{:S(2)}) collective-permute-start(bf16[216,128]{1,0:T(8,128)(2,1)S(1)} %get-tuple-element.46), channel_id=1, source_target_pairs={{0,64},{64,0},{1,65},{65,1},{2,66},{66,2},{3,67},{67,3},{4,68},{68... | collective-permute-start | bytes 165896 | tf_op jit(solution)/shard_map/ppermute | solution.py:341
  160.9 4.5 %collective-permute-start.15 = (bf16[216,128]{1,0:T(8,128)(2,1)S(1)}, bf16[216,128]{1,0:T(8,128)(2,1)S(1)}, u32[]{:S(2)}, u32[]{:S(2)}) collective-permute-start(bf16[216,128]{1,0:T(8,128)(2,1)S(1)} %get-tuple-element.47), channel_id=1, source_target_pairs={{0,128},{128,0},{1,129},{129,1},{2,130},{130,2},{3,131},{131,3},{4... | collective-permute-start | bytes 165896 | tf_op jit(solution)/shard_map/ppermute | solution.py:342
  162.4 4.5 %collective-permute-start.16 = (bf16[216,128]{1,0:T(8,128)(2,1)S(1)}, bf16[216,128]{1,0:T(8,128)(2,1)S(1)}, u32[]{:S(2)}, u32[]{:S(2)}) collective-permute-start(bf16[216,128]{1,0:T(8,128)(2,1)S(1)} %get-tuple-element.48), channel_id=1, source_target_pairs={{0,192},{192,0},{64,128},{128,64},{1,193},{193,1},{65,129},{129,65... | collective-permute-start | bytes 165896 | tf_op jit(solution)/shard_map/ppermute | solution.py:343
Sparse Core Ops, SparseCore 0:
  9.2 53.9 all-gather.3
  65.0 62.2 all-gather.5

commit v10 on v9

--- a/solution.py
+++ b/solution.py
@@ -328,10 +328,8 @@
     diagonal = [(0, 3), (3, 0), (1, 2), (2, 1)]
     sent = []
     moved = [lax.ppermute(norm, "xl", swap) for _, norm in steps]
-    moved[0], _ = lax.optimization_barrier((moved[0], steps[1][1]))
+    moved = lax.optimization_barrier(moved)
     for (_, norm), norm_x in zip(steps, moved):
-        if sent:
-            norm_x, sent[0][0] = lax.optimization_barrier((norm_x, sent[0][0]))
         args = [norm, lax.ppermute(norm, "c", swap), norm_x, lax.ppermute(norm_x, "c", swap)]
         args += [turned, gains]
         mixed = once(temporal, args, [full(a) for a in args], [shape(BF, 3 * HD, 128)] * 4)

time: 176 us -> 177 us (level)
  waiting for transfers between devices: 38.4 us -> 40.2 us
  transfers between devices with their start and end apart: 24 -> 24, of which waited for: 8 -> 9; matrix products, arithmetic and copies ran while one was open for 2% -> 2% of each run, Pallas kernels for 20% -> 20%
where the time goes in v10:
time: 177 us; the launch traced here: 176 us
  blocking collectives  46.7 us (26%)
  waiting for transfers between devices  40.2 us (23%)
  Pallas kernels  38.1 us (22%)
  starting transfers between devices  29.3 us (17%)
  between operations  13.7 us (8%)
  local copies, waits for them, and re-layouts  8.01 us (5%)
    all_to_all x1, blocking collectives, per_device(): shard = lax.all_to_all(shard, ('xh', 'y'), 0, 0, tiled=True).reshape(D, 768)  27 us
    all_to_all x1, blocking collectives, per_device(): lax.all_to_all(shard, 'z', 0, 0, tiled=True).reshape(1, NZ * 18, 768)  19.7 us
    pallas_call x2, Pallas kernels, attention(): pl.pallas_call(functools.partial(attend, count, part is not None, finish)...  18.3 us
    pallas_call x7, Pallas kernels, once(): pl.pallas_call(kernel, grid=(1,), in_specs=specs, out_specs=out_specs or...  13.3 us
    all_gather x1, waiting for transfers between devices, per_device(): rest = lax.all_gather(rest, 'z', axis=0)  12.3 us
    ppermute x4, starting transfers between devices, per_device(): others = [lax.ppermute(block[:, :2 * HD], 'xh', swap) for block in blocks]  8.82 us
    ppermute x3, waiting for transfers between devices, per_device(): lax.ppermute(slots[n], 'y', [(i, (i + n) % NY) for i in range(NY)])  8.36 us
    ppermute x2, waiting for transfers between devices, per_device(): moved = [lax.ppermute(norm, 'xl', swap) for _, norm in steps]  8.15 us
  transfers between devices with their start and end apart: 24, of which 9 were waited for; matrix products, arithmetic and copies ran while one was open for 2% of the time, Pallas kernels for 20%

profile of v10, /device:TPU:1, one launch (start us, length us, event | category | flops | bytes accessed | tf_op | source)
XLA Modules:
  0.0 176.3 jit_solution(2069318551487244604)
XLA Ops:
  6.5 0.7 all-gather.4.cloned.1.call-update
  7.3 1.2 reshape.36
  8.7 0.2 reshape.37
  9.6 19.7 %all_to_all.15 = bf16[8,18,768]{2,1,0:T(8,128)(2,1)S(1)} all-to-all(bf16[8,18,768]{2,1,0:T(8,128)(2,1)S(1)} %copy.16), channel_id=1, replica_groups=mesh['xl'=2,'c'=2,'xh'=2,'y'=4,'z'=8] {'z'}, dimensions={0} | all-to-all | bytes 442368 | tf_op jit(solution)/shard_map/all_to_all | solution.py:278
  29.4 27.0 %all_to_all.16 = bf16[8,144,768]{2,1,0:T(8,128)(2,1)S(1)} all-to-all(bf16[8,144,768]{2,1,0:T(8,128)(2,1)S(1)} %broadcast_in_dim.8), channel_id=1, replica_groups=mesh['xl'=2,'c'=2,'xh'=2,'y'=4,'z'=8] {'xh','y'}, dimensions={0} | all-to-all | bytes 3538944 | tf_op jit(solution)/shard_map/all_to_all | solution.py:280
  56.5 0.9 slice.36
  57.4 5.8 %all-gather.4.cloned.1.call-done.tok_ref = bf16[8,192,1152]{2,1,0:T(8,128)(2,1)} async-done(((bf16[1,192,1152]{2,1,0:T(8,128)(2,1)}), bf16[8,192,1152]{2,1,0:T(8,128)(2,1)}) %all-gather.4.cloned.1.call-update) | async-done | bytes 3538960 | tf_op jit(solution)/shard_map/all_gather | solution.py:282
  63.3 6.5 %spatial_proj.1 = (bf16[1,224,768]{2,1,0:T(8,128)(2,1)S(1)}, bf16[1,224,768]{2,1,0:T(8,128)(2,1)S(1)}, bf16[1,224,768]{2,1,0:T(8,128)(2,1)S(1)}, bf16[1,224,768]{2,1,0:T(8,128)(2,1)S(1)}) custom-call(s32[1]{0:T(128)} %bitcast.2.y_ref, bf16[8,192,1152]{2,1,0:T(8,128)(2,1)} %all-gather.4.cloned.1.call-done.tok_ref, f32[6,1152]{1,0:T(8,128)S(1)} %copy-done.1, ...), custom_call_target="tpu_custom_call" | custom-call | tf_op jit(solution)/shard_map/spatial_proj/pallas_call | solution.py:288
  69.8 1.3 collective-permute-start
  71.1 1.5 collective-permute-start.2
  72.6 1.5 collective-permute-start.1
  74.0 2.7 %collective-permute-start.3 = (bf16[1,144,768]{2,1,0:T(8,128)(2,1)S(1)}, bf16[1,144,768]{2,1,0:T(8,128)(2,1)S(1)}, u32[]{:S(2)}, u32[]{:S(2)}) collective-permute-start(bf16[1,144,768]{2,1,0:T(8,128)(2,1)S(1)} %slice.32), channel_id=1, source_target_pairs={{0,32},{32,0},{1,33},{33,1},{2,34},{34,2},{3,35},{35,3},{4,36},{36... | collective-permute-start | bytes 663560 | tf_op jit(solution)/shard_map/ppermute | solution.py:309
  76.8 3.6 %collective-permute-done.refs_1_.refs_5_ = bf16[1,224,768]{2,1,0:T(8,128)(2,1)S(1)} collective-permute-done((bf16[1,224,768]{2,1,0:T(8,128)(2,1)S(1)}, bf16[1,224,768]{2,1,0:T(8,128)(2,1)S(1)}, u32[]{:S(2)}, u32[]{:S(2)}) %collective-permute-start) | collective-permute-done | bytes 344096 | tf_op jit(solution)/shard_map/ppermute | solution.py:308
  80.4 2.8 %collective-permute-start.4 = (bf16[1,144,768]{2,1,0:T(8,128)(2,1)S(1)}, bf16[1,144,768]{2,1,0:T(8,128)(2,1)S(1)}, u32[]{:S(2)}, u32[]{:S(2)}) collective-permute-start(bf16[1,144,768]{2,1,0:T(8,128)(2,1)S(1)} %slice.37), channel_id=1, source_target_pairs={{0,32},{32,0},{1,33},{33,1},{2,34},{34,2},{3,35},{35,3},{4,36},{36... | collective-permute-start | bytes 663560 | tf_op jit(solution)/shard_map/ppermute | solution.py:309
  83.2 0.3 collective-permute-start.5
  83.6 4.8 %collective-permute-done.1.refs_2_.refs_7_ = bf16[1,224,768]{2,1,0:T(8,128)(2,1)S(1)} collective-permute-done((bf16[1,224,768]{2,1,0:T(8,128)(2,1)S(1)}, bf16[1,224,768]{2,1,0:T(8,128)(2,1)S(1)}, u32[]{:S(2)}, u32[]{:S(2)}) %collective-permute-start.1) | collective-permute-done | bytes 344096 | tf_op jit(solution)/shard_map/ppermute | solution.py:308
  88.4 2.9 %collective-permute-start.6 = (bf16[1,144,768]{2,1,0:T(8,128)(2,1)S(1)}, bf16[1,144,768]{2,1,0:T(8,128)(2,1)S(1)}, u32[]{:S(2)}, u32[]{:S(2)}) collective-permute-start(bf16[1,144,768]{2,1,0:T(8,128)(2,1)S(1)} %slice.39), channel_id=1, source_target_pairs={{0,32},{32,0},{1,33},{33,1},{2,34},{34,2},{3,35},{35,3},{4,36},{36... | collective-permute-start | bytes 663560 | tf_op jit(solution)/shard_map/ppermute | solution.py:309
  91.3 8.5 %attend.2.refs_8_ = f32[4,80,768]{2,1,0:T(8,128)S(1)} custom-call(s32[1]{0:T(128)} %bitcast.2.y_ref, bf16[1,224,768]{2,1,0:T(8,128)(2,1)S(1)} %get-tuple-element.31.refs_0_.refs_4_, bf16[1,224,768]{2,1,0:T(8,128)(2,1)S(1)} %collective-permute-done.refs_1_.refs_5_, bf16[1,224,768]{2,1,0:T(8,128)(2,1)S(1)} %collective-permute-done.1.refs_2_.refs_7_, ...), custom_call_target="tpu_custom_call" | custom-call | flops 37748736 | bytes 1000000 | tf_op jit(solution)/shard_map/attend/pallas_call | solution.py:148
  99.9 9.8 %attend.3 = bf16[4,8,56,128]{3,2,1,0:T(8,128)(2,1)} custom-call(s32[1]{0:T(128)} %bitcast.2.y_ref, bf16[1,224,768]{2,1,0:T(8,128)(2,1)S(1)} %get-tuple-element.31.refs_0_.refs_4_, bf16[1,224,768]{2,1,0:T(8,128)(2,1)S(1)} %collective-permute-done.refs_1_.refs_5_, bf16[1,224,768]{2,1,0:T(8,128)(2,1)S(1)} %collective-permute-done.1.refs_2_.refs_7_, ...), custom_call_target="tpu_custom_call" | custom-call | flops 37748736 | bytes 1000000 | tf_op jit(solution)/shard_map/attend/pallas_call | solution.py:148
  109.6 5.3 %all-to-all-start.2 = ((bf16[32,56,128]{2,1,0:T(8,128)(2,1)}), bf16[32,56,128]{2,1,0:T(8,128)(2,1)S(1)}, u32[]{:S(2)}, u32[]{:S(2)}) async-start(bf16[32,56,128]{2,1,0:T(8,128)(2,1)} %bitcast.8), calls=%async_computation.2 | async-start | bytes 917504 | tf_op jit(solution)/shard_map/all_to_all | solution.py:313
  115.0 12.3 %all-gather.6.cloned.1.call-done = bf16[9216,256]{1,0:T(8,128)(2,1)} async-done(((bf16[1152,256]{1,0:T(8,128)(2,1)}), bf16[9216,256]{1,0:T(8,128)(2,1)}) %all-gather.6.cloned.1.call-update) | async-done | bytes 4718608 | tf_op jit(solution)/shard_map/all_gather | solution.py:285
  127.3 2.3 %copy-done.2 = bf16[9216,256]{1,0:T(8,128)(2,1)S(1)} copy-done((bf16[9216,256]{1,0:T(8,128)(2,1)S(1)}, bf16[9216,256]{1,0:T(8,128)(2,1)}, u32[]{:S(2)}) %copy-start.2) | copy-done | bytes 4718616
  129.6 1.1 prepare.1
  130.7 1.1 copy-done.3
  131.8 1.3 copy-done.5
  133.1 2.0 %collective-permute-start.7 = (bf16[1152,640]{1,0:T(8,128)(2,1)S(1)}, bf16[1152,640]{1,0:T(8,128)(2,1)S(1)}, u32[]{:S(2)}, u32[]{:S(2)}) collective-permute-start(bf16[1152,640]{1,0:T(8,128)(2,1)S(1)} %get-tuple-element.37.own), channel_id=1, source_target_pairs={{0,64},{64,0},{1,65},{65,1},{2,66},{66,2},{3,67},{67,3},{4,68},{68... | collective-permute-start | bytes 4423688 | tf_op jit(solution)/shard_map/ppermute | solution.py:318
  135.1 2.9 %collective-permute-done.7.got = bf16[1152,640]{1,0:T(8,128)(2,1)S(1)} collective-permute-done((bf16[1152,640]{1,0:T(8,128)(2,1)S(1)}, bf16[1152,640]{1,0:T(8,128)(2,1)S(1)}, u32[]{:S(2)}, u32[]{:S(2)}) %collective-permute-start.7) | collective-permute-done | bytes 1474592 | tf_op jit(solution)/shard_map/ppermute | solution.py:318
  138.0 0.4 collective-permute-start.15
  138.4 1.6 spatial_end.3
  140.0 2.2 %collective-permute-start.9 = (bf16[96,1152]{1,0:T(8,128)(2,1)S(1)}, bf16[96,1152]{1,0:T(8,128)(2,1)S(1)}, u32[]{:S(2)}, u32[]{:S(2)}) collective-permute-start(bf16[96,1152]{1,0:T(8,128)(2,1)S(1)} %get-tuple-element.39.n0), channel_id=1, source_target_pairs={{0,128},{128,0},{1,129},{129,1},{2,130},{130,2},{3,131},{131,3},{4... | collective-permute-start | bytes 663560 | tf_op jit(solution)/shard_map/ppermute | solution.py:330
  142.2 1.6 spatial_end.2
  144.0 0.5 collective-permute-start.16
  144.5 3.4 %collective-permute-done.9.n2 = bf16[96,1152]{1,0:T(8,128)(2,1)S(1)} collective-permute-done((bf16[96,1152]{1,0:T(8,128)(2,1)S(1)}, bf16[96,1152]{1,0:T(8,128)(2,1)S(1)}, u32[]{:S(2)}, u32[]{:S(2)}) %collective-permute-start.9) | collective-permute-done | bytes 221216 | tf_op jit(solution)/shard_map/ppermute | solution.py:330
  147.9 4.7 %collective-permute-done.10.n2 = bf16[96,1152]{1,0:T(8,128)(2,1)S(1)} collective-permute-done((bf16[96,1152]{1,0:T(8,128)(2,1)S(1)}, bf16[96,1152]{1,0:T(8,128)(2,1)S(1)}, u32[]{:S(2)}, u32[]{:S(2)}) %collective-permute-start.10) | collective-permute-done | bytes 221216 | tf_op jit(solution)/shard_map/ppermute | solution.py:330
  152.6 0.7 collective-permute-start.17
  153.4 0.5 collective-permute-start.11
  153.9 0.6 collective-permute-done.17.n3
  154.5 2.1 %temporal.3 = (bf16[216,128]{1,0:T(8,128)(2,1)S(1)}, bf16[216,128]{1,0:T(8,128)(2,1)S(1)}, bf16[216,128]{1,0:T(8,128)(2,1)S(1)}, bf16[216,128]{1,0:T(8,128)(2,1)S(1)}) custom-call(bf16[96,1152]{1,0:T(8,128)(2,1)S(1)} %get-tuple-element.39.n0, bf16[96,1152]{1,0:T(8,128)(2,1)S(1)} %collective-permute-done.16.n1, ...), custom_call_target="tpu_custom_call" | custom-call | flops 2000000000 | bytes 8000000 | tf_op jit(solution)/shard_map/temporal/pallas_call | solution.py:239
  156.6 0.5 collective-permute-start.18
  157.0 1.5 collective-permute-start.19
  158.5 0.3 collective-permute-start.20
  158.8 2.1 %temporal.2 = (bf16[216,128]{1,0:T(8,128)(2,1)S(1)}, bf16[216,128]{1,0:T(8,128)(2,1)S(1)}, bf16[216,128]{1,0:T(8,128)(2,1)S(1)}, bf16[216,128]{1,0:T(8,128)(2,1)S(1)}) custom-call(bf16[96,1152]{1,0:T(8,128)(2,1)S(1)} %get-tuple-element.38.n0, bf16[96,1152]{1,0:T(8,128)(2,1)S(1)} %collective-permute-done.8.n1, ...), custom_call_target="tpu_custom_call" | custom-call | flops 2000000000 | bytes 8000000 | tf_op jit(solution)/shard_map/temporal/pallas_call | solution.py:239
  160.9 0.2 collective-permute-start.12
  161.2 1.4 collective-permute-start.13
  162.6 0.6 collective-permute-start.14
  163.2 2.4 %temporal_end.2.refs_0_ = bf16[192,1152]{1,0:T(8,128)(2,1)} custom-call(s32[2]{0:T(128)S(1)} %pad_add_fusion.place_ref, bf16[216,128]{1,0:T(8,128)(2,1)S(1)} %get-tuple-element.50.m0, bf16[216,128]{1,0:T(8,128)(2,1)S(1)} %collective-permute-done.18.m1, bf16[216,128]{1,0:T(8,128)(2,1)S(1)} %collective-permute-done.19.m2, ...), custom_call_target="tpu_custom_call" | custom-call | flops 2000000000 | bytes 8000000 | tf_op jit(solution)/shard_map/temporal_end/pallas_call | solution.py:239
  165.6 1.4 collective-permute-done.14.m3
  167.0 2.4 %temporal_end.3 = bf16[192,1152]{1,0:T(8,128)(2,1)} custom-call(s32[2]{0:T(128)S(1)} %pad_add_fusion.place_ref, bf16[216,128]{1,0:T(8,128)(2,1)S(1)} %get-tuple-element.42.m0, bf16[216,128]{1,0:T(8,128)(2,1)S(1)} %collective-permute-done.12.m1, bf16[216,128]{1,0:T(8,128)(2,1)S(1)} %collective-permute-done.13.m2, ...), custom_call_target="tpu_custom_call", output_to_operand_aliasing={{}: (9, {})} | custom-call | flops 2000000000 | bytes 8000000 | tf_op jit(solution)/shard_map/temporal_end/pallas_call | solution.py:239
  (58 shorter events, 1.4 us)
Async XLA Ops:
  6.5 2.3 %copy-start.7 = (bf16[18,3456]{1,0:T(8,128)(2,1)S(1)}, bf16[18,3456]{1,0:T(8,128)(2,1)}, u32[]{:S(2)}) copy-start(bf16[18,3456]{1,0:T(8,128)(2,1)} %param.11) | copy-start | bytes 373252
  6.5 2.6 %copy-start.8 = (bf16[18,1152]{1,0:T(8,128)(2,1)S(1)}, bf16[18,1152]{1,0:T(8,128)(2,1)}, u32[]{:S(2)}) copy-start(bf16[18,1152]{1,0:T(8,128)(2,1)} %param.12) | copy-start | bytes 124420
  6.5 2.6 %copy-start.9 = (bf16[18,1152]{1,0:T(8,128)(2,1)S(1)}, bf16[18,1152]{1,0:T(8,128)(2,1)}, u32[]{:S(2)}) copy-start(bf16[18,1152]{1,0:T(8,128)(2,1)} %param.10) | copy-start | bytes 124420
  6.5 56.6 %all-gather.4.cloned.1.call-start = ((), (), s32[]{:S(2)}) async-start(), calls=%async_computation.3 | async-start | bytes 3981312 | tf_op jit(solution)/shard_map/all_gather | solution.py:282
  7.3 120.0 %all-gather.6.cloned.1.call-start = ((), (), s32[]{:S(2)}) async-start(), calls=%async_computation.4 | async-start | bytes 5308416 | tf_op jit(solution)/shard_map/all_gather | solution.py:285
  56.4 6.8 %copy-start.10 = (f32[4,72]{1,0:T(4,128)S(1)}, f32[4,72]{1,0:T(4,128)}, u32[]{:S(2)}) copy-start(f32[4,72]{1,0:T(4,128)} %param.13) | copy-start | bytes 3460
  56.4 6.9 %copy-start.1 = (f32[6,1152]{1,0:T(8,128)S(1)}, f32[6,1152]{1,0:T(8,128)}, u32[]{:S(2)}) copy-start(f32[6,1152]{1,0:T(8,128)} %mod_ref.9) | copy-start | bytes 82948
  69.8 10.6 %collective-permute-start = (bf16[1,224,768]{2,1,0:T(8,128)(2,1)S(1)}, bf16[1,224,768]{2,1,0:T(8,128)(2,1)S(1)}, u32[]{:S(2)}, u32[]{:S(2)}) collective-permute-start(bf16[1,224,768]{2,1,0:T(8,128)(2,1)S(1)} %get-tuple-element.32), channel_id=1, source_target_pairs={{0,8},{8,16},{16,24},{24,0},{1,9},{9,17},{17,25},{25,1},{2,10},{10... | collective-permute-start | bytes 1032200 | tf_op jit(solution)/shard_map/ppermute | solution.py:308
  71.1 12.1 %collective-permute-start.2 = (bf16[1,224,768]{2,1,0:T(8,128)(2,1)S(1)}, bf16[1,224,768]{2,1,0:T(8,128)(2,1)S(1)}, u32[]{:S(2)}, u32[]{:S(2)}) collective-permute-start(bf16[1,224,768]{2,1,0:T(8,128)(2,1)S(1)} %get-tuple-element.34), channel_id=1, source_target_pairs={{0,24},{8,0},{16,8},{24,16},{1,25},{9,1},{17,9},{25,17},{2,26},{10... | collective-permute-start | bytes 1032200 | tf_op jit(solution)/shard_map/ppermute | solution.py:308
  72.6 15.8 %collective-permute-start.1 = (bf16[1,224,768]{2,1,0:T(8,128)(2,1)S(1)}, bf16[1,224,768]{2,1,0:T(8,128)(2,1)S(1)}, u32[]{:S(2)}, u32[]{:S(2)}) collective-permute-start(bf16[1,224,768]{2,1,0:T(8,128)(2,1)S(1)} %get-tuple-element.33), channel_id=1, source_target_pairs={{0,16},{8,24},{16,0},{24,8},{1,17},{9,25},{17,1},{25,9},{2,18},{10... | collective-permute-start | bytes 1032200 | tf_op jit(solution)/shard_map/ppermute | solution.py:308
  74.0 25.8 %collective-permute-start.3 = (bf16[1,144,768]{2,1,0:T(8,128)(2,1)S(1)}, bf16[1,144,768]{2,1,0:T(8,128)(2,1)S(1)}, u32[]{:S(2)}, u32[]{:S(2)}) collective-permute-start(bf16[1,144,768]{2,1,0:T(8,128)(2,1)S(1)} %slice.32), channel_id=1, source_target_pairs={{0,32},{32,0},{1,33},{33,1},{2,34},{34,2},{3,35},{35,3},{4,36},{36... | collective-permute-start | bytes 663560 | tf_op jit(solution)/shard_map/ppermute | solution.py:309
  80.4 19.4 %collective-permute-start.4 = (bf16[1,144,768]{2,1,0:T(8,128)(2,1)S(1)}, bf16[1,144,768]{2,1,0:T(8,128)(2,1)S(1)}, u32[]{:S(2)}, u32[]{:S(2)}) collective-permute-start(bf16[1,144,768]{2,1,0:T(8,128)(2,1)S(1)} %slice.37), channel_id=1, source_target_pairs={{0,32},{32,0},{1,33},{33,1},{2,34},{34,2},{3,35},{35,3},{4,36},{36... | collective-permute-start | bytes 663560 | tf_op jit(solution)/shard_map/ppermute | solution.py:309
  83.2 16.6 %collective-permute-start.5 = (bf16[1,144,768]{2,1,0:T(8,128)(2,1)S(1)}, bf16[1,144,768]{2,1,0:T(8,128)(2,1)S(1)}, u32[]{:S(2)}, u32[]{:S(2)}) collective-permute-start(bf16[1,144,768]{2,1,0:T(8,128)(2,1)S(1)} %slice.38), channel_id=1, source_target_pairs={{0,32},{32,0},{1,33},{33,1},{2,34},{34,2},{3,35},{35,3},{4,36},{36... | collective-permute-start | bytes 663560 | tf_op jit(solution)/shard_map/ppermute | solution.py:309
  88.4 11.5 %collective-permute-start.6 = (bf16[1,144,768]{2,1,0:T(8,128)(2,1)S(1)}, bf16[1,144,768]{2,1,0:T(8,128)(2,1)S(1)}, u32[]{:S(2)}, u32[]{:S(2)}) collective-permute-start(bf16[1,144,768]{2,1,0:T(8,128)(2,1)S(1)} %slice.39), channel_id=1, source_target_pairs={{0,32},{32,0},{1,33},{33,1},{2,34},{34,2},{3,35},{35,3},{4,36},{36... | collective-permute-start | bytes 663560 | tf_op jit(solution)/shard_map/ppermute | solution.py:309
  109.6 23.4 %all-to-all-start.2 = ((bf16[32,56,128]{2,1,0:T(8,128)(2,1)}), bf16[32,56,128]{2,1,0:T(8,128)(2,1)S(1)}, u32[]{:S(2)}, u32[]{:S(2)}) async-start(bf16[32,56,128]{2,1,0:T(8,128)(2,1)} %bitcast.8), calls=%async_computation.2 | async-start | bytes 917504 | tf_op jit(solution)/shard_map/all_to_all | solution.py:313
  127.3 2.3 %copy-start.2 = (bf16[9216,256]{1,0:T(8,128)(2,1)S(1)}, bf16[9216,256]{1,0:T(8,128)(2,1)}, u32[]{:S(2)}) copy-start(bf16[9216,256]{1,0:T(8,128)(2,1)} %all-gather.6.cloned.1.call-done) | copy-start | bytes 14155780
  129.6 8.8 %copy-start = (bf16[2,1,96,1152]{3,2,1,0:T(8,128)(2,1)S(1)}, bf16[2,1,96,1152]{3,2,1,0:T(8,128)(2,1)}, u32[]{:S(2)}) copy-start(bf16[2,1,96,1152]{3,2,1,0:T(8,128)(2,1)} %param.7) | copy-start | bytes 1327108
  130.7 1.1 copy-start.3
  131.8 1.3 copy-start.5
  133.1 4.9 %collective-permute-start.7 = (bf16[1152,640]{1,0:T(8,128)(2,1)S(1)}, bf16[1152,640]{1,0:T(8,128)(2,1)S(1)}, u32[]{:S(2)}, u32[]{:S(2)}) collective-permute-start(bf16[1152,640]{1,0:T(8,128)(2,1)S(1)} %get-tuple-element.37.own), channel_id=1, source_target_pairs={{0,64},{64,0},{1,65},{65,1},{2,66},{66,2},{3,67},{67,3},{4,68},{68... | collective-permute-start | bytes 4423688 | tf_op jit(solution)/shard_map/ppermute | solution.py:318
  138.0 25.3 %collective-permute-start.15 = (bf16[576,1152]{1,0:T(8,128)(2,1)}, bf16[576,1152]{1,0:T(8,128)(2,1)S(1)}, u32[]{:S(2)}, u32[]{:S(2)}) collective-permute-start(bf16[576,1152]{1,0:T(8,128)(2,1)} %copy-done.3), channel_id=1, source_target_pairs={{0,64},{64,0},{1,65},{65,1},{2,66},{66,2},{3,67},{67,3},{4,68},{68... | collective-permute-start | bytes 3981320 | tf_op jit(solution)/shard_map/ppermute | solution.py:320
  140.0 14.4 %copy-start.6 = (bf16[864,1152]{1,0:T(8,128)(2,1)S(1)}, bf16[864,1152]{1,0:T(8,128)(2,1)}, u32[]{:S(2)}) copy-start(bf16[864,1152]{1,0:T(8,128)(2,1)} %copy-done.5) | copy-start | bytes 5971972
  140.0 7.9 %collective-permute-start.9 = (bf16[96,1152]{1,0:T(8,128)(2,1)S(1)}, bf16[96,1152]{1,0:T(8,128)(2,1)S(1)}, u32[]{:S(2)}, u32[]{:S(2)}) collective-permute-start(bf16[96,1152]{1,0:T(8,128)(2,1)S(1)} %get-tuple-element.39.n0), channel_id=1, source_target_pairs={{0,128},{128,0},{1,129},{129,1},{2,130},{130,2},{3,131},{131,3},{4... | collective-permute-start | bytes 663560 | tf_op jit(solution)/shard_map/ppermute | solution.py:330
  143.9 8.8 %collective-permute-start.10 = (bf16[96,1152]{1,0:T(8,128)(2,1)S(1)}, bf16[96,1152]{1,0:T(8,128)(2,1)S(1)}, u32[]{:S(2)}, u32[]{:S(2)}) collective-permute-start(bf16[96,1152]{1,0:T(8,128)(2,1)S(1)} %get-tuple-element.38.n0), channel_id=1, source_target_pairs={{0,128},{128,0},{1,129},{129,1},{2,130},{130,2},{3,131},{131,3},{4... | collective-permute-start | bytes 663560 | tf_op jit(solution)/shard_map/ppermute | solution.py:330
  144.0 9.9 %collective-permute-start.16 = (bf16[96,1152]{1,0:T(8,128)(2,1)S(1)}, bf16[96,1152]{1,0:T(8,128)(2,1)S(1)}, u32[]{:S(2)}, u32[]{:S(2)}) collective-permute-start(bf16[96,1152]{1,0:T(8,128)(2,1)S(1)} %get-tuple-element.39.n0), channel_id=1, source_target_pairs={{0,64},{64,0},{1,65},{65,1},{2,66},{66,2},{3,67},{67,3},{4,68},{68... | collective-permute-start | bytes 663560 | tf_op jit(solution)/shard_map/ppermute | solution.py:333
  152.6 1.8 %collective-permute-start.17 = (bf16[96,1152]{1,0:T(8,128)(2,1)S(1)}, bf16[96,1152]{1,0:T(8,128)(2,1)S(1)}, u32[]{:S(2)}, u32[]{:S(2)}) collective-permute-start(bf16[96,1152]{1,0:T(8,128)(2,1)S(1)} %collective-permute-done.9.n2), channel_id=1, source_target_pairs={{0,64},{64,0},{1,65},{65,1},{2,66},{66,2},{3,67},{67,3},{4,68},{68... | collective-permute-start | bytes 663560 | tf_op jit(solution)/shard_map/ppermute | solution.py:333
  153.4 5.1 %collective-permute-start.8 = (bf16[96,1152]{1,0:T(8,128)(2,1)S(1)}, bf16[96,1152]{1,0:T(8,128)(2,1)S(1)}, u32[]{:S(2)}, u32[]{:S(2)}) collective-permute-start(bf16[96,1152]{1,0:T(8,128)(2,1)S(1)} %get-tuple-element.38.n0), channel_id=1, source_target_pairs={{0,64},{64,0},{1,65},{65,1},{2,66},{66,2},{3,67},{67,3},{4,68},{68... | collective-permute-start | bytes 663560 | tf_op jit(solution)/shard_map/ppermute | solution.py:333
  153.4 5.5 %collective-permute-start.11 = (bf16[96,1152]{1,0:T(8,128)(2,1)S(1)}, bf16[96,1152]{1,0:T(8,128)(2,1)S(1)}, u32[]{:S(2)}, u32[]{:S(2)}) collective-permute-start(bf16[96,1152]{1,0:T(8,128)(2,1)S(1)} %collective-permute-done.10.n2), channel_id=1, source_target_pairs={{0,64},{64,0},{1,65},{65,1},{2,66},{66,2},{3,67},{67,3},{4,68},{68... | collective-permute-start | bytes 663560 | tf_op jit(solution)/shard_map/ppermute | solution.py:333
  156.6 4.6 %collective-permute-start.18 = (bf16[216,128]{1,0:T(8,128)(2,1)S(1)}, bf16[216,128]{1,0:T(8,128)(2,1)S(1)}, u32[]{:S(2)}, u32[]{:S(2)}) collective-permute-start(bf16[216,128]{1,0:T(8,128)(2,1)S(1)} %get-tuple-element.51), channel_id=1, source_target_pairs={{0,64},{64,0},{1,65},{65,1},{2,66},{66,2},{3,67},{67,3},{4,68},{68... | collective-permute-start | bytes 165896 | tf_op jit(solution)/shard_map/ppermute | solution.py:339
  157.0 5.5 %collective-permute-start.19 = (bf16[216,128]{1,0:T(8,128)(2,1)S(1)}, bf16[216,128]{1,0:T(8,128)(2,1)S(1)}, u32[]{:S(2)}, u32[]{:S(2)}) collective-permute-start(bf16[216,128]{1,0:T(8,128)(2,1)S(1)} %get-tuple-element.52), channel_id=1, source_target_pairs={{0,128},{128,0},{1,129},{129,1},{2,130},{130,2},{3,131},{131,3},{4... | collective-permute-start | bytes 165896 | tf_op jit(solution)/shard_map/ppermute | solution.py:340
  158.5 4.7 %copy-start.4 = (bf16[576,1152]{1,0:T(8,128)(2,1)S(1)}, bf16[576,1152]{1,0:T(8,128)(2,1)}, u32[]{:S(2)}) copy-start(bf16[576,1152]{1,0:T(8,128)(2,1)} %copy-done.3) | copy-start | bytes 3981316
  158.5 4.7 %collective-permute-start.20 = (bf16[216,128]{1,0:T(8,128)(2,1)S(1)}, bf16[216,128]{1,0:T(8,128)(2,1)S(1)}, u32[]{:S(2)}, u32[]{:S(2)}) collective-permute-start(bf16[216,128]{1,0:T(8,128)(2,1)S(1)} %get-tuple-element.53), channel_id=1, source_target_pairs={{0,192},{192,0},{64,128},{128,64},{1,193},{193,1},{65,129},{129,65... | collective-permute-start | bytes 165896 | tf_op jit(solution)/shard_map/ppermute | solution.py:341
  160.9 4.7 %collective-permute-start.12 = (bf16[216,128]{1,0:T(8,128)(2,1)S(1)}, bf16[216,128]{1,0:T(8,128)(2,1)S(1)}, u32[]{:S(2)}, u32[]{:S(2)}) collective-permute-start(bf16[216,128]{1,0:T(8,128)(2,1)S(1)} %get-tuple-element.43), channel_id=1, source_target_pairs={{0,64},{64,0},{1,65},{65,1},{2,66},{66,2},{3,67},{67,3},{4,68},{68... | collective-permute-start | bytes 165896 | tf_op jit(solution)/shard_map/ppermute | solution.py:339
  161.2 4.5 %collective-permute-start.13 = (bf16[216,128]{1,0:T(8,128)(2,1)S(1)}, bf16[216,128]{1,0:T(8,128)(2,1)S(1)}, u32[]{:S(2)}, u32[]{:S(2)}) collective-permute-start(bf16[216,128]{1,0:T(8,128)(2,1)S(1)} %get-tuple-element.44), channel_id=1, source_target_pairs={{0,128},{128,0},{1,129},{129,1},{2,130},{130,2},{3,131},{131,3},{4... | collective-permute-start | bytes 165896 | tf_op jit(solution)/shard_map/ppermute | solution.py:340
  162.6 4.5 %collective-permute-start.14 = (bf16[216,128]{1,0:T(8,128)(2,1)S(1)}, bf16[216,128]{1,0:T(8,128)(2,1)S(1)}, u32[]{:S(2)}, u32[]{:S(2)}) collective-permute-start(bf16[216,128]{1,0:T(8,128)(2,1)S(1)} %get-tuple-element.45), channel_id=1, source_target_pairs={{0,192},{192,0},{64,128},{128,64},{1,193},{193,1},{65,129},{129,65... | collective-permute-start | bytes 165896 | tf_op jit(solution)/shard_map/ppermute | solution.py:341
Sparse Core Ops, SparseCore 0:
  9.2 53.9 all-gather.3
  65.0 62.2 all-gather.5

commit v11 on v10

--- a/solution.py
+++ b/solution.py
@@ -332,15 +332,17 @@
     for (_, norm), norm_x in zip(steps, moved):
         args = [norm, lax.ppermute(norm, "c", swap), norm_x, lax.ppermute(norm_x, "c", swap)]
         args += [turned, gains]
-        mixed = once(temporal, args, [full(a) for a in args], [shape(BF, 3 * HD, 128)] * 4)
-        sent.append(
-            [
-                mixed[0],
-                lax.ppermute(mixed[1], "c", swap),
-                lax.ppermute(mixed[2], "xl", swap),
-                lax.ppermute(mixed[3], ("xl", "c"), diagonal),
-            ]
-        )
+        sent.append(once(temporal, args, [full(a) for a in args], [shape(BF, 3 * HD, 128)] * 4))
+    sent[0], _ = lax.optimization_barrier((sent[0], sent[1][0]))
+    sent = [
+        [
+            mixed[0],
+            lax.ppermute(mixed[1], "c", swap),
+            lax.ppermute(mixed[2], "xl", swap),
+            lax.ppermute(mixed[3], ("xl", "c"), diagonal),
+        ]
+        for mixed in sent
+    ]
     result = None
     for clip in range(2):
         args = sent[clip] + [steps[clip][0], modulation, out_b, got_b]

time: 177 us -> 177 us (level)
  starting transfers between devices: 29.3 us -> 31.5 us
    ppermute x2, starting transfers between devices: 0.96 us -> 3.19 us  [per_device(): lax.ppermute(mixed[3], ('xl', 'c'), diagonal)]
  transfers between devices with their start and end apart: 24 -> 24, of which waited for: 9 -> 8; matrix products, arithmetic and copies ran while one was open for 2% -> 2% of each run, Pallas kernels for 20% -> 20%
where the time goes in v11:
time: 177 us
  blocking collectives  46.7 us (26%)
  waiting for transfers between devices  38.9 us (22%)
  Pallas kernels  38.1 us (22%)
  starting transfers between devices  31.5 us (18%)
  between operations  13.7 us (8%)
  local copies, waits for them, and re-layouts  8.01 us (5%)
    all_to_all x1, blocking collectives, per_device(): shard = lax.all_to_all(shard, ('xh', 'y'), 0, 0, tiled=True).reshape(D, 768)  27 us
    all_to_all x1, blocking collectives, per_device(): lax.all_to_all(shard, 'z', 0, 0, tiled=True).reshape(1, NZ * 18, 768)  19.7 us
    pallas_call x2, Pallas kernels, attention(): pl.pallas_call(functools.partial(attend, count, part is not None, finish)...  18.3 us
    pallas_call x7, Pallas kernels, once(): pl.pallas_call(kernel, grid=(1,), in_specs=specs, out_specs=out_specs or...  13.3 us
    all_gather x1, waiting for transfers between devices, per_device(): rest = lax.all_gather(rest, 'z', axis=0)  12.3 us
    ppermute x4, starting transfers between devices, per_device(): others = [lax.ppermute(block[:, :2 * HD], 'xh', swap) for block in blocks]  8.82 us
    ppermute x3, waiting for transfers between devices, per_device(): lax.ppermute(slots[n], 'y', [(i, (i + n) % NY) for i in range(NY)])  8.36 us
    ppermute x2, waiting for transfers between devices, per_device(): moved = [lax.ppermute(norm, 'xl', swap) for _, norm in steps]  8.15 us
  transfers between devices with their start and end apart: 24, of which 8 were waited for; matrix products, arithmetic and copies ran while one was open for 2% of the time, Pallas kernels for 20%

profile of v11, /device:TPU:1, one launch (start us, length us, event | category | flops | bytes accessed | tf_op | source)
XLA Modules:
  0.0 177.1 jit_solution(9505845255059163408)
XLA Ops:
  6.5 0.7 all-gather.4.cloned.1.call-update
  7.3 1.2 reshape.36
  8.5 0.1 copy.21
  8.7 0.2 reshape.37
  9.6 19.7 %all_to_all.15 = bf16[8,18,768]{2,1,0:T(8,128)(2,1)S(1)} all-to-all(bf16[8,18,768]{2,1,0:T(8,128)(2,1)S(1)} %copy.16), channel_id=1, replica_groups=mesh['xl'=2,'c'=2,'xh'=2,'y'=4,'z'=8] {'z'}, dimensions={0} | all-to-all | bytes 442368 | tf_op jit(solution)/shard_map/all_to_all | solution.py:278
  29.4 27.0 %all_to_all.16 = bf16[8,144,768]{2,1,0:T(8,128)(2,1)S(1)} all-to-all(bf16[8,144,768]{2,1,0:T(8,128)(2,1)S(1)} %broadcast_in_dim.8), channel_id=1, replica_groups=mesh['xl'=2,'c'=2,'xh'=2,'y'=4,'z'=8] {'xh','y'}, dimensions={0} | all-to-all | bytes 3538944 | tf_op jit(solution)/shard_map/all_to_all | solution.py:280
  56.5 0.9 slice.36
  57.4 5.8 %all-gather.4.cloned.1.call-done.tok_ref = bf16[8,192,1152]{2,1,0:T(8,128)(2,1)} async-done(((bf16[1,192,1152]{2,1,0:T(8,128)(2,1)}), bf16[8,192,1152]{2,1,0:T(8,128)(2,1)}) %all-gather.4.cloned.1.call-update) | async-done | bytes 3538960 | tf_op jit(solution)/shard_map/all_gather | solution.py:282
  63.3 6.5 %spatial_proj.1 = (bf16[1,224,768]{2,1,0:T(8,128)(2,1)S(1)}, bf16[1,224,768]{2,1,0:T(8,128)(2,1)S(1)}, bf16[1,224,768]{2,1,0:T(8,128)(2,1)S(1)}, bf16[1,224,768]{2,1,0:T(8,128)(2,1)S(1)}) custom-call(s32[1]{0:T(128)} %bitcast.2.y_ref, bf16[8,192,1152]{2,1,0:T(8,128)(2,1)} %all-gather.4.cloned.1.call-done.tok_ref, f32[6,1152]{1,0:T(8,128)S(1)} %copy-done.1, ...), custom_call_target="tpu_custom_call" | custom-call | tf_op jit(solution)/shard_map/spatial_proj/pallas_call | solution.py:288
  69.8 1.3 collective-permute-start
  71.1 1.5 collective-permute-start.2
  72.6 1.5 collective-permute-start.1
  74.0 2.7 %collective-permute-start.3 = (bf16[1,144,768]{2,1,0:T(8,128)(2,1)S(1)}, bf16[1,144,768]{2,1,0:T(8,128)(2,1)S(1)}, u32[]{:S(2)}, u32[]{:S(2)}) collective-permute-start(bf16[1,144,768]{2,1,0:T(8,128)(2,1)S(1)} %slice.32), channel_id=1, source_target_pairs={{0,32},{32,0},{1,33},{33,1},{2,34},{34,2},{3,35},{35,3},{4,36},{36... | collective-permute-start | bytes 663560 | tf_op jit(solution)/shard_map/ppermute | solution.py:309
  76.8 3.6 %collective-permute-done.refs_1_.refs_5_ = bf16[1,224,768]{2,1,0:T(8,128)(2,1)S(1)} collective-permute-done((bf16[1,224,768]{2,1,0:T(8,128)(2,1)S(1)}, bf16[1,224,768]{2,1,0:T(8,128)(2,1)S(1)}, u32[]{:S(2)}, u32[]{:S(2)}) %collective-permute-start) | collective-permute-done | bytes 344096 | tf_op jit(solution)/shard_map/ppermute | solution.py:308
  80.4 2.8 %collective-permute-start.4 = (bf16[1,144,768]{2,1,0:T(8,128)(2,1)S(1)}, bf16[1,144,768]{2,1,0:T(8,128)(2,1)S(1)}, u32[]{:S(2)}, u32[]{:S(2)}) collective-permute-start(bf16[1,144,768]{2,1,0:T(8,128)(2,1)S(1)} %slice.37), channel_id=1, source_target_pairs={{0,32},{32,0},{1,33},{33,1},{2,34},{34,2},{3,35},{35,3},{4,36},{36... | collective-permute-start | bytes 663560 | tf_op jit(solution)/shard_map/ppermute | solution.py:309
  83.2 0.3 collective-permute-start.5
  83.6 4.8 %collective-permute-done.1.refs_2_.refs_7_ = bf16[1,224,768]{2,1,0:T(8,128)(2,1)S(1)} collective-permute-done((bf16[1,224,768]{2,1,0:T(8,128)(2,1)S(1)}, bf16[1,224,768]{2,1,0:T(8,128)(2,1)S(1)}, u32[]{:S(2)}, u32[]{:S(2)}) %collective-permute-start.1) | collective-permute-done | bytes 344096 | tf_op jit(solution)/shard_map/ppermute | solution.py:308
  88.4 2.9 %collective-permute-start.6 = (bf16[1,144,768]{2,1,0:T(8,128)(2,1)S(1)}, bf16[1,144,768]{2,1,0:T(8,128)(2,1)S(1)}, u32[]{:S(2)}, u32[]{:S(2)}) collective-permute-start(bf16[1,144,768]{2,1,0:T(8,128)(2,1)S(1)} %slice.39), channel_id=1, source_target_pairs={{0,32},{32,0},{1,33},{33,1},{2,34},{34,2},{3,35},{35,3},{4,36},{36... | collective-permute-start | bytes 663560 | tf_op jit(solution)/shard_map/ppermute | solution.py:309
  91.3 8.5 %attend.2.refs_8_ = f32[4,80,768]{2,1,0:T(8,128)S(1)} custom-call(s32[1]{0:T(128)} %bitcast.2.y_ref, bf16[1,224,768]{2,1,0:T(8,128)(2,1)S(1)} %get-tuple-element.35.refs_0_.refs_4_, bf16[1,224,768]{2,1,0:T(8,128)(2,1)S(1)} %collective-permute-done.refs_1_.refs_5_, bf16[1,224,768]{2,1,0:T(8,128)(2,1)S(1)} %collective-permute-done.1.refs_2_.refs_7_, ...), custom_call_target="tpu_custom_call" | custom-call | flops 37748736 | bytes 1000000 | tf_op jit(solution)/shard_map/attend/pallas_call | solution.py:148
  99.9 9.8 %attend.3 = bf16[4,8,56,128]{3,2,1,0:T(8,128)(2,1)} custom-call(s32[1]{0:T(128)} %bitcast.2.y_ref, bf16[1,224,768]{2,1,0:T(8,128)(2,1)S(1)} %get-tuple-element.35.refs_0_.refs_4_, bf16[1,224,768]{2,1,0:T(8,128)(2,1)S(1)} %collective-permute-done.refs_1_.refs_5_, bf16[1,224,768]{2,1,0:T(8,128)(2,1)S(1)} %collective-permute-done.1.refs_2_.refs_7_, ...), custom_call_target="tpu_custom_call" | custom-call | flops 37748736 | bytes 1000000 | tf_op jit(solution)/shard_map/attend/pallas_call | solution.py:148
  109.6 5.3 %all-to-all-start.2 = ((bf16[32,56,128]{2,1,0:T(8,128)(2,1)}), bf16[32,56,128]{2,1,0:T(8,128)(2,1)S(1)}, u32[]{:S(2)}, u32[]{:S(2)}) async-start(bf16[32,56,128]{2,1,0:T(8,128)(2,1)} %bitcast.8), calls=%async_computation.2 | async-start | bytes 917504 | tf_op jit(solution)/shard_map/all_to_all | solution.py:313
  115.0 12.3 %all-gather.6.cloned.1.call-done = bf16[9216,256]{1,0:T(8,128)(2,1)} async-done(((bf16[1152,256]{1,0:T(8,128)(2,1)}), bf16[9216,256]{1,0:T(8,128)(2,1)}) %all-gather.6.cloned.1.call-update) | async-done | bytes 4718608 | tf_op jit(solution)/shard_map/all_gather | solution.py:285
  127.3 2.3 %copy-done.2 = bf16[9216,256]{1,0:T(8,128)(2,1)S(1)} copy-done((bf16[9216,256]{1,0:T(8,128)(2,1)S(1)}, bf16[9216,256]{1,0:T(8,128)(2,1)}, u32[]{:S(2)}) %copy-start.2) | copy-done | bytes 4718616
  129.6 1.1 prepare.1
  130.7 1.1 copy-done.3
  131.8 1.3 copy-done.5
  133.1 2.0 %collective-permute-start.7 = (bf16[1152,640]{1,0:T(8,128)(2,1)S(1)}, bf16[1152,640]{1,0:T(8,128)(2,1)S(1)}, u32[]{:S(2)}, u32[]{:S(2)}) collective-permute-start(bf16[1152,640]{1,0:T(8,128)(2,1)S(1)} %get-tuple-element.41.own), channel_id=1, source_target_pairs={{0,64},{64,0},{1,65},{65,1},{2,66},{66,2},{3,67},{67,3},{4,68},{68... | collective-permute-start | bytes 4423688 | tf_op jit(solution)/shard_map/ppermute | solution.py:318
  135.1 2.9 %collective-permute-done.7.got = bf16[1152,640]{1,0:T(8,128)(2,1)S(1)} collective-permute-done((bf16[1152,640]{1,0:T(8,128)(2,1)S(1)}, bf16[1152,640]{1,0:T(8,128)(2,1)S(1)}, u32[]{:S(2)}, u32[]{:S(2)}) %collective-permute-start.7) | collective-permute-done | bytes 1474592 | tf_op jit(solution)/shard_map/ppermute | solution.py:318
  138.0 0.4 collective-permute-start.15
  138.4 1.6 spatial_end.3
  140.0 2.2 %collective-permute-start.9 = (bf16[96,1152]{1,0:T(8,128)(2,1)S(1)}, bf16[96,1152]{1,0:T(8,128)(2,1)S(1)}, u32[]{:S(2)}, u32[]{:S(2)}) collective-permute-start(bf16[96,1152]{1,0:T(8,128)(2,1)S(1)} %get-tuple-element.43.n0), channel_id=1, source_target_pairs={{0,128},{128,0},{1,129},{129,1},{2,130},{130,2},{3,131},{131,3},{4... | collective-permute-start | bytes 663560 | tf_op jit(solution)/shard_map/ppermute | solution.py:330
  142.2 1.6 spatial_end.2
  144.0 0.5 collective-permute-start.8
  144.5 3.4 %collective-permute-done.9.n2 = bf16[96,1152]{1,0:T(8,128)(2,1)S(1)} collective-permute-done((bf16[96,1152]{1,0:T(8,128)(2,1)S(1)}, bf16[96,1152]{1,0:T(8,128)(2,1)S(1)}, u32[]{:S(2)}, u32[]{:S(2)}) %collective-permute-start.9) | collective-permute-done | bytes 221216 | tf_op jit(solution)/shard_map/ppermute | solution.py:330
  147.9 4.7 %collective-permute-done.10.n2 = bf16[96,1152]{1,0:T(8,128)(2,1)S(1)} collective-permute-done((bf16[96,1152]{1,0:T(8,128)(2,1)S(1)}, bf16[96,1152]{1,0:T(8,128)(2,1)S(1)}, u32[]{:S(2)}, u32[]{:S(2)}) %collective-permute-start.10) | collective-permute-done | bytes 221216 | tf_op jit(solution)/shard_map/ppermute | solution.py:330
  152.6 0.7 collective-permute-start.11
  153.4 0.5 collective-permute-start.17
  153.9 0.6 collective-permute-done.11.n3
  154.5 2.1 %temporal.2 = (bf16[216,128]{1,0:T(8,128)(2,1)S(1)}, bf16[216,128]{1,0:T(8,128)(2,1)S(1)}, bf16[216,128]{1,0:T(8,128)(2,1)S(1)}, bf16[216,128]{1,0:T(8,128)(2,1)S(1)}) custom-call(bf16[96,1152]{1,0:T(8,128)(2,1)S(1)} %get-tuple-element.42.n0, bf16[96,1152]{1,0:T(8,128)(2,1)S(1)} %collective-permute-done.8.n1, ...), custom_call_target="tpu_custom_call" | custom-call | flops 2000000000 | bytes 8000000 | tf_op jit(solution)/shard_map/temporal/pallas_call | solution.py:239
  156.6 2.1 %temporal.3 = (bf16[216,128]{1,0:T(8,128)(2,1)S(1)}, bf16[216,128]{1,0:T(8,128)(2,1)S(1)}, bf16[216,128]{1,0:T(8,128)(2,1)S(1)}, bf16[216,128]{1,0:T(8,128)(2,1)S(1)}) custom-call(bf16[96,1152]{1,0:T(8,128)(2,1)S(1)} %get-tuple-element.43.n0, bf16[96,1152]{1,0:T(8,128)(2,1)S(1)} %collective-permute-done.16.n1, ...), custom_call_target="tpu_custom_call" | custom-call | flops 2000000000 | bytes 8000000 | tf_op jit(solution)/shard_map/temporal/pallas_call | solution.py:239
  158.7 0.5 collective-permute-start.18
  159.2 1.5 collective-permute-start.19
  160.6 0.3 collective-permute-start.20
  160.9 0.1 collective-permute-start.12
  161.1 1.4 collective-permute-start.13
  162.5 2.9 %collective-permute-start.14 = (bf16[216,128]{1,0:T(8,128)(2,1)S(1)}, bf16[216,128]{1,0:T(8,128)(2,1)S(1)}, u32[]{:S(2)}, u32[]{:S(2)}) collective-permute-start(bf16[216,128]{1,0:T(8,128)(2,1)S(1)} %get-tuple-element.49), channel_id=1, source_target_pairs={{0,192},{192,0},{64,128},{128,64},{1,193},{193,1},{65,129},{129,65... | collective-permute-start | bytes 165896 | tf_op jit(solution)/shard_map/ppermute | solution.py:342
  165.4 2.4 %temporal_end.2.refs_0_ = bf16[192,1152]{1,0:T(8,128)(2,1)} custom-call(s32[2]{0:T(128)S(1)} %pad_add_fusion.place_ref, bf16[216,128]{1,0:T(8,128)(2,1)S(1)} %get-tuple-element.58.m0, bf16[216,128]{1,0:T(8,128)(2,1)S(1)} %collective-permute-done.18.m1, bf16[216,128]{1,0:T(8,128)(2,1)S(1)} %collective-permute-done.19.m2, ...), custom_call_target="tpu_custom_call" | custom-call | flops 2000000000 | bytes 8000000 | tf_op jit(solution)/shard_map/temporal_end/pallas_call | solution.py:239
  167.8 2.4 %temporal_end.3 = bf16[192,1152]{1,0:T(8,128)(2,1)} custom-call(s32[2]{0:T(128)S(1)} %pad_add_fusion.place_ref, bf16[216,128]{1,0:T(8,128)(2,1)S(1)} %get-tuple-element.46.m0, bf16[216,128]{1,0:T(8,128)(2,1)S(1)} %collective-permute-done.12.m1, bf16[216,128]{1,0:T(8,128)(2,1)S(1)} %collective-permute-done.13.m2, ...), custom_call_target="tpu_custom_call", output_to_operand_aliasing={{}: (9, {})} | custom-call | flops 2000000000 | bytes 8000000 | tf_op jit(solution)/shard_map/temporal_end/pallas_call | solution.py:239
  (58 shorter events, 1.2 us)
Async XLA Ops:
  6.5 2.3 %copy-start.7 = (bf16[18,3456]{1,0:T(8,128)(2,1)S(1)}, bf16[18,3456]{1,0:T(8,128)(2,1)}, u32[]{:S(2)}) copy-start(bf16[18,3456]{1,0:T(8,128)(2,1)} %param.11) | copy-start | bytes 373252
  6.5 2.6 %copy-start.8 = (bf16[18,1152]{1,0:T(8,128)(2,1)S(1)}, bf16[18,1152]{1,0:T(8,128)(2,1)}, u32[]{:S(2)}) copy-start(bf16[18,1152]{1,0:T(8,128)(2,1)} %param.12) | copy-start | bytes 124420
  6.5 2.6 %copy-start.9 = (bf16[18,1152]{1,0:T(8,128)(2,1)S(1)}, bf16[18,1152]{1,0:T(8,128)(2,1)}, u32[]{:S(2)}) copy-start(bf16[18,1152]{1,0:T(8,128)(2,1)} %param.10) | copy-start | bytes 124420
  6.5 56.6 %all-gather.4.cloned.1.call-start = ((), (), s32[]{:S(2)}) async-start(), calls=%async_computation.3 | async-start | bytes 3981312 | tf_op jit(solution)/shard_map/all_gather | solution.py:282
  7.3 120.0 %all-gather.6.cloned.1.call-start = ((), (), s32[]{:S(2)}) async-start(), calls=%async_computation.4 | async-start | bytes 5308416 | tf_op jit(solution)/shard_map/all_gather | solution.py:285
  56.4 6.8 %copy-start.10 = (f32[4,72]{1,0:T(4,128)S(1)}, f32[4,72]{1,0:T(4,128)}, u32[]{:S(2)}) copy-start(f32[4,72]{1,0:T(4,128)} %param.13) | copy-start | bytes 3460
  56.4 6.9 %copy-start.1 = (f32[6,1152]{1,0:T(8,128)S(1)}, f32[6,1152]{1,0:T(8,128)}, u32[]{:S(2)}) copy-start(f32[6,1152]{1,0:T(8,128)} %mod_ref.9) | copy-start | bytes 82948
  69.8 10.6 %collective-permute-start = (bf16[1,224,768]{2,1,0:T(8,128)(2,1)S(1)}, bf16[1,224,768]{2,1,0:T(8,128)(2,1)S(1)}, u32[]{:S(2)}, u32[]{:S(2)}) collective-permute-start(bf16[1,224,768]{2,1,0:T(8,128)(2,1)S(1)} %get-tuple-element.36), channel_id=1, source_target_pairs={{0,8},{8,16},{16,24},{24,0},{1,9},{9,17},{17,25},{25,1},{2,10},{10... | collective-permute-start | bytes 1032200 | tf_op jit(solution)/shard_map/ppermute | solution.py:308
  71.1 12.1 %collective-permute-start.2 = (bf16[1,224,768]{2,1,0:T(8,128)(2,1)S(1)}, bf16[1,224,768]{2,1,0:T(8,128)(2,1)S(1)}, u32[]{:S(2)}, u32[]{:S(2)}) collective-permute-start(bf16[1,224,768]{2,1,0:T(8,128)(2,1)S(1)} %get-tuple-element.38), channel_id=1, source_target_pairs={{0,24},{8,0},{16,8},{24,16},{1,25},{9,1},{17,9},{25,17},{2,26},{10... | collective-permute-start | bytes 1032200 | tf_op jit(solution)/shard_map/ppermute | solution.py:308
  72.6 15.8 %collective-permute-start.1 = (bf16[1,224,768]{2,1,0:T(8,128)(2,1)S(1)}, bf16[1,224,768]{2,1,0:T(8,128)(2,1)S(1)}, u32[]{:S(2)}, u32[]{:S(2)}) collective-permute-start(bf16[1,224,768]{2,1,0:T(8,128)(2,1)S(1)} %get-tuple-element.37), channel_id=1, source_target_pairs={{0,16},{8,24},{16,0},{24,8},{1,17},{9,25},{17,1},{25,9},{2,18},{10... | collective-permute-start | bytes 1032200 | tf_op jit(solution)/shard_map/ppermute | solution.py:308
  74.0 25.8 %collective-permute-start.3 = (bf16[1,144,768]{2,1,0:T(8,128)(2,1)S(1)}, bf16[1,144,768]{2,1,0:T(8,128)(2,1)S(1)}, u32[]{:S(2)}, u32[]{:S(2)}) collective-permute-start(bf16[1,144,768]{2,1,0:T(8,128)(2,1)S(1)} %slice.32), channel_id=1, source_target_pairs={{0,32},{32,0},{1,33},{33,1},{2,34},{34,2},{3,35},{35,3},{4,36},{36... | collective-permute-start | bytes 663560 | tf_op jit(solution)/shard_map/ppermute | solution.py:309
  80.4 19.4 %collective-permute-start.4 = (bf16[1,144,768]{2,1,0:T(8,128)(2,1)S(1)}, bf16[1,144,768]{2,1,0:T(8,128)(2,1)S(1)}, u32[]{:S(2)}, u32[]{:S(2)}) collective-permute-start(bf16[1,144,768]{2,1,0:T(8,128)(2,1)S(1)} %slice.37), channel_id=1, source_target_pairs={{0,32},{32,0},{1,33},{33,1},{2,34},{34,2},{3,35},{35,3},{4,36},{36... | collective-permute-start | bytes 663560 | tf_op jit(solution)/shard_map/ppermute | solution.py:309
  83.2 16.6 %collective-permute-start.5 = (bf16[1,144,768]{2,1,0:T(8,128)(2,1)S(1)}, bf16[1,144,768]{2,1,0:T(8,128)(2,1)S(1)}, u32[]{:S(2)}, u32[]{:S(2)}) collective-permute-start(bf16[1,144,768]{2,1,0:T(8,128)(2,1)S(1)} %slice.38), channel_id=1, source_target_pairs={{0,32},{32,0},{1,33},{33,1},{2,34},{34,2},{3,35},{35,3},{4,36},{36... | collective-permute-start | bytes 663560 | tf_op jit(solution)/shard_map/ppermute | solution.py:309
  88.4 11.5 %collective-permute-start.6 = (bf16[1,144,768]{2,1,0:T(8,128)(2,1)S(1)}, bf16[1,144,768]{2,1,0:T(8,128)(2,1)S(1)}, u32[]{:S(2)}, u32[]{:S(2)}) collective-permute-start(bf16[1,144,768]{2,1,0:T(8,128)(2,1)S(1)} %slice.39), channel_id=1, source_target_pairs={{0,32},{32,0},{1,33},{33,1},{2,34},{34,2},{3,35},{35,3},{4,36},{36... | collective-permute-start | bytes 663560 | tf_op jit(solution)/shard_map/ppermute | solution.py:309
  109.6 23.4 %all-to-all-start.2 = ((bf16[32,56,128]{2,1,0:T(8,128)(2,1)}), bf16[32,56,128]{2,1,0:T(8,128)(2,1)S(1)}, u32[]{:S(2)}, u32[]{:S(2)}) async-start(bf16[32,56,128]{2,1,0:T(8,128)(2,1)} %bitcast.8), calls=%async_computation.2 | async-start | bytes 917504 | tf_op jit(solution)/shard_map/all_to_all | solution.py:313
  127.3 2.3 %copy-start.2 = (bf16[9216,256]{1,0:T(8,128)(2,1)S(1)}, bf16[9216,256]{1,0:T(8,128)(2,1)}, u32[]{:S(2)}) copy-start(bf16[9216,256]{1,0:T(8,128)(2,1)} %all-gather.6.cloned.1.call-done) | copy-start | bytes 14155780
  129.6 8.8 %copy-start = (bf16[2,1,96,1152]{3,2,1,0:T(8,128)(2,1)S(1)}, bf16[2,1,96,1152]{3,2,1,0:T(8,128)(2,1)}, u32[]{:S(2)}) copy-start(bf16[2,1,96,1152]{3,2,1,0:T(8,128)(2,1)} %param.7) | copy-start | bytes 1327108
  130.7 1.1 copy-start.3
  131.8 1.3 copy-start.5
  133.1 4.9 %collective-permute-start.7 = (bf16[1152,640]{1,0:T(8,128)(2,1)S(1)}, bf16[1152,640]{1,0:T(8,128)(2,1)S(1)}, u32[]{:S(2)}, u32[]{:S(2)}) collective-permute-start(bf16[1152,640]{1,0:T(8,128)(2,1)S(1)} %get-tuple-element.41.own), channel_id=1, source_target_pairs={{0,64},{64,0},{1,65},{65,1},{2,66},{66,2},{3,67},{67,3},{4,68},{68... | collective-permute-start | bytes 4423688 | tf_op jit(solution)/shard_map/ppermute | solution.py:318
  138.0 27.4 %collective-permute-start.15 = (bf16[576,1152]{1,0:T(8,128)(2,1)}, bf16[576,1152]{1,0:T(8,128)(2,1)S(1)}, u32[]{:S(2)}, u32[]{:S(2)}) collective-permute-start(bf16[576,1152]{1,0:T(8,128)(2,1)} %copy-done.3), channel_id=1, source_target_pairs={{0,64},{64,0},{1,65},{65,1},{2,66},{66,2},{3,67},{67,3},{4,68},{68... | collective-permute-start | bytes 3981320 | tf_op jit(solution)/shard_map/ppermute | solution.py:320
  140.0 14.4 %copy-start.6 = (bf16[864,1152]{1,0:T(8,128)(2,1)S(1)}, bf16[864,1152]{1,0:T(8,128)(2,1)}, u32[]{:S(2)}) copy-start(bf16[864,1152]{1,0:T(8,128)(2,1)} %copy-done.5) | copy-start | bytes 5971972
  140.0 7.9 %collective-permute-start.9 = (bf16[96,1152]{1,0:T(8,128)(2,1)S(1)}, bf16[96,1152]{1,0:T(8,128)(2,1)S(1)}, u32[]{:S(2)}, u32[]{:S(2)}) collective-permute-start(bf16[96,1152]{1,0:T(8,128)(2,1)S(1)} %get-tuple-element.43.n0), channel_id=1, source_target_pairs={{0,128},{128,0},{1,129},{129,1},{2,130},{130,2},{3,131},{131,3},{4... | collective-permute-start | bytes 663560 | tf_op jit(solution)/shard_map/ppermute | solution.py:330
  143.9 8.8 %collective-permute-start.10 = (bf16[96,1152]{1,0:T(8,128)(2,1)S(1)}, bf16[96,1152]{1,0:T(8,128)(2,1)S(1)}, u32[]{:S(2)}, u32[]{:S(2)}) collective-permute-start(bf16[96,1152]{1,0:T(8,128)(2,1)S(1)} %get-tuple-element.42.n0), channel_id=1, source_target_pairs={{0,128},{128,0},{1,129},{129,1},{2,130},{130,2},{3,131},{131,3},{4... | collective-permute-start | bytes 663560 | tf_op jit(solution)/shard_map/ppermute | solution.py:330
  144.0 9.9 %collective-permute-start.8 = (bf16[96,1152]{1,0:T(8,128)(2,1)S(1)}, bf16[96,1152]{1,0:T(8,128)(2,1)S(1)}, u32[]{:S(2)}, u32[]{:S(2)}) collective-permute-start(bf16[96,1152]{1,0:T(8,128)(2,1)S(1)} %get-tuple-element.42.n0), channel_id=1, source_target_pairs={{0,64},{64,0},{1,65},{65,1},{2,66},{66,2},{3,67},{67,3},{4,68},{68... | collective-permute-start | bytes 663560 | tf_op jit(solution)/shard_map/ppermute | solution.py:333
  152.6 1.8 %collective-permute-start.11 = (bf16[96,1152]{1,0:T(8,128)(2,1)S(1)}, bf16[96,1152]{1,0:T(8,128)(2,1)S(1)}, u32[]{:S(2)}, u32[]{:S(2)}) collective-permute-start(bf16[96,1152]{1,0:T(8,128)(2,1)S(1)} %collective-permute-done.10.n2), channel_id=1, source_target_pairs={{0,64},{64,0},{1,65},{65,1},{2,66},{66,2},{3,67},{67,3},{4,68},{68... | collective-permute-start | bytes 663560 | tf_op jit(solution)/shard_map/ppermute | solution.py:333
  153.4 3.2 %collective-permute-start.16 = (bf16[96,1152]{1,0:T(8,128)(2,1)S(1)}, bf16[96,1152]{1,0:T(8,128)(2,1)S(1)}, u32[]{:S(2)}, u32[]{:S(2)}) collective-permute-start(bf16[96,1152]{1,0:T(8,128)(2,1)S(1)} %get-tuple-element.43.n0), channel_id=1, source_target_pairs={{0,64},{64,0},{1,65},{65,1},{2,66},{66,2},{3,67},{67,3},{4,68},{68... | collective-permute-start | bytes 663560 | tf_op jit(solution)/shard_map/ppermute | solution.py:333
  153.4 3.2 %collective-permute-start.17 = (bf16[96,1152]{1,0:T(8,128)(2,1)S(1)}, bf16[96,1152]{1,0:T(8,128)(2,1)S(1)}, u32[]{:S(2)}, u32[]{:S(2)}) collective-permute-start(bf16[96,1152]{1,0:T(8,128)(2,1)S(1)} %collective-permute-done.9.n2), channel_id=1, source_target_pairs={{0,64},{64,0},{1,65},{65,1},{2,66},{66,2},{3,67},{67,3},{4,68},{68... | collective-permute-start | bytes 663560 | tf_op jit(solution)/shard_map/ppermute | solution.py:333
  156.6 8.8 %copy-start.4 = (bf16[576,1152]{1,0:T(8,128)(2,1)S(1)}, bf16[576,1152]{1,0:T(8,128)(2,1)}, u32[]{:S(2)}) copy-start(bf16[576,1152]{1,0:T(8,128)(2,1)} %copy-done.3) | copy-start | bytes 3981316
  158.7 2.4 %collective-permute-start.18 = (bf16[216,128]{1,0:T(8,128)(2,1)S(1)}, bf16[216,128]{1,0:T(8,128)(2,1)S(1)}, u32[]{:S(2)}, u32[]{:S(2)}) collective-permute-start(bf16[216,128]{1,0:T(8,128)(2,1)S(1)} %get-tuple-element.59), channel_id=1, source_target_pairs={{0,64},{64,0},{1,65},{65,1},{2,66},{66,2},{3,67},{67,3},{4,68},{68... | collective-permute-start | bytes 165896 | tf_op jit(solution)/shard_map/ppermute | solution.py:340
  159.2 3.3 %collective-permute-start.19 = (bf16[216,128]{1,0:T(8,128)(2,1)S(1)}, bf16[216,128]{1,0:T(8,128)(2,1)S(1)}, u32[]{:S(2)}, u32[]{:S(2)}) collective-permute-start(bf16[216,128]{1,0:T(8,128)(2,1)S(1)} %get-tuple-element.60), channel_id=1, source_target_pairs={{0,128},{128,0},{1,129},{129,1},{2,130},{130,2},{3,131},{131,3},{4... | collective-permute-start | bytes 165896 | tf_op jit(solution)/shard_map/ppermute | solution.py:341
  160.6 4.7 %collective-permute-start.20 = (bf16[216,128]{1,0:T(8,128)(2,1)S(1)}, bf16[216,128]{1,0:T(8,128)(2,1)S(1)}, u32[]{:S(2)}, u32[]{:S(2)}) collective-permute-start(bf16[216,128]{1,0:T(8,128)(2,1)S(1)} %get-tuple-element.61), channel_id=1, source_target_pairs={{0,192},{192,0},{64,128},{128,64},{1,193},{193,1},{65,129},{129,65... | collective-permute-start | bytes 165896 | tf_op jit(solution)/shard_map/ppermute | solution.py:342
  160.9 6.9 %collective-permute-start.12 = (bf16[216,128]{1,0:T(8,128)(2,1)S(1)}, bf16[216,128]{1,0:T(8,128)(2,1)S(1)}, u32[]{:S(2)}, u32[]{:S(2)}) collective-permute-start(bf16[216,128]{1,0:T(8,128)(2,1)S(1)} %get-tuple-element.47), channel_id=1, source_target_pairs={{0,64},{64,0},{1,65},{65,1},{2,66},{66,2},{3,67},{67,3},{4,68},{68... | collective-permute-start | bytes 165896 | tf_op jit(solution)/shard_map/ppermute | solution.py:340
  161.1 6.7 %collective-permute-start.13 = (bf16[216,128]{1,0:T(8,128)(2,1)S(1)}, bf16[216,128]{1,0:T(8,128)(2,1)S(1)}, u32[]{:S(2)}, u32[]{:S(2)}) collective-permute-start(bf16[216,128]{1,0:T(8,128)(2,1)S(1)} %get-tuple-element.48), channel_id=1, source_target_pairs={{0,128},{128,0},{1,129},{129,1},{2,130},{130,2},{3,131},{131,3},{4... | collective-permute-start | bytes 165896 | tf_op jit(solution)/shard_map/ppermute | solution.py:341
  162.5 5.3 %collective-permute-start.14 = (bf16[216,128]{1,0:T(8,128)(2,1)S(1)}, bf16[216,128]{1,0:T(8,128)(2,1)S(1)}, u32[]{:S(2)}, u32[]{:S(2)}) collective-permute-start(bf16[216,128]{1,0:T(8,128)(2,1)S(1)} %get-tuple-element.49), channel_id=1, source_target_pairs={{0,192},{192,0},{64,128},{128,64},{1,193},{193,1},{65,129},{129,65... | collective-permute-start | bytes 165896 | tf_op jit(solution)/shard_map/ppermute | solution.py:342
Sparse Core Ops, SparseCore 0:
  9.2 53.9 all-gather.3
  65.0 62.2 all-gather.5

commit v12 on v11

--- a/solution.py
+++ b/solution.py
@@ -313,7 +313,7 @@
     attended = lax.all_to_all(attended, ("y", "z"), 0, 0, tiled=True)
     attended = attended.reshape(4, NZ, 56, 128)
     shapes = [shape(BF, D, 640), shape(BF, 12 * HD, D), shape(BF, half, D)]
-    out_a, turned, out_b = once(prepare, [rest], [full(rest)], shapes, grant=24)
+    out_a, turned, out_b = once(prepare, [rest], [full(rest)], shapes, grant=44)
     swapped, _ = lax.optimization_barrier((out_a, attended))
     got_a = lax.ppermute(swapped, "c", swap)
     swapped, _ = lax.optimization_barrier((out_b, got_a))

time: 177 us -> 177 us (level)
  no operation moved by 1% of the time
where the time goes in v12:
time: 177 us
  blocking collectives  46.7 us (26%)
  waiting for transfers between devices  38.9 us (22%)
  Pallas kernels  38.1 us (22%)
  starting transfers between devices  31.5 us (18%)
  between operations  13.7 us (8%)
  local copies, waits for them, and re-layouts  8.01 us (5%)
    all_to_all x1, blocking collectives, per_device(): shard = lax.all_to_all(shard, ('xh', 'y'), 0, 0, tiled=True).reshape(D, 768)  27 us
    all_to_all x1, blocking collectives, per_device(): lax.all_to_all(shard, 'z', 0, 0, tiled=True).reshape(1, NZ * 18, 768)  19.7 us
    pallas_call x2, Pallas kernels, attention(): pl.pallas_call(functools.partial(attend, count, part is not None, finish)...  18.3 us
    pallas_call x7, Pallas kernels, once(): pl.pallas_call(kernel, grid=(1,), in_specs=specs, out_specs=out_specs or...  13.3 us
    all_gather x1, waiting for transfers between devices, per_device(): rest = lax.all_gather(rest, 'z', axis=0)  12.3 us
    ppermute x4, starting transfers between devices, per_device(): others = [lax.ppermute(block[:, :2 * HD], 'xh', swap) for block in blocks]  8.82 us
    ppermute x3, waiting for transfers between devices, per_device(): lax.ppermute(slots[n], 'y', [(i, (i + n) % NY) for i in range(NY)])  8.36 us
    ppermute x2, waiting for transfers between devices, per_device(): moved = [lax.ppermute(norm, 'xl', swap) for _, norm in steps]  8.15 us
  transfers between devices with their start and end apart: 24, of which 8 were waited for; matrix products, arithmetic and copies ran while one was open for 2% of the time, Pallas kernels for 20%

profile of v12, /device:TPU:1, one launch (start us, length us, event | category | flops | bytes accessed | tf_op | source)
XLA Modules:
  0.0 177.1 jit_solution(10671440005710644513)
XLA Ops:
  6.5 0.7 all-gather.4.cloned.1.call-update
  7.3 1.2 reshape.36
  8.5 0.1 copy.21
  8.7 0.2 reshape.37
  9.6 19.7 %all_to_all.15 = bf16[8,18,768]{2,1,0:T(8,128)(2,1)S(1)} all-to-all(bf16[8,18,768]{2,1,0:T(8,128)(2,1)S(1)} %copy.16), channel_id=1, replica_groups=mesh['xl'=2,'c'=2,'xh'=2,'y'=4,'z'=8] {'z'}, dimensions={0} | all-to-all | bytes 442368 | tf_op jit(solution)/shard_map/all_to_all | solution.py:278
  29.4 27.0 %all_to_all.16 = bf16[8,144,768]{2,1,0:T(8,128)(2,1)S(1)} all-to-all(bf16[8,144,768]{2,1,0:T(8,128)(2,1)S(1)} %broadcast_in_dim.8), channel_id=1, replica_groups=mesh['xl'=2,'c'=2,'xh'=2,'y'=4,'z'=8] {'xh','y'}, dimensions={0} | all-to-all | bytes 3538944 | tf_op jit(solution)/shard_map/all_to_all | solution.py:280
  56.5 0.9 slice.36
  57.4 5.8 %all-gather.4.cloned.1.call-done.tok_ref = bf16[8,192,1152]{2,1,0:T(8,128)(2,1)} async-done(((bf16[1,192,1152]{2,1,0:T(8,128)(2,1)}), bf16[8,192,1152]{2,1,0:T(8,128)(2,1)}) %all-gather.4.cloned.1.call-update) | async-done | bytes 3538960 | tf_op jit(solution)/shard_map/all_gather | solution.py:282
  63.3 6.5 %spatial_proj.1 = (bf16[1,224,768]{2,1,0:T(8,128)(2,1)S(1)}, bf16[1,224,768]{2,1,0:T(8,128)(2,1)S(1)}, bf16[1,224,768]{2,1,0:T(8,128)(2,1)S(1)}, bf16[1,224,768]{2,1,0:T(8,128)(2,1)S(1)}) custom-call(s32[1]{0:T(128)} %bitcast.2.y_ref, bf16[8,192,1152]{2,1,0:T(8,128)(2,1)} %all-gather.4.cloned.1.call-done.tok_ref, f32[6,1152]{1,0:T(8,128)S(1)} %copy-done.1, ...), custom_call_target="tpu_custom_call" | custom-call | tf_op jit(solution)/shard_map/spatial_proj/pallas_call | solution.py:288
  69.8 1.3 collective-permute-start
  71.1 1.5 collective-permute-start.2
  72.6 1.5 collective-permute-start.1
  74.0 2.7 %collective-permute-start.3 = (bf16[1,144,768]{2,1,0:T(8,128)(2,1)S(1)}, bf16[1,144,768]{2,1,0:T(8,128)(2,1)S(1)}, u32[]{:S(2)}, u32[]{:S(2)}) collective-permute-start(bf16[1,144,768]{2,1,0:T(8,128)(2,1)S(1)} %slice.32), channel_id=1, source_target_pairs={{0,32},{32,0},{1,33},{33,1},{2,34},{34,2},{3,35},{35,3},{4,36},{36... | collective-permute-start | bytes 663560 | tf_op jit(solution)/shard_map/ppermute | solution.py:309
  76.8 3.6 %collective-permute-done.refs_1_.refs_5_ = bf16[1,224,768]{2,1,0:T(8,128)(2,1)S(1)} collective-permute-done((bf16[1,224,768]{2,1,0:T(8,128)(2,1)S(1)}, bf16[1,224,768]{2,1,0:T(8,128)(2,1)S(1)}, u32[]{:S(2)}, u32[]{:S(2)}) %collective-permute-start) | collective-permute-done | bytes 344096 | tf_op jit(solution)/shard_map/ppermute | solution.py:308
  80.4 2.8 %collective-permute-start.4 = (bf16[1,144,768]{2,1,0:T(8,128)(2,1)S(1)}, bf16[1,144,768]{2,1,0:T(8,128)(2,1)S(1)}, u32[]{:S(2)}, u32[]{:S(2)}) collective-permute-start(bf16[1,144,768]{2,1,0:T(8,128)(2,1)S(1)} %slice.37), channel_id=1, source_target_pairs={{0,32},{32,0},{1,33},{33,1},{2,34},{34,2},{3,35},{35,3},{4,36},{36... | collective-permute-start | bytes 663560 | tf_op jit(solution)/shard_map/ppermute | solution.py:309
  83.2 0.3 collective-permute-start.5
  83.6 4.8 %collective-permute-done.1.refs_2_.refs_7_ = bf16[1,224,768]{2,1,0:T(8,128)(2,1)S(1)} collective-permute-done((bf16[1,224,768]{2,1,0:T(8,128)(2,1)S(1)}, bf16[1,224,768]{2,1,0:T(8,128)(2,1)S(1)}, u32[]{:S(2)}, u32[]{:S(2)}) %collective-permute-start.1) | collective-permute-done | bytes 344096 | tf_op jit(solution)/shard_map/ppermute | solution.py:308
  88.4 2.9 %collective-permute-start.6 = (bf16[1,144,768]{2,1,0:T(8,128)(2,1)S(1)}, bf16[1,144,768]{2,1,0:T(8,128)(2,1)S(1)}, u32[]{:S(2)}, u32[]{:S(2)}) collective-permute-start(bf16[1,144,768]{2,1,0:T(8,128)(2,1)S(1)} %slice.39), channel_id=1, source_target_pairs={{0,32},{32,0},{1,33},{33,1},{2,34},{34,2},{3,35},{35,3},{4,36},{36... | collective-permute-start | bytes 663560 | tf_op jit(solution)/shard_map/ppermute | solution.py:309
  91.3 8.5 %attend.2.refs_8_ = f32[4,80,768]{2,1,0:T(8,128)S(1)} custom-call(s32[1]{0:T(128)} %bitcast.2.y_ref, bf16[1,224,768]{2,1,0:T(8,128)(2,1)S(1)} %get-tuple-element.35.refs_0_.refs_4_, bf16[1,224,768]{2,1,0:T(8,128)(2,1)S(1)} %collective-permute-done.refs_1_.refs_5_, bf16[1,224,768]{2,1,0:T(8,128)(2,1)S(1)} %collective-permute-done.1.refs_2_.refs_7_, ...), custom_call_target="tpu_custom_call" | custom-call | flops 37748736 | bytes 1000000 | tf_op jit(solution)/shard_map/attend/pallas_call | solution.py:148
  99.9 9.8 %attend.3 = bf16[4,8,56,128]{3,2,1,0:T(8,128)(2,1)} custom-call(s32[1]{0:T(128)} %bitcast.2.y_ref, bf16[1,224,768]{2,1,0:T(8,128)(2,1)S(1)} %get-tuple-element.35.refs_0_.refs_4_, bf16[1,224,768]{2,1,0:T(8,128)(2,1)S(1)} %collective-permute-done.refs_1_.refs_5_, bf16[1,224,768]{2,1,0:T(8,128)(2,1)S(1)} %collective-permute-done.1.refs_2_.refs_7_, ...), custom_call_target="tpu_custom_call" | custom-call | flops 37748736 | bytes 1000000 | tf_op jit(solution)/shard_map/attend/pallas_call | solution.py:148
  109.6 5.3 %all-to-all-start.2 = ((bf16[32,56,128]{2,1,0:T(8,128)(2,1)}), bf16[32,56,128]{2,1,0:T(8,128)(2,1)S(1)}, u32[]{:S(2)}, u32[]{:S(2)}) async-start(bf16[32,56,128]{2,1,0:T(8,128)(2,1)} %bitcast.8), calls=%async_computation.2 | async-start | bytes 917504 | tf_op jit(solution)/shard_map/all_to_all | solution.py:313
  115.0 12.3 %all-gather.6.cloned.1.call-done = bf16[9216,256]{1,0:T(8,128)(2,1)} async-done(((bf16[1152,256]{1,0:T(8,128)(2,1)}), bf16[9216,256]{1,0:T(8,128)(2,1)}) %all-gather.6.cloned.1.call-update) | async-done | bytes 4718608 | tf_op jit(solution)/shard_map/all_gather | solution.py:285
  127.3 2.3 %copy-done.2 = bf16[9216,256]{1,0:T(8,128)(2,1)S(1)} copy-done((bf16[9216,256]{1,0:T(8,128)(2,1)S(1)}, bf16[9216,256]{1,0:T(8,128)(2,1)}, u32[]{:S(2)}) %copy-start.2) | copy-done | bytes 4718616
  129.6 1.1 prepare.1
  130.7 1.1 copy-done.3
  131.8 1.3 copy-done.5
  133.1 2.0 %collective-permute-start.7 = (bf16[1152,640]{1,0:T(8,128)(2,1)S(1)}, bf16[1152,640]{1,0:T(8,128)(2,1)S(1)}, u32[]{:S(2)}, u32[]{:S(2)}) collective-permute-start(bf16[1152,640]{1,0:T(8,128)(2,1)S(1)} %get-tuple-element.41.own), channel_id=1, source_target_pairs={{0,64},{64,0},{1,65},{65,1},{2,66},{66,2},{3,67},{67,3},{4,68},{68... | collective-permute-start | bytes 4423688 | tf_op jit(solution)/shard_map/ppermute | solution.py:318
  135.1 2.9 %collective-permute-done.7.got = bf16[1152,640]{1,0:T(8,128)(2,1)S(1)} collective-permute-done((bf16[1152,640]{1,0:T(8,128)(2,1)S(1)}, bf16[1152,640]{1,0:T(8,128)(2,1)S(1)}, u32[]{:S(2)}, u32[]{:S(2)}) %collective-permute-start.7) | collective-permute-done | bytes 1474592 | tf_op jit(solution)/shard_map/ppermute | solution.py:318
  138.0 0.4 collective-permute-start.15
  138.4 1.6 spatial_end.3
  140.0 2.2 %collective-permute-start.9 = (bf16[96,1152]{1,0:T(8,128)(2,1)S(1)}, bf16[96,1152]{1,0:T(8,128)(2,1)S(1)}, u32[]{:S(2)}, u32[]{:S(2)}) collective-permute-start(bf16[96,1152]{1,0:T(8,128)(2,1)S(1)} %get-tuple-element.43.n0), channel_id=1, source_target_pairs={{0,128},{128,0},{1,129},{129,1},{2,130},{130,2},{3,131},{131,3},{4... | collective-permute-start | bytes 663560 | tf_op jit(solution)/shard_map/ppermute | solution.py:330
  142.2 1.6 spatial_end.2
  144.0 0.5 collective-permute-start.8
  144.5 3.4 %collective-permute-done.9.n2 = bf16[96,1152]{1,0:T(8,128)(2,1)S(1)} collective-permute-done((bf16[96,1152]{1,0:T(8,128)(2,1)S(1)}, bf16[96,1152]{1,0:T(8,128)(2,1)S(1)}, u32[]{:S(2)}, u32[]{:S(2)}) %collective-permute-start.9) | collective-permute-done | bytes 221216 | tf_op jit(solution)/shard_map/ppermute | solution.py:330
  147.9 4.7 %collective-permute-done.10.n2 = bf16[96,1152]{1,0:T(8,128)(2,1)S(1)} collective-permute-done((bf16[96,1152]{1,0:T(8,128)(2,1)S(1)}, bf16[96,1152]{1,0:T(8,128)(2,1)S(1)}, u32[]{:S(2)}, u32[]{:S(2)}) %collective-permute-start.10) | collective-permute-done | bytes 221216 | tf_op jit(solution)/shard_map/ppermute | solution.py:330
  152.6 0.7 collective-permute-start.11
  153.4 0.5 collective-permute-start.17
  153.9 0.6 collective-permute-done.11.n3
  154.5 2.1 %temporal.2 = (bf16[216,128]{1,0:T(8,128)(2,1)S(1)}, bf16[216,128]{1,0:T(8,128)(2,1)S(1)}, bf16[216,128]{1,0:T(8,128)(2,1)S(1)}, bf16[216,128]{1,0:T(8,128)(2,1)S(1)}) custom-call(bf16[96,1152]{1,0:T(8,128)(2,1)S(1)} %get-tuple-element.42.n0, bf16[96,1152]{1,0:T(8,128)(2,1)S(1)} %collective-permute-done.8.n1, ...), custom_call_target="tpu_custom_call" | custom-call | flops 2000000000 | bytes 8000000 | tf_op jit(solution)/shard_map/temporal/pallas_call | solution.py:239
  156.6 2.1 %temporal.3 = (bf16[216,128]{1,0:T(8,128)(2,1)S(1)}, bf16[216,128]{1,0:T(8,128)(2,1)S(1)}, bf16[216,128]{1,0:T(8,128)(2,1)S(1)}, bf16[216,128]{1,0:T(8,128)(2,1)S(1)}) custom-call(bf16[96,1152]{1,0:T(8,128)(2,1)S(1)} %get-tuple-element.43.n0, bf16[96,1152]{1,0:T(8,128)(2,1)S(1)} %collective-permute-done.16.n1, ...), custom_call_target="tpu_custom_call" | custom-call | flops 2000000000 | bytes 8000000 | tf_op jit(solution)/shard_map/temporal/pallas_call | solution.py:239
  158.7 0.5 collective-permute-start.18
  159.2 1.5 collective-permute-start.19
  160.6 0.3 collective-permute-start.20
  160.9 0.1 collective-permute-start.12
  161.1 1.4 collective-permute-start.13
  162.5 2.9 %collective-permute-start.14 = (bf16[216,128]{1,0:T(8,128)(2,1)S(1)}, bf16[216,128]{1,0:T(8,128)(2,1)S(1)}, u32[]{:S(2)}, u32[]{:S(2)}) collective-permute-start(bf16[216,128]{1,0:T(8,128)(2,1)S(1)} %get-tuple-element.49), channel_id=1, source_target_pairs={{0,192},{192,0},{64,128},{128,64},{1,193},{193,1},{65,129},{129,65... | collective-permute-start | bytes 165896 | tf_op jit(solution)/shard_map/ppermute | solution.py:342
  165.4 2.4 %temporal_end.2.refs_0_ = bf16[192,1152]{1,0:T(8,128)(2,1)} custom-call(s32[2]{0:T(128)S(1)} %pad_add_fusion.place_ref, bf16[216,128]{1,0:T(8,128)(2,1)S(1)} %get-tuple-element.58.m0, bf16[216,128]{1,0:T(8,128)(2,1)S(1)} %collective-permute-done.18.m1, bf16[216,128]{1,0:T(8,128)(2,1)S(1)} %collective-permute-done.19.m2, ...), custom_call_target="tpu_custom_call" | custom-call | flops 2000000000 | bytes 8000000 | tf_op jit(solution)/shard_map/temporal_end/pallas_call | solution.py:239
  167.8 2.4 %temporal_end.3 = bf16[192,1152]{1,0:T(8,128)(2,1)} custom-call(s32[2]{0:T(128)S(1)} %pad_add_fusion.place_ref, bf16[216,128]{1,0:T(8,128)(2,1)S(1)} %get-tuple-element.46.m0, bf16[216,128]{1,0:T(8,128)(2,1)S(1)} %collective-permute-done.12.m1, bf16[216,128]{1,0:T(8,128)(2,1)S(1)} %collective-permute-done.13.m2, ...), custom_call_target="tpu_custom_call", output_to_operand_aliasing={{}: (9, {})} | custom-call | flops 2000000000 | bytes 8000000 | tf_op jit(solution)/shard_map/temporal_end/pallas_call | solution.py:239
  (58 shorter events, 1.2 us)
Async XLA Ops:
  6.5 2.3 %copy-start.7 = (bf16[18,3456]{1,0:T(8,128)(2,1)S(1)}, bf16[18,3456]{1,0:T(8,128)(2,1)}, u32[]{:S(2)}) copy-start(bf16[18,3456]{1,0:T(8,128)(2,1)} %param.11) | copy-start | bytes 373252
  6.5 2.6 %copy-start.8 = (bf16[18,1152]{1,0:T(8,128)(2,1)S(1)}, bf16[18,1152]{1,0:T(8,128)(2,1)}, u32[]{:S(2)}) copy-start(bf16[18,1152]{1,0:T(8,128)(2,1)} %param.12) | copy-start | bytes 124420
  6.5 2.6 %copy-start.9 = (bf16[18,1152]{1,0:T(8,128)(2,1)S(1)}, bf16[18,1152]{1,0:T(8,128)(2,1)}, u32[]{:S(2)}) copy-start(bf16[18,1152]{1,0:T(8,128)(2,1)} %param.10) | copy-start | bytes 124420
  6.5 56.6 %all-gather.4.cloned.1.call-start = ((), (), s32[]{:S(2)}) async-start(), calls=%async_computation.3 | async-start | bytes 3981312 | tf_op jit(solution)/shard_map/all_gather | solution.py:282
  7.3 120.0 %all-gather.6.cloned.1.call-start = ((), (), s32[]{:S(2)}) async-start(), calls=%async_computation.4 | async-start | bytes 5308416 | tf_op jit(solution)/shard_map/all_gather | solution.py:285
  56.4 6.8 %copy-start.10 = (f32[4,72]{1,0:T(4,128)S(1)}, f32[4,72]{1,0:T(4,128)}, u32[]{:S(2)}) copy-start(f32[4,72]{1,0:T(4,128)} %param.13) | copy-start | bytes 3460
  56.4 6.9 %copy-start.1 = (f32[6,1152]{1,0:T(8,128)S(1)}, f32[6,1152]{1,0:T(8,128)}, u32[]{:S(2)}) copy-start(f32[6,1152]{1,0:T(8,128)} %mod_ref.9) | copy-start | bytes 82948
  69.8 10.6 %collective-permute-start = (bf16[1,224,768]{2,1,0:T(8,128)(2,1)S(1)}, bf16[1,224,768]{2,1,0:T(8,128)(2,1)S(1)}, u32[]{:S(2)}, u32[]{:S(2)}) collective-permute-start(bf16[1,224,768]{2,1,0:T(8,128)(2,1)S(1)} %get-tuple-element.36), channel_id=1, source_target_pairs={{0,8},{8,16},{16,24},{24,0},{1,9},{9,17},{17,25},{25,1},{2,10},{10... | collective-permute-start | bytes 1032200 | tf_op jit(solution)/shard_map/ppermute | solution.py:308
  71.1 12.1 %collective-permute-start.2 = (bf16[1,224,768]{2,1,0:T(8,128)(2,1)S(1)}, bf16[1,224,768]{2,1,0:T(8,128)(2,1)S(1)}, u32[]{:S(2)}, u32[]{:S(2)}) collective-permute-start(bf16[1,224,768]{2,1,0:T(8,128)(2,1)S(1)} %get-tuple-element.38), channel_id=1, source_target_pairs={{0,24},{8,0},{16,8},{24,16},{1,25},{9,1},{17,9},{25,17},{2,26},{10... | collective-permute-start | bytes 1032200 | tf_op jit(solution)/shard_map/ppermute | solution.py:308
  72.6 15.8 %collective-permute-start.1 = (bf16[1,224,768]{2,1,0:T(8,128)(2,1)S(1)}, bf16[1,224,768]{2,1,0:T(8,128)(2,1)S(1)}, u32[]{:S(2)}, u32[]{:S(2)}) collective-permute-start(bf16[1,224,768]{2,1,0:T(8,128)(2,1)S(1)} %get-tuple-element.37), channel_id=1, source_target_pairs={{0,16},{8,24},{16,0},{24,8},{1,17},{9,25},{17,1},{25,9},{2,18},{10... | collective-permute-start | bytes 1032200 | tf_op jit(solution)/shard_map/ppermute | solution.py:308
  74.0 25.8 %collective-permute-start.3 = (bf16[1,144,768]{2,1,0:T(8,128)(2,1)S(1)}, bf16[1,144,768]{2,1,0:T(8,128)(2,1)S(1)}, u32[]{:S(2)}, u32[]{:S(2)}) collective-permute-start(bf16[1,144,768]{2,1,0:T(8,128)(2,1)S(1)} %slice.32), channel_id=1, source_target_pairs={{0,32},{32,0},{1,33},{33,1},{2,34},{34,2},{3,35},{35,3},{4,36},{36... | collective-permute-start | bytes 663560 | tf_op jit(solution)/shard_map/ppermute | solution.py:309
  80.4 19.4 %collective-permute-start.4 = (bf16[1,144,768]{2,1,0:T(8,128)(2,1)S(1)}, bf16[1,144,768]{2,1,0:T(8,128)(2,1)S(1)}, u32[]{:S(2)}, u32[]{:S(2)}) collective-permute-start(bf16[1,144,768]{2,1,0:T(8,128)(2,1)S(1)} %slice.37), channel_id=1, source_target_pairs={{0,32},{32,0},{1,33},{33,1},{2,34},{34,2},{3,35},{35,3},{4,36},{36... | collective-permute-start | bytes 663560 | tf_op jit(solution)/shard_map/ppermute | solution.py:309
  83.2 16.6 %collective-permute-start.5 = (bf16[1,144,768]{2,1,0:T(8,128)(2,1)S(1)}, bf16[1,144,768]{2,1,0:T(8,128)(2,1)S(1)}, u32[]{:S(2)}, u32[]{:S(2)}) collective-permute-start(bf16[1,144,768]{2,1,0:T(8,128)(2,1)S(1)} %slice.38), channel_id=1, source_target_pairs={{0,32},{32,0},{1,33},{33,1},{2,34},{34,2},{3,35},{35,3},{4,36},{36... | collective-permute-start | bytes 663560 | tf_op jit(solution)/shard_map/ppermute | solution.py:309
  88.4 11.5 %collective-permute-start.6 = (bf16[1,144,768]{2,1,0:T(8,128)(2,1)S(1)}, bf16[1,144,768]{2,1,0:T(8,128)(2,1)S(1)}, u32[]{:S(2)}, u32[]{:S(2)}) collective-permute-start(bf16[1,144,768]{2,1,0:T(8,128)(2,1)S(1)} %slice.39), channel_id=1, source_target_pairs={{0,32},{32,0},{1,33},{33,1},{2,34},{34,2},{3,35},{35,3},{4,36},{36... | collective-permute-start | bytes 663560 | tf_op jit(solution)/shard_map/ppermute | solution.py:309
  109.6 23.4 %all-to-all-start.2 = ((bf16[32,56,128]{2,1,0:T(8,128)(2,1)}), bf16[32,56,128]{2,1,0:T(8,128)(2,1)S(1)}, u32[]{:S(2)}, u32[]{:S(2)}) async-start(bf16[32,56,128]{2,1,0:T(8,128)(2,1)} %bitcast.8), calls=%async_computation.2 | async-start | bytes 917504 | tf_op jit(solution)/shard_map/all_to_all | solution.py:313
  127.3 2.3 %copy-start.2 = (bf16[9216,256]{1,0:T(8,128)(2,1)S(1)}, bf16[9216,256]{1,0:T(8,128)(2,1)}, u32[]{:S(2)}) copy-start(bf16[9216,256]{1,0:T(8,128)(2,1)} %all-gather.6.cloned.1.call-done) | copy-start | bytes 14155780
  129.6 8.8 %copy-start = (bf16[2,1,96,1152]{3,2,1,0:T(8,128)(2,1)S(1)}, bf16[2,1,96,1152]{3,2,1,0:T(8,128)(2,1)}, u32[]{:S(2)}) copy-start(bf16[2,1,96,1152]{3,2,1,0:T(8,128)(2,1)} %param.7) | copy-start | bytes 1327108
  130.7 1.1 copy-start.3
  131.8 1.3 copy-start.5
  133.1 4.9 %collective-permute-start.7 = (bf16[1152,640]{1,0:T(8,128)(2,1)S(1)}, bf16[1152,640]{1,0:T(8,128)(2,1)S(1)}, u32[]{:S(2)}, u32[]{:S(2)}) collective-permute-start(bf16[1152,640]{1,0:T(8,128)(2,1)S(1)} %get-tuple-element.41.own), channel_id=1, source_target_pairs={{0,64},{64,0},{1,65},{65,1},{2,66},{66,2},{3,67},{67,3},{4,68},{68... | collective-permute-start | bytes 4423688 | tf_op jit(solution)/shard_map/ppermute | solution.py:318
  138.0 27.4 %collective-permute-start.15 = (bf16[576,1152]{1,0:T(8,128)(2,1)}, bf16[576,1152]{1,0:T(8,128)(2,1)S(1)}, u32[]{:S(2)}, u32[]{:S(2)}) collective-permute-start(bf16[576,1152]{1,0:T(8,128)(2,1)} %copy-done.3), channel_id=1, source_target_pairs={{0,64},{64,0},{1,65},{65,1},{2,66},{66,2},{3,67},{67,3},{4,68},{68... | collective-permute-start | bytes 3981320 | tf_op jit(solution)/shard_map/ppermute | solution.py:320
  140.0 14.4 %copy-start.6 = (bf16[864,1152]{1,0:T(8,128)(2,1)S(1)}, bf16[864,1152]{1,0:T(8,128)(2,1)}, u32[]{:S(2)}) copy-start(bf16[864,1152]{1,0:T(8,128)(2,1)} %copy-done.5) | copy-start | bytes 5971972
  140.0 7.9 %collective-permute-start.9 = (bf16[96,1152]{1,0:T(8,128)(2,1)S(1)}, bf16[96,1152]{1,0:T(8,128)(2,1)S(1)}, u32[]{:S(2)}, u32[]{:S(2)}) collective-permute-start(bf16[96,1152]{1,0:T(8,128)(2,1)S(1)} %get-tuple-element.43.n0), channel_id=1, source_target_pairs={{0,128},{128,0},{1,129},{129,1},{2,130},{130,2},{3,131},{131,3},{4... | collective-permute-start | bytes 663560 | tf_op jit(solution)/shard_map/ppermute | solution.py:330
  143.9 8.8 %collective-permute-start.10 = (bf16[96,1152]{1,0:T(8,128)(2,1)S(1)}, bf16[96,1152]{1,0:T(8,128)(2,1)S(1)}, u32[]{:S(2)}, u32[]{:S(2)}) collective-permute-start(bf16[96,1152]{1,0:T(8,128)(2,1)S(1)} %get-tuple-element.42.n0), channel_id=1, source_target_pairs={{0,128},{128,0},{1,129},{129,1},{2,130},{130,2},{3,131},{131,3},{4... | collective-permute-start | bytes 663560 | tf_op jit(solution)/shard_map/ppermute | solution.py:330
  144.0 9.9 %collective-permute-start.8 = (bf16[96,1152]{1,0:T(8,128)(2,1)S(1)}, bf16[96,1152]{1,0:T(8,128)(2,1)S(1)}, u32[]{:S(2)}, u32[]{:S(2)}) collective-permute-start(bf16[96,1152]{1,0:T(8,128)(2,1)S(1)} %get-tuple-element.42.n0), channel_id=1, source_target_pairs={{0,64},{64,0},{1,65},{65,1},{2,66},{66,2},{3,67},{67,3},{4,68},{68... | collective-permute-start | bytes 663560 | tf_op jit(solution)/shard_map/ppermute | solution.py:333
  152.6 1.8 %collective-permute-start.11 = (bf16[96,1152]{1,0:T(8,128)(2,1)S(1)}, bf16[96,1152]{1,0:T(8,128)(2,1)S(1)}, u32[]{:S(2)}, u32[]{:S(2)}) collective-permute-start(bf16[96,1152]{1,0:T(8,128)(2,1)S(1)} %collective-permute-done.10.n2), channel_id=1, source_target_pairs={{0,64},{64,0},{1,65},{65,1},{2,66},{66,2},{3,67},{67,3},{4,68},{68... | collective-permute-start | bytes 663560 | tf_op jit(solution)/shard_map/ppermute | solution.py:333
  153.4 3.2 %collective-permute-start.16 = (bf16[96,1152]{1,0:T(8,128)(2,1)S(1)}, bf16[96,1152]{1,0:T(8,128)(2,1)S(1)}, u32[]{:S(2)}, u32[]{:S(2)}) collective-permute-start(bf16[96,1152]{1,0:T(8,128)(2,1)S(1)} %get-tuple-element.43.n0), channel_id=1, source_target_pairs={{0,64},{64,0},{1,65},{65,1},{2,66},{66,2},{3,67},{67,3},{4,68},{68... | collective-permute-start | bytes 663560 | tf_op jit(solution)/shard_map/ppermute | solution.py:333
  153.4 3.2 %collective-permute-start.17 = (bf16[96,1152]{1,0:T(8,128)(2,1)S(1)}, bf16[96,1152]{1,0:T(8,128)(2,1)S(1)}, u32[]{:S(2)}, u32[]{:S(2)}) collective-permute-start(bf16[96,1152]{1,0:T(8,128)(2,1)S(1)} %collective-permute-done.9.n2), channel_id=1, source_target_pairs={{0,64},{64,0},{1,65},{65,1},{2,66},{66,2},{3,67},{67,3},{4,68},{68... | collective-permute-start | bytes 663560 | tf_op jit(solution)/shard_map/ppermute | solution.py:333
  156.6 8.8 %copy-start.4 = (bf16[576,1152]{1,0:T(8,128)(2,1)S(1)}, bf16[576,1152]{1,0:T(8,128)(2,1)}, u32[]{:S(2)}) copy-start(bf16[576,1152]{1,0:T(8,128)(2,1)} %copy-done.3) | copy-start | bytes 3981316
  158.7 2.4 %collective-permute-start.18 = (bf16[216,128]{1,0:T(8,128)(2,1)S(1)}, bf16[216,128]{1,0:T(8,128)(2,1)S(1)}, u32[]{:S(2)}, u32[]{:S(2)}) collective-permute-start(bf16[216,128]{1,0:T(8,128)(2,1)S(1)} %get-tuple-element.59), channel_id=1, source_target_pairs={{0,64},{64,0},{1,65},{65,1},{2,66},{66,2},{3,67},{67,3},{4,68},{68... | collective-permute-start | bytes 165896 | tf_op jit(solution)/shard_map/ppermute | solution.py:340
  159.2 3.3 %collective-permute-start.19 = (bf16[216,128]{1,0:T(8,128)(2,1)S(1)}, bf16[216,128]{1,0:T(8,128)(2,1)S(1)}, u32[]{:S(2)}, u32[]{:S(2)}) collective-permute-start(bf16[216,128]{1,0:T(8,128)(2,1)S(1)} %get-tuple-element.60), channel_id=1, source_target_pairs={{0,128},{128,0},{1,129},{129,1},{2,130},{130,2},{3,131},{131,3},{4... | collective-permute-start | bytes 165896 | tf_op jit(solution)/shard_map/ppermute | solution.py:341
  160.6 4.7 %collective-permute-start.20 = (bf16[216,128]{1,0:T(8,128)(2,1)S(1)}, bf16[216,128]{1,0:T(8,128)(2,1)S(1)}, u32[]{:S(2)}, u32[]{:S(2)}) collective-permute-start(bf16[216,128]{1,0:T(8,128)(2,1)S(1)} %get-tuple-element.61), channel_id=1, source_target_pairs={{0,192},{192,0},{64,128},{128,64},{1,193},{193,1},{65,129},{129,65... | collective-permute-start | bytes 165896 | tf_op jit(solution)/shard_map/ppermute | solution.py:342
  160.9 6.9 %collective-permute-start.12 = (bf16[216,128]{1,0:T(8,128)(2,1)S(1)}, bf16[216,128]{1,0:T(8,128)(2,1)S(1)}, u32[]{:S(2)}, u32[]{:S(2)}) collective-permute-start(bf16[216,128]{1,0:T(8,128)(2,1)S(1)} %get-tuple-element.47), channel_id=1, source_target_pairs={{0,64},{64,0},{1,65},{65,1},{2,66},{66,2},{3,67},{67,3},{4,68},{68... | collective-permute-start | bytes 165896 | tf_op jit(solution)/shard_map/ppermute | solution.py:340
  161.1 6.7 %collective-permute-start.13 = (bf16[216,128]{1,0:T(8,128)(2,1)S(1)}, bf16[216,128]{1,0:T(8,128)(2,1)S(1)}, u32[]{:S(2)}, u32[]{:S(2)}) collective-permute-start(bf16[216,128]{1,0:T(8,128)(2,1)S(1)} %get-tuple-element.48), channel_id=1, source_target_pairs={{0,128},{128,0},{1,129},{129,1},{2,130},{130,2},{3,131},{131,3},{4... | collective-permute-start | bytes 165896 | tf_op jit(solution)/shard_map/ppermute | solution.py:341
  162.5 5.3 %collective-permute-start.14 = (bf16[216,128]{1,0:T(8,128)(2,1)S(1)}, bf16[216,128]{1,0:T(8,128)(2,1)S(1)}, u32[]{:S(2)}, u32[]{:S(2)}) collective-permute-start(bf16[216,128]{1,0:T(8,128)(2,1)S(1)} %get-tuple-element.49), channel_id=1, source_target_pairs={{0,192},{192,0},{64,128},{128,64},{1,193},{193,1},{65,129},{129,65... | collective-permute-start | bytes 165896 | tf_op jit(solution)/shard_map/ppermute | solution.py:342
Sparse Core Ops, SparseCore 0:
  9.2 53.9 all-gather.3
  65.0 62.2 all-gather.5
